TPU v7x, 32 devices: a whole 2x2x4 slice. The times are simulated.
32 devices in a mesh: dom: 8 (over z, y), rep: 4 (over x, core).
Axes of the slice: x: 2, y: 2, z: 4, core: 2. Of those that a mesh axis runs over, the one named last changes fastest.
Arguments:
- node_feats: bfloat16 [4, 1024, 256], P('rep', 'dom'), may hold values from -6 to 6
- out_grad: bfloat16 [4, 1024, 256], P('rep', 'dom'), may hold values from -6 to 6
- norm1_gain: float32 [256], replicated, may hold values from 0.1 to 1.9
- w_query: bfloat16 [256, 256], replicated, may hold values from -0.375 to 0.375
- w_key: bfloat16 [256, 256], replicated, may hold values from -0.375 to 0.375
- w_value: bfloat16 [256, 256], replicated, may hold values from -0.375 to 0.375
- w_out: bfloat16 [256, 256], replicated, may hold values from -0.375 to 0.375
- norm2_gain: float32 [256], replicated, may hold values from 0.1 to 1.9
- w_up: bfloat16 [256, 512], replicated, may hold values from -0.375 to 0.375
- w_down: bfloat16 [512, 256], replicated, may hold values from -0.25 to 0.25
- local_gain: float32 [4], replicated, may hold values from 0.5 to 2
- expander_gain: float32 [4], replicated, may hold values from 2 to 8
- partner_perm: int32 [4, 4, 8, 128], P('rep', None, 'dom'), may hold values from 0 to 127, each once within a row
- block_pairs: int32 [4, 8, 1], P('rep', 'dom'), may hold values from 0 to 0, as said below
- pair_count: int32 [4, 8], P('rep', 'dom'), may hold values from 1 to 1, as said below
Outputs:
- node_out: bfloat16 [4, 1024, 256], P('rep', 'dom')
- grad_feats: bfloat16 [4, 1024, 256], P('rep', 'dom')
- grad_norm1_gain: float32 [256], replicated
- grad_w_query: float32 [256, 256], replicated
- grad_w_key: float32 [256, 256], replicated
- grad_w_value: float32 [256, 256], replicated
- grad_w_out: float32 [256, 256], replicated
- grad_norm2_gain: float32 [256], replicated
- grad_w_up: float32 [256, 512], replicated
- grad_w_down: float32 [512, 256], replicated
- grad_local_gain: float32 [4], replicated
- grad_expander_gain: float32 [4], replicated
Inputs may be any that keep to these rules, and one draw needn't show every extreme that they name: `partner_perm`: each row is a permutation of the 128 local node indices. `block_pairs`: an entry e names query block e // 1 and key block e % 1 of the same partition; the first pair_count entries of a partition are distinct, the rest are not edges. `pair_count`: in every cluster some partition has exactly 1 pairs and another exactly 1.
All inputs are finite; a program needn't handle non-finite values.
Results may differ from a plain program's by a relative error of at most 0.029.
Values may be sent and summed in bfloat16 or wider, within the bound.
No kernel may reach another device: no remote copies, remote signals or barrier semaphores. Data moves between devices by JAX's collectives and lax.ppermute only.
A program may use at most 64 MiB of HBM per device.

v0:
```python
import jax
import jax.numpy as jnp
from jax import lax
from jax.sharding import PartitionSpec as P

BLK = 128


EPSILON = 1e-05
SCORE_CAP = 5.0
GELU_ROOT = 0.7978845608028654
GELU_CUBIC = 0.044715


def swapped(x, axis, bit):
    return lax.ppermute(x, axis, [(i, i ^ 1 << bit) for i in range(lax.axis_size(axis))])


def gelu_parts(preact):
    tangent = jnp.tanh(GELU_ROOT * (preact + GELU_CUBIC * preact * preact * preact))
    result = 0.5 * preact * (1.0 + tangent)
    derivative = 0.5 * (1.0 + tangent) + 0.5 * preact * (1.0 - tangent * tangent) * GELU_ROOT * (
        1.0 + 3.0 * GELU_CUBIC * preact * preact
    )
    return (result, derivative)


def norm_forward(matrix):
    center = jnp.mean(matrix, axis=-1, keepdims=True)
    shifted = matrix - center
    inverse = lax.rsqrt(jnp.mean(shifted * shifted, axis=-1, keepdims=True) + EPSILON)
    return (shifted * inverse, inverse)


def norm_backward(upstream, normed, inverse, gain):
    scaled_up = upstream * gain
    return inverse * (
        scaled_up
        - jnp.mean(scaled_up, axis=-1, keepdims=True)
        - normed * jnp.mean(scaled_up * normed, axis=-1, keepdims=True)
    )


def project(first_op, second_op):
    return jnp.dot(first_op, second_op, preferred_element_type=jnp.float32)


def project_back(first_op, second_op):
    return lax.dot_general(
        first_op, second_op, (((1,), (1,)), ((), ())), preferred_element_type=jnp.float32
    )


def project_outer(first_op, second_op):
    return lax.dot_general(
        first_op, second_op, (((0,), (0,)), ((), ())), preferred_element_type=jnp.float32
    )


def soft_scores(query_tile, key_tile, gain_col, score_scale):
    raw_scores = (
        jnp.einsum("ihd,jhd->hij", query_tile, key_tile, preferred_element_type=jnp.float32)
        / score_scale
    )
    tangent = jnp.tanh(gain_col * raw_scores / SCORE_CAP)
    return (raw_scores, tangent, jnp.exp(SCORE_CAP * tangent))


def add_block(running, addend):
    return running + addend


def local(
    node_feats,
    out_grad,
    norm1_gain,
    w_query,
    w_key,
    w_value,
    w_out,
    norm2_gain,
    w_up,
    w_down,
    local_gain,
    expander_gain,
    partner_perm,
    block_pairs,
    pair_count,
):
    node_rows = node_feats[0]
    upstream = out_grad[0]
    partners = partner_perm[0, :, 0, :]
    listed = pair_count[0, 0]
    count_rows = node_rows.shape[0]
    width = node_rows.shape[1]
    heads = local_gain.shape[0]
    head_dim = width // heads
    matchings = partners.shape[0]
    levels = lax.axis_size("dom").bit_length() - 1
    score_scale = float(head_dim) ** 0.5
    local_col = local_gain[:, None, None]
    far_col = expander_gain[None, :, None]
    features = node_rows.astype(jnp.float32)
    normed1, inverse1 = norm_forward(features)
    hidden = (normed1 * norm1_gain).astype(jnp.bfloat16)
    queries = project(hidden, w_query).astype(jnp.bfloat16)
    key_rows = project(hidden, w_key).astype(jnp.bfloat16)
    value_rows = project(hidden, w_value).astype(jnp.bfloat16)
    far_keys = []
    far_values = []
    for matching in range(matchings):
        flip_bit = (levels - 1 - matching) % levels
        picked = partners[matching]
        their_keys, their_values = swapped((key_rows, value_rows), "dom", flip_bit)
        far_keys.append(their_keys[picked])
        far_values.append(their_values[picked])
    query_heads = queries.reshape(count_rows, heads, head_dim)
    far_key_heads = jnp.stack(far_keys).reshape(matchings, count_rows, heads, head_dim)
    far_value_heads = jnp.stack(far_values).reshape(matchings, count_rows, heads, head_dim)
    raw_far = (
        jnp.einsum("ihd,mihd->mhi", query_heads, far_key_heads, preferred_element_type=jnp.float32)
        / score_scale
    )
    tanh_far = jnp.tanh(far_col * raw_far / SCORE_CAP)
    exp_far = jnp.exp(SCORE_CAP * tanh_far)
    far_total = jnp.sum(exp_far, axis=0)

    def slice_heads(matrix):
        return matrix.reshape(BLK, heads, head_dim)

    def add_total(position, running):
        _, _, exp_tile = soft_scores(
            slice_heads(queries), slice_heads(key_rows), local_col, score_scale
        )
        return add_block(running, jnp.sum(exp_tile, axis=-1))

    denominator = lax.fori_loop(0, listed, add_total, far_total)
    weight_far = (exp_far / denominator[None]).astype(jnp.bfloat16)
    far_part = jnp.einsum(
        "mhi,mihd->ihd", weight_far, far_value_heads, preferred_element_type=jnp.float32
    ).reshape(count_rows, width)

    def add_rows(position, running):
        _, _, exp_tile = soft_scores(
            slice_heads(queries), slice_heads(key_rows), local_col, score_scale
        )
        weight_tile = (exp_tile / denominator[:, :, None]).astype(jnp.bfloat16)
        addend = jnp.einsum(
            "hij,jhd->ihd", weight_tile, slice_heads(value_rows), preferred_element_type=jnp.float32
        ).reshape(BLK, width)
        return add_block(running, addend)

    attended32 = lax.fori_loop(0, listed, add_rows, far_part)
    attended = attended32.astype(jnp.bfloat16)
    mixed = (features + project(attended, w_out)).astype(jnp.bfloat16)
    normed2, inverse2 = norm_forward(mixed.astype(jnp.float32))
    hidden2 = (normed2 * norm2_gain).astype(jnp.bfloat16)
    preact = project(hidden2, w_up)
    activ, derivative = gelu_parts(preact)
    activ = activ.astype(jnp.bfloat16)
    node_out = (mixed.astype(jnp.float32) + project(activ, w_down)).astype(jnp.bfloat16)
    grad_down = project_outer(activ, upstream)
    grad_pre = (project_back(upstream, w_down) * derivative).astype(jnp.bfloat16)
    grad_up = project_outer(hidden2, grad_pre)
    grad_hidden2 = project_back(grad_pre, w_up)
    grad_gain2 = jnp.sum(grad_hidden2 * normed2, axis=0)
    grad_mixed = upstream.astype(jnp.float32) + norm_backward(
        grad_hidden2, normed2, inverse2, norm2_gain
    )
    grad_mixed16 = grad_mixed.astype(jnp.bfloat16)
    grad_wout = project_outer(attended, grad_mixed16)
    grad_att = project_back(grad_mixed16, w_out).astype(jnp.bfloat16)
    grad_heads = grad_att.reshape(count_rows, heads, head_dim)
    delta = jnp.sum(
        (grad_att.astype(jnp.float32) * attended32).reshape(count_rows, heads, head_dim), axis=-1
    ).T
    dots_far = jnp.einsum(
        "ihd,mihd->mhi", grad_heads, far_value_heads, preferred_element_type=jnp.float32
    )
    dlogit_far = weight_far.astype(jnp.float32) * (dots_far - delta[None])
    slope_far = 1.0 - tanh_far * tanh_far
    far_gain_grad = jnp.sum(dlogit_far * raw_far * slope_far, axis=(0, 2))
    dscore_far = (dlogit_far * far_col * slope_far / score_scale).astype(jnp.bfloat16)
    grad_query32 = jnp.einsum(
        "mhi,mihd->ihd", dscore_far, far_key_heads, preferred_element_type=jnp.float32
    ).reshape(count_rows, width)
    key_terms = (
        jnp.einsum("mhi,ihd->mihd", dscore_far, query_heads, preferred_element_type=jnp.float32)
        .astype(jnp.bfloat16)
        .reshape(matchings, count_rows, width)
    )
    value_terms = (
        jnp.einsum("mhi,ihd->mihd", weight_far, grad_heads, preferred_element_type=jnp.float32)
        .astype(jnp.bfloat16)
        .reshape(matchings, count_rows, width)
    )
    returned = []
    for matching in range(matchings):
        flip_bit = (levels - 1 - matching) % levels
        placed_keys = (
            jnp.zeros((count_rows, width), jnp.bfloat16)
            .at[partners[matching]]
            .set(key_terms[matching])
        )
        placed_values = (
            jnp.zeros((count_rows, width), jnp.bfloat16)
            .at[partners[matching]]
            .set(value_terms[matching])
        )
        returned.append(swapped((placed_keys, placed_values), "dom", flip_bit))
    zero_rows = jnp.zeros((count_rows, width), jnp.float32)
    zero_gain = jnp.zeros((heads,), jnp.float32)

    def add_grads(position, running):
        query_acc, key_acc, value_acc, gain_acc = running
        query_tile = slice_heads(queries)
        key_tile = slice_heads(key_rows)
        value_tile = slice_heads(value_rows)
        grad_tile = slice_heads(grad_att)
        raw_tile, tanh_tile, exp_tile = soft_scores(query_tile, key_tile, local_col, score_scale)
        weight_tile = (exp_tile / denominator[:, :, None]).astype(jnp.bfloat16)
        dots_tile = jnp.einsum(
            "ihd,jhd->hij", grad_tile, value_tile, preferred_element_type=jnp.float32
        )
        dlogit_tile = weight_tile.astype(jnp.float32) * (dots_tile - delta[:, :, None])
        slope_tile = 1.0 - tanh_tile * tanh_tile
        gain_acc = gain_acc + jnp.sum(dlogit_tile * raw_tile * slope_tile, axis=(1, 2))
        dscore_tile = (dlogit_tile * local_col * slope_tile / score_scale).astype(jnp.bfloat16)
        query_acc = add_block(
            query_acc,
            jnp.einsum(
                "hij,jhd->ihd", dscore_tile, key_tile, preferred_element_type=jnp.float32
            ).reshape(BLK, width),
        )
        key_acc = add_block(
            key_acc,
            jnp.einsum(
                "hij,ihd->jhd", dscore_tile, query_tile, preferred_element_type=jnp.float32
            ).reshape(BLK, width),
        )
        value_acc = add_block(
            value_acc,
            jnp.einsum(
                "hij,ihd->jhd", weight_tile, grad_tile, preferred_element_type=jnp.float32
            ).reshape(BLK, width),
        )
        return (query_acc, key_acc, value_acc, gain_acc)

    grad_query32, grad_key32, grad_value32, local_gain_grad = lax.fori_loop(
        0, listed, add_grads, (grad_query32, zero_rows, zero_rows, zero_gain)
    )
    for back_keys, back_values in returned:
        grad_key32 = grad_key32 + back_keys.astype(jnp.float32)
        grad_value32 = grad_value32 + back_values.astype(jnp.float32)
    grad_query16 = grad_query32.astype(jnp.bfloat16)
    grad_key16 = grad_key32.astype(jnp.bfloat16)
    grad_value16 = grad_value32.astype(jnp.bfloat16)
    grad_wq = project_outer(hidden, grad_query16)
    grad_wk = project_outer(hidden, grad_key16)
    grad_wv = project_outer(hidden, grad_value16)
    grad_hidden = (
        project_back(grad_query16, w_query)
        + project_back(grad_key16, w_key)
        + project_back(grad_value16, w_value)
    )
    grad_gain1 = jnp.sum(grad_hidden * normed1, axis=0)
    grad_feats = (grad_mixed + norm_backward(grad_hidden, normed1, inverse1, norm1_gain)).astype(
        jnp.bfloat16
    )
    (
        grad_gain1,
        grad_wq,
        grad_wk,
        grad_wv,
        grad_wout,
        grad_gain2,
        grad_up,
        grad_down,
        local_gain_grad,
        far_gain_grad,
    ) = lax.psum(
        (
            grad_gain1,
            grad_wq,
            grad_wk,
            grad_wv,
            grad_wout,
            grad_gain2,
            grad_up,
            grad_down,
            local_gain_grad,
            far_gain_grad,
        ),
        ("dom", "rep"),
    )
    return (
        node_out[None],
        grad_feats[None],
        grad_gain1,
        grad_wq,
        grad_wk,
        grad_wv,
        grad_wout,
        grad_gain2,
        grad_up,
        grad_down,
        local_gain_grad,
        far_gain_grad,
    )


def solution(mesh):
    return jax.shard_map(
        local,
        mesh=mesh,
        in_specs=(
            P("rep", "dom", None),
            P("rep", "dom", None),
            P(),
            P(),
            P(),
            P(),
            P(),
            P(),
            P(),
            P(),
            P(),
            P(),
            P("rep", None, "dom", None),
            P("rep", "dom", None),
            P("rep", "dom"),
        ),
        out_specs=(
            P("rep", "dom", None),
            P("rep", "dom", None),
            P(),
            P(),
            P(),
            P(),
            P(),
            P(),
            P(),
            P(),
            P(),
            P(),
        ),
        check_vma=False,
    )
```

profile of v0, /device:TPU:0, one launch (start us, length us, event | category | flops | bytes accessed | tf_op | source)
XLA Modules:
  0.0 221.4 jit_solution(14727711323036403174)
XLA Ops:
  7.2 1.0 convert_reduce_fusion
  9.1 1.2 convolution_convert_fusion.3
  10.3 3.0 %collective-permute-start.2 = (bf16[128,256]{1,0:T(8,128)(2,1)S(1)}, bf16[128,256]{1,0:T(8,128)(2,1)S(1)}, u32[]{:S(2)}, u32[]{:S(2)}) collective-permute-start(bf16[128,256]{1,0:T(8,128)(2,1)S(1)} %convolution_convert_fusion.3), channel_id=1, source_target_pairs={{0,4},{4,0},{8,12},{12,8},{16,20},{20,16},{24,28},{28,24},{1,5},{5... | collective-permute-start | bytes 196616 | tf_op jit(solution)/shard_map/ppermute | solution.py:16
  13.3 1.6 collective-permute-start.1
  14.9 2.6 %collective-permute-start = (bf16[128,256]{1,0:T(8,128)(2,1)S(1)}, bf16[128,256]{1,0:T(8,128)(2,1)S(1)}, u32[]{:S(2)}, u32[]{:S(2)}) collective-permute-start(bf16[128,256]{1,0:T(8,128)(2,1)S(1)} %convolution_convert_fusion.3), channel_id=1, source_target_pairs={{0,16},{4,20},{8,24},{12,28},{16,0},{20,4},{24,8},{28,12},{1,17},{... | collective-permute-start | bytes 196616 | tf_op jit(solution)/shard_map/ppermute | solution.py:16
  21.8 0.8 gather_fusion.2
  22.7 0.8 gather_fusion.1
  23.7 0.8 gather_fusion
  24.7 0.9 gather_fusion.3
  25.7 0.8 gather_fusion.6
  26.6 0.8 gather_fusion.5
  27.6 0.8 gather_fusion.4
  28.6 0.9 gather_fusion.7
  29.7 1.3 while.42
  31.5 1.3 while.43
  33.0 0.8 copy-done.4
  38.2 0.9 fusion.53
  39.4 1.4 while.44
  41.0 1.0 fusion.49
  42.0 1.1 fusion.67
  43.2 1.1 fusion.30
  44.7 1.0 scatter_custom_fusion.4
  45.7 1.0 scatter_custom_fusion.7
  46.9 1.0 scatter_custom_fusion.6
  48.0 1.0 scatter_custom_fusion.5
  49.1 2.0 collective-permute-start.11
  51.1 1.5 collective-permute-start.12
  52.6 2.6 %collective-permute-start.13 = (bf16[128,256]{1,0:T(8,128)(2,1)S(1)}, bf16[128,256]{1,0:T(8,128)(2,1)S(1)}, u32[]{:S(2)}, u32[]{:S(2)}) collective-permute-start(bf16[128,256]{1,0:T(8,128)(2,1)S(1)} %scatter_custom_fusion.7), channel_id=1, source_target_pairs={{0,16},{4,20},{8,24},{12,28},{16,0},{20,4},{24,8},{28,12},{1,17},{... | collective-permute-start | bytes 196616 | tf_op jit(solution)/shard_map/ppermute | solution.py:16
  55.5 0.9 fusion.5
  56.5 1.0 scatter_custom_fusion
  57.6 1.2 scatter_custom_fusion.3
  59.0 1.0 scatter_custom_fusion.2
  60.2 1.0 scatter_custom_fusion.1
  62.2 2.9 %collective-permute-start.9 = (bf16[128,256]{1,0:T(8,128)(2,1)S(1)}, bf16[128,256]{1,0:T(8,128)(2,1)S(1)}, u32[]{:S(2)}, u32[]{:S(2)}) collective-permute-start(bf16[128,256]{1,0:T(8,128)(2,1)S(1)} %scatter_custom_fusion.3), channel_id=1, source_target_pairs={{0,16},{4,20},{8,24},{12,28},{16,0},{20,4},{24,8},{28,12},{1,17},{... | collective-permute-start | bytes 196616 | tf_op jit(solution)/shard_map/ppermute | solution.py:16
  65.2 1.0 fusion.69
  66.3 1.1 collective-permute-done.9
  67.4 2.9 %collective-permute-done.6 = bf16[128,256]{1,0:T(8,128)(2,1)S(1)} collective-permute-done((bf16[128,256]{1,0:T(8,128)(2,1)S(1)}, bf16[128,256]{1,0:T(8,128)(2,1)S(1)}, u32[]{:S(2)}, u32[]{:S(2)}) %collective-permute-start.6) | collective-permute-done | bytes 65568 | tf_op jit(solution)/shard_map/ppermute | solution.py:16
  70.3 1.0 fusion.71
  71.3 0.9 copy-done.10
  72.7 40.5 %all-reduce = (f32[256]{0:T(256)}, f32[256]{0:T(256)}, f32[4]{0:T(128)}, f32[4]{0:T(128)}) all-reduce(f32[256]{0:T(256)S(1)} %get-tuple-element.340, f32[256]{0:T(256)S(1)} %get-tuple-element.338, f32[4]{0:T(128)S(1)} %get-tuple-element.323, f32[4]{0:T(128)S(1)} %get-tuple-element.406), channel_id=1, replica_groups=mesh['dom'=8,'rep'=4] {'dom','rep'}, use_global_device_ids=true, to_apply=%region_27.0 | all-reduce | flops 520 | bytes 4160 | tf_op jit(solution)/shard_map/psum | solution.py:281
  113.3 0.8 fusion.29
  114.1 94.3 %all-reduce.4.cloned.1.call-done = (f32[256,256]{1,0:T(8,128)}, f32[256,256]{1,0:T(8,128)}, f32[256,256]{1,0:T(8,128)}, f32[256,256]{1,0:T(8,128)}, f32[256,512]{1,0:T(8,128)}, /*index=5*/f32[512,256]{1,0:T(8,128)}) async-done(((f32[256,256]{1,0:T(8,128)}, f32[256,256]{1,0:T(8,128)}, f32[256,256]{1,0:T(8,128)}, f32[256,256]{1,0:T(8,128)}, f32[256,512]{1,0:T(8,128)}, /*index=5*/f32[512,256]{1,0:T(8,128)}), ...) | async-done | bytes 2097168 | tf_op jit(solution)/shard_map/psum | solution.py:281
  208.4 1.7 copy.167
  210.1 0.7 copy.168
  211.1 0.7 copy.169
  211.8 0.7 copy.170
  212.5 0.8 copy.171
  213.8 0.8 copy.172
  (143 shorter events, 15.5 us)
Async XLA Ops:
  7.2 27.1 %copy-start = (bf16[256,512]{1,0:T(8,128)(2,1)S(1)}, bf16[256,512]{1,0:T(8,128)(2,1)}, u32[]{:S(2)}) copy-start(bf16[256,512]{1,0:T(8,128)(2,1)} %param.29) | copy-start | bytes 786436
  7.2 1.1 copy-start.1
  7.2 201.2 %all-reduce.4.cloned.1.call-start = ((), (), s32[]{:S(2)}) async-start(), calls=%async_computation | async-start | bytes 4194304 | tf_op jit(solution)/shard_map/psum | solution.py:281
  8.4 0.7 copy-start.12
  9.1 8.4 %copy-start.11 = (bf16[256,256]{1,0:T(8,128)(2,1)S(1)}, bf16[256,256]{1,0:T(8,128)(2,1)}, u32[]{:S(2)}) copy-start(bf16[256,256]{1,0:T(8,128)(2,1)} %param.26) | copy-start | bytes 393220
  10.3 11.4 %collective-permute-start.2 = (bf16[128,256]{1,0:T(8,128)(2,1)S(1)}, bf16[128,256]{1,0:T(8,128)(2,1)S(1)}, u32[]{:S(2)}, u32[]{:S(2)}) collective-permute-start(bf16[128,256]{1,0:T(8,128)(2,1)S(1)} %convolution_convert_fusion.3), channel_id=1, source_target_pairs={{0,4},{4,0},{8,12},{12,8},{16,20},{20,16},{24,28},{28,24},{1,5},{5... | collective-permute-start | bytes 196616 | tf_op jit(solution)/shard_map/ppermute | solution.py:16
  13.3 9.4 %collective-permute-start.1 = (bf16[128,256]{1,0:T(8,128)(2,1)S(1)}, bf16[128,256]{1,0:T(8,128)(2,1)S(1)}, u32[]{:S(2)}, u32[]{:S(2)}) collective-permute-start(bf16[128,256]{1,0:T(8,128)(2,1)S(1)} %convolution_convert_fusion.3), channel_id=1, source_target_pairs={{0,8},{4,12},{8,0},{12,4},{16,24},{20,28},{24,16},{28,20},{1,9},{5... | collective-permute-start | bytes 196616 | tf_op jit(solution)/shard_map/ppermute | solution.py:16
  14.9 8.8 %collective-permute-start = (bf16[128,256]{1,0:T(8,128)(2,1)S(1)}, bf16[128,256]{1,0:T(8,128)(2,1)S(1)}, u32[]{:S(2)}, u32[]{:S(2)}) collective-permute-start(bf16[128,256]{1,0:T(8,128)(2,1)S(1)} %convolution_convert_fusion.3), channel_id=1, source_target_pairs={{0,16},{4,20},{8,24},{12,28},{16,0},{20,4},{24,8},{28,12},{1,17},{... | collective-permute-start | bytes 196616 | tf_op jit(solution)/shard_map/ppermute | solution.py:16
  17.7 8.0 %collective-permute-start.5 = (bf16[128,256]{1,0:T(8,128)(2,1)S(1)}, bf16[128,256]{1,0:T(8,128)(2,1)S(1)}, u32[]{:S(2)}, u32[]{:S(2)}) collective-permute-start(bf16[128,256]{1,0:T(8,128)(2,1)S(1)} %convolution_convert_fusion.1), channel_id=1, source_target_pairs={{0,4},{4,0},{8,12},{12,8},{16,20},{20,16},{24,28},{28,24},{1,5},{5... | collective-permute-start | bytes 196616 | tf_op jit(solution)/shard_map/ppermute | solution.py:16
  18.3 8.4 %collective-permute-start.4 = (bf16[128,256]{1,0:T(8,128)(2,1)S(1)}, bf16[128,256]{1,0:T(8,128)(2,1)S(1)}, u32[]{:S(2)}, u32[]{:S(2)}) collective-permute-start(bf16[128,256]{1,0:T(8,128)(2,1)S(1)} %convolution_convert_fusion.1), channel_id=1, source_target_pairs={{0,8},{4,12},{8,0},{12,4},{16,24},{20,28},{24,16},{28,20},{1,9},{5... | collective-permute-start | bytes 196616 | tf_op jit(solution)/shard_map/ppermute | solution.py:16
  18.7 0.9 copy-start.9
  20.0 0.7 copy-start.18
  20.0 0.7 copy-start.15
  20.7 0.7 copy-start.14
  21.7 5.9 %collective-permute-start.3 = (bf16[128,256]{1,0:T(8,128)(2,1)S(1)}, bf16[128,256]{1,0:T(8,128)(2,1)S(1)}, u32[]{:S(2)}, u32[]{:S(2)}) collective-permute-start(bf16[128,256]{1,0:T(8,128)(2,1)S(1)} %convolution_convert_fusion.1), channel_id=1, source_target_pairs={{0,16},{4,20},{8,24},{12,28},{16,0},{20,4},{24,8},{28,12},{1,17},{... | collective-permute-start | bytes 196616 | tf_op jit(solution)/shard_map/ppermute | solution.py:16
  32.9 0.9 copy-start.4
  34.3 0.7 copy-start.13
  35.0 0.8 copy-start.8
  35.0 1.0 copy-start.16
  44.7 10.8 %copy-start.17 = (bf16[512,256]{1,0:T(8,128)(2,1)S(1)}, bf16[512,256]{1,0:T(8,128)(2,1)}, u32[]{:S(2)}) copy-start(bf16[512,256]{1,0:T(8,128)(2,1)} %param.30) | copy-start | bytes 786436
  49.1 12.8 %collective-permute-start.11 = (bf16[128,256]{1,0:T(8,128)(2,1)S(1)}, bf16[128,256]{1,0:T(8,128)(2,1)S(1)}, u32[]{:S(2)}, u32[]{:S(2)}) collective-permute-start(bf16[128,256]{1,0:T(8,128)(2,1)S(1)} %scatter_custom_fusion.5), channel_id=1, source_target_pairs={{0,8},{4,12},{8,0},{12,4},{16,24},{20,28},{24,16},{28,20},{1,9},{5... | collective-permute-start | bytes 196616 | tf_op jit(solution)/shard_map/ppermute | solution.py:16
  51.1 11.2 %collective-permute-start.12 = (bf16[128,256]{1,0:T(8,128)(2,1)S(1)}, bf16[128,256]{1,0:T(8,128)(2,1)S(1)}, u32[]{:S(2)}, u32[]{:S(2)}) collective-permute-start(bf16[128,256]{1,0:T(8,128)(2,1)S(1)} %scatter_custom_fusion.6), channel_id=1, source_target_pairs={{0,4},{4,0},{8,12},{12,8},{16,20},{20,16},{24,28},{28,24},{1,5},{5... | collective-permute-start | bytes 196616 | tf_op jit(solution)/shard_map/ppermute | solution.py:16
  52.6 12.5 %collective-permute-start.13 = (bf16[128,256]{1,0:T(8,128)(2,1)S(1)}, bf16[128,256]{1,0:T(8,128)(2,1)S(1)}, u32[]{:S(2)}, u32[]{:S(2)}) collective-permute-start(bf16[128,256]{1,0:T(8,128)(2,1)S(1)} %scatter_custom_fusion.7), channel_id=1, source_target_pairs={{0,16},{4,20},{8,24},{12,28},{16,0},{20,4},{24,8},{28,12},{1,17},{... | collective-permute-start | bytes 196616 | tf_op jit(solution)/shard_map/ppermute | solution.py:16
  55.2 10.0 %collective-permute-start.10 = (bf16[128,256]{1,0:T(8,128)(2,1)S(1)}, bf16[128,256]{1,0:T(8,128)(2,1)S(1)}, u32[]{:S(2)}, u32[]{:S(2)}) collective-permute-start(bf16[128,256]{1,0:T(8,128)(2,1)S(1)} %scatter_custom_fusion.4), channel_id=1, source_target_pairs={{0,16},{4,20},{8,24},{12,28},{16,0},{20,4},{24,8},{28,12},{1,17},{... | collective-permute-start | bytes 196616 | tf_op jit(solution)/shard_map/ppermute | solution.py:16
  61.2 5.0 %collective-permute-start.7 = (bf16[128,256]{1,0:T(8,128)(2,1)S(1)}, bf16[128,256]{1,0:T(8,128)(2,1)S(1)}, u32[]{:S(2)}, u32[]{:S(2)}) collective-permute-start(bf16[128,256]{1,0:T(8,128)(2,1)S(1)} %scatter_custom_fusion.1), channel_id=1, source_target_pairs={{0,8},{4,12},{8,0},{12,4},{16,24},{20,28},{24,16},{28,20},{1,9},{5... | collective-permute-start | bytes 196616 | tf_op jit(solution)/shard_map/ppermute | solution.py:16
  61.9 4.3 %collective-permute-start.8 = (bf16[128,256]{1,0:T(8,128)(2,1)S(1)}, bf16[128,256]{1,0:T(8,128)(2,1)S(1)}, u32[]{:S(2)}, u32[]{:S(2)}) collective-permute-start(bf16[128,256]{1,0:T(8,128)(2,1)S(1)} %scatter_custom_fusion.2), channel_id=1, source_target_pairs={{0,4},{4,0},{8,12},{12,8},{16,20},{20,16},{24,28},{28,24},{1,5},{5... | collective-permute-start | bytes 196616 | tf_op jit(solution)/shard_map/ppermute | solution.py:16
  62.2 5.2 %collective-permute-start.9 = (bf16[128,256]{1,0:T(8,128)(2,1)S(1)}, bf16[128,256]{1,0:T(8,128)(2,1)S(1)}, u32[]{:S(2)}, u32[]{:S(2)}) collective-permute-start(bf16[128,256]{1,0:T(8,128)(2,1)S(1)} %scatter_custom_fusion.3), channel_id=1, source_target_pairs={{0,16},{4,20},{8,24},{12,28},{16,0},{20,4},{24,8},{28,12},{1,17},{... | collective-permute-start | bytes 196616 | tf_op jit(solution)/shard_map/ppermute | solution.py:16
  65.1 5.2 %collective-permute-start.6 = (bf16[128,256]{1,0:T(8,128)(2,1)S(1)}, bf16[128,256]{1,0:T(8,128)(2,1)S(1)}, u32[]{:S(2)}, u32[]{:S(2)}) collective-permute-start(bf16[128,256]{1,0:T(8,128)(2,1)S(1)} %scatter_custom_fusion), channel_id=1, source_target_pairs={{0,16},{4,20},{8,24},{12,28},{16,0},{20,4},{24,8},{28,12},{1,17},{... | collective-permute-start | bytes 196616 | tf_op jit(solution)/shard_map/ppermute | solution.py:16
  71.3 0.9 copy-start.10
  208.4 1.7 copy-start.7
  210.1 1.0 copy-start.6
  210.1 1.8 copy-start.5
  211.1 1.4 copy-start.3
  212.5 1.2 copy-start.2
Sparse Core Ops, SparseCore 0:
  71.5 136.8 all-reduce.3
where the time goes:
time: 222 us; the launch traced here: 221 us
  waiting for transfers between devices  98.4 us (44%)
  blocking collectives  40.5 us (18%)
  local copies, waits for them, and re-layouts  29.9 us (13%)
  starting transfers between devices  18.5 us (8%)
  between operations  14.8 us (7%)
  matrix products  11.9 us (5%)
  loops' own time  3.96 us (2%)
  other arithmetic  3.5 us (2%)
    psum x1, waiting for transfers between devices, local(): lax.psum((grad_gain1, grad_wq, grad_wk, grad_wv, grad_wout, grad_gain2, g...  94.3 us
    psum x1, blocking collectives, local(): lax.psum((grad_gain1, grad_wq, grad_wk, grad_wv, grad_wout, grad_gain2, g...  40.5 us
    ppermute x14, starting transfers between devices, swapped(): lax.ppermute(x, axis, [(i, i ^ 1 << bit) for i in range(lax.axis_size(axi...  18.4 us
    unnamed x46, local copies, waits for them, and re-layouts  12.2 us
    dot_general x6, matrix products, project_outer(): lax.dot_general(first_op, second_op, (((0,), (0,)), ((), ())), preferred_...  6.09 us
  transfers between devices with their start and end apart: 15, of which 3 were waited for; matrix products, arithmetic and copies ran while one was open for 7% of the time, Pallas kernels for 0%

commit v1 on v0

v1 whole, which is shorter than its diff:
```python
import functools

import jax
import jax.numpy as jnp
from jax import lax
from jax.experimental import pallas as pl
from jax.experimental.pallas import tpu as pltpu
from jax.sharding import PartitionSpec as P

EPSILON = 1e-05
SCORE_CAP = 5.0
GELU_ROOT = 0.7978845608028654
GELU_CUBIC = 0.044715
SMALL = 16
AXES = ("dom", "rep")
VMEM_LIMIT = 48 * 1024 * 1024
F32 = jnp.float32
BF16 = jnp.bfloat16


def dot(a, b):
    return lax.dot_general(a, b, (((1,), (0,)), ((), ())), preferred_element_type=F32)


def dot_rhs_t(a, b):
    return lax.dot_general(a, b, (((1,), (1,)), ((), ())), preferred_element_type=F32)


def dot_lhs_t(a, b):
    return lax.dot_general(a, b, (((0,), (0,)), ((), ())), preferred_element_type=F32)


def norm_forward(matrix):
    center = jnp.mean(matrix, axis=-1, keepdims=True)
    shifted = matrix - center
    inverse = lax.rsqrt(jnp.mean(shifted * shifted, axis=-1, keepdims=True) + EPSILON)
    return (shifted * inverse, inverse)


def norm_backward(upstream, normed, inverse, gain):
    scaled_up = upstream * gain
    return inverse * (
        scaled_up
        - jnp.mean(scaled_up, axis=-1, keepdims=True)
        - normed * jnp.mean(scaled_up * normed, axis=-1, keepdims=True)
    )


def gelu_parts(preact):
    tangent = jnp.tanh(GELU_ROOT * (preact + GELU_CUBIC * preact * preact * preact))
    result = 0.5 * preact * (1.0 + tangent)
    derivative = 0.5 * (1.0 + tangent) + 0.5 * preact * (1.0 - tangent * tangent) * GELU_ROOT * (
        1.0 + 3.0 * GELU_CUBIC * preact * preact
    )
    return (result, derivative)


def split_parts(rows):
    high = rows.astype(BF16).astype(F32)
    return jnp.concatenate([high, rows - high], axis=0).astype(BF16)


def join_parts(packed):
    wide = packed.astype(F32)
    return wide[: SMALL // 2] + wide[SMALL // 2 :]


def device_bits():
    flat = lax.axis_index("dom") * lax.axis_size("rep") + lax.axis_index("rep")
    core = flat & 1
    first = (flat >> 1) & 1
    second = (flat >> 2) & 1
    swap = core == 1
    return (core, jnp.where(swap, second, first), jnp.where(swap, first, second))


def layer_kernel(groups, *refs):
    count = len(groups)
    feats_refs = refs[: count + 1]
    (
        up_ref,
        gain1_ref,
        wq_ref,
        wk_ref,
        wv_ref,
        wo_ref,
        gain2_ref,
        wup_ref,
        wdown_ref,
        local_ref,
        far_ref,
        perm_ref,
    ) = refs[count + 1 : count + 13]
    out_ref, keep_ref, send_ref, small_ref, own_ref, mixed_ref = refs[count + 13 : count + 19]
    back_refs = refs[count + 19 : 2 * count + 19]
    raw_s, tanh_s, weight_s, dscore_s = refs[2 * count + 19 :]

    rows, width = out_ref.shape
    heads = local_ref.shape[0]
    head_dim = width // heads
    scale = 1.0 / float(head_dim) ** 0.5
    core, level1, level2 = device_bits()
    half = 4 * width

    def put(chunk, value):
        value = value.astype(BF16)
        upper = (chunk >> 1) & 1
        lower = chunk & 1
        same = core == (chunk >> 2)

        @pl.when(same)
        def _():
            rel = (upper ^ level1) * 2 + (lower ^ level2)
            keep_ref[pl.ds(pl.multiple_of(rel * width, width), width), :] = value

        @pl.when(jnp.logical_not(same))
        def _():
            rel = (upper ^ level2) * 2 + (lower ^ level1)
            send_ref[pl.ds(pl.multiple_of(rel * width, width), width), :] = value

    gain1 = gain1_ref[...]
    gain2 = gain2_ref[...]
    upstream = up_ref[...]
    feats = jnp.concatenate([ref[...] for ref in feats_refs], axis=0).astype(F32)
    normed1, _ = norm_forward(feats)
    hidden = (normed1 * gain1).astype(BF16)
    queries = dot(hidden[:rows], wq_ref[...])
    key_all = dot(hidden, wk_ref[...]).astype(BF16)
    value_all = dot(hidden, wv_ref[...]).astype(BF16)

    lane = lax.broadcasted_iota(jnp.int32, (rows, width), 1) // head_dim
    head_masks = [lane == h for h in range(heads)]

    def stacked(matrix):
        return jnp.concatenate([jnp.where(m, matrix, 0.0) for m in head_masks], axis=0).astype(BF16)

    query_stack = stacked(queries)
    raw_s[...] = dot_rhs_t(query_stack, key_all) * scale

    target = lax.broadcasted_iota(jnp.int32, (rows, rows), 0)
    counts = []
    for members in groups:
        total = 0.0
        for m in members:
            total = total + jnp.where(target == perm_ref[m : m + 1, :], 1.0, 0.0)
        counts.append(total.T)
    far_counts = jnp.concatenate(counts, axis=1)

    for h in range(heads):
        block = pl.ds(h * rows, rows)
        tl = jnp.tanh(raw_s[block, :rows] * (local_ref[h] / SCORE_CAP))
        tf = jnp.tanh(raw_s[block, rows:] * (far_ref[h] / SCORE_CAP))
        el = jnp.exp(SCORE_CAP * tl)
        ef = jnp.exp(SCORE_CAP * tf) * far_counts
        inv = 1.0 / (jnp.sum(el, axis=1, keepdims=True) + jnp.sum(ef, axis=1, keepdims=True))
        tanh_s[block, :rows] = tl
        tanh_s[block, rows:] = tf
        weight_s[block, :rows] = (el * inv).astype(BF16)
        weight_s[block, rows:] = (ef * inv).astype(BF16)

    def collapse(matrix):
        total = jnp.where(head_masks[0], matrix[:rows], 0.0)
        for h in range(1, heads):
            total = total + jnp.where(head_masks[h], matrix[h * rows : (h + 1) * rows], 0.0)
        return total

    attended32 = collapse(dot(weight_s[...], value_all))
    attended = attended32.astype(BF16)
    mixed = (feats[:rows] + dot(attended, wo_ref[...])).astype(BF16)
    normed2, inverse2 = norm_forward(mixed.astype(F32))
    hidden2 = (normed2 * gain2).astype(BF16)
    preact = dot(hidden2, wup_ref[...])
    act32, derivative = gelu_parts(preact)
    act = act32.astype(BF16)
    out_ref[...] = (mixed.astype(F32) + dot(act, wdown_ref[...])).astype(BF16)
    grad_down = dot_lhs_t(act, upstream)
    put(6, grad_down[:width])
    put(7, grad_down[width:])
    grad_pre = (dot_rhs_t(upstream, wdown_ref[...]) * derivative).astype(BF16)
    grad_up = dot_lhs_t(hidden2, grad_pre)
    put(4, grad_up[:, :width])
    put(5, grad_up[:, width:])
    grad_hidden2 = dot_rhs_t(grad_pre, wup_ref[...])
    grad_gain2 = jnp.sum(grad_hidden2 * normed2, axis=0, keepdims=True)
    grad_mixed = upstream.astype(F32) + norm_backward(grad_hidden2, normed2, inverse2, gain2)
    mixed_ref[...] = grad_mixed
    grad_mixed16 = grad_mixed.astype(BF16)
    put(3, dot_lhs_t(attended, grad_mixed16))
    grad_att = dot_rhs_t(grad_mixed16, wo_ref[...]).astype(BF16).astype(F32)
    grad_stack = stacked(grad_att)
    product = grad_att * attended32
    dots = dot_rhs_t(grad_stack, value_all)

    local_terms = []
    far_terms = []
    for h in range(heads):
        block = pl.ds(h * rows, rows)
        delta = jnp.sum(jnp.where(head_masks[h], product, 0.0), axis=1, keepdims=True)
        tangent = tanh_s[block, :]
        slope = 1.0 - tangent * tangent
        dlogit = weight_s[block, :].astype(F32) * (dots[h * rows : (h + 1) * rows] - delta)
        sloped = dlogit * slope
        terms = jnp.sum(sloped * raw_s[block, :], axis=0, keepdims=True)
        local_terms.append(jnp.sum(terms[:, :rows], axis=1, keepdims=True))
        far_terms.append(jnp.sum(terms[:, rows:], axis=1, keepdims=True))
        dscore_s[block, :rows] = (sloped[:, :rows] * (local_ref[h] * scale)).astype(BF16)
        dscore_s[block, rows:] = (sloped[:, rows:] * (far_ref[h] * scale)).astype(BF16)

    grad_query = collapse(dot(dscore_s[...], key_all)).astype(BF16)
    grad_key = dot_lhs_t(dscore_s[...], query_stack).astype(BF16)
    grad_value = dot_lhs_t(weight_s[...], grad_stack).astype(BF16)
    put(0, dot_lhs_t(hidden[:rows], grad_query))
    put(1, dot_lhs_t(hidden, grad_key))
    put(2, dot_lhs_t(hidden, grad_value))
    grad_hidden = dot_rhs_t(grad_key, wk_ref[...]) + dot_rhs_t(grad_value, wv_ref[...])
    own = grad_hidden[:rows] + dot_rhs_t(grad_query, wq_ref[...])
    own_ref[...] = own
    grad_gain1 = jnp.sum(own * normed1[:rows], axis=0, keepdims=True)
    grad_gain1 = grad_gain1 + jnp.sum(grad_hidden[rows:] * normed1[rows:], axis=0, keepdims=True)
    for k, ref in enumerate(back_refs):
        ref[...] = grad_hidden[(k + 1) * rows : (k + 2) * rows].astype(BF16)

    column = lax.broadcasted_iota(jnp.int32, (1, width), 1)
    gains = jnp.zeros((1, width), F32)
    for h in range(heads):
        gains = jnp.where(column == h, local_terms[h], gains)
        gains = jnp.where(column == heads + h, far_terms[h], gains)
    line = lax.broadcasted_iota(jnp.int32, (SMALL // 2, width), 0)
    small = jnp.where(line == 0, grad_gain1, jnp.where(line == 1, grad_gain2, jnp.where(line == 2, gains, 0.0)))
    packed = split_parts(small)
    small_ref[...] = packed
    send_ref[half:, :] = packed


def merge_kernel(keep_ref, small_ref, recv_ref, *out_refs):
    rows = keep_ref.shape[0]
    total = keep_ref[...].astype(F32) + recv_ref[:rows, :].astype(F32)
    total = total.astype(BF16)
    packed = split_parts(join_parts(small_ref[...]) + join_parts(recv_ref[rows:, :]))
    if len(out_refs) == 3:
        kept, sent, small = out_refs
        kept[...] = total[: rows // 2]
        sent[: rows // 2, :] = total[rows // 2 :]
        sent[rows // 2 :, :] = packed
        small[...] = packed
    else:
        out_refs[0][:rows, :] = total
        out_refs[0][rows:, :] = packed


def double_kernel(own_ref, recv_ref, out_ref):
    rows = own_ref.shape[0] - SMALL
    out_ref[:rows, :] = (own_ref[:rows, :].astype(F32) + recv_ref[:rows, :].astype(F32)).astype(BF16)
    out_ref[rows:, :] = split_parts(join_parts(own_ref[rows:, :]) + join_parts(recv_ref[rows:, :]))


def tail_kernel(*refs):
    count = len(refs) - 5
    feats_ref, own_ref, mixed_ref, gain_ref = refs[:4]
    normed, inverse = norm_forward(feats_ref[...].astype(F32))
    grad_hidden = own_ref[...]
    for ref in refs[4 : 4 + count]:
        grad_hidden = grad_hidden + ref[...].astype(F32)
    refs[-1][...] = (mixed_ref[...] + norm_backward(grad_hidden, normed, inverse, gain_ref[...])).astype(BF16)


def spread_kernel(*refs):
    pieces = refs[:7]
    gain1_ref, wq_ref, wk_ref, wv_ref, wo_ref, gain2_ref, up_ref, down_ref, tiny_ref, chunks, sems = refs[7:]
    width = wq_ref.shape[0]
    core, level1, level2 = device_bits()

    def place(rel, value):
        upper, lower = (level2, level1) if rel >= 4 else (level1, level2)
        index = (core ^ (rel >> 2)) * 4 + (upper ^ ((rel >> 1) & 1)) * 2 + (lower ^ (rel & 1))
        chunks[index] = value.astype(F32)

    base, one, two, far_base, far_one, far_two, _ = pieces
    place(0, base[:width, :])
    place(1, one[...])
    place(2, two[:width, :])
    place(3, two[width:, :])
    place(4, far_base[:width, :])
    place(5, far_one[...])
    place(6, far_two[:width, :])
    place(7, far_two[width:, :])
    targets = [
        wq_ref,
        wk_ref,
        wv_ref,
        wo_ref,
        up_ref.at[:, :width],
        up_ref.at[:, width:],
        down_ref.at[:width, :],
        down_ref.at[width:, :],
    ]
    copies = [pltpu.make_async_copy(chunks.at[k], t, sems.at[k]) for k, t in enumerate(targets)]
    for copy in copies:
        copy.start()
    small = join_parts(base[width:, :])
    gain1_ref[...] = small[0:1]
    gain2_ref[...] = small[1:2]
    tiny_ref[...] = small[2:3, :128]
    for copy in copies:
        copy.wait()


def struct(shape, dtype):
    return jax.ShapeDtypeStruct(shape, dtype)


VM = pl.BlockSpec(memory_space=pltpu.VMEM)
SM = pl.BlockSpec(memory_space=pltpu.SMEM)
ANY = pl.BlockSpec(memory_space=pl.ANY)
PARAMS = pltpu.CompilerParams(vmem_limit_bytes=VMEM_LIMIT)


def call(kernel, outs, *args, in_specs=None, **kwargs):
    return pl.pallas_call(
        kernel,
        out_shape=outs,
        in_specs=in_specs or [VM] * len(args),
        out_specs=jax.tree.map(lambda _: VM, outs),
        compiler_params=PARAMS,
        **kwargs,
    )(*args)


def flipped(x, bits_even, bits_odd):
    size = lax.axis_size("dom") * lax.axis_size("rep")
    pairs = [(i, i ^ (bits_odd if i & 1 else bits_even)) for i in range(size)]
    return lax.ppermute(x, AXES, pairs)


def local(
    node_feats,
    out_grad,
    norm1_gain,
    w_query,
    w_key,
    w_value,
    w_out,
    norm2_gain,
    w_up,
    w_down,
    local_gain,
    expander_gain,
    partner_perm,
    block_pairs,
    pair_count,
):
    feats = node_feats[0]
    partners = partner_perm[0, :, 0, :]
    rows, width = feats.shape
    heads = local_gain.shape[0]
    size = lax.axis_size("dom") * lax.axis_size("rep")
    levels = lax.axis_size("dom").bit_length() - 1
    by_bit = {}
    for matching in range(partners.shape[0]):
        by_bit.setdefault((levels - 1 - matching) % levels, []).append(matching)
    bits = list(by_bit)
    groups = [by_bit[b] for b in bits]

    def swapped(x, bit):
        return lax.ppermute(x, "dom", [(i, i ^ 1 << bit) for i in range(lax.axis_size("dom"))])

    others = [swapped(feats, b) for b in bits]
    count = len(bits)
    tall = (count + 1) * rows
    gain1 = norm1_gain.reshape(1, width)
    outs = (
        struct((rows, width), BF16),
        struct((4 * width, width), BF16),
        struct((4 * width + SMALL, width), BF16),
        struct((SMALL, width), BF16),
        struct((rows, width), F32),
        struct((rows, width), F32),
    ) + tuple(struct((rows, width), BF16) for _ in bits)
    node_out, keep, send, small, own, grad_mixed, *back = call(
        functools.partial(layer_kernel, groups),
        outs,
        feats,
        *others,
        out_grad[0],
        gain1,
        w_query,
        w_key,
        w_value,
        w_out,
        norm2_gain.reshape(1, width),
        w_up,
        w_down,
        local_gain,
        expander_gain,
        partners,
        in_specs=[VM] * (count + 10) + [SM, SM, VM],
        scratch_shapes=[
            pltpu.VMEM((heads * rows, tall), F32),
            pltpu.VMEM((heads * rows, tall), F32),
            pltpu.VMEM((heads * rows, tall), BF16),
            pltpu.VMEM((heads * rows, tall), BF16),
        ],
    )

    recv = flipped(send, 1, 1)
    keep, send, small = call(
        merge_kernel,
        (struct((2 * width, width), BF16), struct((2 * width + SMALL, width), BF16), struct((SMALL, width), BF16)),
        keep,
        small,
        recv,
    )
    recv = flipped(send, 2, 4)
    keep, send, small = call(
        merge_kernel,
        (struct((width, width), BF16), struct((width + SMALL, width), BF16), struct((SMALL, width), BF16)),
        keep,
        small,
        recv,
    )
    recv = flipped(send, 4, 2)
    (base,) = call(merge_kernel, (struct((width + SMALL, width), BF16),), keep, small, recv)

    returned = [swapped(x, b) for x, b in zip(back, bits)]
    grad_feats = call(tail_kernel, struct((rows, width), BF16), feats, own, grad_mixed, gain1, *returned)

    high_bits = [1 << k for k in range(3, size.bit_length() - 1)]
    for even, odd in zip(high_bits, high_bits[::-1]):
        base = call(double_kernel, struct(base.shape, BF16), base, flipped(base, even, odd))

    one = flipped(base[:width], 4, 2)
    two = flipped(jnp.concatenate([base[:width], one], axis=0), 2, 4)
    far_base = flipped(base[:width], 1, 1)
    far_one = flipped(one, 1, 1)
    far_two = flipped(two, 1, 1)
    square = struct((width, width), F32)
    results = pl.pallas_call(
        spread_kernel,
        out_shape=(
            struct((1, width), F32),
            square,
            square,
            square,
            square,
            struct((1, width), F32),
            struct((width, 2 * width), F32),
            struct((2 * width, width), F32),
            struct((1, 128), F32),
        ),
        in_specs=[VM] * 7,
        out_specs=(VM, ANY, ANY, ANY, ANY, VM, ANY, ANY, VM),
        scratch_shapes=[pltpu.VMEM((8, width, width), F32), pltpu.SemaphoreType.DMA((8,))],
        compiler_params=PARAMS,
    )(base, one, two, far_base, far_one, far_two, gain1)
    grad_gain1, grad_wq, grad_wk, grad_wv, grad_wout, grad_gain2, grad_up, grad_down, tiny = results
    return (
        node_out[None],
        grad_feats[None],
        grad_gain1.reshape(width),
        grad_wq,
        grad_wk,
        grad_wv,
        grad_wout,
        grad_gain2.reshape(width),
        grad_up,
        grad_down,
        tiny[0, :heads],
        tiny[0, heads : 2 * heads],
    )


def solution(mesh):
    whole = P()
    rows = P("rep", "dom", None)
    return jax.shard_map(
        local,
        mesh=mesh,
        in_specs=(rows, rows)
        + (whole,) * 10
        + (P("rep", None, "dom", None), rows, P("rep", "dom")),
        out_specs=(rows, rows) + (whole,) * 10,
        check_vma=False,
    )
```

time: 222 us -> 79.9 us (0.36)
  waiting for transfers between devices: 98.4 us -> 43.7 us
  blocking collectives: 40.5 us -> 0 us
  local copies, waits for them, and re-layouts: 29.9 us -> 8.51 us
  between operations: 14.8 us -> 0.73 us
  matrix products: 11.9 us -> 0 us
  Pallas kernels: 0 us -> 9.68 us
  loops' own time: 3.96 us -> 0 us
  other arithmetic: 3.5 us -> 0.02 us
    psum x1 -> x0, waiting for transfers between devices: 94.3 us -> none  [local(): lax.psum((grad_gain1, grad_wq, grad_wk, grad_wv, grad_wout, grad_gain2, g...]
    psum x1 -> x0, blocking collectives: 40.5 us -> none  [local(): lax.psum((grad_gain1, grad_wq, grad_wk, grad_wv, grad_wout, grad_gain2, g...]
    ppermute x14 -> x16, waiting for transfers between devices: 4.07 us -> 43.7 us  [the longest x10 33.3 us: flipped(): return lax.ppermute(x, AXES, pairs)]
    dot_general x24 -> x0, matrix products: 11.9 us -> none  [the longest x6 6.09 us: project_outer(): lax.dot_general(first_op, second_op, (((0,), (0,)), ((), ())), preferred_...]
    pallas_call x0 -> x8, Pallas kernels: none -> 9.68 us  [the longest x7 7.59 us: call(): pl.pallas_call(kernel, out_shape=outs, in_specs=in_specs or [VM] * len(ar...]
    scatter x8 -> x0, local copies, waits for them, and re-layouts: 8.52 us -> none  [the longest x4 4.35 us: local(): placed_keys = jnp.zeros((count_rows, width), jnp.bfloat16).at[partners[ma...]
    gather x16 -> x0, local copies, waits for them, and re-layouts: 7.68 us -> none  [the longest x8 3.84 us: local(): far_keys.append(their_keys[picked])]
    unnamed x46 -> x28, local copies, waits for them, and re-layouts: 12.2 us -> 7.91 us
  transfers between devices with their start and end apart: 15 -> 16, of which waited for: 3 -> 12; matrix products, arithmetic and copies ran while one was open for 7% -> 0% of each run, Pallas kernels for 0% -> 1%
where the time goes in v1:
time: 79.9 us; the launch traced here: 79.5 us
  waiting for transfers between devices  43.7 us (55%)
  starting transfers between devices  16.8 us (21%)
  Pallas kernels  9.68 us (12%)
  local copies, waits for them, and re-layouts  8.51 us (11%)
    ppermute x10, waiting for transfers between devices, flipped(): return lax.ppermute(x, AXES, pairs)  33.3 us
    ppermute x6, starting transfers between devices, swapped(): lax.ppermute(x, 'dom', [(i, i ^ 1 << bit) for i in range(lax.axis_size('d...  10.5 us
    ppermute x6, waiting for transfers between devices, swapped(): lax.ppermute(x, 'dom', [(i, i ^ 1 << bit) for i in range(lax.axis_size('d...  10.4 us
    unnamed x28, local copies, waits for them, and re-layouts  7.91 us
    pallas_call x7, Pallas kernels, call(): pl.pallas_call(kernel, out_shape=outs, in_specs=in_specs or [VM] * len(ar...  7.59 us
    ppermute x10, starting transfers between devices, flipped(): return lax.ppermute(x, AXES, pairs)  6.35 us
    pallas_call x1, Pallas kernels, local(): pl.pallas_call(spread_kernel, out_shape=(struct((1, width), F32), square,...  2.09 us
  transfers between devices with their start and end apart: 16, of which 12 were waited for; matrix products, arithmetic and copies ran while one was open for 0% of the time, Pallas kernels for 1%

profile of v1, /device:TPU:0, one launch (start us, length us, event | category | flops | bytes accessed | tf_op | source)
XLA Modules:
  0.0 79.5 jit_solution(2314095718073147992)
XLA Ops:
  0.6 3.0 %collective-permute-start.2 = (bf16[128,256]{1,0:T(8,128)(2,1)}, bf16[128,256]{1,0:T(8,128)(2,1)S(1)}, u32[]{:S(2)}, u32[]{:S(2)}) collective-permute-start(bf16[128,256]{1,0:T(8,128)(2,1)} %bitcast.13), channel_id=1, source_target_pairs={{0,4},{4,0},{8,12},{12,8},{16,20},{20,16},{24,28},{28,24},{1,5},{5... | collective-permute-start | bytes 196616 | tf_op jit(solution)/shard_map/ppermute | solution.py:365
  3.7 1.6 %collective-permute-start.1 = (bf16[128,256]{1,0:T(8,128)(2,1)}, bf16[128,256]{1,0:T(8,128)(2,1)S(1)}, u32[]{:S(2)}, u32[]{:S(2)}) collective-permute-start(bf16[128,256]{1,0:T(8,128)(2,1)} %bitcast.14), channel_id=1, source_target_pairs={{0,8},{4,12},{8,0},{12,4},{16,24},{20,28},{24,16},{28,20},{1,9},{5... | collective-permute-start | bytes 196616 | tf_op jit(solution)/shard_map/ppermute | solution.py:365
  5.3 2.6 %collective-permute-start = (bf16[128,256]{1,0:T(8,128)(2,1)}, bf16[128,256]{1,0:T(8,128)(2,1)S(1)}, u32[]{:S(2)}, u32[]{:S(2)}) collective-permute-start(bf16[128,256]{1,0:T(8,128)(2,1)} %bitcast.15), channel_id=1, source_target_pairs={{0,16},{4,20},{8,24},{12,28},{16,0},{20,4},{24,8},{28,12},{1,17},{... | collective-permute-start | bytes 196616 | tf_op jit(solution)/shard_map/ppermute | solution.py:365
  7.8 0.0 collective-permute-done.2.refs_3_
  7.8 0.3 collective-permute-done.1.refs_2_
  8.2 3.2 %collective-permute-done.refs_1_ = bf16[128,256]{1,0:T(8,128)(2,1)S(1)} collective-permute-done((bf16[128,256]{1,0:T(8,128)(2,1)}, bf16[128,256]{1,0:T(8,128)(2,1)S(1)}, u32[]{:S(2)}, u32[]{:S(2)}) %collective-permute-start) | collective-permute-done | bytes 65568 | tf_op jit(solution)/shard_map/ppermute | solution.py:365
  11.4 0.7 copy-done.11
  12.0 0.0 copy-done.10
  12.0 0.0 copy-done.9
  12.1 0.8 %copy-done = bf16[1,128,256]{2,1,0:T(8,128)(2,1)S(1)} copy-done((bf16[1,128,256]{2,1,0:T(8,128)(2,1)S(1)}, bf16[1,128,256]{2,1,0:T(8,128)(2,1)}, u32[]{:S(2)}) %copy-start) | copy-done | bytes 65560
  12.9 0.9 %copy-done.2 = bf16[256,512]{1,0:T(8,128)(2,1)S(1)} copy-done((bf16[256,512]{1,0:T(8,128)(2,1)S(1)}, bf16[256,512]{1,0:T(8,128)(2,1)}, u32[]{:S(2)}) %copy-start.2) | copy-done | bytes 262168
  13.9 0.9 %copy-done.3 = bf16[512,256]{1,0:T(8,128)(2,1)S(1)} copy-done((bf16[512,256]{1,0:T(8,128)(2,1)S(1)}, bf16[512,256]{1,0:T(8,128)(2,1)}, u32[]{:S(2)}) %copy-start.3) | copy-done | bytes 262168
  14.8 0.9 %copy-done.4 = bf16[256,256]{1,0:T(8,128)(2,1)S(1)} copy-done((bf16[256,256]{1,0:T(8,128)(2,1)S(1)}, bf16[256,256]{1,0:T(8,128)(2,1)}, u32[]{:S(2)}) %copy-start.4) | copy-done | bytes 131096
  15.7 0.9 %copy-done.5 = bf16[256,256]{1,0:T(8,128)(2,1)S(1)} copy-done((bf16[256,256]{1,0:T(8,128)(2,1)S(1)}, bf16[256,256]{1,0:T(8,128)(2,1)}, u32[]{:S(2)}) %copy-start.5) | copy-done | bytes 131096
  16.6 0.9 %copy-done.6 = bf16[256,256]{1,0:T(8,128)(2,1)S(1)} copy-done((bf16[256,256]{1,0:T(8,128)(2,1)S(1)}, bf16[256,256]{1,0:T(8,128)(2,1)}, u32[]{:S(2)}) %copy-start.6) | copy-done | bytes 131096
  17.5 0.9 %copy-done.7 = bf16[256,256]{1,0:T(8,128)(2,1)S(1)} copy-done((bf16[256,256]{1,0:T(8,128)(2,1)S(1)}, bf16[256,256]{1,0:T(8,128)(2,1)}, u32[]{:S(2)}) %copy-start.7) | copy-done | bytes 131096
  18.4 0.8 %copy-done.8 = bf16[1,128,256]{2,1,0:T(8,128)(2,1)S(1)} copy-done((bf16[1,128,256]{2,1,0:T(8,128)(2,1)S(1)}, bf16[1,128,256]{2,1,0:T(8,128)(2,1)}, u32[]{:S(2)}) %copy-start.8) | copy-done | bytes 65560
  19.3 6.4 %shard_map.220 = (bf16[128,256]{1,0:T(8,128)(2,1)}, bf16[1024,256]{1,0:T(8,128)(2,1)S(1)}, bf16[1040,256]{1,0:T(8,128)(2,1)S(1)}, bf16[16,256]{1,0:T(8,128)(2,1)...) custom-call(bf16[128,256]{1,0:T(8,128)(2,1)S(1)} %bitcast.16, ...), custom_call_target="tpu_custom_call" | custom-call | tf_op jit(solution)/shard_map/pallas_call | solution.py:319
  25.6 0.0 collective-permute-start.6
  25.6 1.9 %collective-permute-done.6.recv_ref = bf16[1040,256]{1,0:T(8,128)(2,1)S(1)} collective-permute-done((bf16[1040,256]{1,0:T(8,128)(2,1)S(1)}, bf16[1040,256]{1,0:T(8,128)(2,1)S(1)}, u32[]{:S(2)}, u32[]{:S(2)}) %collective-permute-start.6) | collective-permute-done | bytes 532512 | tf_op jit(solution)/shard_map/ppermute | solution.py:332
  27.6 0.1 shard_map.222
  27.7 1.6 %collective-permute-start.7 = (bf16[528,256]{1,0:T(8,128)(2,1)S(1)}, bf16[528,256]{1,0:T(8,128)(2,1)S(1)}, u32[]{:S(2)}, u32[]{:S(2)}) collective-permute-start(bf16[528,256]{1,0:T(8,128)(2,1)S(1)} %get-tuple-element.47), channel_id=1, source_target_pairs={{0,2},{1,5},{2,0},{3,7},{4,6},{5,1},{6,4},{7,3},{8,10},{9,13},{10,... | collective-permute-start | bytes 811016 | tf_op jit(solution)/shard_map/ppermute | solution.py:332
  29.3 5.0 %collective-permute-done.7.recv_ref = bf16[528,256]{1,0:T(8,128)(2,1)S(1)} collective-permute-done((bf16[528,256]{1,0:T(8,128)(2,1)S(1)}, bf16[528,256]{1,0:T(8,128)(2,1)S(1)}, u32[]{:S(2)}, u32[]{:S(2)}) %collective-permute-start.7) | collective-permute-done | bytes 270368 | tf_op jit(solution)/shard_map/ppermute | solution.py:332
  34.2 0.1 shard_map.223
  34.3 0.6 collective-permute-start.8
  34.9 4.5 %collective-permute-done.8.recv_ref = bf16[272,256]{1,0:T(8,128)(2,1)S(1)} collective-permute-done((bf16[272,256]{1,0:T(8,128)(2,1)S(1)}, bf16[272,256]{1,0:T(8,128)(2,1)S(1)}, u32[]{:S(2)}, u32[]{:S(2)}) %collective-permute-start.8) | collective-permute-done | bytes 139296 | tf_op jit(solution)/shard_map/ppermute | solution.py:332
  39.4 0.3 collective-permute-start.9
  39.7 5.5 %collective-permute-done.9.recv_ref = bf16[272,256]{1,0:T(8,128)(2,1)S(1)} collective-permute-done((bf16[272,256]{1,0:T(8,128)(2,1)S(1)}, bf16[272,256]{1,0:T(8,128)(2,1)S(1)}, u32[]{:S(2)}, u32[]{:S(2)}) %collective-permute-start.9) | collective-permute-done | bytes 139296 | tf_op jit(solution)/shard_map/ppermute | solution.py:332
  45.3 1.3 %collective-permute-start.10 = (bf16[272,256]{1,0:T(8,128)(2,1)S(1)}, bf16[272,256]{1,0:T(8,128)(2,1)S(1)}, u32[]{:S(2)}, u32[]{:S(2)}) collective-permute-start(bf16[272,256]{1,0:T(8,128)(2,1)S(1)} %shard_map.225.own_ref), channel_id=1, source_target_pairs={{0,16},{1,9},{2,18},{3,11},{4,20},{5,13},{6,22},{7,15},{8,24},{9,1... | collective-permute-start | bytes 417800 | tf_op jit(solution)/shard_map/ppermute | solution.py:332
  46.6 5.6 %collective-permute-done.10.recv_ref = bf16[272,256]{1,0:T(8,128)(2,1)S(1)} collective-permute-done((bf16[272,256]{1,0:T(8,128)(2,1)S(1)}, bf16[272,256]{1,0:T(8,128)(2,1)S(1)}, u32[]{:S(2)}, u32[]{:S(2)}) %collective-permute-start.10) | collective-permute-done | bytes 139296 | tf_op jit(solution)/shard_map/ppermute | solution.py:332
  52.2 0.0 copy-start.1
  52.2 0.6 collective-permute-start.11
  52.8 5.9 %collective-permute-done.11.refs_1_ = bf16[256,256]{1,0:T(8,128)(2,1)S(1)} collective-permute-done((bf16[256,256]{1,0:T(8,128)(2,1)S(1)}, bf16[256,256]{1,0:T(8,128)(2,1)S(1)}, u32[]{:S(2)}, u32[]{:S(2)}) %collective-permute-start.11) | collective-permute-done | bytes 131104 | tf_op jit(solution)/shard_map/ppermute | solution.py:332
  58.7 1.6 %collective-permute-start.12 = (bf16[512,256]{1,0:T(8,128)(2,1)S(1)}, bf16[512,256]{1,0:T(8,128)(2,1)S(1)}, u32[]{:S(2)}, u32[]{:S(2)}) collective-permute-start(bf16[512,256]{1,0:T(8,128)(2,1)S(1)} %pad_maximum_fusion), channel_id=1, source_target_pairs={{0,2},{1,5},{2,0},{3,7},{4,6},{5,1},{6,4},{7,3},{8,10},{9,13},{10,... | collective-permute-start | bytes 786440 | tf_op jit(solution)/shard_map/ppermute | solution.py:332
  60.3 4.9 %collective-permute-done.12.refs_2_ = bf16[512,256]{1,0:T(8,128)(2,1)S(1)} collective-permute-done((bf16[512,256]{1,0:T(8,128)(2,1)S(1)}, bf16[512,256]{1,0:T(8,128)(2,1)S(1)}, u32[]{:S(2)}, u32[]{:S(2)}) %collective-permute-start.12) | collective-permute-done | bytes 262176 | tf_op jit(solution)/shard_map/ppermute | solution.py:332
  65.1 0.0 collective-permute-start.15
  65.1 0.4 collective-permute-start.3
  65.6 0.2 collective-permute-start.13
  65.8 0.3 collective-permute-start.14
  66.1 2.3 %collective-permute-start.4 = (bf16[128,256]{1,0:T(8,128)(2,1)S(1)}, bf16[128,256]{1,0:T(8,128)(2,1)S(1)}, u32[]{:S(2)}, u32[]{:S(2)}) collective-permute-start(bf16[128,256]{1,0:T(8,128)(2,1)S(1)} %get-tuple-element.40), channel_id=1, source_target_pairs={{0,8},{4,12},{8,0},{12,4},{16,24},{20,28},{24,16},{28,20},{1,9},{5... | collective-permute-start | bytes 196616 | tf_op jit(solution)/shard_map/ppermute | solution.py:365
  68.4 3.2 %collective-permute-done.3.refs_4_ = bf16[128,256]{1,0:T(8,128)(2,1)S(1)} collective-permute-done((bf16[128,256]{1,0:T(8,128)(2,1)S(1)}, bf16[128,256]{1,0:T(8,128)(2,1)S(1)}, u32[]{:S(2)}, u32[]{:S(2)}) %collective-permute-start.3) | collective-permute-done | bytes 65568 | tf_op jit(solution)/shard_map/ppermute | solution.py:365
  71.6 0.5 collective-permute-start.5
  72.1 0.1 collective-permute-done.4.refs_5_
  72.3 3.6 %collective-permute-done.5.refs_6_ = bf16[128,256]{1,0:T(8,128)(2,1)S(1)} collective-permute-done((bf16[128,256]{1,0:T(8,128)(2,1)S(1)}, bf16[128,256]{1,0:T(8,128)(2,1)S(1)}, u32[]{:S(2)}, u32[]{:S(2)}) %collective-permute-start.5) | collective-permute-done | bytes 65568 | tf_op jit(solution)/shard_map/ppermute | solution.py:365
  75.9 0.9 %shard_map.221 = bf16[128,256]{1,0:T(8,128)(2,1)} custom-call(bf16[128,256]{1,0:T(8,128)(2,1)S(1)} %bitcast.17, f32[128,256]{1,0:T(8,128)S(1)} %get-tuple-element.37.refs_1_, f32[128,256]{1,0:T(8,128)S(1)} %get-tuple-element.38.refs_2_, f32[1,256]{1,0:T(1,128)S(1)} %bitcast.20, bf16[128,256]{1,0:T(8,128)(2,1)S(1)} %collective-permute-done.3.refs_4_, ...), custom_call_target="tpu_custom_call" | custom-call | tf_op jit(solution)/shard_map/pallas_call | solution.py:319
  76.8 0.0 collective-permute-done.13.refs_3_
  76.8 2.1 %shard_map.227 = (f32[1,256]{1,0:T(1,128)}, f32[256,256]{1,0:T(8,128)}, f32[256,256]{1,0:T(8,128)}, f32[256,256]{1,0:T(8,128)}, f32[256,256]{1,0:T(8,128)}, /*in...) custom-call(bf16[272,256]{1,0:T(8,128)(2,1)S(1)} %shard_map.226.refs_0_, ...), custom_call_target="tpu_custom_call" | custom-call | tf_op jit(solution)/shard_map/pallas_call | solution.py:437
  78.9 0.6 slice_bitcast_fusion
  (23 shorter events, 0.2 us)
Async XLA Ops:
  0.6 7.2 %collective-permute-start.2 = (bf16[128,256]{1,0:T(8,128)(2,1)}, bf16[128,256]{1,0:T(8,128)(2,1)S(1)}, u32[]{:S(2)}, u32[]{:S(2)}) collective-permute-start(bf16[128,256]{1,0:T(8,128)(2,1)} %bitcast.13), channel_id=1, source_target_pairs={{0,4},{4,0},{8,12},{12,8},{16,20},{20,16},{24,28},{28,24},{1,5},{5... | collective-permute-start | bytes 196616 | tf_op jit(solution)/shard_map/ppermute | solution.py:365
  3.7 4.5 %collective-permute-start.1 = (bf16[128,256]{1,0:T(8,128)(2,1)}, bf16[128,256]{1,0:T(8,128)(2,1)S(1)}, u32[]{:S(2)}, u32[]{:S(2)}) collective-permute-start(bf16[128,256]{1,0:T(8,128)(2,1)} %bitcast.14), channel_id=1, source_target_pairs={{0,8},{4,12},{8,0},{12,4},{16,24},{20,28},{24,16},{28,20},{1,9},{5... | collective-permute-start | bytes 196616 | tf_op jit(solution)/shard_map/ppermute | solution.py:365
  5.3 6.1 %collective-permute-start = (bf16[128,256]{1,0:T(8,128)(2,1)}, bf16[128,256]{1,0:T(8,128)(2,1)S(1)}, u32[]{:S(2)}, u32[]{:S(2)}) collective-permute-start(bf16[128,256]{1,0:T(8,128)(2,1)} %bitcast.15), channel_id=1, source_target_pairs={{0,16},{4,20},{8,24},{12,28},{16,0},{20,4},{24,8},{28,12},{1,17},{... | collective-permute-start | bytes 196616 | tf_op jit(solution)/shard_map/ppermute | solution.py:365
  11.3 0.7 copy-start.11
  11.3 0.7 copy-start.13
  11.3 0.7 copy-start.10
  11.3 0.7 copy-start.9
  11.3 0.7 copy-start.12
  12.1 0.8 %copy-start = (bf16[1,128,256]{2,1,0:T(8,128)(2,1)S(1)}, bf16[1,128,256]{2,1,0:T(8,128)(2,1)}, u32[]{:S(2)}) copy-start(bf16[1,128,256]{2,1,0:T(8,128)(2,1)} %param.15) | copy-start | bytes 196612
  12.9 0.9 %copy-start.2 = (bf16[256,512]{1,0:T(8,128)(2,1)S(1)}, bf16[256,512]{1,0:T(8,128)(2,1)}, u32[]{:S(2)}) copy-start(bf16[256,512]{1,0:T(8,128)(2,1)} %refs_11_.1) | copy-start | bytes 786436
  13.9 0.9 %copy-start.3 = (bf16[512,256]{1,0:T(8,128)(2,1)S(1)}, bf16[512,256]{1,0:T(8,128)(2,1)}, u32[]{:S(2)}) copy-start(bf16[512,256]{1,0:T(8,128)(2,1)} %refs_12_.1) | copy-start | bytes 786436
  14.8 0.9 %copy-start.4 = (bf16[256,256]{1,0:T(8,128)(2,1)S(1)}, bf16[256,256]{1,0:T(8,128)(2,1)}, u32[]{:S(2)}) copy-start(bf16[256,256]{1,0:T(8,128)(2,1)} %refs_6_.1) | copy-start | bytes 393220
  15.7 0.9 %copy-start.5 = (bf16[256,256]{1,0:T(8,128)(2,1)S(1)}, bf16[256,256]{1,0:T(8,128)(2,1)}, u32[]{:S(2)}) copy-start(bf16[256,256]{1,0:T(8,128)(2,1)} %refs_7_.1) | copy-start | bytes 393220
  16.6 0.9 %copy-start.6 = (bf16[256,256]{1,0:T(8,128)(2,1)S(1)}, bf16[256,256]{1,0:T(8,128)(2,1)}, u32[]{:S(2)}) copy-start(bf16[256,256]{1,0:T(8,128)(2,1)} %refs_8_.1) | copy-start | bytes 393220
  17.5 0.9 %copy-start.7 = (bf16[256,256]{1,0:T(8,128)(2,1)S(1)}, bf16[256,256]{1,0:T(8,128)(2,1)}, u32[]{:S(2)}) copy-start(bf16[256,256]{1,0:T(8,128)(2,1)} %refs_9_.1) | copy-start | bytes 393220
  18.4 0.8 %copy-start.8 = (bf16[1,128,256]{2,1,0:T(8,128)(2,1)S(1)}, bf16[1,128,256]{2,1,0:T(8,128)(2,1)}, u32[]{:S(2)}) copy-start(bf16[1,128,256]{2,1,0:T(8,128)(2,1)} %param.16) | copy-start | bytes 196612
  25.6 1.9 %collective-permute-start.6 = (bf16[1040,256]{1,0:T(8,128)(2,1)S(1)}, bf16[1040,256]{1,0:T(8,128)(2,1)S(1)}, u32[]{:S(2)}, u32[]{:S(2)}) collective-permute-start(bf16[1040,256]{1,0:T(8,128)(2,1)S(1)} %get-tuple-element.44), channel_id=1, source_target_pairs={{0,1},{1,0},{2,3},{3,2},{4,5},{5,4},{6,7},{7,6},{8,9},{9,8},{10,11... | collective-permute-start | bytes 1597448 | tf_op jit(solution)/shard_map/ppermute | solution.py:332
  27.7 6.5 %collective-permute-start.7 = (bf16[528,256]{1,0:T(8,128)(2,1)S(1)}, bf16[528,256]{1,0:T(8,128)(2,1)S(1)}, u32[]{:S(2)}, u32[]{:S(2)}) collective-permute-start(bf16[528,256]{1,0:T(8,128)(2,1)S(1)} %get-tuple-element.47), channel_id=1, source_target_pairs={{0,2},{1,5},{2,0},{3,7},{4,6},{5,1},{6,4},{7,3},{8,10},{9,13},{10,... | collective-permute-start | bytes 811016 | tf_op jit(solution)/shard_map/ppermute | solution.py:332
  34.3 5.1 %collective-permute-start.8 = (bf16[272,256]{1,0:T(8,128)(2,1)S(1)}, bf16[272,256]{1,0:T(8,128)(2,1)S(1)}, u32[]{:S(2)}, u32[]{:S(2)}) collective-permute-start(bf16[272,256]{1,0:T(8,128)(2,1)S(1)} %get-tuple-element.50), channel_id=1, source_target_pairs={{0,4},{1,3},{2,6},{3,1},{4,0},{5,7},{6,2},{7,5},{8,12},{9,11},{10,... | collective-permute-start | bytes 417800 | tf_op jit(solution)/shard_map/ppermute | solution.py:332
  39.4 5.8 %collective-permute-start.9 = (bf16[272,256]{1,0:T(8,128)(2,1)S(1)}, bf16[272,256]{1,0:T(8,128)(2,1)S(1)}, u32[]{:S(2)}, u32[]{:S(2)}) collective-permute-start(bf16[272,256]{1,0:T(8,128)(2,1)S(1)} %shard_map.224.own_ref), channel_id=1, source_target_pairs={{0,8},{1,17},{2,10},{3,19},{4,12},{5,21},{6,14},{7,23},{8,0},{9,25... | collective-permute-start | bytes 417800 | tf_op jit(solution)/shard_map/ppermute | solution.py:332
  45.3 6.8 %collective-permute-start.10 = (bf16[272,256]{1,0:T(8,128)(2,1)S(1)}, bf16[272,256]{1,0:T(8,128)(2,1)S(1)}, u32[]{:S(2)}, u32[]{:S(2)}) collective-permute-start(bf16[272,256]{1,0:T(8,128)(2,1)S(1)} %shard_map.225.own_ref), channel_id=1, source_target_pairs={{0,16},{1,9},{2,18},{3,11},{4,20},{5,13},{6,22},{7,15},{8,24},{9,1... | collective-permute-start | bytes 417800 | tf_op jit(solution)/shard_map/ppermute | solution.py:332
  52.2 23.7 %copy-start.1 = (bf16[1,128,256]{2,1,0:T(8,128)(2,1)S(1)}, bf16[1,128,256]{2,1,0:T(8,128)(2,1)}, u32[]{:S(2)}) copy-start(bf16[1,128,256]{2,1,0:T(8,128)(2,1)} %param.15) | copy-start | bytes 196612
  52.2 6.5 %collective-permute-start.11 = (bf16[256,256]{1,0:T(8,128)(2,1)S(1)}, bf16[256,256]{1,0:T(8,128)(2,1)S(1)}, u32[]{:S(2)}, u32[]{:S(2)}) collective-permute-start(bf16[256,256]{1,0:T(8,128)(2,1)S(1)} %slice.14), channel_id=1, source_target_pairs={{0,4},{1,3},{2,6},{3,1},{4,0},{5,7},{6,2},{7,5},{8,12},{9,11},{10,... | collective-permute-start | bytes 393224 | tf_op jit(solution)/shard_map/ppermute | solution.py:332
  58.7 6.4 %collective-permute-start.12 = (bf16[512,256]{1,0:T(8,128)(2,1)S(1)}, bf16[512,256]{1,0:T(8,128)(2,1)S(1)}, u32[]{:S(2)}, u32[]{:S(2)}) collective-permute-start(bf16[512,256]{1,0:T(8,128)(2,1)S(1)} %pad_maximum_fusion), channel_id=1, source_target_pairs={{0,2},{1,5},{2,0},{3,7},{4,6},{5,1},{6,4},{7,3},{8,10},{9,13},{10,... | collective-permute-start | bytes 786440 | tf_op jit(solution)/shard_map/ppermute | solution.py:332
  65.1 11.7 %collective-permute-start.15 = (bf16[512,256]{1,0:T(8,128)(2,1)S(1)}, bf16[512,256]{1,0:T(8,128)(2,1)S(1)}, u32[]{:S(2)}, u32[]{:S(2)}) collective-permute-start(bf16[512,256]{1,0:T(8,128)(2,1)S(1)} %collective-permute-done.12.refs_2_), channel_id=1, source_target_pairs={{0,1},{1,0},{2,3},{3,2},{4,5},{5,4},{6,7},{7,6},{8,9},{9,8},{10,11... | collective-permute-start | bytes 786440 | tf_op jit(solution)/shard_map/ppermute | solution.py:332
  65.1 6.5 %collective-permute-start.3 = (bf16[128,256]{1,0:T(8,128)(2,1)S(1)}, bf16[128,256]{1,0:T(8,128)(2,1)S(1)}, u32[]{:S(2)}, u32[]{:S(2)}) collective-permute-start(bf16[128,256]{1,0:T(8,128)(2,1)S(1)} %get-tuple-element.39), channel_id=1, source_target_pairs={{0,16},{4,20},{8,24},{12,28},{16,0},{20,4},{24,8},{28,12},{1,17},{... | collective-permute-start | bytes 196616 | tf_op jit(solution)/shard_map/ppermute | solution.py:365
  65.6 11.2 %collective-permute-start.13 = (bf16[256,256]{1,0:T(8,128)(2,1)S(1)}, bf16[256,256]{1,0:T(8,128)(2,1)S(1)}, u32[]{:S(2)}, u32[]{:S(2)}) collective-permute-start(bf16[256,256]{1,0:T(8,128)(2,1)S(1)} %slice.14), channel_id=1, source_target_pairs={{0,1},{1,0},{2,3},{3,2},{4,5},{5,4},{6,7},{7,6},{8,9},{9,8},{10,11... | collective-permute-start | bytes 393224 | tf_op jit(solution)/shard_map/ppermute | solution.py:332
  65.8 11.0 %collective-permute-start.14 = (bf16[256,256]{1,0:T(8,128)(2,1)S(1)}, bf16[256,256]{1,0:T(8,128)(2,1)S(1)}, u32[]{:S(2)}, u32[]{:S(2)}) collective-permute-start(bf16[256,256]{1,0:T(8,128)(2,1)S(1)} %collective-permute-done.11.refs_1_), channel_id=1, source_target_pairs={{0,1},{1,0},{2,3},{3,2},{4,5},{5,4},{6,7},{7,6},{8,9},{9,8},{10,11... | collective-permute-start | bytes 393224 | tf_op jit(solution)/shard_map/ppermute | solution.py:332
  66.1 6.2 %collective-permute-start.4 = (bf16[128,256]{1,0:T(8,128)(2,1)S(1)}, bf16[128,256]{1,0:T(8,128)(2,1)S(1)}, u32[]{:S(2)}, u32[]{:S(2)}) collective-permute-start(bf16[128,256]{1,0:T(8,128)(2,1)S(1)} %get-tuple-element.40), channel_id=1, source_target_pairs={{0,8},{4,12},{8,0},{12,4},{16,24},{20,28},{24,16},{28,20},{1,9},{5... | collective-permute-start | bytes 196616 | tf_op jit(solution)/shard_map/ppermute | solution.py:365
  71.6 4.3 %collective-permute-start.5 = (bf16[128,256]{1,0:T(8,128)(2,1)S(1)}, bf16[128,256]{1,0:T(8,128)(2,1)S(1)}, u32[]{:S(2)}, u32[]{:S(2)}) collective-permute-start(bf16[128,256]{1,0:T(8,128)(2,1)S(1)} %get-tuple-element.41), channel_id=1, source_target_pairs={{0,4},{4,0},{8,12},{12,8},{16,20},{20,16},{24,28},{28,24},{1,5},{5... | collective-permute-start | bytes 196616 | tf_op jit(solution)/shard_map/ppermute | solution.py:365

commit v2 on v1

v2 whole, which is shorter than its diff:
```python
import functools

import jax
import jax.numpy as jnp
from jax import lax
from jax.experimental import pallas as pl
from jax.experimental.pallas import tpu as pltpu
from jax.sharding import PartitionSpec as P

EPSILON = 1e-05
SCORE_CAP = 5.0
GELU_ROOT = 0.7978845608028654
GELU_CUBIC = 0.044715
SMALL = 16
AXES = ("dom", "rep")
VMEM_LIMIT = 48 * 1024 * 1024
F32 = jnp.float32
BF16 = jnp.bfloat16


def dot(a, b):
    return lax.dot_general(a, b, (((1,), (0,)), ((), ())), preferred_element_type=F32)


def dot_rhs_t(a, b):
    return lax.dot_general(a, b, (((1,), (1,)), ((), ())), preferred_element_type=F32)


def dot_lhs_t(a, b):
    return lax.dot_general(a, b, (((0,), (0,)), ((), ())), preferred_element_type=F32)


def norm_forward(matrix):
    center = jnp.mean(matrix, axis=-1, keepdims=True)
    shifted = matrix - center
    inverse = lax.rsqrt(jnp.mean(shifted * shifted, axis=-1, keepdims=True) + EPSILON)
    return (shifted * inverse, inverse)


def norm_backward(upstream, normed, inverse, gain):
    scaled_up = upstream * gain
    return inverse * (
        scaled_up
        - jnp.mean(scaled_up, axis=-1, keepdims=True)
        - normed * jnp.mean(scaled_up * normed, axis=-1, keepdims=True)
    )


def gelu_parts(preact):
    tangent = jnp.tanh(GELU_ROOT * (preact + GELU_CUBIC * preact * preact * preact))
    result = 0.5 * preact * (1.0 + tangent)
    derivative = 0.5 * (1.0 + tangent) + 0.5 * preact * (1.0 - tangent * tangent) * GELU_ROOT * (
        1.0 + 3.0 * GELU_CUBIC * preact * preact
    )
    return (result, derivative)


def split_parts(rows):
    high = rows.astype(BF16).astype(F32)
    return jnp.concatenate([high, rows - high], axis=0).astype(BF16)


def join_parts(packed):
    wide = packed.astype(F32)
    return wide[: SMALL // 2] + wide[SMALL // 2 :]


def device_bits():
    flat = lax.axis_index("dom") * lax.axis_size("rep") + lax.axis_index("rep")
    core = flat & 1
    first = (flat >> 1) & 1
    second = (flat >> 2) & 1
    swap = core == 1
    return (core, jnp.where(swap, second, first), jnp.where(swap, first, second))


def fetch(pairs, sems):
    copies = [pltpu.make_async_copy(src, dst, sems.at[k]) for k, (src, dst) in enumerate(pairs)]
    for copy in copies:
        copy.start()
    return copies


def head_masks_of(shape, heads):
    lane = lax.broadcasted_iota(jnp.int32, shape, 1) // (shape[1] // heads)
    return [lane == h for h in range(heads)]


def stack_heads(matrix, masks):
    return jnp.concatenate([jnp.where(m, matrix, 0.0) for m in masks], axis=0).astype(BF16)


def own_kernel(
    groups,
    feats_ref,
    up_ref,
    gain1_ref,
    wq_hbm,
    wk_hbm,
    wv_hbm,
    wo_hbm,
    wup_hbm,
    wdown_hbm,
    local_ref,
    perm_ref,
    wq_ref,
    wk_ref,
    wv_ref,
    wo_ref,
    wup_ref,
    wdown_ref,
    normed_ref,
    query_ref,
    key_ref,
    value_ref,
    raw_ref,
    tanh_ref,
    exp_ref,
    count_ref,
    back_ref,
    sems,
):
    rows, width = feats_ref.shape
    heads = local_ref.shape[0]
    scale = 1.0 / float(width // heads) ** 0.5
    copies = fetch(
        [
            (wq_hbm, wq_ref),
            (wk_hbm, wk_ref),
            (wv_hbm, wv_ref),
            (wdown_hbm, wdown_ref),
            (wo_hbm, wo_ref),
            (wup_hbm, wup_ref),
        ],
        sems,
    )
    target = lax.broadcasted_iota(jnp.int32, (rows, rows), 0)
    for g, members in enumerate(groups):
        total = 0.0
        for m in members:
            total = total + jnp.where(target == perm_ref[m : m + 1, :], 1.0, 0.0)
        count_ref[:, g * rows : (g + 1) * rows] = total.T
    normed, _ = norm_forward(feats_ref[...].astype(F32))
    normed_ref[...] = normed
    hidden = (normed * gain1_ref[...]).astype(BF16)
    copies[0].wait()
    query = stack_heads(dot(hidden, wq_ref[...]), head_masks_of((rows, width), heads))
    query_ref[...] = query
    copies[1].wait()
    key = dot(hidden, wk_ref[...]).astype(BF16)
    key_ref[...] = key
    copies[2].wait()
    value_ref[...] = dot(hidden, wv_ref[...]).astype(BF16)
    raw_ref[...] = dot_rhs_t(query, key) * scale
    for h in range(heads):
        block = pl.ds(h * rows, rows)
        tangent = jnp.tanh(raw_ref[block, :] * (local_ref[h] / SCORE_CAP))
        tanh_ref[block, :] = tangent
        exp_ref[block, :] = jnp.exp(SCORE_CAP * tangent)
    copies[3].wait()
    back_ref[...] = dot_rhs_t(up_ref[...], wdown_ref[...])
    copies[4].wait()
    copies[5].wait()


def layer_kernel(slots, count, *refs):
    others = refs[:count]
    (
        feats_ref,
        up_ref,
        gain1_ref,
        gain2_ref,
        wq_ref,
        wk_ref,
        wv_ref,
        wo_ref,
        wup_ref,
        wdown_ref,
        normed_ref,
        query_ref,
        key_ref,
        value_ref,
        raw_ref,
        tanh_ref,
        exp_ref,
        count_ref,
        back_ref,
        local_ref,
        far_ref,
        out_ref,
        keep_ref,
        send_ref,
        own_ref,
        mixed_ref,
    ) = refs[count : count + 26]
    slot_refs = refs[count + 26 : count + 26 + len(slots)]
    raw_s, tanh_s, wl_s, wf_s, dl_s, df_s = refs[count + 26 + len(slots) :]

    rows, width = out_ref.shape
    heads = local_ref.shape[0]
    scale = 1.0 / float(width // heads) ** 0.5
    core, level1, level2 = device_bits()
    half = 4 * width

    def put(chunk, value):
        value = value.astype(BF16)
        upper = (chunk >> 1) & 1
        lower = chunk & 1
        same = core == (chunk >> 2)

        @pl.when(same)
        def _():
            rel = (upper ^ level1) * 2 + (lower ^ level2)
            keep_ref[pl.ds(pl.multiple_of(rel * width, width), width), :] = value

        @pl.when(jnp.logical_not(same))
        def _():
            rel = (upper ^ level2) * 2 + (lower ^ level1)
            send_ref[pl.ds(pl.multiple_of(rel * width, width), width), :] = value

    gain1 = gain1_ref[...]
    gain2 = gain2_ref[...]
    upstream = up_ref[...]
    masks = head_masks_of((rows, width), heads)
    normed_far, _ = norm_forward(jnp.concatenate([ref[...] for ref in others], axis=0).astype(F32))
    hidden_far = (normed_far * gain1).astype(BF16)
    key_far = dot(hidden_far, wk_ref[...]).astype(BF16)
    value_far = dot(hidden_far, wv_ref[...]).astype(BF16)
    query_stack = query_ref[...]
    raw_s[...] = dot_rhs_t(query_stack, key_far) * scale
    far_counts = count_ref[...]

    for h in range(heads):
        block = pl.ds(h * rows, rows)
        tangent = jnp.tanh(raw_s[block, :] * (far_ref[h] / SCORE_CAP))
        near = exp_ref[block, :]
        far = jnp.exp(SCORE_CAP * tangent) * far_counts
        inv = 1.0 / (jnp.sum(near, axis=1, keepdims=True) + jnp.sum(far, axis=1, keepdims=True))
        tanh_s[block, :] = tangent
        wl_s[block, :] = (near * inv).astype(BF16)
        wf_s[block, :] = (far * inv).astype(BF16)

    def collapse(matrix):
        total = jnp.where(masks[0], matrix[:rows], 0.0)
        for h in range(1, heads):
            total = total + jnp.where(masks[h], matrix[h * rows : (h + 1) * rows], 0.0)
        return total

    attended32 = collapse(dot(wl_s[...], value_ref[...]) + dot(wf_s[...], value_far))
    attended = attended32.astype(BF16)
    mixed = (feats_ref[...].astype(F32) + dot(attended, wo_ref[...])).astype(BF16)
    normed2, inverse2 = norm_forward(mixed.astype(F32))
    hidden2 = (normed2 * gain2).astype(BF16)
    preact = dot(hidden2, wup_ref[...])
    act32, derivative = gelu_parts(preact)
    act = act32.astype(BF16)
    out_ref[...] = (mixed.astype(F32) + dot(act, wdown_ref[...])).astype(BF16)
    grad_down = dot_lhs_t(act, upstream)
    put(6, grad_down[:width])
    put(7, grad_down[width:])
    grad_pre = (back_ref[...] * derivative).astype(BF16)
    grad_up = dot_lhs_t(hidden2, grad_pre)
    put(4, grad_up[:, :width])
    put(5, grad_up[:, width:])
    grad_hidden2 = dot_rhs_t(grad_pre, wup_ref[...])
    grad_gain2 = jnp.sum(grad_hidden2 * normed2, axis=0, keepdims=True)
    grad_mixed = upstream.astype(F32) + norm_backward(grad_hidden2, normed2, inverse2, gain2)
    mixed_ref[...] = grad_mixed
    grad_mixed16 = grad_mixed.astype(BF16)
    put(3, dot_lhs_t(attended, grad_mixed16))
    grad_att = dot_rhs_t(grad_mixed16, wo_ref[...]).astype(BF16).astype(F32)
    grad_stack = stack_heads(grad_att, masks)
    product = grad_att * attended32
    near_dots = dot_rhs_t(grad_stack, value_ref[...])
    far_dots = dot_rhs_t(grad_stack, value_far)

    near_terms = []
    far_terms = []
    for h in range(heads):
        block = pl.ds(h * rows, rows)
        span = slice(h * rows, (h + 1) * rows)
        delta = jnp.sum(jnp.where(masks[h], product, 0.0), axis=1, keepdims=True)
        for weights, dots, tangents, raw, dscore, gain, terms in (
            (wl_s, near_dots, tanh_ref, raw_ref, dl_s, local_ref[h], near_terms),
            (wf_s, far_dots, tanh_s, raw_s, df_s, far_ref[h], far_terms),
        ):
            tangent = tangents[block, :]
            slope = 1.0 - tangent * tangent
            sloped = weights[block, :].astype(F32) * (dots[span] - delta) * slope
            total = jnp.sum(sloped * raw[block, :], axis=0, keepdims=True)
            terms.append(jnp.sum(total, axis=1, keepdims=True))
            dscore[block, :] = (sloped * (gain * scale)).astype(BF16)

    grad_query = collapse(dot(dl_s[...], key_ref[...]) + dot(df_s[...], key_far)).astype(BF16)
    key_near16 = dot_lhs_t(dl_s[...], query_stack).astype(BF16)
    value_near16 = dot_lhs_t(wl_s[...], grad_stack).astype(BF16)
    key_far16 = dot_lhs_t(df_s[...], query_stack).astype(BF16)
    value_far16 = dot_lhs_t(wf_s[...], grad_stack).astype(BF16)
    normed1 = normed_ref[...]
    hidden = (normed1 * gain1).astype(BF16)
    put(0, dot_lhs_t(hidden, grad_query))
    put(1, dot_lhs_t(hidden, key_near16) + dot_lhs_t(hidden_far, key_far16))
    put(2, dot_lhs_t(hidden, value_near16) + dot_lhs_t(hidden_far, value_far16))
    own = (
        dot_rhs_t(key_near16, wk_ref[...])
        + dot_rhs_t(value_near16, wv_ref[...])
        + dot_rhs_t(grad_query, wq_ref[...])
    )
    own_ref[...] = own
    theirs = dot_rhs_t(key_far16, wk_ref[...]) + dot_rhs_t(value_far16, wv_ref[...])
    grad_gain1 = jnp.sum(own * normed1, axis=0, keepdims=True)
    grad_gain1 = grad_gain1 + jnp.sum(theirs * normed_far, axis=0, keepdims=True)
    back = [theirs[k * rows : (k + 1) * rows] for k in range(count)]
    for (even, odd), ref in zip(slots, slot_refs):
        ref[...] = jnp.where(
            core == 1, 0.0 if odd is None else back[odd], 0.0 if even is None else back[even]
        ).astype(BF16)

    column = lax.broadcasted_iota(jnp.int32, (1, width), 1)
    gains = jnp.zeros((1, width), F32)
    for h in range(heads):
        gains = jnp.where(column == h, near_terms[h], gains)
        gains = jnp.where(column == heads + h, far_terms[h], gains)
    line = lax.broadcasted_iota(jnp.int32, (SMALL // 2, width), 0)
    small = jnp.where(line == 0, grad_gain1, jnp.where(line == 1, grad_gain2, jnp.where(line == 2, gains, 0.0)))
    send_ref[half:, :] = split_parts(small)


def merge_kernel(rows, halve, *refs):
    keep_ref, sent_ref, recv_ref = refs[:3]
    slot = refs[3:4] if len(refs) == (6 if halve else 5) else ()
    total = keep_ref[:rows, :].astype(F32) + recv_ref[:rows, :].astype(F32)
    total = total.astype(BF16)
    span = slice(rows, rows + SMALL)
    packed = split_parts(join_parts(sent_ref[span, :]) + join_parts(recv_ref[span, :]))
    next_ref = refs[-1]
    size = rows // 2 if halve else rows
    if halve:
        refs[-2][...] = total[:size]
    next_ref[:size, :] = total[size:] if halve else total
    next_ref[size : size + SMALL, :] = packed
    if slot:
        next_ref[size + SMALL :, :] = slot[0][...]


def tail_kernel(start, *refs):
    feats_ref, own_ref, mixed_ref, gain_ref = refs[:4]
    normed, inverse = norm_forward(feats_ref[...].astype(F32))
    grad_hidden = own_ref[...]
    for ref, first in zip(refs[4:-1], start):
        grad_hidden = grad_hidden + ref[first:, :].astype(F32)
    refs[-1][...] = (mixed_ref[...] + norm_backward(grad_hidden, normed, inverse, gain_ref[...])).astype(BF16)


def spread_kernel(
    pieces_ref,
    base_ref,
    gain1_ref,
    wq_ref,
    wk_ref,
    wv_ref,
    wo_ref,
    gain2_ref,
    up_ref,
    down_ref,
    local_ref,
    far_ref,
    chunks,
    sems,
):
    width = wq_ref.shape[0]
    heads = local_ref.shape[0]
    core, level1, level2 = device_bits()
    targets = [
        wq_ref,
        wk_ref,
        wv_ref,
        wo_ref,
        up_ref.at[:, :width],
        up_ref.at[:, width:],
        down_ref.at[:width, :],
        down_ref.at[width:, :],
    ]
    copies = []
    for chunk, target in enumerate(targets):
        other = core ^ (chunk >> 2)
        upper = (chunk >> 1) & 1
        lower = chunk & 1
        rel = jnp.where(
            other == 1,
            4 + (upper ^ level2) * 2 + (lower ^ level1),
            (upper ^ level1) * 2 + (lower ^ level2),
        )
        start = pl.multiple_of(rel * width, width)
        chunks[chunk] = pieces_ref[pl.ds(start, width), :].astype(F32)
        copy = pltpu.make_async_copy(chunks.at[chunk], target, sems.at[chunk])
        copy.start()
        copies.append(copy)
    small = join_parts(base_ref[width:, :])
    gain1_ref[...] = small[0:1]
    gain2_ref[...] = small[1:2]
    local_ref[...] = small[2, :heads]
    far_ref[...] = small[2, heads : 2 * heads]
    for copy in copies:
        copy.wait()


def struct(shape, dtype):
    return jax.ShapeDtypeStruct(shape, dtype)


VM = pl.BlockSpec(memory_space=pltpu.VMEM)
SM = pl.BlockSpec(memory_space=pltpu.SMEM)
ANY = pl.BlockSpec(memory_space=pl.ANY)
PARAMS = pltpu.CompilerParams(vmem_limit_bytes=VMEM_LIMIT)


def call(kernel, outs, *args, in_specs=None, **kwargs):
    return pl.pallas_call(
        kernel,
        out_shape=outs,
        in_specs=in_specs or [VM] * len(args),
        out_specs=jax.tree.map(lambda _: VM, outs),
        compiler_params=PARAMS,
        **kwargs,
    )(*args)


def flipped(x, bits_even, bits_odd):
    size = lax.axis_size("dom") * lax.axis_size("rep")
    pairs = [(i, i ^ (bits_odd if i & 1 else bits_even)) for i in range(size)]
    return lax.ppermute(x, AXES, pairs)


def local(
    node_feats,
    out_grad,
    norm1_gain,
    w_query,
    w_key,
    w_value,
    w_out,
    norm2_gain,
    w_up,
    w_down,
    local_gain,
    expander_gain,
    partner_perm,
    block_pairs,
    pair_count,
):
    feats = node_feats[0]
    partners = partner_perm[0, :, 0, :]
    rows, width = feats.shape
    heads = local_gain.shape[0]
    size = lax.axis_size("dom") * lax.axis_size("rep")
    levels = lax.axis_size("dom").bit_length() - 1
    by_bit = {}
    for matching in range(partners.shape[0]):
        by_bit.setdefault((levels - 1 - matching) % levels, []).append(matching)
    bits = list(by_bit)
    groups = [by_bit[b] for b in bits]

    def swapped(x, bit):
        return lax.ppermute(x, "dom", [(i, i ^ 1 << bit) for i in range(lax.axis_size("dom"))])

    rep_bits = lax.axis_size("rep").bit_length() - 1
    high_bits = [1 << k for k in range(3, size.bit_length() - 1)]
    steps = [(1, 1), (2, 4), (4, 2)] + list(zip(high_bits, high_bits[::-1]))
    flat = {1 << (b + rep_bits): k for k, b in enumerate(bits)}
    slots = [(flat.get(even), flat.get(odd)) for even, odd in steps]
    filled = [k for k, pair in enumerate(slots) if pair != (None, None)]
    assert filled[0] > 0 and len(set(flat)) == len(bits)

    others = [swapped(feats, b) for b in bits]
    count = len(bits)
    tall = count * rows
    stacked = heads * rows
    gain1 = norm1_gain.reshape(1, width)
    gain2 = norm2_gain.reshape(1, width)
    upstream = out_grad[0]
    weights = (w_query, w_key, w_value, w_out, w_up, w_down)
    prepared = call(
        functools.partial(own_kernel, groups),
        tuple(struct(w.shape, BF16) for w in weights)
        + (
            struct((rows, width), F32),
            struct((stacked, width), BF16),
            struct((rows, width), BF16),
            struct((rows, width), BF16),
            struct((stacked, rows), F32),
            struct((stacked, rows), F32),
            struct((stacked, rows), F32),
            struct((rows, tall), F32),
            struct((rows, w_up.shape[1]), F32),
        ),
        feats,
        upstream,
        gain1,
        *weights,
        local_gain,
        partners,
        in_specs=[VM] * 3 + [ANY] * 6 + [SM, VM],
        scratch_shapes=[pltpu.SemaphoreType.DMA((6,))],
    )
    node_out, keep, send, own, grad_mixed, *slot_rows = call(
        functools.partial(layer_kernel, [slots[k] for k in filled], count),
        (
            struct((rows, width), BF16),
            struct((4 * width, width), BF16),
            struct((4 * width + SMALL, width), BF16),
            struct((rows, width), F32),
            struct((rows, width), F32),
        )
        + tuple(struct((rows, width), BF16) for _ in filled),
        *others,
        feats,
        upstream,
        gain1,
        gain2,
        *prepared,
        local_gain,
        expander_gain,
        in_specs=[VM] * (count + 19) + [SM, SM],
        scratch_shapes=[
            pltpu.VMEM((stacked, tall), F32),
            pltpu.VMEM((stacked, tall), F32),
            pltpu.VMEM((stacked, rows), BF16),
            pltpu.VMEM((stacked, tall), BF16),
            pltpu.VMEM((stacked, rows), BF16),
            pltpu.VMEM((stacked, tall), BF16),
        ],
    )
    slot_at = dict(zip(filled, slot_rows))

    returned = []
    starts = []
    data = 4 * width
    for k, (even, odd) in enumerate(steps):
        recv = flipped(send, even, odd)
        if k in slot_at:
            returned.append(recv)
            starts.append(data + SMALL)
        halve = k < 2
        size_next = data // 2 if halve else data
        extra = [slot_at[k + 1]] if k + 1 in slot_at else []
        outs = (struct((size_next + SMALL + rows * len(extra), width), BF16),)
        if halve:
            outs = (struct((size_next, width), BF16),) + outs
        res = call(
            functools.partial(merge_kernel, data, halve),
            outs,
            keep if k <= 2 else send,
            send,
            recv,
            *extra,
        )
        keep, send = res[0], res[-1]
        data = size_next
    base = send
    grad_feats = call(
        functools.partial(tail_kernel, starts),
        struct((rows, width), BF16),
        feats,
        own,
        grad_mixed,
        gain1,
        *returned,
    )

    one = flipped(base[:width], 4, 2)
    near = jnp.concatenate([base[:width], one], axis=0)
    near = jnp.concatenate([near, flipped(near, 2, 4)], axis=0)
    pieces = jnp.concatenate([near, flipped(near, 1, 1)], axis=0)
    square = struct((width, width), F32)
    results = pl.pallas_call(
        spread_kernel,
        out_shape=(
            struct((1, width), F32),
            square,
            square,
            square,
            square,
            struct((1, width), F32),
            struct((width, 2 * width), F32),
            struct((2 * width, width), F32),
            struct((heads,), F32),
            struct((heads,), F32),
        ),
        in_specs=[VM] * 2,
        out_specs=(VM, ANY, ANY, ANY, ANY, VM, ANY, ANY, VM, VM),
        scratch_shapes=[pltpu.VMEM((8, width, width), F32), pltpu.SemaphoreType.DMA((8,))],
        compiler_params=PARAMS,
    )(pieces, base)
    grad_gain1, grad_wq, grad_wk, grad_wv, grad_wout, grad_gain2, grad_up, grad_down, grad_local, grad_far = results
    return (
        node_out[None],
        grad_feats[None],
        grad_gain1.reshape(width),
        grad_wq,
        grad_wk,
        grad_wv,
        grad_wout,
        grad_gain2.reshape(width),
        grad_up,
        grad_down,
        grad_local,
        grad_far,
    )


def solution(mesh):
    whole = P()
    rows = P("rep", "dom", None)
    return jax.shard_map(
        local,
        mesh=mesh,
        in_specs=(rows, rows)
        + (whole,) * 10
        + (P("rep", None, "dom", None), rows, P("rep", "dom")),
        out_specs=(rows, rows) + (whole,) * 10,
        check_vma=False,
    )
```

time: 79.9 us -> 74.6 us (0.934)
  starting transfers between devices: 16.8 us -> 12.1 us
  waiting for transfers between devices: 43.7 us -> 39.5 us
  Pallas kernels: 9.68 us -> 12.4 us
    ppermute x6 -> x3, waiting for transfers between devices: 10.4 us -> 0.01 us  [swapped(): lax.ppermute(x, 'dom', [(i, i ^ 1 << bit) for i in range(lax.axis_size('d...]
    ppermute x10 -> x8, waiting for transfers between devices: 33.3 us -> 39.5 us  [flipped(): return lax.ppermute(x, AXES, pairs)]
    ppermute x6 -> x3, starting transfers between devices: 10.5 us -> 7.2 us  [swapped(): lax.ppermute(x, 'dom', [(i, i ^ 1 << bit) for i in range(lax.axis_size('d...]
    pallas_call x7 -> x8, Pallas kernels: 7.59 us -> 10.4 us  [call(): pl.pallas_call(kernel, out_shape=outs, in_specs=in_specs or [VM] * len(ar...]
    ppermute x10 -> x8, starting transfers between devices: 6.35 us -> 4.9 us  [flipped(): return lax.ppermute(x, AXES, pairs)]
    unnamed x28 -> x30, local copies, waits for them, and re-layouts: 7.91 us -> 9.26 us
  transfers between devices with their start and end apart: 16 -> 11, of which waited for: 12 -> 8; matrix products, arithmetic and copies ran while one was open for 0% -> 0% of each run, Pallas kernels for 1% -> 5%
where the time goes in v2:
time: 74.6 us; the launch traced here: 74.2 us
  waiting for transfers between devices  39.5 us (53%)
  Pallas kernels  12.4 us (17%)
  starting transfers between devices  12.1 us (16%)
  local copies, waits for them, and re-layouts  9.27 us (12%)
  between operations  0.8 us (1%)
    ppermute x8, waiting for transfers between devices, flipped(): return lax.ppermute(x, AXES, pairs)  39.5 us
    pallas_call x8, Pallas kernels, call(): pl.pallas_call(kernel, out_shape=outs, in_specs=in_specs or [VM] * len(ar...  10.4 us
    unnamed x30, local copies, waits for them, and re-layouts  9.26 us
    ppermute x3, starting transfers between devices, swapped(): lax.ppermute(x, 'dom', [(i, i ^ 1 << bit) for i in range(lax.axis_size('d...  7.2 us
    ppermute x8, starting transfers between devices, flipped(): return lax.ppermute(x, AXES, pairs)  4.9 us
    pallas_call x1, Pallas kernels, local(): pl.pallas_call(spread_kernel, out_shape=(struct((1, width), F32), square,...  1.98 us
  transfers between devices with their start and end apart: 11, of which 8 were waited for; matrix products, arithmetic and copies ran while one was open for 0% of the time, Pallas kernels for 5%

profile of v2, /device:TPU:0, one launch (start us, length us, event | category | flops | bytes accessed | tf_op | source)
XLA Modules:
  0.0 74.2 jit_solution(9171006351597314999)
XLA Ops:
  0.6 0.0 copy-start.14
  0.7 0.0 copy-start.13
  0.7 3.0 %collective-permute-start.2 = (bf16[128,256]{1,0:T(8,128)(2,1)}, bf16[128,256]{1,0:T(8,128)(2,1)S(1)}, u32[]{:S(2)}, u32[]{:S(2)}) collective-permute-start(bf16[128,256]{1,0:T(8,128)(2,1)} %bitcast.9), channel_id=1, source_target_pairs={{0,4},{4,0},{8,12},{12,8},{16,20},{20,16},{24,28},{28,24},{1,5},{5... | collective-permute-start | bytes 196616 | tf_op jit(solution)/shard_map/ppermute | solution.py:465
  3.7 1.6 %collective-permute-start.1 = (bf16[128,256]{1,0:T(8,128)(2,1)}, bf16[128,256]{1,0:T(8,128)(2,1)S(1)}, u32[]{:S(2)}, u32[]{:S(2)}) collective-permute-start(bf16[128,256]{1,0:T(8,128)(2,1)} %bitcast.10), channel_id=1, source_target_pairs={{0,8},{4,12},{8,0},{12,4},{16,24},{20,28},{24,16},{28,20},{1,9},{5... | collective-permute-start | bytes 196616 | tf_op jit(solution)/shard_map/ppermute | solution.py:465
  5.3 2.6 %collective-permute-start = (bf16[128,256]{1,0:T(8,128)(2,1)}, bf16[128,256]{1,0:T(8,128)(2,1)S(1)}, u32[]{:S(2)}, u32[]{:S(2)}) collective-permute-start(bf16[128,256]{1,0:T(8,128)(2,1)} %bitcast.11), channel_id=1, source_target_pairs={{0,16},{4,20},{8,24},{12,28},{16,0},{20,4},{24,8},{28,12},{1,17},{... | collective-permute-start | bytes 196616 | tf_op jit(solution)/shard_map/ppermute | solution.py:465
  7.9 0.9 %copy-done = bf16[1,128,256]{2,1,0:T(8,128)(2,1)S(1)} copy-done((bf16[1,128,256]{2,1,0:T(8,128)(2,1)S(1)}, bf16[1,128,256]{2,1,0:T(8,128)(2,1)}, u32[]{:S(2)}) %copy-start) | copy-done | bytes 65560
  8.7 0.9 %copy-done.2 = bf16[256,512]{1,0:T(8,128)(2,1)S(1)} copy-done((bf16[256,512]{1,0:T(8,128)(2,1)S(1)}, bf16[256,512]{1,0:T(8,128)(2,1)}, u32[]{:S(2)}) %copy-start.2) | copy-done | bytes 262168
  9.7 0.9 %copy-done.3 = bf16[512,256]{1,0:T(8,128)(2,1)S(1)} copy-done((bf16[512,256]{1,0:T(8,128)(2,1)S(1)}, bf16[512,256]{1,0:T(8,128)(2,1)}, u32[]{:S(2)}) %copy-start.3) | copy-done | bytes 262168
  10.6 0.8 %copy-done.4 = bf16[1,128,256]{2,1,0:T(8,128)(2,1)S(1)} copy-done((bf16[1,128,256]{2,1,0:T(8,128)(2,1)S(1)}, bf16[1,128,256]{2,1,0:T(8,128)(2,1)}, u32[]{:S(2)}) %copy-start.4) | copy-done | bytes 65560
  11.5 0.9 %copy-done.5 = bf16[256,256]{1,0:T(8,128)(2,1)S(1)} copy-done((bf16[256,256]{1,0:T(8,128)(2,1)S(1)}, bf16[256,256]{1,0:T(8,128)(2,1)}, u32[]{:S(2)}) %copy-start.5) | copy-done | bytes 131096
  12.4 0.9 %copy-done.6 = bf16[256,256]{1,0:T(8,128)(2,1)S(1)} copy-done((bf16[256,256]{1,0:T(8,128)(2,1)S(1)}, bf16[256,256]{1,0:T(8,128)(2,1)}, u32[]{:S(2)}) %copy-start.6) | copy-done | bytes 131096
  13.3 0.9 %copy-done.7 = bf16[256,256]{1,0:T(8,128)(2,1)S(1)} copy-done((bf16[256,256]{1,0:T(8,128)(2,1)S(1)}, bf16[256,256]{1,0:T(8,128)(2,1)}, u32[]{:S(2)}) %copy-start.7) | copy-done | bytes 131096
  14.2 0.9 %copy-done.8 = bf16[256,256]{1,0:T(8,128)(2,1)S(1)} copy-done((bf16[256,256]{1,0:T(8,128)(2,1)S(1)}, bf16[256,256]{1,0:T(8,128)(2,1)}, u32[]{:S(2)}) %copy-start.8) | copy-done | bytes 131096
  15.1 0.7 copy-done.9
  15.8 0.7 copy-done.11
  16.4 0.7 copy-done.12
  17.1 2.6 %shard_map.220 = (bf16[256,256]{1,0:T(8,128)(2,1)S(1)}, bf16[256,256]{1,0:T(8,128)(2,1)S(1)}, bf16[256,256]{1,0:T(8,128)(2,1)S(1)}, bf16[256,256]{1,0:T(8,128)(2...) custom-call(bf16[128,256]{1,0:T(8,128)(2,1)S(1)} %bitcast.12, ...), custom_call_target="tpu_custom_call" | custom-call | tf_op jit(solution)/shard_map/pallas_call | solution.py:419
  19.7 0.0 collective-permute-done.2.refs_2_
  19.7 0.0 collective-permute-done.1.refs_1_
  19.7 0.0 collective-permute-done.refs_0_
  19.8 0.0 copy-done.14
  19.8 0.0 copy-done.13
  19.8 6.6 %shard_map.221 = (bf16[128,256]{1,0:T(8,128)(2,1)}, bf16[1024,256]{1,0:T(8,128)(2,1)S(1)}, bf16[1040,256]{1,0:T(8,128)(2,1)S(1)}, f32[128,256]{1,0:T(8,128)S(1)}...) custom-call(bf16[128,256]{1,0:T(8,128)(2,1)S(1)} %collective-permute, ...), custom_call_target="tpu_custom_call" | custom-call | tf_op jit(solution)/shard_map/pallas_call | solution.py:419
  26.4 0.0 collective-permute-start.3
  26.4 1.9 %collective-permute-done.3.refs_2_ = bf16[1040,256]{1,0:T(8,128)(2,1)S(1)} collective-permute-done((bf16[1040,256]{1,0:T(8,128)(2,1)S(1)}, bf16[1040,256]{1,0:T(8,128)(2,1)S(1)}, u32[]{:S(2)}, u32[]{:S(2)}) %collective-permute-start.3) | collective-permute-done | bytes 532512 | tf_op jit(solution)/shard_map/ppermute | solution.py:432
  28.3 0.1 shard_map.222
  28.5 1.6 %collective-permute-start.4 = (bf16[656,256]{1,0:T(8,128)(2,1)S(1)}, bf16[656,256]{1,0:T(8,128)(2,1)S(1)}, u32[]{:S(2)}, u32[]{:S(2)}) collective-permute-start(bf16[656,256]{1,0:T(8,128)(2,1)S(1)} %get-tuple-element.71.refs_1_), channel_id=1, source_target_pairs={{0,2},{1,5},{2,0},{3,7},{4,6},{5,1},{6,4},{7,3},{8,10},{9,13},{10,... | collective-permute-start | bytes 1007624 | tf_op jit(solution)/shard_map/ppermute | solution.py:432
  30.0 5.7 %collective-permute-done.4.refs_2_.refs_4_ = bf16[656,256]{1,0:T(8,128)(2,1)S(1)} collective-permute-done((bf16[656,256]{1,0:T(8,128)(2,1)S(1)}, bf16[656,256]{1,0:T(8,128)(2,1)S(1)}, u32[]{:S(2)}, u32[]{:S(2)}) %collective-permute-start.4) | collective-permute-done | bytes 335904 | tf_op jit(solution)/shard_map/ppermute | solution.py:432
  35.7 0.1 shard_map.223
  35.8 0.6 collective-permute-start.5
  36.3 5.3 %collective-permute-done.5.refs_2_.refs_5_ = bf16[400,256]{1,0:T(8,128)(2,1)S(1)} collective-permute-done((bf16[400,256]{1,0:T(8,128)(2,1)S(1)}, bf16[400,256]{1,0:T(8,128)(2,1)S(1)}, u32[]{:S(2)}, u32[]{:S(2)}) %collective-permute-start.5) | collective-permute-done | bytes 204832 | tf_op jit(solution)/shard_map/ppermute | solution.py:432
  41.6 0.5 collective-permute-start.6
  42.1 7.4 %collective-permute-done.6.refs_2_.refs_6_ = bf16[400,256]{1,0:T(8,128)(2,1)S(1)} collective-permute-done((bf16[400,256]{1,0:T(8,128)(2,1)S(1)}, bf16[400,256]{1,0:T(8,128)(2,1)S(1)}, u32[]{:S(2)}, u32[]{:S(2)}) %collective-permute-start.6) | collective-permute-done | bytes 204832 | tf_op jit(solution)/shard_map/ppermute | solution.py:432
  49.6 0.1 collective-permute-start.7
  49.7 7.8 %collective-permute-done.7.refs_7_.refs_2_ = bf16[400,256]{1,0:T(8,128)(2,1)S(1)} collective-permute-done((bf16[400,256]{1,0:T(8,128)(2,1)S(1)}, bf16[400,256]{1,0:T(8,128)(2,1)S(1)}, u32[]{:S(2)}, u32[]{:S(2)}) %collective-permute-start.7) | collective-permute-done | bytes 204832 | tf_op jit(solution)/shard_map/ppermute | solution.py:432
  57.5 0.0 copy-start.1
  57.5 0.0 copy-start.10
  57.6 0.6 collective-permute-start.8
  58.1 5.6 %collective-permute-done.8 = bf16[256,256]{1,0:T(8,128)(2,1)S(1)} collective-permute-done((bf16[256,256]{1,0:T(8,128)(2,1)S(1)}, bf16[256,256]{1,0:T(8,128)(2,1)S(1)}, u32[]{:S(2)}, u32[]{:S(2)}) %collective-permute-start.8) | collective-permute-done | bytes 131104 | tf_op jit(solution)/shard_map/ppermute | solution.py:432
  63.7 1.6 %collective-permute-start.9 = (bf16[512,256]{1,0:T(8,128)(2,1)S(1)}, bf16[512,256]{1,0:T(8,128)(2,1)S(1)}, u32[]{:S(2)}, u32[]{:S(2)}) collective-permute-start(bf16[512,256]{1,0:T(8,128)(2,1)S(1)} %pad_maximum_fusion.2), channel_id=1, source_target_pairs={{0,2},{1,5},{2,0},{3,7},{4,6},{5,1},{6,4},{7,3},{8,10},{9,13},{10,... | collective-permute-start | bytes 786440 | tf_op jit(solution)/shard_map/ppermute | solution.py:432
  65.3 4.9 %collective-permute-done.9 = bf16[512,256]{1,0:T(8,128)(2,1)S(1)} collective-permute-done((bf16[512,256]{1,0:T(8,128)(2,1)S(1)}, bf16[512,256]{1,0:T(8,128)(2,1)S(1)}, u32[]{:S(2)}, u32[]{:S(2)}) %collective-permute-start.9) | collective-permute-done | bytes 262176 | tf_op jit(solution)/shard_map/ppermute | solution.py:432
  70.2 0.1 collective-permute-start.10
  70.3 0.0 copy-done.1
  70.3 0.0 copy-done.10
  70.3 0.9 %shard_map.226 = bf16[128,256]{1,0:T(8,128)(2,1)} custom-call(bf16[128,256]{1,0:T(8,128)(2,1)S(1)} %bitcast.14, f32[128,256]{1,0:T(8,128)S(1)} %get-tuple-element.66.refs_1_, f32[128,256]{1,0:T(8,128)S(1)} %get-tuple-element.67.refs_2_, f32[1,256]{1,0:T(1,128)S(1)} %bitcast.19, bf16[656,256]{1,0:T(8,128)(2,1)S(1)} %collective-permute-done.4.refs_2_.refs_4_, ...), custom_call_target="tpu_custom_call" | custom-call | tf_op jit(solution)/shard_map/pallas_call | solution.py:419
  71.2 1.0 %collective-permute-done.10 = bf16[1024,256]{1,0:T(8,128)(2,1)S(1)} collective-permute-done((bf16[1024,256]{1,0:T(8,128)(2,1)S(1)}, bf16[1024,256]{1,0:T(8,128)(2,1)S(1)}, u32[]{:S(2)}, u32[]{:S(2)}) %collective-permute-start.10) | collective-permute-done | bytes 524320 | tf_op jit(solution)/shard_map/ppermute | solution.py:432
  72.2 0.1 pad_maximum_fusion.pieces_ref
  72.2 2.0 %shard_map.228 = (f32[1,256]{1,0:T(1,128)}, f32[256,256]{1,0:T(8,128)}, f32[256,256]{1,0:T(8,128)}, f32[256,256]{1,0:T(8,128)}, f32[256,256]{1,0:T(8,128)}, /*in...) custom-call(bf16[2048,256]{1,0:T(8,128)(2,1)S(1)} %pad_maximum_fusion.pieces_ref, ...), custom_call_target="tpu_custom_call" | custom-call | tf_op jit(solution)/shard_map/pallas_call | solution.py:576
  (17 shorter events, 0.2 us)
Async XLA Ops:
  0.6 19.1 %copy-start.14 = (f32[4]{0:T(128)S(1)}, f32[4]{0:T(128)}, u32[]{:S(2)}) copy-start(f32[4]{0:T(128)} %refs_23_.1) | copy-start | bytes 52
  0.7 19.1 %copy-start.13 = (f32[256]{0:T(256)S(1)}, f32[256]{0:T(256)}, u32[]{:S(2)}) copy-start(f32[256]{0:T(256)} %param.22) | copy-start | bytes 3076
  0.7 19.1 %collective-permute-start.2 = (bf16[128,256]{1,0:T(8,128)(2,1)}, bf16[128,256]{1,0:T(8,128)(2,1)S(1)}, u32[]{:S(2)}, u32[]{:S(2)}) collective-permute-start(bf16[128,256]{1,0:T(8,128)(2,1)} %bitcast.9), channel_id=1, source_target_pairs={{0,4},{4,0},{8,12},{12,8},{16,20},{20,16},{24,28},{28,24},{1,5},{5... | collective-permute-start | bytes 196616 | tf_op jit(solution)/shard_map/ppermute | solution.py:465
  3.7 16.0 %collective-permute-start.1 = (bf16[128,256]{1,0:T(8,128)(2,1)}, bf16[128,256]{1,0:T(8,128)(2,1)S(1)}, u32[]{:S(2)}, u32[]{:S(2)}) collective-permute-start(bf16[128,256]{1,0:T(8,128)(2,1)} %bitcast.10), channel_id=1, source_target_pairs={{0,8},{4,12},{8,0},{12,4},{16,24},{20,28},{24,16},{28,20},{1,9},{5... | collective-permute-start | bytes 196616 | tf_op jit(solution)/shard_map/ppermute | solution.py:465
  5.3 14.5 %collective-permute-start = (bf16[128,256]{1,0:T(8,128)(2,1)}, bf16[128,256]{1,0:T(8,128)(2,1)S(1)}, u32[]{:S(2)}, u32[]{:S(2)}) collective-permute-start(bf16[128,256]{1,0:T(8,128)(2,1)} %bitcast.11), channel_id=1, source_target_pairs={{0,16},{4,20},{8,24},{12,28},{16,0},{20,4},{24,8},{28,12},{1,17},{... | collective-permute-start | bytes 196616 | tf_op jit(solution)/shard_map/ppermute | solution.py:465
  7.9 0.9 %copy-start = (bf16[1,128,256]{2,1,0:T(8,128)(2,1)S(1)}, bf16[1,128,256]{2,1,0:T(8,128)(2,1)}, u32[]{:S(2)}) copy-start(bf16[1,128,256]{2,1,0:T(8,128)(2,1)} %param.15) | copy-start | bytes 196612
  8.7 0.9 %copy-start.2 = (bf16[256,512]{1,0:T(8,128)(2,1)S(1)}, bf16[256,512]{1,0:T(8,128)(2,1)}, u32[]{:S(2)}) copy-start(bf16[256,512]{1,0:T(8,128)(2,1)} %wup_hbm.1) | copy-start | bytes 786436
  9.7 0.9 %copy-start.3 = (bf16[512,256]{1,0:T(8,128)(2,1)S(1)}, bf16[512,256]{1,0:T(8,128)(2,1)}, u32[]{:S(2)}) copy-start(bf16[512,256]{1,0:T(8,128)(2,1)} %wdown_hbm.1) | copy-start | bytes 786436
  10.6 0.8 %copy-start.4 = (bf16[1,128,256]{2,1,0:T(8,128)(2,1)S(1)}, bf16[1,128,256]{2,1,0:T(8,128)(2,1)}, u32[]{:S(2)}) copy-start(bf16[1,128,256]{2,1,0:T(8,128)(2,1)} %param.16) | copy-start | bytes 196612
  11.5 0.9 %copy-start.5 = (bf16[256,256]{1,0:T(8,128)(2,1)S(1)}, bf16[256,256]{1,0:T(8,128)(2,1)}, u32[]{:S(2)}) copy-start(bf16[256,256]{1,0:T(8,128)(2,1)} %wq_hbm.1) | copy-start | bytes 393220
  12.4 0.9 %copy-start.6 = (bf16[256,256]{1,0:T(8,128)(2,1)S(1)}, bf16[256,256]{1,0:T(8,128)(2,1)}, u32[]{:S(2)}) copy-start(bf16[256,256]{1,0:T(8,128)(2,1)} %wk_hbm.1) | copy-start | bytes 393220
  13.3 0.9 %copy-start.7 = (bf16[256,256]{1,0:T(8,128)(2,1)S(1)}, bf16[256,256]{1,0:T(8,128)(2,1)}, u32[]{:S(2)}) copy-start(bf16[256,256]{1,0:T(8,128)(2,1)} %wv_hbm.1) | copy-start | bytes 393220
  14.2 0.9 %copy-start.8 = (bf16[256,256]{1,0:T(8,128)(2,1)S(1)}, bf16[256,256]{1,0:T(8,128)(2,1)}, u32[]{:S(2)}) copy-start(bf16[256,256]{1,0:T(8,128)(2,1)} %wo_hbm.1) | copy-start | bytes 393220
  15.1 0.7 copy-start.9
  15.8 0.7 copy-start.11
  16.4 0.7 copy-start.12
  26.4 1.9 %collective-permute-start.3 = (bf16[1040,256]{1,0:T(8,128)(2,1)S(1)}, bf16[1040,256]{1,0:T(8,128)(2,1)S(1)}, u32[]{:S(2)}, u32[]{:S(2)}) collective-permute-start(bf16[1040,256]{1,0:T(8,128)(2,1)S(1)} %get-tuple-element.69.refs_1_), channel_id=1, source_target_pairs={{0,1},{1,0},{2,3},{3,2},{4,5},{5,4},{6,7},{7,6},{8,9},{9,8},{10,11... | collective-permute-start | bytes 1597448 | tf_op jit(solution)/shard_map/ppermute | solution.py:432
  28.5 7.2 %collective-permute-start.4 = (bf16[656,256]{1,0:T(8,128)(2,1)S(1)}, bf16[656,256]{1,0:T(8,128)(2,1)S(1)}, u32[]{:S(2)}, u32[]{:S(2)}) collective-permute-start(bf16[656,256]{1,0:T(8,128)(2,1)S(1)} %get-tuple-element.71.refs_1_), channel_id=1, source_target_pairs={{0,2},{1,5},{2,0},{3,7},{4,6},{5,1},{6,4},{7,3},{8,10},{9,13},{10,... | collective-permute-start | bytes 1007624 | tf_op jit(solution)/shard_map/ppermute | solution.py:432
  35.8 5.8 %collective-permute-start.5 = (bf16[400,256]{1,0:T(8,128)(2,1)S(1)}, bf16[400,256]{1,0:T(8,128)(2,1)S(1)}, u32[]{:S(2)}, u32[]{:S(2)}) collective-permute-start(bf16[400,256]{1,0:T(8,128)(2,1)S(1)} %get-tuple-element.74.refs_1_), channel_id=1, source_target_pairs={{0,4},{1,3},{2,6},{3,1},{4,0},{5,7},{6,2},{7,5},{8,12},{9,11},{10,... | collective-permute-start | bytes 614408 | tf_op jit(solution)/shard_map/ppermute | solution.py:432
  41.6 7.9 %collective-permute-start.6 = (bf16[400,256]{1,0:T(8,128)(2,1)S(1)}, bf16[400,256]{1,0:T(8,128)(2,1)S(1)}, u32[]{:S(2)}, u32[]{:S(2)}) collective-permute-start(bf16[400,256]{1,0:T(8,128)(2,1)S(1)} %shard_map.224.refs_0_.refs_1_), channel_id=1, source_target_pairs={{0,8},{1,17},{2,10},{3,19},{4,12},{5,21},{6,14},{7,23},{8,0},{9,25... | collective-permute-start | bytes 614408 | tf_op jit(solution)/shard_map/ppermute | solution.py:432
  49.6 7.9 %collective-permute-start.7 = (bf16[400,256]{1,0:T(8,128)(2,1)S(1)}, bf16[400,256]{1,0:T(8,128)(2,1)S(1)}, u32[]{:S(2)}, u32[]{:S(2)}) collective-permute-start(bf16[400,256]{1,0:T(8,128)(2,1)S(1)} %shard_map.225.refs_0_.refs_1_), channel_id=1, source_target_pairs={{0,16},{1,9},{2,18},{3,11},{4,20},{5,13},{6,22},{7,15},{8,24},{9,1... | collective-permute-start | bytes 614408 | tf_op jit(solution)/shard_map/ppermute | solution.py:432
  57.5 12.7 %copy-start.1 = (bf16[1,128,256]{2,1,0:T(8,128)(2,1)S(1)}, bf16[1,128,256]{2,1,0:T(8,128)(2,1)}, u32[]{:S(2)}) copy-start(bf16[1,128,256]{2,1,0:T(8,128)(2,1)} %param.15) | copy-start | bytes 196612
  57.5 12.7 %copy-start.10 = (f32[256]{0:T(256)S(1)}, f32[256]{0:T(256)}, u32[]{:S(2)}) copy-start(f32[256]{0:T(256)} %param.17) | copy-start | bytes 3076
  57.6 6.1 %collective-permute-start.8 = (bf16[256,256]{1,0:T(8,128)(2,1)S(1)}, bf16[256,256]{1,0:T(8,128)(2,1)S(1)}, u32[]{:S(2)}, u32[]{:S(2)}) collective-permute-start(bf16[256,256]{1,0:T(8,128)(2,1)S(1)} %slice.5), channel_id=1, source_target_pairs={{0,4},{1,3},{2,6},{3,1},{4,0},{5,7},{6,2},{7,5},{8,12},{9,11},{10,... | collective-permute-start | bytes 393224 | tf_op jit(solution)/shard_map/ppermute | solution.py:432
  63.7 6.4 %collective-permute-start.9 = (bf16[512,256]{1,0:T(8,128)(2,1)S(1)}, bf16[512,256]{1,0:T(8,128)(2,1)S(1)}, u32[]{:S(2)}, u32[]{:S(2)}) collective-permute-start(bf16[512,256]{1,0:T(8,128)(2,1)S(1)} %pad_maximum_fusion.2), channel_id=1, source_target_pairs={{0,2},{1,5},{2,0},{3,7},{4,6},{5,1},{6,4},{7,3},{8,10},{9,13},{10,... | collective-permute-start | bytes 786440 | tf_op jit(solution)/shard_map/ppermute | solution.py:432
  70.2 2.0 %collective-permute-start.10 = (bf16[1024,256]{1,0:T(8,128)(2,1)S(1)}, bf16[1024,256]{1,0:T(8,128)(2,1)S(1)}, u32[]{:S(2)}, u32[]{:S(2)}) collective-permute-start(bf16[1024,256]{1,0:T(8,128)(2,1)S(1)} %pad_maximum_fusion.1), channel_id=1, source_target_pairs={{0,1},{1,0},{2,3},{3,2},{4,5},{5,4},{6,7},{7,6},{8,9},{9,8},{10,11... | collective-permute-start | bytes 1572872 | tf_op jit(solution)/shard_map/ppermute | solution.py:432

commit v3 on v2

v3 whole, which is shorter than its diff:
```python
import functools

import jax
import jax.numpy as jnp
from jax import lax
from jax.experimental import pallas as pl
from jax.experimental.pallas import tpu as pltpu
from jax.sharding import PartitionSpec as P

EPSILON = 1e-05
SCORE_CAP = 5.0
GELU_ROOT = 0.7978845608028654
GELU_CUBIC = 0.044715
SMALL = 16
AXES = ("dom", "rep")
VMEM_LIMIT = 48 * 1024 * 1024
F32 = jnp.float32
BF16 = jnp.bfloat16


def dot(a, b):
    return lax.dot_general(a, b, (((1,), (0,)), ((), ())), preferred_element_type=F32)


def dot_rhs_t(a, b):
    return lax.dot_general(a, b, (((1,), (1,)), ((), ())), preferred_element_type=F32)


def dot_lhs_t(a, b):
    return lax.dot_general(a, b, (((0,), (0,)), ((), ())), preferred_element_type=F32)


def norm_forward(matrix):
    center = jnp.mean(matrix, axis=-1, keepdims=True)
    shifted = matrix - center
    inverse = lax.rsqrt(jnp.mean(shifted * shifted, axis=-1, keepdims=True) + EPSILON)
    return (shifted * inverse, inverse)


def norm_backward(upstream, normed, inverse, gain):
    scaled_up = upstream * gain
    return inverse * (
        scaled_up
        - jnp.mean(scaled_up, axis=-1, keepdims=True)
        - normed * jnp.mean(scaled_up * normed, axis=-1, keepdims=True)
    )


def gelu_parts(preact):
    tangent = jnp.tanh(GELU_ROOT * (preact + GELU_CUBIC * preact * preact * preact))
    result = 0.5 * preact * (1.0 + tangent)
    derivative = 0.5 * (1.0 + tangent) + 0.5 * preact * (1.0 - tangent * tangent) * GELU_ROOT * (
        1.0 + 3.0 * GELU_CUBIC * preact * preact
    )
    return (result, derivative)


def split_parts(rows):
    high = rows.astype(BF16).astype(F32)
    return jnp.concatenate([high, rows - high], axis=0).astype(BF16)


def join_parts(packed):
    wide = packed.astype(F32)
    return wide[: SMALL // 2] + wide[SMALL // 2 :]


def device_bits():
    flat = lax.axis_index("dom") * lax.axis_size("rep") + lax.axis_index("rep")
    return (flat & 1, (flat >> 1) & 3)


def head_masks_of(shape, heads):
    lane = lax.broadcasted_iota(jnp.int32, shape, 1) // (shape[1] // heads)
    return [lane == h for h in range(heads)]


def stack_heads(matrix, masks):
    return jnp.concatenate([jnp.where(m, matrix, 0.0) for m in masks], axis=0).astype(BF16)


def first_kernel(groups, feats_ref, gain1_ref, perm_ref, normed_ref, hidden_ref, count_ref):
    rows = feats_ref.shape[0]
    target = lax.broadcasted_iota(jnp.int32, (rows, rows), 0)
    for g, members in enumerate(groups):
        total = 0.0
        for m in members:
            total = total + jnp.where(target == perm_ref[m : m + 1, :], 1.0, 0.0)
        count_ref[:, g * rows : (g + 1) * rows] = total.T
    normed, _ = norm_forward(feats_ref[...].astype(F32))
    normed_ref[...] = normed
    hidden_ref[...] = (normed * gain1_ref[...]).astype(BF16)


def own_kernel(
    hidden_ref,
    up_ref,
    wq_ref,
    wk_ref,
    wv_ref,
    wdown_ref,
    local_ref,
    query_ref,
    key_ref,
    value_ref,
    raw_ref,
    tanh_ref,
    exp_ref,
    back_ref,
):
    rows, width = hidden_ref.shape
    heads = local_ref.shape[0]
    scale = 1.0 / float(width // heads) ** 0.5
    hidden = hidden_ref[...]
    query = stack_heads(dot(hidden, wq_ref[...]), head_masks_of((rows, width), heads))
    query_ref[...] = query
    key = dot(hidden, wk_ref[...]).astype(BF16)
    key_ref[...] = key
    value_ref[...] = dot(hidden, wv_ref[...]).astype(BF16)
    raw_ref[...] = dot_rhs_t(query, key) * scale
    for h in range(heads):
        block = pl.ds(h * rows, rows)
        tangent = jnp.tanh(raw_ref[block, :] * (local_ref[h] / SCORE_CAP))
        tanh_ref[block, :] = tangent
        exp_ref[block, :] = jnp.exp(SCORE_CAP * tangent)
    back_ref[...] = dot_rhs_t(up_ref[...], wdown_ref[...])


def put_unit(keep_ref, send_ref, bits, unit, value):
    core, quad = bits
    rows = value.shape[0]
    span = pl.ds(pl.multiple_of(((unit & 3) ^ quad) * rows, rows), rows)
    same = core == (unit >> 2)

    @pl.when(same)
    def _():
        keep_ref[span, :] = value

    @pl.when(jnp.logical_not(same))
    def _():
        send_ref[span, :] = value


def put_square(keep_ref, send_ref, bits, chunk, value):
    value = value.astype(BF16)
    half = value.shape[0] // 2
    put_unit(keep_ref, send_ref, bits, 2 * chunk, value[:half])
    put_unit(keep_ref, send_ref, bits, 2 * chunk + 1, value[half:])


def collapse(matrix, masks):
    rows = matrix.shape[0] // len(masks)
    total = jnp.where(masks[0], matrix[:rows], 0.0)
    for h in range(1, len(masks)):
        total = total + jnp.where(masks[h], matrix[h * rows : (h + 1) * rows], 0.0)
    return total


def forward_kernel(count, *refs):
    others = refs[:count]
    (
        feats_ref,
        up_ref,
        gain1_ref,
        gain2_ref,
        wk_ref,
        wv_ref,
        wo_ref,
        wup_ref,
        wdown_ref,
        query_ref,
        value_ref,
        exp_ref,
        count_ref,
        back_ref,
        far_ref,
        out_ref,
        keep_ref,
        send_ref,
        mixed_ref,
        gain_ref,
        normed_ref,
        hidden_ref,
        keyf_ref,
        valuef_ref,
        raw_ref,
        tanh_ref,
        wl_ref,
        wf_ref,
        att_ref,
    ) = refs[count:]
    rows, width = out_ref.shape
    heads = far_ref.shape[0]
    scale = 1.0 / float(width // heads) ** 0.5
    bits = device_bits()
    upstream = up_ref[...]
    masks = head_masks_of((rows, width), heads)
    normed_far, _ = norm_forward(jnp.concatenate([ref[...] for ref in others], axis=0).astype(F32))
    normed_ref[...] = normed_far
    hidden_far = (normed_far * gain1_ref[...]).astype(BF16)
    hidden_ref[...] = hidden_far
    key_far = dot(hidden_far, wk_ref[...]).astype(BF16)
    value_far = dot(hidden_far, wv_ref[...]).astype(BF16)
    keyf_ref[...] = key_far
    valuef_ref[...] = value_far
    raw_ref[...] = dot_rhs_t(query_ref[...], key_far) * scale
    far_counts = count_ref[...]
    for h in range(heads):
        block = pl.ds(h * rows, rows)
        tangent = jnp.tanh(raw_ref[block, :] * (far_ref[h] / SCORE_CAP))
        near = exp_ref[block, :]
        far = jnp.exp(SCORE_CAP * tangent) * far_counts
        inv = 1.0 / (jnp.sum(near, axis=1, keepdims=True) + jnp.sum(far, axis=1, keepdims=True))
        tanh_ref[block, :] = tangent
        wl_ref[block, :] = (near * inv).astype(BF16)
        wf_ref[block, :] = (far * inv).astype(BF16)

    attended32 = collapse(dot(wl_ref[...], value_ref[...]) + dot(wf_ref[...], value_far), masks)
    att_ref[...] = attended32
    mixed = (feats_ref[...].astype(F32) + dot(attended32.astype(BF16), wo_ref[...])).astype(BF16)
    normed2, inverse2 = norm_forward(mixed.astype(F32))
    gain2 = gain2_ref[...]
    hidden2 = (normed2 * gain2).astype(BF16)
    preact = dot(hidden2, wup_ref[...])
    act32, derivative = gelu_parts(preact)
    act = act32.astype(BF16)
    grad_down = dot_lhs_t(act, upstream)
    put_square(keep_ref, send_ref, bits, 2, grad_down[:width])
    put_square(keep_ref, send_ref, bits, 3, grad_down[width:])
    grad_pre = (back_ref[...] * derivative).astype(BF16)
    grad_up = dot_lhs_t(hidden2, grad_pre)
    put_square(keep_ref, send_ref, bits, 0, grad_up[:, :width])
    put_square(keep_ref, send_ref, bits, 1, grad_up[:, width:])
    out_ref[...] = (mixed.astype(F32) + dot(act, wdown_ref[...])).astype(BF16)
    grad_hidden2 = dot_rhs_t(grad_pre, wup_ref[...])
    gain_ref[...] = jnp.sum(grad_hidden2 * normed2, axis=0, keepdims=True)
    mixed_ref[...] = upstream.astype(F32) + norm_backward(grad_hidden2, normed2, inverse2, gain2)


def backward_kernel(slots, count, *refs):
    (
        gain1_ref,
        gain2g_ref,
        wq_ref,
        wk_ref,
        wv_ref,
        wo_ref,
        near_hidden_ref,
        near_normed_ref,
        query_ref,
        key_ref,
        value_ref,
        rawl_ref,
        tanhl_ref,
        mixed_ref,
        normed_ref,
        hidden_ref,
        keyf_ref,
        valuef_ref,
        rawf_ref,
        tanhf_ref,
        wl_ref,
        wf_ref,
        att_ref,
        local_ref,
        far_ref,
        keep_ref,
        send_ref,
        own_ref,
    ) = refs[:28]
    slot_refs = refs[28 : 28 + len(slots)]
    dl_s, df_s = refs[28 + len(slots) :]
    rows, width = own_ref.shape
    heads = far_ref.shape[0]
    scale = 1.0 / float(width // heads) ** 0.5
    bits = device_bits()
    core = bits[0]
    masks = head_masks_of((rows, width), heads)
    attended32 = att_ref[...]
    grad_mixed16 = mixed_ref[...].astype(BF16)
    put_square(keep_ref, send_ref, bits, 3, dot_lhs_t(attended32.astype(BF16), grad_mixed16))
    grad_att = dot_rhs_t(grad_mixed16, wo_ref[...]).astype(BF16).astype(F32)
    grad_stack = stack_heads(grad_att, masks)
    product = grad_att * attended32
    near_dots = dot_rhs_t(grad_stack, value_ref[...])
    far_dots = dot_rhs_t(grad_stack, valuef_ref[...])

    near_terms = []
    far_terms = []
    for h in range(heads):
        block = pl.ds(h * rows, rows)
        span = slice(h * rows, (h + 1) * rows)
        delta = jnp.sum(jnp.where(masks[h], product, 0.0), axis=1, keepdims=True)
        for weights, dots, tangents, raw, dscore, gain, terms in (
            (wl_ref, near_dots, tanhl_ref, rawl_ref, dl_s, local_ref[h], near_terms),
            (wf_ref, far_dots, tanhf_ref, rawf_ref, df_s, far_ref[h], far_terms),
        ):
            tangent = tangents[block, :]
            slope = 1.0 - tangent * tangent
            sloped = weights[block, :].astype(F32) * (dots[span] - delta) * slope
            total = jnp.sum(sloped * raw[block, :], axis=0, keepdims=True)
            terms.append(jnp.sum(total, axis=1, keepdims=True))
            dscore[block, :] = (sloped * (gain * scale)).astype(BF16)

    query_stack = query_ref[...]
    grad_query = collapse(dot(dl_s[...], key_ref[...]) + dot(df_s[...], keyf_ref[...]), masks).astype(BF16)
    key_near = dot_lhs_t(dl_s[...], query_stack).astype(BF16)
    value_near = dot_lhs_t(wl_ref[...], grad_stack).astype(BF16)
    key_far = dot_lhs_t(df_s[...], query_stack).astype(BF16)
    value_far = dot_lhs_t(wf_ref[...], grad_stack).astype(BF16)
    hidden = near_hidden_ref[...]
    hidden_far = hidden_ref[...]
    put_square(keep_ref, send_ref, bits, 0, dot_lhs_t(hidden, grad_query))
    put_square(keep_ref, send_ref, bits, 1, dot_lhs_t(hidden, key_near) + dot_lhs_t(hidden_far, key_far))
    put_square(keep_ref, send_ref, bits, 2, dot_lhs_t(hidden, value_near) + dot_lhs_t(hidden_far, value_far))
    own = (
        dot_rhs_t(key_near, wk_ref[...])
        + dot_rhs_t(value_near, wv_ref[...])
        + dot_rhs_t(grad_query, wq_ref[...])
    )
    own_ref[...] = own
    theirs = dot_rhs_t(key_far, wk_ref[...]) + dot_rhs_t(value_far, wv_ref[...])
    grad_gain1 = jnp.sum(own * near_normed_ref[...], axis=0, keepdims=True)
    grad_gain1 = grad_gain1 + jnp.sum(theirs * normed_ref[...], axis=0, keepdims=True)
    back = [theirs[k * rows : (k + 1) * rows] for k in range(count)]
    for (even, odd), ref in zip(slots, slot_refs):
        ref[...] = jnp.where(
            core == 1, 0.0 if odd is None else back[odd], 0.0 if even is None else back[even]
        ).astype(BF16)

    column = lax.broadcasted_iota(jnp.int32, (1, width), 1)
    gains = jnp.zeros((1, width), F32)
    for h in range(heads):
        gains = jnp.where(column == h, near_terms[h], gains)
        gains = jnp.where(column == heads + h, far_terms[h], gains)
    line = lax.broadcasted_iota(jnp.int32, (SMALL // 2, width), 0)
    small = jnp.where(line == 0, grad_gain1, jnp.where(line == 1, gain2g_ref[...], jnp.where(line == 2, gains, 0.0)))
    send_ref[keep_ref.shape[0] :, :] = split_parts(small)


def pair_kernel(slots, keepw_ref, recvw_ref, keeps_ref, sents_ref, recvs_ref, *refs):
    slot_refs = refs[: sum(slots)]
    out_refs = refs[sum(slots) :]
    rows = keepw_ref.shape[0] // 4
    wide = (keepw_ref[...].astype(F32) + recvw_ref[...].astype(F32)).astype(BF16)
    square = (keeps_ref[...].astype(F32) + recvs_ref[: 4 * rows, :].astype(F32)).astype(BF16)
    packed = split_parts(join_parts(sents_ref[4 * rows :, :]) + join_parts(recvs_ref[4 * rows :, :]))
    used = 0
    for r in range(4):
        span = slice(r * rows, (r + 1) * rows)
        out_refs[r][:rows, :] = wide[span]
        out_refs[r][rows : 2 * rows, :] = square[span]
        out_refs[r][2 * rows : 2 * rows + SMALL, :] = packed
        if r and slots[r - 1]:
            out_refs[r][2 * rows + SMALL :, :] = slot_refs[used][...]
            used += 1


def quad_kernel(has_slot, own_ref, one_ref, two_ref, three_ref, *refs):
    wide_ref, square_ref = refs[-2:]
    total_rows = own_ref.shape[0]
    rows = (total_rows - SMALL) // 2
    data = [ref[: 2 * rows, :].astype(F32) for ref in (own_ref, one_ref, two_ref, three_ref)]
    small = [join_parts(ref[2 * rows : total_rows, :]) for ref in (own_ref, one_ref, two_ref, three_ref)]
    total = ((data[0] + data[1]) + (data[2] + data[3])).astype(BF16)
    wide_ref[:rows, :] = total[:rows]
    square_ref[:rows, :] = total[rows:]
    square_ref[rows:, :] = split_parts((small[0] + small[1]) + (small[2] + small[3]))
    if has_slot:
        wide_ref[rows:, :] = refs[0][...]


def double_kernel(rows, small, has_slot, own_ref, recv_ref, *refs):
    out_ref = refs[-1]
    total = own_ref[:rows, :].astype(F32) + recv_ref[:rows, :].astype(F32)
    out_ref[:rows, :] = total.astype(BF16)
    if small:
        span = slice(rows, rows + SMALL)
        out_ref[span, :] = split_parts(join_parts(own_ref[span, :]) + join_parts(recv_ref[span, :]))
    if has_slot:
        out_ref[rows:, :] = refs[0][...]


def join_kernel(wide_ref, square_ref, out_ref):
    rows = out_ref.shape[0] // 2
    out_ref[:rows, :] = wide_ref[:rows, :]
    out_ref[rows:, :] = square_ref[:rows, :]


def tail_kernel(start, *refs):
    feats_ref, own_ref, mixed_ref, gain_ref = refs[:4]
    normed, inverse = norm_forward(feats_ref[...].astype(F32))
    grad_hidden = own_ref[...]
    for ref, first in zip(refs[4:-1], start):
        grad_hidden = grad_hidden + ref[first:, :].astype(F32)
    refs[-1][...] = (mixed_ref[...] + norm_backward(grad_hidden, normed, inverse, gain_ref[...])).astype(BF16)


def spread_kernel(*refs):
    piece_refs = refs[:8]
    small_ref = refs[8]
    (
        gain1_ref,
        wq_ref,
        wk_ref,
        wv_ref,
        wo_ref,
        gain2_ref,
        up_ref,
        down_ref,
        local_ref,
        far_ref,
        pieces,
        chunks,
        sems,
    ) = refs[9:]
    width = wq_ref.shape[0]
    half = width // 2
    heads = local_ref.shape[0]
    core, quad = device_bits()
    for k, ref in enumerate(piece_refs):
        pieces[k] = ref[...]
    targets = [
        up_ref.at[:, :width],
        up_ref.at[:, width:],
        down_ref.at[:width, :],
        down_ref.at[width:, :],
        wq_ref,
        wk_ref,
        wv_ref,
        wo_ref,
    ]
    copies = []
    for chunk, target in enumerate(targets):
        first = 0 if chunk < 4 else half
        for part in range(2):
            unit = 2 * (chunk % 4) + part
            rel = (core ^ (unit >> 2)) * 4 + (quad ^ (unit & 3))
            value = pieces[rel, first : first + half, :]
            chunks[chunk, part * half : (part + 1) * half, :] = value.astype(F32)
        copy = pltpu.make_async_copy(chunks.at[chunk], target, sems.at[chunk])
        copy.start()
        copies.append(copy)
    small = join_parts(small_ref[small_ref.shape[0] - SMALL :, :])
    gain1_ref[...] = small[0:1]
    gain2_ref[...] = small[1:2]
    local_ref[...] = small[2, :heads]
    far_ref[...] = small[2, heads : 2 * heads]
    for copy in copies:
        copy.wait()


def struct(shape, dtype):
    return jax.ShapeDtypeStruct(shape, dtype)


VM = pl.BlockSpec(memory_space=pltpu.VMEM)
SM = pl.BlockSpec(memory_space=pltpu.SMEM)
ANY = pl.BlockSpec(memory_space=pl.ANY)
PARAMS = pltpu.CompilerParams(vmem_limit_bytes=VMEM_LIMIT)


def call(kernel, outs, *args, in_specs=None, **kwargs):
    return pl.pallas_call(
        kernel,
        out_shape=outs,
        in_specs=in_specs or [VM] * len(args),
        out_specs=jax.tree.map(lambda _: VM, outs),
        compiler_params=PARAMS,
        **kwargs,
    )(*args)


def flipped(x, bits_even, bits_odd):
    size = lax.axis_size("dom") * lax.axis_size("rep")
    pairs = [(i, i ^ (bits_odd if i & 1 else bits_even)) for i in range(size)]
    return lax.ppermute(x, AXES, pairs)


def local(
    node_feats,
    out_grad,
    norm1_gain,
    w_query,
    w_key,
    w_value,
    w_out,
    norm2_gain,
    w_up,
    w_down,
    local_gain,
    expander_gain,
    partner_perm,
    block_pairs,
    pair_count,
):
    feats = node_feats[0]
    partners = partner_perm[0, :, 0, :]
    rows, width = feats.shape
    heads = local_gain.shape[0]
    size = lax.axis_size("dom") * lax.axis_size("rep")
    levels = lax.axis_size("dom").bit_length() - 1
    by_bit = {}
    for matching in range(partners.shape[0]):
        by_bit.setdefault((levels - 1 - matching) % levels, []).append(matching)
    bits = list(by_bit)
    groups = [by_bit[b] for b in bits]

    def swapped(x, bit):
        return lax.ppermute(x, "dom", [(i, i ^ 1 << bit) for i in range(lax.axis_size("dom"))])

    rep_bits = lax.axis_size("rep").bit_length() - 1
    high_bits = [1 << k for k in range(3, size.bit_length() - 1)]
    flat = {1 << (b + rep_bits): k for k, b in enumerate(bits)}
    quad_slots = [flat.get(bit) for bit in (2, 4, 6)]
    orders = (list(zip(high_bits, high_bits[::-1])), list(zip(high_bits[::-1], high_bits)))
    high_slots = [(flat.get(even), flat.get(odd)) for even, odd in orders[0]]
    slots = [(k, k) for k in quad_slots if k is not None]
    slots += [pair for pair in high_slots if pair != (None, None)]

    others = [swapped(feats, b) for b in bits]
    count = len(bits)
    tall = count * rows
    stacked = heads * rows
    gain1 = norm1_gain.reshape(1, width)
    gain2 = norm2_gain.reshape(1, width)
    upstream = out_grad[0]
    normed, hidden, counts = call(
        functools.partial(first_kernel, groups),
        (struct((rows, width), F32), struct((rows, width), BF16), struct((rows, tall), F32)),
        feats,
        gain1,
        partners,
        cost_estimate=pl.CostEstimate(flops=10**10, bytes_accessed=1, transcendentals=0),
    )
    query, key, value, raw, tangent, powers, back = call(
        own_kernel,
        (
            struct((stacked, width), BF16),
            struct((rows, width), BF16),
            struct((rows, width), BF16),
            struct((stacked, rows), F32),
            struct((stacked, rows), F32),
            struct((stacked, rows), F32),
            struct((rows, w_up.shape[1]), F32),
        ),
        hidden,
        upstream,
        w_query,
        w_key,
        w_value,
        w_down,
        local_gain,
        in_specs=[VM] * 6 + [SM],
    )
    half = width // 2
    (
        node_out,
        keep_wide,
        send_wide,
        grad_mixed,
        grad_gain2,
        normed_far,
        hidden_far,
        key_far,
        value_far,
        raw_far,
        tanh_far,
        weight_near,
        weight_far,
        attended,
    ) = call(
        functools.partial(forward_kernel, count),
        (
            struct((rows, width), BF16),
            struct((4 * half, width), BF16),
            struct((4 * half, width), BF16),
            struct((rows, width), F32),
            struct((1, width), F32),
            struct((tall, width), F32),
            struct((tall, width), BF16),
            struct((tall, width), BF16),
            struct((tall, width), BF16),
            struct((stacked, tall), F32),
            struct((stacked, tall), F32),
            struct((stacked, rows), BF16),
            struct((stacked, tall), BF16),
            struct((rows, width), F32),
        ),
        *others,
        feats,
        upstream,
        gain1,
        gain2,
        w_key,
        w_value,
        w_out,
        w_up,
        w_down,
        query,
        value,
        powers,
        counts,
        back,
        expander_gain,
        in_specs=[VM] * (count + 14) + [SM],
    )
    keep_square, send_square, own, *slot_rows = call(
        functools.partial(backward_kernel, slots, count),
        (
            struct((4 * half, width), BF16),
            struct((4 * half + SMALL, width), BF16),
            struct((rows, width), F32),
        )
        + tuple(struct((rows, width), BF16) for _ in slots),
        gain1,
        grad_gain2,
        w_query,
        w_key,
        w_value,
        w_out,
        hidden,
        normed,
        query,
        key,
        value,
        raw,
        tangent,
        grad_mixed,
        normed_far,
        hidden_far,
        key_far,
        value_far,
        raw_far,
        tanh_far,
        weight_near,
        weight_far,
        attended,
        local_gain,
        expander_gain,
        in_specs=[VM] * 23 + [SM, SM],
        scratch_shapes=[pltpu.VMEM((stacked, rows), BF16), pltpu.VMEM((stacked, tall), BF16)],
    )
    slot_rows = iter(slot_rows)
    slot_quad = [None if k is None else next(slot_rows) for k in quad_slots]
    slot_high = [None if pair == (None, None) else next(slot_rows) for pair in high_slots]

    def present(*items):
        return [x for x in items if x is not None]

    def sized(base, slot):
        return struct((base + (0 if slot is None else rows), width), BF16)

    half = width // 2
    recv_wide = flipped(send_wide, 1, 1)
    recv_square = flipped(send_square, 1, 1)
    data = 2 * half + SMALL
    own_quad, *send_quad = call(
        functools.partial(pair_kernel, [x is not None for x in slot_quad]),
        (struct((data, width), BF16),) + tuple(sized(data, x) for x in slot_quad),
        keep_wide,
        recv_wide,
        keep_square,
        send_square,
        recv_square,
        *present(*slot_quad),
    )
    recv_quad = [flipped(x, bit, bit) for x, bit in zip(send_quad, (2, 4, 6))]
    returned = [x for x, slot in zip(recv_quad, slot_quad) if slot is not None]
    starts = [data] * len(returned)
    wide, square = call(
        functools.partial(quad_kernel, slot_high[0] is not None),
        (sized(half, slot_high[0]), struct((half + SMALL, width), BF16)),
        own_quad,
        *recv_quad,
        *present(slot_high[0]),
    )
    for k in range(len(high_bits)):
        recv_wide = flipped(wide, *orders[0][k])
        recv_square = flipped(square, *orders[1][k])
        if slot_high[k] is not None:
            returned.append(recv_wide)
            starts.append(half)
        slot = slot_high[k + 1] if k + 1 < len(high_bits) else None
        wide = call(
            functools.partial(double_kernel, half, False, slot is not None),
            sized(half, slot),
            wide,
            recv_wide,
            *present(slot, square),
        )
        square = call(
            functools.partial(double_kernel, half, True, False),
            struct((half + SMALL, width), BF16),
            square,
            recv_square,
            wide,
        )
    base = call(join_kernel, struct((2 * half, width), BF16), wide, square)
    near = [base] + [flipped(base, bit, bit) for bit in (2, 4, 6)]
    over = [flipped(x, 1, 1) for x in near]
    grad_feats = call(
        functools.partial(tail_kernel, starts),
        struct((rows, width), BF16),
        feats,
        own,
        grad_mixed,
        gain1,
        *returned,
    )
    one = struct((1, width), F32)
    full = struct((width, width), F32)
    few = struct((heads,), F32)
    results = pl.pallas_call(
        spread_kernel,
        out_shape=(
            one,
            full,
            full,
            full,
            full,
            one,
            struct((width, 2 * width), F32),
            struct((2 * width, width), F32),
            few,
            few,
        ),
        in_specs=[VM] * 9,
        out_specs=(VM, ANY, ANY, ANY, ANY, VM, ANY, ANY, VM, VM),
        scratch_shapes=[
            pltpu.VMEM((8, width, width), BF16),
            pltpu.VMEM((8, width, width), F32),
            pltpu.SemaphoreType.DMA((8,)),
        ],
        compiler_params=PARAMS,
    )(*near, *over, square)
    grad_gain1, grad_wq, grad_wk, grad_wv, grad_wout, grad_gain2, grad_up, grad_down, grad_local, grad_far = results
    return (
        node_out[None],
        grad_feats[None],
        grad_gain1.reshape(width),
        grad_wq,
        grad_wk,
        grad_wv,
        grad_wout,
        grad_gain2.reshape(width),
        grad_up,
        grad_down,
        grad_local,
        grad_far,
    )


def solution(mesh):
    whole = P()
    rows = P("rep", "dom", None)
    return jax.shard_map(
        local,
        mesh=mesh,
        in_specs=(rows, rows)
        + (whole,) * 10
        + (P("rep", None, "dom", None), rows, P("rep", "dom")),
        out_specs=(rows, rows) + (whole,) * 10,
        check_vma=False,
    )
```

time: 74.6 us -> 57.3 us (0.77)
  waiting for transfers between devices: 39.5 us -> 23.4 us
  local copies, waits for them, and re-layouts: 9.27 us -> 3.09 us
  starting transfers between devices: 12.1 us -> 18.1 us
  Pallas kernels: 12.4 us -> 11.6 us
    ppermute x8 -> x16, waiting for transfers between devices: 39.5 us -> 23.4 us  [flipped(): return lax.ppermute(x, AXES, pairs)]
    unnamed x30 -> x28, local copies, waits for them, and re-layouts: 9.26 us -> 3.09 us
    ppermute x8 -> x16, starting transfers between devices: 4.9 us -> 10.9 us  [flipped(): return lax.ppermute(x, AXES, pairs)]
    pallas_call x8 -> x12, Pallas kernels: 10.4 us -> 9.59 us  [call(): pl.pallas_call(kernel, out_shape=outs, in_specs=in_specs or [VM] * len(ar...]
  transfers between devices with their start and end apart: 11 -> 19, of which waited for: 8 -> 10; matrix products, arithmetic and copies ran while one was open for 0% -> 0% of each run, Pallas kernels for 5% -> 4%
where the time goes in v3:
time: 57.3 us; the launch traced here: 57.1 us
  waiting for transfers between devices  23.4 us (41%)
  starting transfers between devices  18.1 us (32%)
  Pallas kernels  11.6 us (20%)
  local copies, waits for them, and re-layouts  3.09 us (5%)
  between operations  0.85 us (1%)
    ppermute x16, waiting for transfers between devices, flipped(): return lax.ppermute(x, AXES, pairs)  23.4 us
    ppermute x16, starting transfers between devices, flipped(): return lax.ppermute(x, AXES, pairs)  10.9 us
    pallas_call x12, Pallas kernels, call(): pl.pallas_call(kernel, out_shape=outs, in_specs=in_specs or [VM] * len(ar...  9.59 us
    ppermute x3, starting transfers between devices, swapped(): lax.ppermute(x, 'dom', [(i, i ^ 1 << bit) for i in range(lax.axis_size('d...  7.2 us
    unnamed x28, local copies, waits for them, and re-layouts  3.09 us
    pallas_call x1, Pallas kernels, local(): pl.pallas_call(spread_kernel, out_shape=(one, full, full, full, full, one...  2.03 us
  transfers between devices with their start and end apart: 19, of which 10 were waited for; matrix products, arithmetic and copies ran while one was open for 0% of the time, Pallas kernels for 4%

profile of v3, /device:TPU:0, one launch (start us, length us, event | category | flops | bytes accessed | tf_op | source)
XLA Modules:
  0.0 57.1 jit_solution(13266623268559753457)
XLA Ops:
  0.7 3.0 %collective-permute-start.2 = (bf16[128,256]{1,0:T(8,128)(2,1)}, bf16[128,256]{1,0:T(8,128)(2,1)S(1)}, u32[]{:S(2)}, u32[]{:S(2)}) collective-permute-start(bf16[128,256]{1,0:T(8,128)(2,1)} %bitcast.11), channel_id=1, source_target_pairs={{0,4},{4,0},{8,12},{12,8},{16,20},{20,16},{24,28},{28,24},{1,5},{5... | collective-permute-start | bytes 196616 | tf_op jit(solution)/shard_map/ppermute | solution.py:510
  3.7 1.6 %collective-permute-start.1 = (bf16[128,256]{1,0:T(8,128)(2,1)}, bf16[128,256]{1,0:T(8,128)(2,1)S(1)}, u32[]{:S(2)}, u32[]{:S(2)}) collective-permute-start(bf16[128,256]{1,0:T(8,128)(2,1)} %bitcast.12), channel_id=1, source_target_pairs={{0,8},{4,12},{8,0},{12,4},{16,24},{20,28},{24,16},{28,20},{1,9},{5... | collective-permute-start | bytes 196616 | tf_op jit(solution)/shard_map/ppermute | solution.py:510
  5.3 2.6 %collective-permute-start = (bf16[128,256]{1,0:T(8,128)(2,1)}, bf16[128,256]{1,0:T(8,128)(2,1)S(1)}, u32[]{:S(2)}, u32[]{:S(2)}) collective-permute-start(bf16[128,256]{1,0:T(8,128)(2,1)} %bitcast.13), channel_id=1, source_target_pairs={{0,16},{4,20},{8,24},{12,28},{16,0},{20,4},{24,8},{28,12},{1,17},{... | collective-permute-start | bytes 196616 | tf_op jit(solution)/shard_map/ppermute | solution.py:510
  7.9 0.7 %copy-done.9 = f32[256]{0:T(256)S(1)} copy-done((f32[256]{0:T(256)S(1)}, f32[256]{0:T(256)}, u32[]{:S(2)}) %copy-start.9) | copy-done | bytes 1048
  8.5 0.8 %copy-done.7 = bf16[1,128,256]{2,1,0:T(8,128)(2,1)S(1)} copy-done((bf16[1,128,256]{2,1,0:T(8,128)(2,1)S(1)}, bf16[1,128,256]{2,1,0:T(8,128)(2,1)}, u32[]{:S(2)}) %copy-start.7) | copy-done | bytes 65560
  9.4 0.2 shard_map.220
  9.6 0.0 copy-start.11
  9.6 0.7 %copy-done = bf16[256,256]{1,0:T(8,128)(2,1)S(1)} copy-done((bf16[256,256]{1,0:T(8,128)(2,1)S(1)}, bf16[256,256]{1,0:T(8,128)(2,1)}, u32[]{:S(2)}) %copy-start) | copy-done | bytes 131096
  10.3 0.1 copy-done.1
  10.3 0.1 copy-done.2
  10.5 0.0 copy-done.4
  10.5 1.0 %shard_map.221 = (bf16[512,256]{1,0:T(8,128)(2,1)S(1)}, bf16[128,256]{1,0:T(8,128)(2,1)S(1)}, bf16[128,256]{1,0:T(8,128)(2,1)S(1)}, f32[512,128]{1,0:T(8,128)S(1...) custom-call(bf16[128,256]{1,0:T(8,128)(2,1)S(1)} %get-tuple-element.58.hidden_ref.refs_6_, ...), custom_call_target="tpu_custom_call" | custom-call | tf_op jit(solution)/shard_map/pallas_call | solution.py:464
  11.5 0.0 collective-permute-done.2.refs_2_
  11.6 0.0 copy-start.10
  11.6 0.0 copy-start.12
  11.6 0.6 %copy-done.10 = f32[4]{0:T(128)S(1)} copy-done((f32[4]{0:T(128)S(1)}, f32[4]{0:T(128)}, u32[]{:S(2)}) %copy-start.10) | copy-done | bytes 40
  12.2 0.0 copy-done.12
  12.3 3.9 %shard_map.222 = (bf16[128,256]{1,0:T(8,128)(2,1)}, bf16[512,256]{1,0:T(8,128)(2,1)S(1)}, bf16[512,256]{1,0:T(8,128)(2,1)S(1)}, f32[128,256]{1,0:T(8,128)S(1)}, ...) custom-call(bf16[128,256]{1,0:T(8,128)(2,1)S(1)} %collective-permute, ...), custom_call_target="tpu_custom_call" | custom-call | tf_op jit(solution)/shard_map/pallas_call | solution.py:464
  16.2 3.3 %shard_map.223 = (bf16[512,256]{1,0:T(8,128)(2,1)S(1)}, bf16[528,256]{1,0:T(8,128)(2,1)S(1)}, f32[128,256]{1,0:T(8,128)S(1)}, bf16[128,256]{1,0:T(8,128)(2,1)S(1...) custom-call(f32[1,256]{1,0:T(1,128)S(1)} %bitcast.19, f32[1,256]{1,0:T(1,128)S(1)} %get-tuple-element.65.refs_1_, ...), custom_call_target="tpu_custom_call" | custom-call | tf_op jit(solution)/shard_map/pallas_call | solution.py:464
  19.4 0.1 collective-permute-start.4
  19.5 0.5 collective-permute-start.3
  20.0 1.4 %collective-permute-done.3.recvw_ref = bf16[512,256]{1,0:T(8,128)(2,1)S(1)} collective-permute-done((bf16[512,256]{1,0:T(8,128)(2,1)S(1)}, bf16[512,256]{1,0:T(8,128)(2,1)S(1)}, u32[]{:S(2)}, u32[]{:S(2)}) %collective-permute-start.3) | collective-permute-done | bytes 262176 | tf_op jit(solution)/shard_map/ppermute | solution.py:477
  21.4 0.0 collective-permute-done.4.recvs_ref
  21.4 0.1 shard_map.224
  21.6 0.6 %collective-permute-start.5 = (bf16[400,256]{1,0:T(8,128)(2,1)S(1)}, bf16[400,256]{1,0:T(8,128)(2,1)S(1)}, u32[]{:S(2)}, u32[]{:S(2)}) collective-permute-start(bf16[400,256]{1,0:T(8,128)(2,1)S(1)} %get-tuple-element.86), channel_id=1, source_target_pairs={{0,4},{1,5},{2,6},{3,7},{4,0},{5,1},{6,2},{7,3},{8,12},{9,13},{10,... | collective-permute-start | bytes 614408 | tf_op jit(solution)/shard_map/ppermute | solution.py:477
  22.1 1.5 %collective-permute-start.6 = (bf16[272,256]{1,0:T(8,128)(2,1)S(1)}, bf16[272,256]{1,0:T(8,128)(2,1)S(1)}, u32[]{:S(2)}, u32[]{:S(2)}) collective-permute-start(bf16[272,256]{1,0:T(8,128)(2,1)S(1)} %get-tuple-element.88), channel_id=1, source_target_pairs={{0,2},{1,3},{2,0},{3,1},{4,6},{5,7},{6,4},{7,5},{8,10},{9,11},{10,... | collective-permute-start | bytes 417800 | tf_op jit(solution)/shard_map/ppermute | solution.py:477
  23.6 1.5 %collective-permute-start.7 = (bf16[272,256]{1,0:T(8,128)(2,1)S(1)}, bf16[272,256]{1,0:T(8,128)(2,1)S(1)}, u32[]{:S(2)}, u32[]{:S(2)}) collective-permute-start(bf16[272,256]{1,0:T(8,128)(2,1)S(1)} %get-tuple-element.89), channel_id=1, source_target_pairs={{0,6},{1,7},{2,4},{3,5},{4,2},{5,3},{6,0},{7,1},{8,14},{9,15},{10,... | collective-permute-start | bytes 417800 | tf_op jit(solution)/shard_map/ppermute | solution.py:477
  25.1 3.3 %collective-permute-done.6.one_ref = bf16[272,256]{1,0:T(8,128)(2,1)S(1)} collective-permute-done((bf16[272,256]{1,0:T(8,128)(2,1)S(1)}, bf16[272,256]{1,0:T(8,128)(2,1)S(1)}, u32[]{:S(2)}, u32[]{:S(2)}) %collective-permute-start.6) | collective-permute-done | bytes 139296 | tf_op jit(solution)/shard_map/ppermute | solution.py:477
  28.4 3.2 %collective-permute-done.7.three_ref = bf16[272,256]{1,0:T(8,128)(2,1)S(1)} collective-permute-done((bf16[272,256]{1,0:T(8,128)(2,1)S(1)}, bf16[272,256]{1,0:T(8,128)(2,1)S(1)}, u32[]{:S(2)}, u32[]{:S(2)}) %collective-permute-start.7) | collective-permute-done | bytes 139296 | tf_op jit(solution)/shard_map/ppermute | solution.py:477
  31.6 0.1 collective-permute-done.5.two_ref.refs_4_
  31.7 0.1 shard_map.225
  31.8 0.5 collective-permute-start.8
  32.3 1.7 %collective-permute-start.10 = (bf16[144,256]{1,0:T(8,128)(2,1)S(1)}, bf16[144,256]{1,0:T(8,128)(2,1)S(1)}, u32[]{:S(2)}, u32[]{:S(2)}) collective-permute-start(bf16[144,256]{1,0:T(8,128)(2,1)S(1)} %get-tuple-element.93.refs_1_.own_ref), channel_id=1, source_target_pairs={{0,16},{1,9},{2,18},{3,11},{4,20},{5,13},{6,22},{7,15},{8,24},{9,1... | collective-permute-start | bytes 221192 | tf_op jit(solution)/shard_map/ppermute | solution.py:477
  34.0 5.0 %collective-permute-done.8.recv_ref.refs_5_ = bf16[256,256]{1,0:T(8,128)(2,1)S(1)} collective-permute-done((bf16[256,256]{1,0:T(8,128)(2,1)S(1)}, bf16[256,256]{1,0:T(8,128)(2,1)S(1)}, u32[]{:S(2)}, u32[]{:S(2)}) %collective-permute-start.8) | collective-permute-done | bytes 131104 | tf_op jit(solution)/shard_map/ppermute | solution.py:477
  39.0 0.1 collective-permute-start.9
  39.1 0.0 collective-permute-done.10.recv_ref
  39.1 0.9 %collective-permute-start.11 = (bf16[144,256]{1,0:T(8,128)(2,1)S(1)}, bf16[144,256]{1,0:T(8,128)(2,1)S(1)}, u32[]{:S(2)}, u32[]{:S(2)}) collective-permute-start(bf16[144,256]{1,0:T(8,128)(2,1)S(1)} %shard_map.228.refs_0_.own_ref), channel_id=1, source_target_pairs={{0,8},{1,17},{2,10},{3,19},{4,12},{5,21},{6,14},{7,23},{8,0},{9,25... | collective-permute-start | bytes 221192 | tf_op jit(solution)/shard_map/ppermute | solution.py:477
  40.1 5.4 %collective-permute-done.9.refs_6_.recv_ref = bf16[256,256]{1,0:T(8,128)(2,1)S(1)} collective-permute-done((bf16[256,256]{1,0:T(8,128)(2,1)S(1)}, bf16[256,256]{1,0:T(8,128)(2,1)S(1)}, u32[]{:S(2)}, u32[]{:S(2)}) %collective-permute-start.9) | collective-permute-done | bytes 131104 | tf_op jit(solution)/shard_map/ppermute | solution.py:477
  45.5 0.0 copy-start.8
  45.6 1.5 %collective-permute-start.14 = (bf16[256,256]{1,0:T(8,128)(2,1)S(1)}, bf16[256,256]{1,0:T(8,128)(2,1)S(1)}, u32[]{:S(2)}, u32[]{:S(2)}) collective-permute-start(bf16[256,256]{1,0:T(8,128)(2,1)S(1)} %shard_map.231.refs_0_), channel_id=1, source_target_pairs={{0,6},{1,7},{2,4},{3,5},{4,2},{5,3},{6,0},{7,1},{8,14},{9,15},{10,... | collective-permute-start | bytes 393224 | tf_op jit(solution)/shard_map/ppermute | solution.py:477
  47.1 1.5 %collective-permute-start.13 = (bf16[256,256]{1,0:T(8,128)(2,1)S(1)}, bf16[256,256]{1,0:T(8,128)(2,1)S(1)}, u32[]{:S(2)}, u32[]{:S(2)}) collective-permute-start(bf16[256,256]{1,0:T(8,128)(2,1)S(1)} %shard_map.231.refs_0_), channel_id=1, source_target_pairs={{0,4},{1,5},{2,6},{3,7},{4,0},{5,1},{6,2},{7,3},{8,12},{9,13},{10,... | collective-permute-start | bytes 393224 | tf_op jit(solution)/shard_map/ppermute | solution.py:477
  48.6 0.5 collective-permute-start.12
  49.1 3.0 %collective-permute-done.14.refs_3_ = bf16[256,256]{1,0:T(8,128)(2,1)S(1)} collective-permute-done((bf16[256,256]{1,0:T(8,128)(2,1)S(1)}, bf16[256,256]{1,0:T(8,128)(2,1)S(1)}, u32[]{:S(2)}, u32[]{:S(2)}) %collective-permute-start.14) | collective-permute-done | bytes 131104 | tf_op jit(solution)/shard_map/ppermute | solution.py:477
  52.1 1.0 %collective-permute-done.13.refs_2_ = bf16[256,256]{1,0:T(8,128)(2,1)S(1)} collective-permute-done((bf16[256,256]{1,0:T(8,128)(2,1)S(1)}, bf16[256,256]{1,0:T(8,128)(2,1)S(1)}, u32[]{:S(2)}, u32[]{:S(2)}) %collective-permute-start.13) | collective-permute-done | bytes 131104 | tf_op jit(solution)/shard_map/ppermute | solution.py:477
  53.1 0.5 collective-permute-done.12.refs_1_
  53.7 0.9 %shard_map.227 = bf16[128,256]{1,0:T(8,128)(2,1)} custom-call(bf16[128,256]{1,0:T(8,128)(2,1)S(1)} %bitcast.16, f32[128,256]{1,0:T(8,128)S(1)} %get-tuple-element.80.refs_1_, f32[128,256]{1,0:T(8,128)S(1)} %get-tuple-element.70.refs_13_.refs_2_, f32[1,256]{1,0:T(1,128)S(1)} %bitcast.20, bf16[400,256]{1,0:T(8,128)(2,1)S(1)} %collective-permute-done.5.two_ref.refs_4_, ...), custom_call_target="tpu_custom_call" | custom-call | tf_op jit(solution)/shard_map/pallas_call | solution.py:464
  54.6 0.4 collective-permute-done.16.refs_5_
  55.0 2.0 %shard_map.232 = (f32[1,256]{1,0:T(1,128)}, f32[256,256]{1,0:T(8,128)}, f32[256,256]{1,0:T(8,128)}, f32[256,256]{1,0:T(8,128)}, f32[256,256]{1,0:T(8,128)}, /*in...) custom-call(bf16[256,256]{1,0:T(8,128)(2,1)S(1)} %shard_map.231.refs_0_, ...), custom_call_target="tpu_custom_call" | custom-call | tf_op jit(solution)/shard_map/pallas_call | solution.py:714
  (31 shorter events, 0.2 us)
Async XLA Ops:
  0.6 7.2 %copy-start.13 = (s32[1,4,1,128]{3,2,1,0:T(1,128)S(1)}, s32[1,4,1,128]{3,2,1,0:T(1,128)}, u32[]{:S(2)}) copy-start(s32[1,4,1,128]{3,2,1,0:T(1,128)} %param.27) | copy-start | bytes 6148
  0.7 10.9 %collective-permute-start.2 = (bf16[128,256]{1,0:T(8,128)(2,1)}, bf16[128,256]{1,0:T(8,128)(2,1)S(1)}, u32[]{:S(2)}, u32[]{:S(2)}) collective-permute-start(bf16[128,256]{1,0:T(8,128)(2,1)} %bitcast.11), channel_id=1, source_target_pairs={{0,4},{4,0},{8,12},{12,8},{16,20},{20,16},{24,28},{28,24},{1,5},{5... | collective-permute-start | bytes 196616 | tf_op jit(solution)/shard_map/ppermute | solution.py:510
  3.7 7.9 %collective-permute-start.1 = (bf16[128,256]{1,0:T(8,128)(2,1)}, bf16[128,256]{1,0:T(8,128)(2,1)S(1)}, u32[]{:S(2)}, u32[]{:S(2)}) collective-permute-start(bf16[128,256]{1,0:T(8,128)(2,1)} %bitcast.12), channel_id=1, source_target_pairs={{0,8},{4,12},{8,0},{12,4},{16,24},{20,28},{24,16},{28,20},{1,9},{5... | collective-permute-start | bytes 196616 | tf_op jit(solution)/shard_map/ppermute | solution.py:510
  5.3 6.3 %collective-permute-start = (bf16[128,256]{1,0:T(8,128)(2,1)}, bf16[128,256]{1,0:T(8,128)(2,1)S(1)}, u32[]{:S(2)}, u32[]{:S(2)}) collective-permute-start(bf16[128,256]{1,0:T(8,128)(2,1)} %bitcast.13), channel_id=1, source_target_pairs={{0,16},{4,20},{8,24},{12,28},{16,0},{20,4},{24,8},{28,12},{1,17},{... | collective-permute-start | bytes 196616 | tf_op jit(solution)/shard_map/ppermute | solution.py:510
  7.9 0.7 %copy-start.9 = (f32[256]{0:T(256)S(1)}, f32[256]{0:T(256)}, u32[]{:S(2)}) copy-start(f32[256]{0:T(256)} %param.17) | copy-start | bytes 3076
  8.5 0.8 %copy-start.7 = (bf16[1,128,256]{2,1,0:T(8,128)(2,1)S(1)}, bf16[1,128,256]{2,1,0:T(8,128)(2,1)}, u32[]{:S(2)}) copy-start(bf16[1,128,256]{2,1,0:T(8,128)(2,1)} %param.15) | copy-start | bytes 196612
  9.4 0.9 %copy-start = (bf16[256,256]{1,0:T(8,128)(2,1)S(1)}, bf16[256,256]{1,0:T(8,128)(2,1)}, u32[]{:S(2)}) copy-start(bf16[256,256]{1,0:T(8,128)(2,1)} %refs_3_.1) | copy-start | bytes 393220
  9.4 1.0 %copy-start.1 = (bf16[256,256]{1,0:T(8,128)(2,1)S(1)}, bf16[256,256]{1,0:T(8,128)(2,1)}, u32[]{:S(2)}) copy-start(bf16[256,256]{1,0:T(8,128)(2,1)} %refs_4_.1) | copy-start | bytes 393220
  9.4 1.1 %copy-start.2 = (bf16[512,256]{1,0:T(8,128)(2,1)S(1)}, bf16[512,256]{1,0:T(8,128)(2,1)}, u32[]{:S(2)}) copy-start(bf16[512,256]{1,0:T(8,128)(2,1)} %refs_11_.1) | copy-start | bytes 786436
  9.4 1.1 %copy-start.4 = (bf16[256,256]{1,0:T(8,128)(2,1)S(1)}, bf16[256,256]{1,0:T(8,128)(2,1)}, u32[]{:S(2)}) copy-start(bf16[256,256]{1,0:T(8,128)(2,1)} %refs_2_.1) | copy-start | bytes 393220
  9.4 1.1 %copy-start.6 = (bf16[1,128,256]{2,1,0:T(8,128)(2,1)S(1)}, bf16[1,128,256]{2,1,0:T(8,128)(2,1)}, u32[]{:S(2)}) copy-start(bf16[1,128,256]{2,1,0:T(8,128)(2,1)} %param.16) | copy-start | bytes 196612
  9.6 0.9 %copy-start.11 = (f32[4]{0:T(128)S(1)}, f32[4]{0:T(128)}, u32[]{:S(2)}) copy-start(f32[4]{0:T(128)} %refs_23_.1) | copy-start | bytes 52
  10.5 1.1 %copy-start.3 = (bf16[256,256]{1,0:T(8,128)(2,1)S(1)}, bf16[256,256]{1,0:T(8,128)(2,1)}, u32[]{:S(2)}) copy-start(bf16[256,256]{1,0:T(8,128)(2,1)} %refs_5_.1) | copy-start | bytes 393220
  10.5 1.1 %copy-start.5 = (bf16[256,512]{1,0:T(8,128)(2,1)S(1)}, bf16[256,512]{1,0:T(8,128)(2,1)}, u32[]{:S(2)}) copy-start(bf16[256,512]{1,0:T(8,128)(2,1)} %refs_10_.1) | copy-start | bytes 786436
  11.6 0.7 %copy-start.10 = (f32[4]{0:T(128)S(1)}, f32[4]{0:T(128)}, u32[]{:S(2)}) copy-start(f32[4]{0:T(128)} %refs_24_.1) | copy-start | bytes 52
  11.6 0.7 %copy-start.12 = (f32[256]{0:T(256)S(1)}, f32[256]{0:T(256)}, u32[]{:S(2)}) copy-start(f32[256]{0:T(256)} %param.22) | copy-start | bytes 3076
  19.4 2.0 %collective-permute-start.4 = (bf16[528,256]{1,0:T(8,128)(2,1)S(1)}, bf16[528,256]{1,0:T(8,128)(2,1)S(1)}, u32[]{:S(2)}, u32[]{:S(2)}) collective-permute-start(bf16[528,256]{1,0:T(8,128)(2,1)S(1)} %get-tuple-element.84.sents_ref), channel_id=1, source_target_pairs={{0,1},{1,0},{2,3},{3,2},{4,5},{5,4},{6,7},{7,6},{8,9},{9,8},{10,11... | collective-permute-start | bytes 811016 | tf_op jit(solution)/shard_map/ppermute | solution.py:477
  19.5 1.9 %collective-permute-start.3 = (bf16[512,256]{1,0:T(8,128)(2,1)S(1)}, bf16[512,256]{1,0:T(8,128)(2,1)S(1)}, u32[]{:S(2)}, u32[]{:S(2)}) collective-permute-start(bf16[512,256]{1,0:T(8,128)(2,1)S(1)} %get-tuple-element.82), channel_id=1, source_target_pairs={{0,1},{1,0},{2,3},{3,2},{4,5},{5,4},{6,7},{7,6},{8,9},{9,8},{10,11... | collective-permute-start | bytes 786440 | tf_op jit(solution)/shard_map/ppermute | solution.py:477
  21.6 10.2 %collective-permute-start.5 = (bf16[400,256]{1,0:T(8,128)(2,1)S(1)}, bf16[400,256]{1,0:T(8,128)(2,1)S(1)}, u32[]{:S(2)}, u32[]{:S(2)}) collective-permute-start(bf16[400,256]{1,0:T(8,128)(2,1)S(1)} %get-tuple-element.86), channel_id=1, source_target_pairs={{0,4},{1,5},{2,6},{3,7},{4,0},{5,1},{6,2},{7,3},{8,12},{9,13},{10,... | collective-permute-start | bytes 614408 | tf_op jit(solution)/shard_map/ppermute | solution.py:477
  22.1 6.2 %collective-permute-start.6 = (bf16[272,256]{1,0:T(8,128)(2,1)S(1)}, bf16[272,256]{1,0:T(8,128)(2,1)S(1)}, u32[]{:S(2)}, u32[]{:S(2)}) collective-permute-start(bf16[272,256]{1,0:T(8,128)(2,1)S(1)} %get-tuple-element.88), channel_id=1, source_target_pairs={{0,2},{1,3},{2,0},{3,1},{4,6},{5,7},{6,4},{7,5},{8,10},{9,11},{10,... | collective-permute-start | bytes 417800 | tf_op jit(solution)/shard_map/ppermute | solution.py:477
  23.6 8.0 %collective-permute-start.7 = (bf16[272,256]{1,0:T(8,128)(2,1)S(1)}, bf16[272,256]{1,0:T(8,128)(2,1)S(1)}, u32[]{:S(2)}, u32[]{:S(2)}) collective-permute-start(bf16[272,256]{1,0:T(8,128)(2,1)S(1)} %get-tuple-element.89), channel_id=1, source_target_pairs={{0,6},{1,7},{2,4},{3,5},{4,2},{5,3},{6,0},{7,1},{8,14},{9,15},{10,... | collective-permute-start | bytes 417800 | tf_op jit(solution)/shard_map/ppermute | solution.py:477
  31.8 7.2 %collective-permute-start.8 = (bf16[256,256]{1,0:T(8,128)(2,1)S(1)}, bf16[256,256]{1,0:T(8,128)(2,1)S(1)}, u32[]{:S(2)}, u32[]{:S(2)}) collective-permute-start(bf16[256,256]{1,0:T(8,128)(2,1)S(1)} %get-tuple-element.91.own_ref), channel_id=1, source_target_pairs={{0,8},{1,17},{2,10},{3,19},{4,12},{5,21},{6,14},{7,23},{8,0},{9,25... | collective-permute-start | bytes 393224 | tf_op jit(solution)/shard_map/ppermute | solution.py:477
  32.3 6.8 %collective-permute-start.10 = (bf16[144,256]{1,0:T(8,128)(2,1)S(1)}, bf16[144,256]{1,0:T(8,128)(2,1)S(1)}, u32[]{:S(2)}, u32[]{:S(2)}) collective-permute-start(bf16[144,256]{1,0:T(8,128)(2,1)S(1)} %get-tuple-element.93.refs_1_.own_ref), channel_id=1, source_target_pairs={{0,16},{1,9},{2,18},{3,11},{4,20},{5,13},{6,22},{7,15},{8,24},{9,1... | collective-permute-start | bytes 221192 | tf_op jit(solution)/shard_map/ppermute | solution.py:477
  39.0 6.5 %collective-permute-start.9 = (bf16[256,256]{1,0:T(8,128)(2,1)S(1)}, bf16[256,256]{1,0:T(8,128)(2,1)S(1)}, u32[]{:S(2)}, u32[]{:S(2)}) collective-permute-start(bf16[256,256]{1,0:T(8,128)(2,1)S(1)} %shard_map.226.refs_0_.own_ref), channel_id=1, source_target_pairs={{0,16},{1,9},{2,18},{3,11},{4,20},{5,13},{6,22},{7,15},{8,24},{9,1... | collective-permute-start | bytes 393224 | tf_op jit(solution)/shard_map/ppermute | solution.py:477
  39.1 6.4 %collective-permute-start.11 = (bf16[144,256]{1,0:T(8,128)(2,1)S(1)}, bf16[144,256]{1,0:T(8,128)(2,1)S(1)}, u32[]{:S(2)}, u32[]{:S(2)}) collective-permute-start(bf16[144,256]{1,0:T(8,128)(2,1)S(1)} %shard_map.228.refs_0_.own_ref), channel_id=1, source_target_pairs={{0,8},{1,17},{2,10},{3,19},{4,12},{5,21},{6,14},{7,23},{8,0},{9,25... | collective-permute-start | bytes 221192 | tf_op jit(solution)/shard_map/ppermute | solution.py:477
  45.5 8.2 %copy-start.8 = (bf16[1,128,256]{2,1,0:T(8,128)(2,1)S(1)}, bf16[1,128,256]{2,1,0:T(8,128)(2,1)}, u32[]{:S(2)}) copy-start(bf16[1,128,256]{2,1,0:T(8,128)(2,1)} %param.15) | copy-start | bytes 196612
  45.6 6.6 %collective-permute-start.14 = (bf16[256,256]{1,0:T(8,128)(2,1)S(1)}, bf16[256,256]{1,0:T(8,128)(2,1)S(1)}, u32[]{:S(2)}, u32[]{:S(2)}) collective-permute-start(bf16[256,256]{1,0:T(8,128)(2,1)S(1)} %shard_map.231.refs_0_), channel_id=1, source_target_pairs={{0,6},{1,7},{2,4},{3,5},{4,2},{5,3},{6,0},{7,1},{8,14},{9,15},{10,... | collective-permute-start | bytes 393224 | tf_op jit(solution)/shard_map/ppermute | solution.py:477
  47.1 6.1 %collective-permute-start.13 = (bf16[256,256]{1,0:T(8,128)(2,1)S(1)}, bf16[256,256]{1,0:T(8,128)(2,1)S(1)}, u32[]{:S(2)}, u32[]{:S(2)}) collective-permute-start(bf16[256,256]{1,0:T(8,128)(2,1)S(1)} %shard_map.231.refs_0_), channel_id=1, source_target_pairs={{0,4},{1,5},{2,6},{3,7},{4,0},{5,1},{6,2},{7,3},{8,12},{9,13},{10,... | collective-permute-start | bytes 393224 | tf_op jit(solution)/shard_map/ppermute | solution.py:477
  48.6 5.1 %collective-permute-start.12 = (bf16[256,256]{1,0:T(8,128)(2,1)S(1)}, bf16[256,256]{1,0:T(8,128)(2,1)S(1)}, u32[]{:S(2)}, u32[]{:S(2)}) collective-permute-start(bf16[256,256]{1,0:T(8,128)(2,1)S(1)} %shard_map.231.refs_0_), channel_id=1, source_target_pairs={{0,2},{1,3},{2,0},{3,1},{4,6},{5,7},{6,4},{7,5},{8,10},{9,11},{10,... | collective-permute-start | bytes 393224 | tf_op jit(solution)/shard_map/ppermute | solution.py:477
  49.1 5.5 %collective-permute-start.15 = (bf16[256,256]{1,0:T(8,128)(2,1)S(1)}, bf16[256,256]{1,0:T(8,128)(2,1)S(1)}, u32[]{:S(2)}, u32[]{:S(2)}) collective-permute-start(bf16[256,256]{1,0:T(8,128)(2,1)S(1)} %shard_map.231.refs_0_), channel_id=1, source_target_pairs={{0,1},{1,0},{2,3},{3,2},{4,5},{5,4},{6,7},{7,6},{8,9},{9,8},{10,11... | collective-permute-start | bytes 393224 | tf_op jit(solution)/shard_map/ppermute | solution.py:477
  52.1 2.5 %collective-permute-start.18 = (bf16[256,256]{1,0:T(8,128)(2,1)S(1)}, bf16[256,256]{1,0:T(8,128)(2,1)S(1)}, u32[]{:S(2)}, u32[]{:S(2)}) collective-permute-start(bf16[256,256]{1,0:T(8,128)(2,1)S(1)} %collective-permute-done.14.refs_3_), channel_id=1, source_target_pairs={{0,1},{1,0},{2,3},{3,2},{4,5},{5,4},{6,7},{7,6},{8,9},{9,8},{10,11... | collective-permute-start | bytes 393224 | tf_op jit(solution)/shard_map/ppermute | solution.py:477
  53.1 1.5 %collective-permute-start.17 = (bf16[256,256]{1,0:T(8,128)(2,1)S(1)}, bf16[256,256]{1,0:T(8,128)(2,1)S(1)}, u32[]{:S(2)}, u32[]{:S(2)}) collective-permute-start(bf16[256,256]{1,0:T(8,128)(2,1)S(1)} %collective-permute-done.13.refs_2_), channel_id=1, source_target_pairs={{0,1},{1,0},{2,3},{3,2},{4,5},{5,4},{6,7},{7,6},{8,9},{9,8},{10,11... | collective-permute-start | bytes 393224 | tf_op jit(solution)/shard_map/ppermute | solution.py:477
  53.7 1.3 %collective-permute-start.16 = (bf16[256,256]{1,0:T(8,128)(2,1)S(1)}, bf16[256,256]{1,0:T(8,128)(2,1)S(1)}, u32[]{:S(2)}, u32[]{:S(2)}) collective-permute-start(bf16[256,256]{1,0:T(8,128)(2,1)S(1)} %collective-permute-done.12.refs_1_), channel_id=1, source_target_pairs={{0,1},{1,0},{2,3},{3,2},{4,5},{5,4},{6,7},{7,6},{8,9},{9,8},{10,11... | collective-permute-start | bytes 393224 | tf_op jit(solution)/shard_map/ppermute | solution.py:477

commit v4 on v1

v4 whole, which is shorter than its diff:
```python
import functools

import jax
import jax.numpy as jnp
from jax import lax
from jax.experimental import pallas as pl
from jax.experimental.pallas import tpu as pltpu
from jax.sharding import PartitionSpec as P

EPSILON = 1e-05
SCORE_CAP = 5.0
GELU_ROOT = 0.7978845608028654
GELU_CUBIC = 0.044715
SMALL = 16
AXES = ("dom", "rep")
VMEM_LIMIT = 48 * 1024 * 1024
F32 = jnp.float32
BF16 = jnp.bfloat16


def dot(a, b):
    return lax.dot_general(a, b, (((1,), (0,)), ((), ())), preferred_element_type=F32)


def dot_rhs_t(a, b):
    return lax.dot_general(a, b, (((1,), (1,)), ((), ())), preferred_element_type=F32)


def dot_lhs_t(a, b):
    return lax.dot_general(a, b, (((0,), (0,)), ((), ())), preferred_element_type=F32)


def norm_forward(matrix):
    center = jnp.mean(matrix, axis=-1, keepdims=True)
    shifted = matrix - center
    inverse = lax.rsqrt(jnp.mean(shifted * shifted, axis=-1, keepdims=True) + EPSILON)
    return (shifted * inverse, inverse)


def norm_backward(upstream, normed, inverse, gain):
    scaled_up = upstream * gain
    return inverse * (
        scaled_up
        - jnp.mean(scaled_up, axis=-1, keepdims=True)
        - normed * jnp.mean(scaled_up * normed, axis=-1, keepdims=True)
    )


def gelu_parts(preact):
    tangent = jnp.tanh(GELU_ROOT * (preact + GELU_CUBIC * preact * preact * preact))
    result = 0.5 * preact * (1.0 + tangent)
    derivative = 0.5 * (1.0 + tangent) + 0.5 * preact * (1.0 - tangent * tangent) * GELU_ROOT * (
        1.0 + 3.0 * GELU_CUBIC * preact * preact
    )
    return (result, derivative)


def split_parts(rows):
    high = rows.astype(BF16).astype(F32)
    return jnp.concatenate([high, rows - high], axis=0).astype(BF16)


def join_parts(packed):
    wide = packed.astype(F32)
    return wide[: SMALL // 2] + wide[SMALL // 2 :]


def device_bits():
    flat = lax.axis_index("dom") * lax.axis_size("rep") + lax.axis_index("rep")
    return (flat & 1, (flat >> 1) & 3)


def head_masks_of(shape, heads):
    lane = lax.broadcasted_iota(jnp.int32, shape, 1) // (shape[1] // heads)
    return [lane == h for h in range(heads)]


def stack_heads(matrix, masks):
    return jnp.concatenate([jnp.where(m, matrix, 0.0) for m in masks], axis=0).astype(BF16)


def relay(source_refs, out_refs):
    for source, out in zip(source_refs, out_refs):
        out[...] = source[...]


def flag_kernel(flag_ref):
    flag_ref[...] = jnp.zeros(flag_ref.shape, F32)


def count_kernel(groups, flag_ref, perm_ref, *refs):
    sources = refs[: len(refs) // 2]
    count_ref = refs[len(sources)]
    relay(sources, refs[len(sources) + 1 :])
    rows = perm_ref.shape[1]
    target = lax.broadcasted_iota(jnp.int32, (rows, rows), 0)
    for g, members in enumerate(groups):
        total = 0.0
        for m in members:
            total = total + jnp.where(target == perm_ref[m : m + 1, :], 1.0, 0.0)
        count_ref[:, g * rows : (g + 1) * rows] = total.T


def sort_units(units_ref, keep_ref, send_ref, bits):
    core, quad = bits
    rows = units_ref.shape[0] // 8
    for r in range(4):
        span = slice(r * rows, (r + 1) * rows)
        for owner, out_ref in ((core, keep_ref), (1 - core, send_ref)):
            start = pl.multiple_of((owner * 4 + (quad ^ r)) * rows, rows)
            out_ref[span, :] = units_ref[pl.ds(start, rows), :]


def collapse(matrix, masks):
    rows = matrix.shape[0] // len(masks)
    total = jnp.where(masks[0], matrix[:rows], 0.0)
    for h in range(1, len(masks)):
        total = total + jnp.where(masks[h], matrix[h * rows : (h + 1) * rows], 0.0)
    return total


def layer_kernel(slots, count, *refs):
    feats_refs = refs[: count + 1]
    (
        up_ref,
        gain1_ref,
        wq_ref,
        wk_ref,
        wv_ref,
        wo_ref,
        gain2_ref,
        wup_ref,
        wdown_ref,
        local_ref,
        far_ref,
        count_ref,
    ) = refs[count + 1 : count + 13]
    out_ref, keepw_ref, sendw_ref, keeps_ref, sends_ref, own_ref, mixed_ref = refs[count + 13 : count + 20]
    slot_refs = refs[count + 20 : count + 20 + len(slots)]
    raw_s, tanh_s, weight_s, dscore_s, wide_s, square_s = refs[count + 20 + len(slots) :]

    rows, width = out_ref.shape
    heads = local_ref.shape[0]
    head_dim = width // heads
    scale = 1.0 / float(head_dim) ** 0.5
    bits = device_bits()
    core = bits[0]

    gain1 = gain1_ref[...]
    gain2 = gain2_ref[...]
    upstream = up_ref[...]
    feats = jnp.concatenate([ref[...] for ref in feats_refs], axis=0).astype(F32)
    normed1, _ = norm_forward(feats)
    hidden = (normed1 * gain1).astype(BF16)
    queries = dot(hidden[:rows], wq_ref[...])
    key_all = dot(hidden, wk_ref[...]).astype(BF16)
    value_all = dot(hidden, wv_ref[...]).astype(BF16)

    head_masks = head_masks_of((rows, width), heads)
    query_stack = stack_heads(queries, head_masks)
    raw_s[...] = dot_rhs_t(query_stack, key_all) * scale

    far_counts = count_ref[...]

    for h in range(heads):
        block = pl.ds(h * rows, rows)
        tl = jnp.tanh(raw_s[block, :rows] * (local_ref[h] / SCORE_CAP))
        tf = jnp.tanh(raw_s[block, rows:] * (far_ref[h] / SCORE_CAP))
        el = jnp.exp(SCORE_CAP * tl)
        ef = jnp.exp(SCORE_CAP * tf) * far_counts
        inv = 1.0 / (jnp.sum(el, axis=1, keepdims=True) + jnp.sum(ef, axis=1, keepdims=True))
        tanh_s[block, :rows] = tl
        tanh_s[block, rows:] = tf
        weight_s[block, :rows] = (el * inv).astype(BF16)
        weight_s[block, rows:] = (ef * inv).astype(BF16)

    attended32 = collapse(dot(weight_s[...], value_all), head_masks)
    attended = attended32.astype(BF16)
    mixed = (feats[:rows] + dot(attended, wo_ref[...])).astype(BF16)
    normed2, inverse2 = norm_forward(mixed.astype(F32))
    hidden2 = (normed2 * gain2).astype(BF16)
    preact = dot(hidden2, wup_ref[...])
    act32, derivative = gelu_parts(preact)
    act = act32.astype(BF16)
    out_ref[...] = (mixed.astype(F32) + dot(act, wdown_ref[...])).astype(BF16)
    grad_down = dot_lhs_t(act, upstream)
    wide_s[2 * width : 3 * width, :] = grad_down[:width].astype(BF16)
    wide_s[3 * width : 4 * width, :] = grad_down[width:].astype(BF16)
    grad_pre = (dot_rhs_t(upstream, wdown_ref[...]) * derivative).astype(BF16)
    grad_up = dot_lhs_t(hidden2, grad_pre)
    wide_s[0 * width : 1 * width, :] = grad_up[:, :width].astype(BF16)
    wide_s[1 * width : 2 * width, :] = grad_up[:, width:].astype(BF16)
    grad_hidden2 = dot_rhs_t(grad_pre, wup_ref[...])
    grad_gain2 = jnp.sum(grad_hidden2 * normed2, axis=0, keepdims=True)
    grad_mixed = upstream.astype(F32) + norm_backward(grad_hidden2, normed2, inverse2, gain2)
    mixed_ref[...] = grad_mixed
    grad_mixed16 = grad_mixed.astype(BF16)
    square_s[3 * width : 4 * width, :] = dot_lhs_t(attended, grad_mixed16).astype(BF16)
    grad_att = dot_rhs_t(grad_mixed16, wo_ref[...]).astype(BF16).astype(F32)
    grad_stack = stack_heads(grad_att, head_masks)
    product = grad_att * attended32
    dots = dot_rhs_t(grad_stack, value_all)

    local_terms = []
    far_terms = []
    for h in range(heads):
        block = pl.ds(h * rows, rows)
        delta = jnp.sum(jnp.where(head_masks[h], product, 0.0), axis=1, keepdims=True)
        tangent = tanh_s[block, :]
        slope = 1.0 - tangent * tangent
        dlogit = weight_s[block, :].astype(F32) * (dots[h * rows : (h + 1) * rows] - delta)
        sloped = dlogit * slope
        terms = jnp.sum(sloped * raw_s[block, :], axis=0, keepdims=True)
        local_terms.append(jnp.sum(terms[:, :rows], axis=1, keepdims=True))
        far_terms.append(jnp.sum(terms[:, rows:], axis=1, keepdims=True))
        dscore_s[block, :rows] = (sloped[:, :rows] * (local_ref[h] * scale)).astype(BF16)
        dscore_s[block, rows:] = (sloped[:, rows:] * (far_ref[h] * scale)).astype(BF16)

    grad_query = collapse(dot(dscore_s[...], key_all), head_masks).astype(BF16)
    grad_key = dot_lhs_t(dscore_s[...], query_stack).astype(BF16)
    grad_value = dot_lhs_t(weight_s[...], grad_stack).astype(BF16)
    square_s[0 * width : 1 * width, :] = dot_lhs_t(hidden[:rows], grad_query).astype(BF16)
    square_s[1 * width : 2 * width, :] = dot_lhs_t(hidden, grad_key).astype(BF16)
    square_s[2 * width : 3 * width, :] = dot_lhs_t(hidden, grad_value).astype(BF16)
    grad_hidden = dot_rhs_t(grad_key, wk_ref[...]) + dot_rhs_t(grad_value, wv_ref[...])
    own = grad_hidden[:rows] + dot_rhs_t(grad_query, wq_ref[...])
    own_ref[...] = own
    grad_gain1 = jnp.sum(own * normed1[:rows], axis=0, keepdims=True)
    grad_gain1 = grad_gain1 + jnp.sum(grad_hidden[rows:] * normed1[rows:], axis=0, keepdims=True)
    back = [grad_hidden[(k + 1) * rows : (k + 2) * rows] for k in range(count)]
    for (even, odd), ref in zip(slots, slot_refs):
        ref[...] = jnp.where(
            core == 1, 0.0 if odd is None else back[odd], 0.0 if even is None else back[even]
        ).astype(BF16)

    column = lax.broadcasted_iota(jnp.int32, (1, width), 1)
    gains = jnp.zeros((1, width), F32)
    for h in range(heads):
        gains = jnp.where(column == h, local_terms[h], gains)
        gains = jnp.where(column == heads + h, far_terms[h], gains)
    line = lax.broadcasted_iota(jnp.int32, (SMALL // 2, width), 0)
    small = jnp.where(line == 0, grad_gain1, jnp.where(line == 1, grad_gain2, jnp.where(line == 2, gains, 0.0)))
    sends_ref[keeps_ref.shape[0] :, :] = split_parts(small)
    sort_units(wide_s, keepw_ref, sendw_ref, bits)
    sort_units(square_s, keeps_ref, sends_ref, bits)


def pair_kernel(slots, keepw_ref, recvw_ref, keeps_ref, sents_ref, recvs_ref, *refs):
    slot_refs = refs[: sum(slots)]
    out_refs = refs[sum(slots) :]
    rows = keepw_ref.shape[0] // 4
    wide = (keepw_ref[...].astype(F32) + recvw_ref[...].astype(F32)).astype(BF16)
    square = (keeps_ref[...].astype(F32) + recvs_ref[: 4 * rows, :].astype(F32)).astype(BF16)
    packed = split_parts(join_parts(sents_ref[4 * rows :, :]) + join_parts(recvs_ref[4 * rows :, :]))
    used = 0
    for r in range(4):
        span = slice(r * rows, (r + 1) * rows)
        out_refs[r][:rows, :] = wide[span]
        out_refs[r][rows : 2 * rows, :] = square[span]
        out_refs[r][2 * rows : 2 * rows + SMALL, :] = packed
        if r and slots[r - 1]:
            out_refs[r][2 * rows + SMALL :, :] = slot_refs[used][...]
            used += 1


def quad_kernel(has_slot, own_ref, one_ref, two_ref, three_ref, *refs):
    wide_ref, square_ref = refs[-2:]
    total_rows = own_ref.shape[0]
    rows = (total_rows - SMALL) // 2
    data = [ref[: 2 * rows, :].astype(F32) for ref in (own_ref, one_ref, two_ref, three_ref)]
    small = [join_parts(ref[2 * rows : total_rows, :]) for ref in (own_ref, one_ref, two_ref, three_ref)]
    total = ((data[0] + data[1]) + (data[2] + data[3])).astype(BF16)
    wide_ref[:rows, :] = total[:rows]
    square_ref[:rows, :] = total[rows:]
    square_ref[rows:, :] = split_parts((small[0] + small[1]) + (small[2] + small[3]))
    if has_slot:
        wide_ref[rows:, :] = refs[0][...]


def double_kernel(rows, small, has_slot, own_ref, recv_ref, *refs):
    out_ref = refs[-1]
    total = own_ref[:rows, :].astype(F32) + recv_ref[:rows, :].astype(F32)
    out_ref[:rows, :] = total.astype(BF16)
    if small:
        span = slice(rows, rows + SMALL)
        out_ref[span, :] = split_parts(join_parts(own_ref[span, :]) + join_parts(recv_ref[span, :]))
    if has_slot:
        out_ref[rows:, :] = refs[0][...]


def join_kernel(wide_ref, square_ref, out_ref):
    rows = out_ref.shape[0] // 2
    out_ref[:rows, :] = wide_ref[:rows, :]
    out_ref[rows:, :] = square_ref[:rows, :]


def tail_kernel(start, *refs):
    count = len(start)
    feats_ref, rows_ref, own_ref, mixed_ref, gain_ref, small_ref = refs[:6]
    out_ref, grad_ref, gain1_ref, gain2_ref, local_ref, far_ref, flag_ref = refs[6 + count :]
    out_ref[...] = rows_ref[...]
    normed, inverse = norm_forward(feats_ref[...].astype(F32))
    grad_hidden = own_ref[...]
    for ref, first in zip(refs[6 : 6 + count], start):
        grad_hidden = grad_hidden + ref[first:, :].astype(F32)
    grad = mixed_ref[...] + norm_backward(grad_hidden, normed, inverse, gain_ref[...])
    grad_ref[...] = grad.astype(BF16)
    heads = local_ref.shape[0]
    small = join_parts(small_ref[small_ref.shape[0] - SMALL :, :])
    gain1_ref[...] = small[0:1]
    gain2_ref[...] = small[1:2]
    local_ref[...] = small[2, :heads]
    far_ref[...] = small[2, heads : 2 * heads]
    flag_ref[...] = jnp.zeros(flag_ref.shape, F32)


def after_kernel(source_ref, flag_ref, out_ref):
    out_ref[...] = source_ref[...]


def spread_kernel(*refs):
    piece_refs = refs[:8]
    wq_ref, wk_ref, wv_ref, wo_ref, up_ref, down_ref, pieces, chunks, sems = refs[8:]
    width = wq_ref.shape[0]
    half = width // 2
    core, quad = device_bits()
    relay(piece_refs, [pieces.at[k] for k in range(8)])
    targets = [
        up_ref.at[:, :width],
        up_ref.at[:, width:],
        down_ref.at[:width, :],
        down_ref.at[width:, :],
        wq_ref,
        wk_ref,
        wv_ref,
        wo_ref,
    ]
    copies = []
    for chunk, target in enumerate(targets):
        first = 0 if chunk < 4 else half
        for part in range(2):
            unit = 2 * (chunk % 4) + part
            rel = (core ^ (unit >> 2)) * 4 + (quad ^ (unit & 3))
            value = pieces[rel, first : first + half, :]
            chunks[chunk, part * half : (part + 1) * half, :] = value.astype(F32)
        copy = pltpu.make_async_copy(chunks.at[chunk], target, sems.at[chunk])
        copy.start()
        copies.append(copy)
    for copy in copies:
        copy.wait()


def struct(shape, dtype):
    return jax.ShapeDtypeStruct(shape, dtype)


VM = pl.BlockSpec(memory_space=pltpu.VMEM)
SM = pl.BlockSpec(memory_space=pltpu.SMEM)
ANY = pl.BlockSpec(memory_space=pl.ANY)
PARAMS = pltpu.CompilerParams(vmem_limit_bytes=VMEM_LIMIT)


def call(kernel, outs, *args, in_specs=None, **kwargs):
    return pl.pallas_call(
        kernel,
        out_shape=outs,
        in_specs=in_specs or [VM] * len(args),
        out_specs=jax.tree.map(lambda _: VM, outs),
        compiler_params=PARAMS,
        **kwargs,
    )(*args)


def flipped(x, bits_even, bits_odd):
    size = lax.axis_size("dom") * lax.axis_size("rep")
    pairs = [(i, i ^ (bits_odd if i & 1 else bits_even)) for i in range(size)]
    return lax.ppermute(x, AXES, pairs)


def local(
    node_feats,
    out_grad,
    norm1_gain,
    w_query,
    w_key,
    w_value,
    w_out,
    norm2_gain,
    w_up,
    w_down,
    local_gain,
    expander_gain,
    partner_perm,
    block_pairs,
    pair_count,
):
    feats = node_feats[0]
    partners = partner_perm[0, :, 0, :]
    rows, width = feats.shape
    heads = local_gain.shape[0]
    size = lax.axis_size("dom") * lax.axis_size("rep")
    levels = lax.axis_size("dom").bit_length() - 1
    by_bit = {}
    for matching in range(partners.shape[0]):
        by_bit.setdefault((levels - 1 - matching) % levels, []).append(matching)
    bits = sorted(by_bit)
    groups = [by_bit[b] for b in bits]

    def swapped(x, bit):
        return lax.ppermute(x, "dom", [(i, i ^ 1 << bit) for i in range(lax.axis_size("dom"))])

    rep_bits = lax.axis_size("rep").bit_length() - 1
    high_bits = [1 << k for k in range(3, size.bit_length() - 1)]
    flat = {1 << (b + rep_bits): k for k, b in enumerate(bits)}
    quad_slots = [flat.get(bit) for bit in (2, 4, 6)]
    orders = (list(zip(high_bits, high_bits[::-1])), list(zip(high_bits[::-1], high_bits)))
    high_slots = [(flat.get(even), flat.get(odd)) for even, odd in orders[0]]
    slots = [(k, k) for k in quad_slots if k is not None]
    slots += [pair for pair in high_slots if pair != (None, None)]

    others = [swapped(feats, b) for b in bits]
    count = len(bits)
    tall = count * rows
    stacked = heads * rows
    gain1 = norm1_gain.reshape(1, width)
    gain2 = norm2_gain.reshape(1, width)
    upstream = out_grad[0]
    flag = struct((8, 128), F32)
    begun = call(
        flag_kernel, flag, cost_estimate=pl.CostEstimate(flops=10**10, bytes_accessed=1, transcendentals=0)
    )
    passed = (feats, upstream, gain1, gain2)
    counts, feats_near, up_near, gain1_near, gain2_near = call(
        functools.partial(count_kernel, groups),
        (struct((rows, tall), F32),) + tuple(struct(x.shape, x.dtype) for x in passed),
        begun,
        partners,
        *passed,
        cost_estimate=pl.CostEstimate(flops=10**10, bytes_accessed=1, transcendentals=0),
    )
    out_rows, keep_wide, send_wide, keep_square, send_square, own, grad_mixed, *slot_rows = call(
        functools.partial(layer_kernel, slots, count),
        (
            struct((rows, width), BF16),
            struct((2 * width, width), BF16),
            struct((2 * width, width), BF16),
            struct((2 * width, width), BF16),
            struct((2 * width + SMALL, width), BF16),
            struct((rows, width), F32),
            struct((rows, width), F32),
        )
        + tuple(struct((rows, width), BF16) for _ in slots),
        feats_near,
        *others,
        up_near,
        gain1_near,
        w_query,
        w_key,
        w_value,
        w_out,
        gain2_near,
        w_up,
        w_down,
        local_gain,
        expander_gain,
        counts,
        in_specs=[VM] * (count + 10) + [SM, SM, VM],
        scratch_shapes=[
            pltpu.VMEM((stacked, tall + rows), F32),
            pltpu.VMEM((stacked, tall + rows), F32),
            pltpu.VMEM((stacked, tall + rows), BF16),
            pltpu.VMEM((stacked, tall + rows), BF16),
            pltpu.VMEM((4 * width, width), BF16),
            pltpu.VMEM((4 * width, width), BF16),
        ],
    )
    slot_rows = iter(slot_rows)
    slot_quad = [None if k is None else next(slot_rows) for k in quad_slots]
    slot_high = [None if pair == (None, None) else next(slot_rows) for pair in high_slots]

    def present(*items):
        return [x for x in items if x is not None]

    def sized(base, slot):
        return struct((base + (0 if slot is None else rows), width), BF16)

    half = width // 2
    recv_wide = flipped(send_wide, 1, 1)
    recv_square = flipped(send_square, 1, 1)
    data = 2 * half + SMALL
    own_quad, *send_quad = call(
        functools.partial(pair_kernel, [x is not None for x in slot_quad]),
        (struct((data, width), BF16),) + tuple(sized(data, x) for x in slot_quad),
        keep_wide,
        recv_wide,
        keep_square,
        send_square,
        recv_square,
        *present(*slot_quad),
    )
    recv_quad = [flipped(x, bit, bit) for x, bit in zip(send_quad, (2, 4, 6))]
    returned = [x for x, slot in zip(recv_quad, slot_quad) if slot is not None]
    starts = [data] * len(returned)
    wide, square = call(
        functools.partial(quad_kernel, slot_high[0] is not None),
        (sized(half, slot_high[0]), struct((half + SMALL, width), BF16)),
        own_quad,
        *recv_quad,
        *present(slot_high[0]),
    )
    for k in range(len(high_bits)):
        recv_wide = flipped(wide, *orders[0][k])
        recv_square = flipped(square, *orders[1][k])
        if slot_high[k] is not None:
            returned.append(recv_wide)
            starts.append(half)
        slot = slot_high[k + 1] if k + 1 < len(high_bits) else None
        extra = present(slot)
        wide = call(
            functools.partial(double_kernel, half, False, slot is not None),
            sized(half, slot),
            wide,
            recv_wide,
            *extra,
            square,
        )
        square = call(
            functools.partial(double_kernel, half, True, False),
            struct((half + SMALL, width), BF16),
            square,
            recv_square,
            wide,
        )
    base = call(join_kernel, struct((2 * half, width), BF16), wide, square)
    near = [base] + [flipped(base, bit, bit) for bit in (2, 4, 6)]
    over = [flipped(x, 1, 1) for x in near]
    block = struct((rows, width), BF16)
    one = struct((1, width), F32)
    full = struct((width, width), F32)
    few = struct((heads,), F32)
    node_out, grad_feats, grad_gain1, grad_gain2, grad_local, grad_far, ended = call(
        functools.partial(tail_kernel, starts),
        (block, block, one, one, few, few, flag),
        feats_near,
        out_rows,
        own,
        grad_mixed,
        gain1_near,
        square,
        *returned,
    )
    base = call(join_kernel, struct((2 * half, width), BF16), wide, square)
    near = [base] + [flipped(base, bit, bit) for bit in (2, 4, 6)]
    near[3] = call(after_kernel, struct(base.shape, BF16), near[3], ended)
    over = [flipped(x, 1, 1) for x in near]
    grad_wq, grad_wk, grad_wv, grad_wout, grad_up, grad_down = pl.pallas_call(
        spread_kernel,
        out_shape=(full,) * 4 + (struct((width, 2 * width), F32), struct((2 * width, width), F32)),
        in_specs=[VM] * 8,
        out_specs=(ANY,) * 6,
        scratch_shapes=[
            pltpu.VMEM((8, width, width), BF16),
            pltpu.VMEM((8, width, width), F32),
            pltpu.SemaphoreType.DMA((8,)),
        ],
        compiler_params=PARAMS,
    )(*near, *over)
    return (
        node_out[None],
        grad_feats[None],
        grad_gain1.reshape(width),
        grad_wq,
        grad_wk,
        grad_wv,
        grad_wout,
        grad_gain2.reshape(width),
        grad_up,
        grad_down,
        grad_local,
        grad_far,
    )


def solution(mesh):
    whole = P()
    rows = P("rep", "dom", None)
    return jax.shard_map(
        local,
        mesh=mesh,
        in_specs=(rows, rows)
        + (whole,) * 10
        + (P("rep", None, "dom", None), rows, P("rep", "dom")),
        out_specs=(rows, rows) + (whole,) * 10,
        check_vma=False,
    )
```

time: 79.9 us -> 53.2 us (0.67)
  waiting for transfers between devices: 43.7 us -> 24.2 us
  local copies, waits for them, and re-layouts: 8.51 us -> 1.34 us
  starting transfers between devices: 16.8 us -> 19.4 us
  Pallas kernels: 9.68 us -> 7.27 us
    ppermute x10 -> x16, waiting for transfers between devices: 33.3 us -> 22.1 us  [flipped(): return lax.ppermute(x, AXES, pairs)]
    ppermute x6 -> x3, waiting for transfers between devices: 10.4 us -> 2.09 us  [swapped(): lax.ppermute(x, 'dom', [(i, i ^ 1 << bit) for i in range(lax.axis_size('d...]
    unnamed x28 -> x26, local copies, waits for them, and re-layouts: 7.91 us -> 1.34 us
    ppermute x10 -> x16, starting transfers between devices: 6.35 us -> 12.2 us  [flipped(): return lax.ppermute(x, AXES, pairs)]
    ppermute x6 -> x3, starting transfers between devices: 10.5 us -> 7.2 us  [swapped(): lax.ppermute(x, 'dom', [(i, i ^ 1 << bit) for i in range(lax.axis_size('d...]
    pallas_call x7 -> x12, Pallas kernels: 7.59 us -> 5.81 us  [call(): pl.pallas_call(kernel, out_shape=outs, in_specs=in_specs or [VM] * len(ar...]
  transfers between devices with their start and end apart: 16 -> 19, of which waited for: 12 -> 13; matrix products, arithmetic and copies ran while one was open for 0% -> 0% of each run, Pallas kernels for 1% -> 2%
where the time goes in v4:
time: 53.2 us; the launch traced here: 53 us
  waiting for transfers between devices  24.2 us (45%)
  starting transfers between devices  19.4 us (36%)
  Pallas kernels  7.27 us (14%)
  local copies, waits for them, and re-layouts  1.34 us (3%)
  between operations  0.85 us (2%)
    ppermute x16, waiting for transfers between devices, flipped(): return lax.ppermute(x, AXES, pairs)  22.1 us
    ppermute x16, starting transfers between devices, flipped(): return lax.ppermute(x, AXES, pairs)  12.2 us
    ppermute x3, starting transfers between devices, swapped(): lax.ppermute(x, 'dom', [(i, i ^ 1 << bit) for i in range(lax.axis_size('d...  7.2 us
    pallas_call x12, Pallas kernels, call(): pl.pallas_call(kernel, out_shape=outs, in_specs=in_specs or [VM] * len(ar...  5.81 us
    ppermute x3, waiting for transfers between devices, swapped(): lax.ppermute(x, 'dom', [(i, i ^ 1 << bit) for i in range(lax.axis_size('d...  2.09 us
    pallas_call x1, Pallas kernels, local(): pl.pallas_call(spread_kernel, out_shape=(full,) * 4 + (struct((width, 2 *...  1.46 us
    unnamed x26, local copies, waits for them, and re-layouts  1.34 us
  transfers between devices with their start and end apart: 19, of which 13 were waited for; matrix products, arithmetic and copies ran while one was open for 0% of the time, Pallas kernels for 2%

profile of v4, /device:TPU:0, one launch (start us, length us, event | category | flops | bytes accessed | tf_op | source)
XLA Modules:
  0.0 53.0 jit_solution(10207714771368349174)
XLA Ops:
  0.7 4.1 %collective-permute-start.2 = (bf16[128,256]{1,0:T(8,128)(2,1)}, bf16[128,256]{1,0:T(8,128)(2,1)S(1)}, u32[]{:S(2)}, u32[]{:S(2)}) collective-permute-start(bf16[128,256]{1,0:T(8,128)(2,1)} %bitcast.10), channel_id=1, source_target_pairs={{0,16},{4,20},{8,24},{12,28},{16,0},{20,4},{24,8},{28,12},{1,17},{... | collective-permute-start | bytes 196616 | tf_op jit(solution)/shard_map/ppermute | solution.py:410
  4.8 1.6 %collective-permute-start.1 = (bf16[128,256]{1,0:T(8,128)(2,1)}, bf16[128,256]{1,0:T(8,128)(2,1)S(1)}, u32[]{:S(2)}, u32[]{:S(2)}) collective-permute-start(bf16[128,256]{1,0:T(8,128)(2,1)} %bitcast.11), channel_id=1, source_target_pairs={{0,8},{4,12},{8,0},{12,4},{16,24},{20,28},{24,16},{28,20},{1,9},{5... | collective-permute-start | bytes 196616 | tf_op jit(solution)/shard_map/ppermute | solution.py:410
  6.3 1.5 %collective-permute-start = (bf16[128,256]{1,0:T(8,128)(2,1)}, bf16[128,256]{1,0:T(8,128)(2,1)S(1)}, u32[]{:S(2)}, u32[]{:S(2)}) collective-permute-start(bf16[128,256]{1,0:T(8,128)(2,1)} %bitcast.12), channel_id=1, source_target_pairs={{0,4},{4,0},{8,12},{12,8},{16,20},{20,16},{24,28},{28,24},{1,5},{5... | collective-permute-start | bytes 196616 | tf_op jit(solution)/shard_map/ppermute | solution.py:410
  7.9 0.6 %copy-done.12 = f32[256]{0:T(256)S(1)} copy-done((f32[256]{0:T(256)S(1)}, f32[256]{0:T(256)}, u32[]{:S(2)}) %copy-start.12) | copy-done | bytes 1048
  8.5 0.0 copy-done.10
  8.6 0.0 copy-done.11
  8.6 0.0 copy-start.4
  8.6 0.0 copy-start.5
  8.6 0.1 shard_map.221
  8.7 0.0 collective-permute-done.2.refs_3_
  8.7 0.5 collective-permute-done.1.refs_2_
  9.2 1.6 %collective-permute-done.refs_1_ = bf16[128,256]{1,0:T(8,128)(2,1)S(1)} collective-permute-done((bf16[128,256]{1,0:T(8,128)(2,1)}, bf16[128,256]{1,0:T(8,128)(2,1)S(1)}, u32[]{:S(2)}, u32[]{:S(2)}) %collective-permute-start) | collective-permute-done | bytes 65568 | tf_op jit(solution)/shard_map/ppermute | solution.py:410
  10.9 0.6 %copy-done.6 = f32[4]{0:T(128)S(1)} copy-done((f32[4]{0:T(128)S(1)}, f32[4]{0:T(128)}, u32[]{:S(2)}) %copy-start.6) | copy-done | bytes 40
  11.5 0.0 copy-done.7
  11.5 4.5 %shard_map.222 = (bf16[128,256]{1,0:T(8,128)(2,1)S(1)}, bf16[512,256]{1,0:T(8,128)(2,1)S(1)}, bf16[512,256]{1,0:T(8,128)(2,1)S(1)}, bf16[512,256]{1,0:T(8,128)(2...) custom-call(bf16[128,256]{1,0:T(8,128)(2,1)S(1)} %get-tuple-element., ...), custom_call_target="tpu_custom_call" | custom-call | tf_op jit(solution)/shard_map/pallas_call | solution.py:364
  16.0 0.1 collective-permute-start.4
  16.1 0.5 collective-permute-start.3
  16.6 1.4 %collective-permute-done.3.recvw_ref = bf16[512,256]{1,0:T(8,128)(2,1)S(1)} collective-permute-done((bf16[512,256]{1,0:T(8,128)(2,1)S(1)}, bf16[512,256]{1,0:T(8,128)(2,1)S(1)}, u32[]{:S(2)}, u32[]{:S(2)}) %collective-permute-start.3) | collective-permute-done | bytes 262176 | tf_op jit(solution)/shard_map/ppermute | solution.py:377
  18.0 0.0 collective-permute-done.4.recvs_ref
  18.0 0.1 shard_map.223
  18.1 1.6 %collective-permute-start.6 = (bf16[400,256]{1,0:T(8,128)(2,1)S(1)}, bf16[400,256]{1,0:T(8,128)(2,1)S(1)}, u32[]{:S(2)}, u32[]{:S(2)}) collective-permute-start(bf16[400,256]{1,0:T(8,128)(2,1)S(1)} %get-tuple-element.61), channel_id=1, source_target_pairs={{0,4},{1,5},{2,6},{3,7},{4,0},{5,1},{6,2},{7,3},{8,12},{9,13},{10,... | collective-permute-start | bytes 614408 | tf_op jit(solution)/shard_map/ppermute | solution.py:377
  19.7 1.5 %collective-permute-start.5 = (bf16[272,256]{1,0:T(8,128)(2,1)S(1)}, bf16[272,256]{1,0:T(8,128)(2,1)S(1)}, u32[]{:S(2)}, u32[]{:S(2)}) collective-permute-start(bf16[272,256]{1,0:T(8,128)(2,1)S(1)} %get-tuple-element.60), channel_id=1, source_target_pairs={{0,2},{1,3},{2,0},{3,1},{4,6},{5,7},{6,4},{7,5},{8,10},{9,11},{10,... | collective-permute-start | bytes 417800 | tf_op jit(solution)/shard_map/ppermute | solution.py:377
  21.2 0.5 collective-permute-start.7
  21.7 4.6 %collective-permute-done.5.one_ref = bf16[272,256]{1,0:T(8,128)(2,1)S(1)} collective-permute-done((bf16[272,256]{1,0:T(8,128)(2,1)S(1)}, bf16[272,256]{1,0:T(8,128)(2,1)S(1)}, u32[]{:S(2)}, u32[]{:S(2)}) %collective-permute-start.5) | collective-permute-done | bytes 139296 | tf_op jit(solution)/shard_map/ppermute | solution.py:377
  26.2 1.9 %collective-permute-done.7.three_ref = bf16[272,256]{1,0:T(8,128)(2,1)S(1)} collective-permute-done((bf16[272,256]{1,0:T(8,128)(2,1)S(1)}, bf16[272,256]{1,0:T(8,128)(2,1)S(1)}, u32[]{:S(2)}, u32[]{:S(2)}) %collective-permute-start.7) | collective-permute-done | bytes 139296 | tf_op jit(solution)/shard_map/ppermute | solution.py:377
  28.2 0.1 collective-permute-done.6.two_ref.refs_6_
  28.3 0.1 shard_map.224
  28.3 0.5 collective-permute-start.9
  28.9 1.3 %collective-permute-start.8 = (bf16[144,256]{1,0:T(8,128)(2,1)S(1)}, bf16[144,256]{1,0:T(8,128)(2,1)S(1)}, u32[]{:S(2)}, u32[]{:S(2)}) collective-permute-start(bf16[144,256]{1,0:T(8,128)(2,1)S(1)} %get-tuple-element.64.refs_1_.own_ref), channel_id=1, source_target_pairs={{0,16},{1,9},{2,18},{3,11},{4,20},{5,13},{6,22},{7,15},{8,24},{9,1... | collective-permute-start | bytes 221192 | tf_op jit(solution)/shard_map/ppermute | solution.py:377
  30.2 5.3 %collective-permute-done.9.recv_ref.refs_7_ = bf16[256,256]{1,0:T(8,128)(2,1)S(1)} collective-permute-done((bf16[256,256]{1,0:T(8,128)(2,1)S(1)}, bf16[256,256]{1,0:T(8,128)(2,1)S(1)}, u32[]{:S(2)}, u32[]{:S(2)}) %collective-permute-start.9) | collective-permute-done | bytes 131104 | tf_op jit(solution)/shard_map/ppermute | solution.py:377
  35.5 0.1 collective-permute-start.11
  35.6 0.0 collective-permute-done.8.recv_ref
  35.6 2.1 %collective-permute-start.10 = (bf16[144,256]{1,0:T(8,128)(2,1)S(1)}, bf16[144,256]{1,0:T(8,128)(2,1)S(1)}, u32[]{:S(2)}, u32[]{:S(2)}) collective-permute-start(bf16[144,256]{1,0:T(8,128)(2,1)S(1)} %shard_map.226.refs_0_.own_ref), channel_id=1, source_target_pairs={{0,8},{1,17},{2,10},{3,19},{4,12},{5,21},{6,14},{7,23},{8,0},{9,25... | collective-permute-start | bytes 221192 | tf_op jit(solution)/shard_map/ppermute | solution.py:377
  37.7 4.9 %collective-permute-done.11.recv_ref.refs_8_ = bf16[256,256]{1,0:T(8,128)(2,1)S(1)} collective-permute-done((bf16[256,256]{1,0:T(8,128)(2,1)S(1)}, bf16[256,256]{1,0:T(8,128)(2,1)S(1)}, u32[]{:S(2)}, u32[]{:S(2)}) %collective-permute-start.11) | collective-permute-done | bytes 131104 | tf_op jit(solution)/shard_map/ppermute | solution.py:377
  42.7 2.0 %collective-permute-start.14 = (bf16[256,256]{1,0:T(8,128)(2,1)S(1)}, bf16[256,256]{1,0:T(8,128)(2,1)S(1)}, u32[]{:S(2)}, u32[]{:S(2)}) collective-permute-start(bf16[256,256]{1,0:T(8,128)(2,1)S(1)} %shard_map.230.refs_0_), channel_id=1, source_target_pairs={{0,6},{1,7},{2,4},{3,5},{4,2},{5,3},{6,0},{7,1},{8,14},{9,15},{10,... | collective-permute-start | bytes 393224 | tf_op jit(solution)/shard_map/ppermute | solution.py:377
  44.6 0.5 collective-permute-start.13
  45.1 1.1 %collective-permute-start.12 = (bf16[256,256]{1,0:T(8,128)(2,1)S(1)}, bf16[256,256]{1,0:T(8,128)(2,1)S(1)}, u32[]{:S(2)}, u32[]{:S(2)}) collective-permute-start(bf16[256,256]{1,0:T(8,128)(2,1)S(1)} %shard_map.230.refs_0_), channel_id=1, source_target_pairs={{0,2},{1,3},{2,0},{3,1},{4,6},{5,7},{6,4},{7,5},{8,10},{9,11},{10,... | collective-permute-start | bytes 393224 | tf_op jit(solution)/shard_map/ppermute | solution.py:377
  46.2 0.0 collective-permute-start.15
  46.2 0.9 %shard_map.229 = (bf16[128,256]{1,0:T(8,128)(2,1)}, bf16[128,256]{1,0:T(8,128)(2,1)}, f32[1,256]{1,0:T(1,128)}, f32[1,256]{1,0:T(1,128)}, f32[4]{0:T(128)}, /*index=5*/f32[4]{0:T(128)}, f32[8,128]{1,0:T(8,128)S(1)}) custom-call(bf16[128,256]{1,0:T(8,128)(2,1)S(1)} %get-tuple-element.46.refs_0_, bf16[128,256]{1,0:T(8,128)(2,1)S(1)} %get-tuple-element.51.refs_1_, ...), custom_call_target="tpu_custom_call" | custom-call | tf_op jit(solution)/shard_map/pallas_call | solution.py:364
  47.1 1.5 %collective-permute-done.14.source_ref = bf16[256,256]{1,0:T(8,128)(2,1)S(1)} collective-permute-done((bf16[256,256]{1,0:T(8,128)(2,1)S(1)}, bf16[256,256]{1,0:T(8,128)(2,1)S(1)}, u32[]{:S(2)}, u32[]{:S(2)}) %collective-permute-start.14) | collective-permute-done | bytes 131104 | tf_op jit(solution)/shard_map/ppermute | solution.py:377
  48.7 0.1 collective-permute-start.18
  48.7 1.3 %collective-permute-done.13.refs_2_ = bf16[256,256]{1,0:T(8,128)(2,1)S(1)} collective-permute-done((bf16[256,256]{1,0:T(8,128)(2,1)S(1)}, bf16[256,256]{1,0:T(8,128)(2,1)S(1)}, u32[]{:S(2)}, u32[]{:S(2)}) %collective-permute-start.13) | collective-permute-done | bytes 131104 | tf_op jit(solution)/shard_map/ppermute | solution.py:377
  50.0 0.0 collective-permute-start.17
  50.0 0.1 collective-permute-done.12.refs_1_
  50.1 0.4 collective-permute-start.16
  50.5 0.8 %collective-permute-done.17.refs_6_ = bf16[256,256]{1,0:T(8,128)(2,1)S(1)} collective-permute-done((bf16[256,256]{1,0:T(8,128)(2,1)S(1)}, bf16[256,256]{1,0:T(8,128)(2,1)S(1)}, u32[]{:S(2)}, u32[]{:S(2)}) %collective-permute-start.17) | collective-permute-done | bytes 131104 | tf_op jit(solution)/shard_map/ppermute | solution.py:377
  51.3 0.2 collective-permute-done.16.refs_5_
  51.5 1.5 %shard_map.232 = (f32[256,256]{1,0:T(8,128)}, f32[256,256]{1,0:T(8,128)}, f32[256,256]{1,0:T(8,128)}, f32[256,256]{1,0:T(8,128)}, f32[256,512]{1,0:T(8,128)}, /*index=5*/f32[512,256]{1,0:T(8,128)}) custom-call(bf16[256,256]{1,0:T(8,128)(2,1)S(1)} %shard_map.230.refs_0_, bf16[256,256]{1,0:T(8,128)(2,1)S(1)} %collective-permute-done.12.refs_1_, ...), custom_call_target="tpu_custom_call" | custom-call | tf_op jit(solution)/shard_map/pallas_call | solution.py:556
  (29 shorter events, 0.2 us)
Async XLA Ops:
  0.6 7.2 %copy-start.8 = (bf16[1,128,256]{2,1,0:T(8,128)(2,1)S(1)}, bf16[1,128,256]{2,1,0:T(8,128)(2,1)}, u32[]{:S(2)}) copy-start(bf16[1,128,256]{2,1,0:T(8,128)(2,1)} %param.16) | copy-start | bytes 196612
  0.7 7.2 %copy-start.9 = (bf16[1,128,256]{2,1,0:T(8,128)(2,1)S(1)}, bf16[1,128,256]{2,1,0:T(8,128)(2,1)}, u32[]{:S(2)}) copy-start(bf16[1,128,256]{2,1,0:T(8,128)(2,1)} %param.15) | copy-start | bytes 196612
  0.7 8.1 %collective-permute-start.2 = (bf16[128,256]{1,0:T(8,128)(2,1)}, bf16[128,256]{1,0:T(8,128)(2,1)S(1)}, u32[]{:S(2)}, u32[]{:S(2)}) collective-permute-start(bf16[128,256]{1,0:T(8,128)(2,1)} %bitcast.10), channel_id=1, source_target_pairs={{0,16},{4,20},{8,24},{12,28},{16,0},{20,4},{24,8},{28,12},{1,17},{... | collective-permute-start | bytes 196616 | tf_op jit(solution)/shard_map/ppermute | solution.py:410
  4.8 4.5 %collective-permute-start.1 = (bf16[128,256]{1,0:T(8,128)(2,1)}, bf16[128,256]{1,0:T(8,128)(2,1)S(1)}, u32[]{:S(2)}, u32[]{:S(2)}) collective-permute-start(bf16[128,256]{1,0:T(8,128)(2,1)} %bitcast.11), channel_id=1, source_target_pairs={{0,8},{4,12},{8,0},{12,4},{16,24},{20,28},{24,16},{28,20},{1,9},{5... | collective-permute-start | bytes 196616 | tf_op jit(solution)/shard_map/ppermute | solution.py:410
  6.3 4.5 %collective-permute-start = (bf16[128,256]{1,0:T(8,128)(2,1)}, bf16[128,256]{1,0:T(8,128)(2,1)S(1)}, u32[]{:S(2)}, u32[]{:S(2)}) collective-permute-start(bf16[128,256]{1,0:T(8,128)(2,1)} %bitcast.12), channel_id=1, source_target_pairs={{0,4},{4,0},{8,12},{12,8},{16,20},{20,16},{24,28},{28,24},{1,5},{5... | collective-permute-start | bytes 196616 | tf_op jit(solution)/shard_map/ppermute | solution.py:410
  7.9 0.7 %copy-start.12 = (f32[256]{0:T(256)S(1)}, f32[256]{0:T(256)}, u32[]{:S(2)}) copy-start(f32[256]{0:T(256)} %param.22) | copy-start | bytes 3076
  7.9 0.7 %copy-start.10 = (s32[1,4,1,128]{3,2,1,0:T(1,128)S(1)}, s32[1,4,1,128]{3,2,1,0:T(1,128)}, u32[]{:S(2)}) copy-start(s32[1,4,1,128]{3,2,1,0:T(1,128)} %param.27) | copy-start | bytes 6148
  7.9 0.7 %copy-start.11 = (f32[256]{0:T(256)S(1)}, f32[256]{0:T(256)}, u32[]{:S(2)}) copy-start(f32[256]{0:T(256)} %param.17) | copy-start | bytes 3076
  8.6 2.3 %copy-start = (bf16[256,512]{1,0:T(8,128)(2,1)S(1)}, bf16[256,512]{1,0:T(8,128)(2,1)}, u32[]{:S(2)}) copy-start(bf16[256,512]{1,0:T(8,128)(2,1)} %refs_11_.1) | copy-start | bytes 786436
  8.6 2.3 %copy-start.1 = (bf16[512,256]{1,0:T(8,128)(2,1)S(1)}, bf16[512,256]{1,0:T(8,128)(2,1)}, u32[]{:S(2)}) copy-start(bf16[512,256]{1,0:T(8,128)(2,1)} %refs_12_.1) | copy-start | bytes 786436
  8.6 2.3 %copy-start.2 = (bf16[256,256]{1,0:T(8,128)(2,1)S(1)}, bf16[256,256]{1,0:T(8,128)(2,1)}, u32[]{:S(2)}) copy-start(bf16[256,256]{1,0:T(8,128)(2,1)} %refs_6_.1) | copy-start | bytes 393220
  8.6 2.3 %copy-start.3 = (bf16[256,256]{1,0:T(8,128)(2,1)S(1)}, bf16[256,256]{1,0:T(8,128)(2,1)}, u32[]{:S(2)}) copy-start(bf16[256,256]{1,0:T(8,128)(2,1)} %refs_7_.1) | copy-start | bytes 393220
  8.6 2.3 %copy-start.4 = (bf16[256,256]{1,0:T(8,128)(2,1)S(1)}, bf16[256,256]{1,0:T(8,128)(2,1)}, u32[]{:S(2)}) copy-start(bf16[256,256]{1,0:T(8,128)(2,1)} %refs_8_.1) | copy-start | bytes 393220
  8.6 2.3 %copy-start.5 = (bf16[256,256]{1,0:T(8,128)(2,1)S(1)}, bf16[256,256]{1,0:T(8,128)(2,1)}, u32[]{:S(2)}) copy-start(bf16[256,256]{1,0:T(8,128)(2,1)} %refs_9_.1) | copy-start | bytes 393220
  10.8 0.7 %copy-start.6 = (f32[4]{0:T(128)S(1)}, f32[4]{0:T(128)}, u32[]{:S(2)}) copy-start(f32[4]{0:T(128)} %refs_13_.1) | copy-start | bytes 52
  10.8 0.7 %copy-start.7 = (f32[4]{0:T(128)S(1)}, f32[4]{0:T(128)}, u32[]{:S(2)}) copy-start(f32[4]{0:T(128)} %refs_14_.1) | copy-start | bytes 52
  16.0 2.0 %collective-permute-start.4 = (bf16[528,256]{1,0:T(8,128)(2,1)S(1)}, bf16[528,256]{1,0:T(8,128)(2,1)S(1)}, u32[]{:S(2)}, u32[]{:S(2)}) collective-permute-start(bf16[528,256]{1,0:T(8,128)(2,1)S(1)} %get-tuple-element.57.sents_ref), channel_id=1, source_target_pairs={{0,1},{1,0},{2,3},{3,2},{4,5},{5,4},{6,7},{7,6},{8,9},{9,8},{10,11... | collective-permute-start | bytes 811016 | tf_op jit(solution)/shard_map/ppermute | solution.py:377
  16.1 1.9 %collective-permute-start.3 = (bf16[512,256]{1,0:T(8,128)(2,1)S(1)}, bf16[512,256]{1,0:T(8,128)(2,1)S(1)}, u32[]{:S(2)}, u32[]{:S(2)}) collective-permute-start(bf16[512,256]{1,0:T(8,128)(2,1)S(1)} %get-tuple-element.55), channel_id=1, source_target_pairs={{0,1},{1,0},{2,3},{3,2},{4,5},{5,4},{6,7},{7,6},{8,9},{9,8},{10,11... | collective-permute-start | bytes 786440 | tf_op jit(solution)/shard_map/ppermute | solution.py:377
  18.1 10.2 %collective-permute-start.6 = (bf16[400,256]{1,0:T(8,128)(2,1)S(1)}, bf16[400,256]{1,0:T(8,128)(2,1)S(1)}, u32[]{:S(2)}, u32[]{:S(2)}) collective-permute-start(bf16[400,256]{1,0:T(8,128)(2,1)S(1)} %get-tuple-element.61), channel_id=1, source_target_pairs={{0,4},{1,5},{2,6},{3,7},{4,0},{5,1},{6,2},{7,3},{8,12},{9,13},{10,... | collective-permute-start | bytes 614408 | tf_op jit(solution)/shard_map/ppermute | solution.py:377
  19.7 6.6 %collective-permute-start.5 = (bf16[272,256]{1,0:T(8,128)(2,1)S(1)}, bf16[272,256]{1,0:T(8,128)(2,1)S(1)}, u32[]{:S(2)}, u32[]{:S(2)}) collective-permute-start(bf16[272,256]{1,0:T(8,128)(2,1)S(1)} %get-tuple-element.60), channel_id=1, source_target_pairs={{0,2},{1,3},{2,0},{3,1},{4,6},{5,7},{6,4},{7,5},{8,10},{9,11},{10,... | collective-permute-start | bytes 417800 | tf_op jit(solution)/shard_map/ppermute | solution.py:377
  21.2 7.0 %collective-permute-start.7 = (bf16[272,256]{1,0:T(8,128)(2,1)S(1)}, bf16[272,256]{1,0:T(8,128)(2,1)S(1)}, u32[]{:S(2)}, u32[]{:S(2)}) collective-permute-start(bf16[272,256]{1,0:T(8,128)(2,1)S(1)} %get-tuple-element.62), channel_id=1, source_target_pairs={{0,6},{1,7},{2,4},{3,5},{4,2},{5,3},{6,0},{7,1},{8,14},{9,15},{10,... | collective-permute-start | bytes 417800 | tf_op jit(solution)/shard_map/ppermute | solution.py:377
  28.3 7.1 %collective-permute-start.9 = (bf16[256,256]{1,0:T(8,128)(2,1)S(1)}, bf16[256,256]{1,0:T(8,128)(2,1)S(1)}, u32[]{:S(2)}, u32[]{:S(2)}) collective-permute-start(bf16[256,256]{1,0:T(8,128)(2,1)S(1)} %get-tuple-element.65.own_ref), channel_id=1, source_target_pairs={{0,8},{1,17},{2,10},{3,19},{4,12},{5,21},{6,14},{7,23},{8,0},{9,25... | collective-permute-start | bytes 393224 | tf_op jit(solution)/shard_map/ppermute | solution.py:377
  28.9 6.7 %collective-permute-start.8 = (bf16[144,256]{1,0:T(8,128)(2,1)S(1)}, bf16[144,256]{1,0:T(8,128)(2,1)S(1)}, u32[]{:S(2)}, u32[]{:S(2)}) collective-permute-start(bf16[144,256]{1,0:T(8,128)(2,1)S(1)} %get-tuple-element.64.refs_1_.own_ref), channel_id=1, source_target_pairs={{0,16},{1,9},{2,18},{3,11},{4,20},{5,13},{6,22},{7,15},{8,24},{9,1... | collective-permute-start | bytes 221192 | tf_op jit(solution)/shard_map/ppermute | solution.py:377
  35.5 7.1 %collective-permute-start.11 = (bf16[256,256]{1,0:T(8,128)(2,1)S(1)}, bf16[256,256]{1,0:T(8,128)(2,1)S(1)}, u32[]{:S(2)}, u32[]{:S(2)}) collective-permute-start(bf16[256,256]{1,0:T(8,128)(2,1)S(1)} %shard_map.225.refs_0_.own_ref), channel_id=1, source_target_pairs={{0,16},{1,9},{2,18},{3,11},{4,20},{5,13},{6,22},{7,15},{8,24},{9,1... | collective-permute-start | bytes 393224 | tf_op jit(solution)/shard_map/ppermute | solution.py:377
  35.6 7.0 %collective-permute-start.10 = (bf16[144,256]{1,0:T(8,128)(2,1)S(1)}, bf16[144,256]{1,0:T(8,128)(2,1)S(1)}, u32[]{:S(2)}, u32[]{:S(2)}) collective-permute-start(bf16[144,256]{1,0:T(8,128)(2,1)S(1)} %shard_map.226.refs_0_.own_ref), channel_id=1, source_target_pairs={{0,8},{1,17},{2,10},{3,19},{4,12},{5,21},{6,14},{7,23},{8,0},{9,25... | collective-permute-start | bytes 221192 | tf_op jit(solution)/shard_map/ppermute | solution.py:377
  42.7 6.0 %collective-permute-start.14 = (bf16[256,256]{1,0:T(8,128)(2,1)S(1)}, bf16[256,256]{1,0:T(8,128)(2,1)S(1)}, u32[]{:S(2)}, u32[]{:S(2)}) collective-permute-start(bf16[256,256]{1,0:T(8,128)(2,1)S(1)} %shard_map.230.refs_0_), channel_id=1, source_target_pairs={{0,6},{1,7},{2,4},{3,5},{4,2},{5,3},{6,0},{7,1},{8,14},{9,15},{10,... | collective-permute-start | bytes 393224 | tf_op jit(solution)/shard_map/ppermute | solution.py:377
  44.6 5.4 %collective-permute-start.13 = (bf16[256,256]{1,0:T(8,128)(2,1)S(1)}, bf16[256,256]{1,0:T(8,128)(2,1)S(1)}, u32[]{:S(2)}, u32[]{:S(2)}) collective-permute-start(bf16[256,256]{1,0:T(8,128)(2,1)S(1)} %shard_map.230.refs_0_), channel_id=1, source_target_pairs={{0,4},{1,5},{2,6},{3,7},{4,0},{5,1},{6,2},{7,3},{8,12},{9,13},{10,... | collective-permute-start | bytes 393224 | tf_op jit(solution)/shard_map/ppermute | solution.py:377
  45.1 5.0 %collective-permute-start.12 = (bf16[256,256]{1,0:T(8,128)(2,1)S(1)}, bf16[256,256]{1,0:T(8,128)(2,1)S(1)}, u32[]{:S(2)}, u32[]{:S(2)}) collective-permute-start(bf16[256,256]{1,0:T(8,128)(2,1)S(1)} %shard_map.230.refs_0_), channel_id=1, source_target_pairs={{0,2},{1,3},{2,0},{3,1},{4,6},{5,7},{6,4},{7,5},{8,10},{9,11},{10,... | collective-permute-start | bytes 393224 | tf_op jit(solution)/shard_map/ppermute | solution.py:377
  46.2 4.3 %collective-permute-start.15 = (bf16[256,256]{1,0:T(8,128)(2,1)S(1)}, bf16[256,256]{1,0:T(8,128)(2,1)S(1)}, u32[]{:S(2)}, u32[]{:S(2)}) collective-permute-start(bf16[256,256]{1,0:T(8,128)(2,1)S(1)} %shard_map.230.refs_0_), channel_id=1, source_target_pairs={{0,1},{1,0},{2,3},{3,2},{4,5},{5,4},{6,7},{7,6},{8,9},{9,8},{10,11... | collective-permute-start | bytes 393224 | tf_op jit(solution)/shard_map/ppermute | solution.py:377
  48.7 1.9 %collective-permute-start.18 = (bf16[256,256]{1,0:T(8,128)(2,1)S(1)}, bf16[256,256]{1,0:T(8,128)(2,1)S(1)}, u32[]{:S(2)}, u32[]{:S(2)}) collective-permute-start(bf16[256,256]{1,0:T(8,128)(2,1)S(1)} %shard_map.231.refs_3_), channel_id=1, source_target_pairs={{0,1},{1,0},{2,3},{3,2},{4,5},{5,4},{6,7},{7,6},{8,9},{9,8},{10,11... | collective-permute-start | bytes 393224 | tf_op jit(solution)/shard_map/ppermute | solution.py:377
  50.0 1.3 %collective-permute-start.17 = (bf16[256,256]{1,0:T(8,128)(2,1)S(1)}, bf16[256,256]{1,0:T(8,128)(2,1)S(1)}, u32[]{:S(2)}, u32[]{:S(2)}) collective-permute-start(bf16[256,256]{1,0:T(8,128)(2,1)S(1)} %collective-permute-done.13.refs_2_), channel_id=1, source_target_pairs={{0,1},{1,0},{2,3},{3,2},{4,5},{5,4},{6,7},{7,6},{8,9},{9,8},{10,11... | collective-permute-start | bytes 393224 | tf_op jit(solution)/shard_map/ppermute | solution.py:377
  50.1 1.5 %collective-permute-start.16 = (bf16[256,256]{1,0:T(8,128)(2,1)S(1)}, bf16[256,256]{1,0:T(8,128)(2,1)S(1)}, u32[]{:S(2)}, u32[]{:S(2)}) collective-permute-start(bf16[256,256]{1,0:T(8,128)(2,1)S(1)} %collective-permute-done.12.refs_1_), channel_id=1, source_target_pairs={{0,1},{1,0},{2,3},{3,2},{4,5},{5,4},{6,7},{7,6},{8,9},{9,8},{10,11... | collective-permute-start | bytes 393224 | tf_op jit(solution)/shard_map/ppermute | solution.py:377

commit v5 on v4

--- a/solution.py
+++ b/solution.py
@@ -88,17 +88,21 @@
     flag_ref[...] = jnp.zeros(flag_ref.shape, F32)
 
 
-def count_kernel(groups, flag_ref, perm_ref, *refs):
-    sources = refs[: len(refs) // 2]
-    count_ref = refs[len(sources)]
-    relay(sources, refs[len(sources) + 1 :])
+def count_kernel(groups, flag_ref, perm_ref, local_ref, far_ref, *refs):
+    sources = refs[: len(refs) // 2 - 1]
+    count_ref, scale_ref = refs[len(sources) : len(sources) + 2]
+    relay(sources, refs[len(sources) + 2 :])
     rows = perm_ref.shape[1]
     target = lax.broadcasted_iota(jnp.int32, (rows, rows), 0)
+    count_ref[:, :rows] = jnp.ones((rows, rows), F32)
     for g, members in enumerate(groups):
         total = 0.0
         for m in members:
             total = total + jnp.where(target == perm_ref[m : m + 1, :], 1.0, 0.0)
-        count_ref[:, g * rows : (g + 1) * rows] = total.T
+        count_ref[:, (g + 1) * rows : (g + 2) * rows] = total.T
+    near = lax.broadcasted_iota(jnp.int32, (1, scale_ref.shape[1]), 1) < rows
+    for h in range(local_ref.shape[0]):
+        scale_ref[h : h + 1, :] = jnp.where(near, local_ref[h], far_ref[h])
 
 
 def sort_units(units_ref, keep_ref, send_ref, bits):
@@ -131,16 +135,15 @@
         gain2_ref,
         wup_ref,
         wdown_ref,
-        local_ref,
-        far_ref,
+        scale_ref,
         count_ref,
-    ) = refs[count + 1 : count + 13]
-    out_ref, keepw_ref, sendw_ref, keeps_ref, sends_ref, own_ref, mixed_ref = refs[count + 13 : count + 20]
-    slot_refs = refs[count + 20 : count + 20 + len(slots)]
-    raw_s, tanh_s, weight_s, dscore_s, wide_s, square_s = refs[count + 20 + len(slots) :]
+    ) = refs[count + 1 : count + 12]
+    out_ref, keepw_ref, sendw_ref, keeps_ref, sends_ref, own_ref, mixed_ref = refs[count + 12 : count + 19]
+    slot_refs = refs[count + 19 : count + 19 + len(slots)]
+    raw_s, tanh_s, weight_s, dscore_s, wide_s, square_s = refs[count + 19 + len(slots) :]
 
     rows, width = out_ref.shape
-    heads = local_ref.shape[0]
+    heads = raw_s.shape[0] // rows
     head_dim = width // heads
     scale = 1.0 / float(head_dim) ** 0.5
     bits = device_bits()
@@ -160,19 +163,13 @@
     query_stack = stack_heads(queries, head_masks)
     raw_s[...] = dot_rhs_t(query_stack, key_all) * scale
 
-    far_counts = count_ref[...]
-
+    counts = count_ref[...]
     for h in range(heads):
         block = pl.ds(h * rows, rows)
-        tl = jnp.tanh(raw_s[block, :rows] * (local_ref[h] / SCORE_CAP))
-        tf = jnp.tanh(raw_s[block, rows:] * (far_ref[h] / SCORE_CAP))
-        el = jnp.exp(SCORE_CAP * tl)
-        ef = jnp.exp(SCORE_CAP * tf) * far_counts
-        inv = 1.0 / (jnp.sum(el, axis=1, keepdims=True) + jnp.sum(ef, axis=1, keepdims=True))
-        tanh_s[block, :rows] = tl
-        tanh_s[block, rows:] = tf
-        weight_s[block, :rows] = (el * inv).astype(BF16)
-        weight_s[block, rows:] = (ef * inv).astype(BF16)
+        tangent = jnp.tanh(raw_s[block, :] * (scale_ref[h : h + 1, :] * (1.0 / SCORE_CAP)))
+        tanh_s[block, :] = tangent
+        powers = jnp.exp(SCORE_CAP * tangent) * counts
+        weight_s[block, :] = (powers * (1.0 / jnp.sum(powers, axis=1, keepdims=True))).astype(BF16)
 
     attended32 = collapse(dot(weight_s[...], value_all), head_masks)
     attended = attended32.astype(BF16)
@@ -213,8 +210,7 @@
         terms = jnp.sum(sloped * raw_s[block, :], axis=0, keepdims=True)
         local_terms.append(jnp.sum(terms[:, :rows], axis=1, keepdims=True))
         far_terms.append(jnp.sum(terms[:, rows:], axis=1, keepdims=True))
-        dscore_s[block, :rows] = (sloped[:, :rows] * (local_ref[h] * scale)).astype(BF16)
-        dscore_s[block, rows:] = (sloped[:, rows:] * (far_ref[h] * scale)).astype(BF16)
+        dscore_s[block, :] = (sloped * (scale_ref[h : h + 1, :] * scale)).astype(BF16)
 
     grad_query = collapse(dot(dscore_s[...], key_all), head_masks).astype(BF16)
     grad_key = dot_lhs_t(dscore_s[...], query_stack).astype(BF16)
@@ -430,12 +426,16 @@
         flag_kernel, flag, cost_estimate=pl.CostEstimate(flops=10**10, bytes_accessed=1, transcendentals=0)
     )
     passed = (feats, upstream, gain1, gain2)
-    counts, feats_near, up_near, gain1_near, gain2_near = call(
+    counts, scales, feats_near, up_near, gain1_near, gain2_near = call(
         functools.partial(count_kernel, groups),
-        (struct((rows, tall), F32),) + tuple(struct(x.shape, x.dtype) for x in passed),
+        (struct((rows, tall + rows), F32), struct((8, tall + rows), F32))
+        + tuple(struct(x.shape, x.dtype) for x in passed),
         begun,
         partners,
+        local_gain,
+        expander_gain,
         *passed,
+        in_specs=[VM, VM, SM, SM] + [VM] * len(passed),
         cost_estimate=pl.CostEstimate(flops=10**10, bytes_accessed=1, transcendentals=0),
     )
     out_rows, keep_wide, send_wide, keep_square, send_square, own, grad_mixed, *slot_rows = call(
@@ -461,10 +461,8 @@
         gain2_near,
         w_up,
         w_down,
-        local_gain,
-        expander_gain,
+        scales,
         counts,
-        in_specs=[VM] * (count + 10) + [SM, SM, VM],
         scratch_shapes=[
             pltpu.VMEM((stacked, tall + rows), F32),
             pltpu.VMEM((stacked, tall + rows), F32),

time: 53.2 us -> 51.9 us (0.976)
  local copies, waits for them, and re-layouts: 1.34 us -> 0.72 us
  waiting for transfers between devices: 24.2 us -> 23.6 us
    unnamed x26, local copies, waits for them, and re-layouts: 1.34 us -> 0.72 us
    ppermute x3, waiting for transfers between devices: 2.09 us -> 1.5 us  [swapped(): lax.ppermute(x, 'dom', [(i, i ^ 1 << bit) for i in range(lax.axis_size('d...]
  transfers between devices with their start and end apart: 19 -> 19, of which waited for: 13 -> 12; matrix products, arithmetic and copies ran while one was open for 0% -> 0% of each run, Pallas kernels for 2% -> 3%
where the time goes in v5:
time: 51.9 us; the launch traced here: 51.7 us
  waiting for transfers between devices  23.6 us (45%)
  starting transfers between devices  19.4 us (37%)
  Pallas kernels  7.17 us (14%)
  between operations  0.88 us (2%)
  local copies, waits for them, and re-layouts  0.72 us (1%)
    ppermute x16, waiting for transfers between devices, flipped(): return lax.ppermute(x, AXES, pairs)  22.1 us
    ppermute x16, starting transfers between devices, flipped(): return lax.ppermute(x, AXES, pairs)  12.2 us
    ppermute x3, starting transfers between devices, swapped(): lax.ppermute(x, 'dom', [(i, i ^ 1 << bit) for i in range(lax.axis_size('d...  7.2 us
    pallas_call x12, Pallas kernels, call(): pl.pallas_call(kernel, out_shape=outs, in_specs=in_specs or [VM] * len(ar...  5.71 us
    ppermute x3, waiting for transfers between devices, swapped(): lax.ppermute(x, 'dom', [(i, i ^ 1 << bit) for i in range(lax.axis_size('d...  1.5 us
    pallas_call x1, Pallas kernels, local(): pl.pallas_call(spread_kernel, out_shape=(full,) * 4 + (struct((width, 2 *...  1.46 us
  transfers between devices with their start and end apart: 19, of which 12 were waited for; matrix products, arithmetic and copies ran while one was open for 0% of the time, Pallas kernels for 3%

profile of v5, /device:TPU:0, one launch (start us, length us, event | category | flops | bytes accessed | tf_op | source)
XLA Modules:
  0.0 51.7 jit_solution(12746112113238719232)
XLA Ops:
  0.7 4.1 %collective-permute-start.2 = (bf16[128,256]{1,0:T(8,128)(2,1)}, bf16[128,256]{1,0:T(8,128)(2,1)S(1)}, u32[]{:S(2)}, u32[]{:S(2)}) collective-permute-start(bf16[128,256]{1,0:T(8,128)(2,1)} %bitcast.10), channel_id=1, source_target_pairs={{0,16},{4,20},{8,24},{12,28},{16,0},{20,4},{24,8},{28,12},{1,17},{... | collective-permute-start | bytes 196616 | tf_op jit(solution)/shard_map/ppermute | solution.py:406
  4.8 1.6 %collective-permute-start.1 = (bf16[128,256]{1,0:T(8,128)(2,1)}, bf16[128,256]{1,0:T(8,128)(2,1)S(1)}, u32[]{:S(2)}, u32[]{:S(2)}) collective-permute-start(bf16[128,256]{1,0:T(8,128)(2,1)} %bitcast.11), channel_id=1, source_target_pairs={{0,8},{4,12},{8,0},{12,4},{16,24},{20,28},{24,16},{28,20},{1,9},{5... | collective-permute-start | bytes 196616 | tf_op jit(solution)/shard_map/ppermute | solution.py:406
  6.3 1.5 %collective-permute-start = (bf16[128,256]{1,0:T(8,128)(2,1)}, bf16[128,256]{1,0:T(8,128)(2,1)S(1)}, u32[]{:S(2)}, u32[]{:S(2)}) collective-permute-start(bf16[128,256]{1,0:T(8,128)(2,1)} %bitcast.12), channel_id=1, source_target_pairs={{0,4},{4,0},{8,12},{12,8},{16,20},{20,16},{24,28},{28,24},{1,5},{5... | collective-permute-start | bytes 196616 | tf_op jit(solution)/shard_map/ppermute | solution.py:406
  7.9 0.0 copy-start.9
  7.9 0.0 copy-start.11
  7.9 0.6 %copy-done.10 = f32[256]{0:T(256)S(1)} copy-done((f32[256]{0:T(256)S(1)}, f32[256]{0:T(256)}, u32[]{:S(2)}) %copy-start.10) | copy-done | bytes 1048
  8.5 0.0 copy-done.8
  8.6 0.0 copy-done.9
  8.6 0.0 copy-start.3
  8.6 0.0 copy-start.4
  8.6 0.0 copy-start.5
  8.6 0.7 %shard_map.221 = (f32[128,512]{1,0:T(8,128)S(1)}, f32[8,512]{1,0:T(8,128)S(1)}, bf16[128,256]{1,0:T(8,128)(2,1)S(1)}, bf16[128,256]{1,0:T(8,128)(2,1)S(1)}, f32[1,256]{1,0:T(1,128)S(1)}, /*index=5*/f32[1,256]{1,0:T(1,128)S(1)}) custom-call(f32[8,128]{1,0:T(8,128)S(1)} %shard_map.220.flag_ref, s32[4,128]{1,0:T(4,128)S(1)} %bitcast.14, f32[4]{0:T(128)S(1)} %copy-done.11, ...), custom_call_target="tpu_custom_call" | custom-call | flops 10000000000 | bytes 1 | tf_op jit(solution)/shard_map/pallas_call | solution.py:360
  9.3 0.0 collective-permute-done.1.refs_2_
  9.3 1.5 %collective-permute-done.refs_1_ = bf16[128,256]{1,0:T(8,128)(2,1)S(1)} collective-permute-done((bf16[128,256]{1,0:T(8,128)(2,1)}, bf16[128,256]{1,0:T(8,128)(2,1)S(1)}, u32[]{:S(2)}, u32[]{:S(2)}) %collective-permute-start) | collective-permute-done | bytes 65568 | tf_op jit(solution)/shard_map/ppermute | solution.py:406
  10.9 3.8 %shard_map.222 = (bf16[128,256]{1,0:T(8,128)(2,1)S(1)}, bf16[512,256]{1,0:T(8,128)(2,1)S(1)}, bf16[512,256]{1,0:T(8,128)(2,1)S(1)}, bf16[512,256]{1,0:T(8,128)(2...) custom-call(bf16[128,256]{1,0:T(8,128)(2,1)S(1)} %get-tuple-element., ...), custom_call_target="tpu_custom_call" | custom-call | tf_op jit(solution)/shard_map/pallas_call | solution.py:360
  14.7 0.1 collective-permute-start.4
  14.8 0.5 collective-permute-start.3
  15.3 1.4 %collective-permute-done.3.recvw_ref = bf16[512,256]{1,0:T(8,128)(2,1)S(1)} collective-permute-done((bf16[512,256]{1,0:T(8,128)(2,1)S(1)}, bf16[512,256]{1,0:T(8,128)(2,1)S(1)}, u32[]{:S(2)}, u32[]{:S(2)}) %collective-permute-start.3) | collective-permute-done | bytes 262176 | tf_op jit(solution)/shard_map/ppermute | solution.py:373
  16.7 0.1 shard_map.223
  16.8 1.6 %collective-permute-start.6 = (bf16[400,256]{1,0:T(8,128)(2,1)S(1)}, bf16[400,256]{1,0:T(8,128)(2,1)S(1)}, u32[]{:S(2)}, u32[]{:S(2)}) collective-permute-start(bf16[400,256]{1,0:T(8,128)(2,1)S(1)} %get-tuple-element.63), channel_id=1, source_target_pairs={{0,4},{1,5},{2,6},{3,7},{4,0},{5,1},{6,2},{7,3},{8,12},{9,13},{10,... | collective-permute-start | bytes 614408 | tf_op jit(solution)/shard_map/ppermute | solution.py:373
  18.4 1.5 %collective-permute-start.5 = (bf16[272,256]{1,0:T(8,128)(2,1)S(1)}, bf16[272,256]{1,0:T(8,128)(2,1)S(1)}, u32[]{:S(2)}, u32[]{:S(2)}) collective-permute-start(bf16[272,256]{1,0:T(8,128)(2,1)S(1)} %get-tuple-element.62), channel_id=1, source_target_pairs={{0,2},{1,3},{2,0},{3,1},{4,6},{5,7},{6,4},{7,5},{8,10},{9,11},{10,... | collective-permute-start | bytes 417800 | tf_op jit(solution)/shard_map/ppermute | solution.py:373
  19.9 0.5 collective-permute-start.7
  20.4 4.6 %collective-permute-done.5.one_ref = bf16[272,256]{1,0:T(8,128)(2,1)S(1)} collective-permute-done((bf16[272,256]{1,0:T(8,128)(2,1)S(1)}, bf16[272,256]{1,0:T(8,128)(2,1)S(1)}, u32[]{:S(2)}, u32[]{:S(2)}) %collective-permute-start.5) | collective-permute-done | bytes 139296 | tf_op jit(solution)/shard_map/ppermute | solution.py:373
  25.0 1.9 %collective-permute-done.7.three_ref = bf16[272,256]{1,0:T(8,128)(2,1)S(1)} collective-permute-done((bf16[272,256]{1,0:T(8,128)(2,1)S(1)}, bf16[272,256]{1,0:T(8,128)(2,1)S(1)}, u32[]{:S(2)}, u32[]{:S(2)}) %collective-permute-start.7) | collective-permute-done | bytes 139296 | tf_op jit(solution)/shard_map/ppermute | solution.py:373
  26.9 0.1 collective-permute-done.6.two_ref.refs_6_
  27.0 0.1 shard_map.224
  27.1 0.5 %collective-permute-start.9 = (bf16[256,256]{1,0:T(8,128)(2,1)S(1)}, bf16[256,256]{1,0:T(8,128)(2,1)S(1)}, u32[]{:S(2)}, u32[]{:S(2)}) collective-permute-start(bf16[256,256]{1,0:T(8,128)(2,1)S(1)} %get-tuple-element.67.own_ref), channel_id=1, source_target_pairs={{0,8},{1,17},{2,10},{3,19},{4,12},{5,21},{6,14},{7,23},{8,0},{9,25... | collective-permute-start | bytes 393224 | tf_op jit(solution)/shard_map/ppermute | solution.py:373
  27.6 1.3 %collective-permute-start.8 = (bf16[144,256]{1,0:T(8,128)(2,1)S(1)}, bf16[144,256]{1,0:T(8,128)(2,1)S(1)}, u32[]{:S(2)}, u32[]{:S(2)}) collective-permute-start(bf16[144,256]{1,0:T(8,128)(2,1)S(1)} %get-tuple-element.66.refs_1_.own_ref), channel_id=1, source_target_pairs={{0,16},{1,9},{2,18},{3,11},{4,20},{5,13},{6,22},{7,15},{8,24},{9,1... | collective-permute-start | bytes 221192 | tf_op jit(solution)/shard_map/ppermute | solution.py:373
  28.9 5.3 %collective-permute-done.9.recv_ref.refs_7_ = bf16[256,256]{1,0:T(8,128)(2,1)S(1)} collective-permute-done((bf16[256,256]{1,0:T(8,128)(2,1)S(1)}, bf16[256,256]{1,0:T(8,128)(2,1)S(1)}, u32[]{:S(2)}, u32[]{:S(2)}) %collective-permute-start.9) | collective-permute-done | bytes 131104 | tf_op jit(solution)/shard_map/ppermute | solution.py:373
  34.2 0.1 collective-permute-start.11
  34.3 0.0 collective-permute-done.8.recv_ref
  34.3 2.1 %collective-permute-start.10 = (bf16[144,256]{1,0:T(8,128)(2,1)S(1)}, bf16[144,256]{1,0:T(8,128)(2,1)S(1)}, u32[]{:S(2)}, u32[]{:S(2)}) collective-permute-start(bf16[144,256]{1,0:T(8,128)(2,1)S(1)} %shard_map.226.refs_0_.own_ref), channel_id=1, source_target_pairs={{0,8},{1,17},{2,10},{3,19},{4,12},{5,21},{6,14},{7,23},{8,0},{9,25... | collective-permute-start | bytes 221192 | tf_op jit(solution)/shard_map/ppermute | solution.py:373
  36.4 4.9 %collective-permute-done.11.recv_ref.refs_8_ = bf16[256,256]{1,0:T(8,128)(2,1)S(1)} collective-permute-done((bf16[256,256]{1,0:T(8,128)(2,1)S(1)}, bf16[256,256]{1,0:T(8,128)(2,1)S(1)}, u32[]{:S(2)}, u32[]{:S(2)}) %collective-permute-start.11) | collective-permute-done | bytes 131104 | tf_op jit(solution)/shard_map/ppermute | solution.py:373
  41.4 1.9 %collective-permute-start.14 = (bf16[256,256]{1,0:T(8,128)(2,1)S(1)}, bf16[256,256]{1,0:T(8,128)(2,1)S(1)}, u32[]{:S(2)}, u32[]{:S(2)}) collective-permute-start(bf16[256,256]{1,0:T(8,128)(2,1)S(1)} %shard_map.230.refs_0_), channel_id=1, source_target_pairs={{0,6},{1,7},{2,4},{3,5},{4,2},{5,3},{6,0},{7,1},{8,14},{9,15},{10,... | collective-permute-start | bytes 393224 | tf_op jit(solution)/shard_map/ppermute | solution.py:373
  43.3 0.5 collective-permute-start.13
  43.8 1.1 %collective-permute-start.12 = (bf16[256,256]{1,0:T(8,128)(2,1)S(1)}, bf16[256,256]{1,0:T(8,128)(2,1)S(1)}, u32[]{:S(2)}, u32[]{:S(2)}) collective-permute-start(bf16[256,256]{1,0:T(8,128)(2,1)S(1)} %shard_map.230.refs_0_), channel_id=1, source_target_pairs={{0,2},{1,3},{2,0},{3,1},{4,6},{5,7},{6,4},{7,5},{8,10},{9,11},{10,... | collective-permute-start | bytes 393224 | tf_op jit(solution)/shard_map/ppermute | solution.py:373
  44.9 0.0 collective-permute-start.15
  44.9 0.9 %shard_map.229 = (bf16[128,256]{1,0:T(8,128)(2,1)}, bf16[128,256]{1,0:T(8,128)(2,1)}, f32[1,256]{1,0:T(1,128)}, f32[1,256]{1,0:T(1,128)}, f32[4]{0:T(128)}, /*index=5*/f32[4]{0:T(128)}, f32[8,128]{1,0:T(8,128)S(1)}) custom-call(bf16[128,256]{1,0:T(8,128)(2,1)S(1)} %get-tuple-element.47.refs_0_, bf16[128,256]{1,0:T(8,128)(2,1)S(1)} %get-tuple-element.53.refs_1_, ...), custom_call_target="tpu_custom_call" | custom-call | tf_op jit(solution)/shard_map/pallas_call | solution.py:360
  45.8 1.5 %collective-permute-done.14.source_ref = bf16[256,256]{1,0:T(8,128)(2,1)S(1)} collective-permute-done((bf16[256,256]{1,0:T(8,128)(2,1)S(1)}, bf16[256,256]{1,0:T(8,128)(2,1)S(1)}, u32[]{:S(2)}, u32[]{:S(2)}) %collective-permute-start.14) | collective-permute-done | bytes 131104 | tf_op jit(solution)/shard_map/ppermute | solution.py:373
  47.4 0.1 collective-permute-start.18
  47.5 1.3 %collective-permute-done.13.refs_2_ = bf16[256,256]{1,0:T(8,128)(2,1)S(1)} collective-permute-done((bf16[256,256]{1,0:T(8,128)(2,1)S(1)}, bf16[256,256]{1,0:T(8,128)(2,1)S(1)}, u32[]{:S(2)}, u32[]{:S(2)}) %collective-permute-start.13) | collective-permute-done | bytes 131104 | tf_op jit(solution)/shard_map/ppermute | solution.py:373
  48.7 0.0 collective-permute-start.17
  48.7 0.1 collective-permute-done.12.refs_1_
  48.8 0.4 collective-permute-start.16
  49.2 0.0 collective-permute-done.15.refs_4_
  49.2 0.8 %collective-permute-done.17.refs_6_ = bf16[256,256]{1,0:T(8,128)(2,1)S(1)} collective-permute-done((bf16[256,256]{1,0:T(8,128)(2,1)S(1)}, bf16[256,256]{1,0:T(8,128)(2,1)S(1)}, u32[]{:S(2)}, u32[]{:S(2)}) %collective-permute-start.17) | collective-permute-done | bytes 131104 | tf_op jit(solution)/shard_map/ppermute | solution.py:373
  50.1 0.2 collective-permute-done.16.refs_5_
  50.3 1.5 %shard_map.232 = (f32[256,256]{1,0:T(8,128)}, f32[256,256]{1,0:T(8,128)}, f32[256,256]{1,0:T(8,128)}, f32[256,256]{1,0:T(8,128)}, f32[256,512]{1,0:T(8,128)}, /*index=5*/f32[512,256]{1,0:T(8,128)}) custom-call(bf16[256,256]{1,0:T(8,128)(2,1)S(1)} %shard_map.230.refs_0_, bf16[256,256]{1,0:T(8,128)(2,1)S(1)} %collective-permute-done.12.refs_1_, ...), custom_call_target="tpu_custom_call" | custom-call | tf_op jit(solution)/shard_map/pallas_call | solution.py:554
  (29 shorter events, 0.2 us)
Async XLA Ops:
  0.6 7.3 %copy-start.6 = (bf16[1,128,256]{2,1,0:T(8,128)(2,1)S(1)}, bf16[1,128,256]{2,1,0:T(8,128)(2,1)}, u32[]{:S(2)}) copy-start(bf16[1,128,256]{2,1,0:T(8,128)(2,1)} %param.16) | copy-start | bytes 196612
  0.7 7.3 %copy-start.7 = (bf16[1,128,256]{2,1,0:T(8,128)(2,1)S(1)}, bf16[1,128,256]{2,1,0:T(8,128)(2,1)}, u32[]{:S(2)}) copy-start(bf16[1,128,256]{2,1,0:T(8,128)(2,1)} %param.15) | copy-start | bytes 196612
  0.7 8.6 %collective-permute-start.2 = (bf16[128,256]{1,0:T(8,128)(2,1)}, bf16[128,256]{1,0:T(8,128)(2,1)S(1)}, u32[]{:S(2)}, u32[]{:S(2)}) collective-permute-start(bf16[128,256]{1,0:T(8,128)(2,1)} %bitcast.10), channel_id=1, source_target_pairs={{0,16},{4,20},{8,24},{12,28},{16,0},{20,4},{24,8},{28,12},{1,17},{... | collective-permute-start | bytes 196616 | tf_op jit(solution)/shard_map/ppermute | solution.py:406
  4.8 4.5 %collective-permute-start.1 = (bf16[128,256]{1,0:T(8,128)(2,1)}, bf16[128,256]{1,0:T(8,128)(2,1)S(1)}, u32[]{:S(2)}, u32[]{:S(2)}) collective-permute-start(bf16[128,256]{1,0:T(8,128)(2,1)} %bitcast.11), channel_id=1, source_target_pairs={{0,8},{4,12},{8,0},{12,4},{16,24},{20,28},{24,16},{28,20},{1,9},{5... | collective-permute-start | bytes 196616 | tf_op jit(solution)/shard_map/ppermute | solution.py:406
  6.3 4.5 %collective-permute-start = (bf16[128,256]{1,0:T(8,128)(2,1)}, bf16[128,256]{1,0:T(8,128)(2,1)S(1)}, u32[]{:S(2)}, u32[]{:S(2)}) collective-permute-start(bf16[128,256]{1,0:T(8,128)(2,1)} %bitcast.12), channel_id=1, source_target_pairs={{0,4},{4,0},{8,12},{12,8},{16,20},{20,16},{24,28},{28,24},{1,5},{5... | collective-permute-start | bytes 196616 | tf_op jit(solution)/shard_map/ppermute | solution.py:406
  7.9 0.7 %copy-start.10 = (f32[256]{0:T(256)S(1)}, f32[256]{0:T(256)}, u32[]{:S(2)}) copy-start(f32[256]{0:T(256)} %param.22) | copy-start | bytes 3076
  7.9 0.7 %copy-start.12 = (f32[4]{0:T(128)S(1)}, f32[4]{0:T(128)}, u32[]{:S(2)}) copy-start(f32[4]{0:T(128)} %far_ref.1) | copy-start | bytes 52
  7.9 0.7 %copy-start.8 = (s32[1,4,1,128]{3,2,1,0:T(1,128)S(1)}, s32[1,4,1,128]{3,2,1,0:T(1,128)}, u32[]{:S(2)}) copy-start(s32[1,4,1,128]{3,2,1,0:T(1,128)} %param.27) | copy-start | bytes 6148
  7.9 0.7 %copy-start.9 = (f32[256]{0:T(256)S(1)}, f32[256]{0:T(256)}, u32[]{:S(2)}) copy-start(f32[256]{0:T(256)} %param.17) | copy-start | bytes 3076
  7.9 0.7 %copy-start.11 = (f32[4]{0:T(128)S(1)}, f32[4]{0:T(128)}, u32[]{:S(2)}) copy-start(f32[4]{0:T(128)} %local_ref.1) | copy-start | bytes 52
  8.6 2.2 %copy-start = (bf16[256,512]{1,0:T(8,128)(2,1)S(1)}, bf16[256,512]{1,0:T(8,128)(2,1)}, u32[]{:S(2)}) copy-start(bf16[256,512]{1,0:T(8,128)(2,1)} %refs_11_.1) | copy-start | bytes 786436
  8.6 2.2 %copy-start.1 = (bf16[512,256]{1,0:T(8,128)(2,1)S(1)}, bf16[512,256]{1,0:T(8,128)(2,1)}, u32[]{:S(2)}) copy-start(bf16[512,256]{1,0:T(8,128)(2,1)} %refs_12_.1) | copy-start | bytes 786436
  8.6 2.2 %copy-start.2 = (bf16[256,256]{1,0:T(8,128)(2,1)S(1)}, bf16[256,256]{1,0:T(8,128)(2,1)}, u32[]{:S(2)}) copy-start(bf16[256,256]{1,0:T(8,128)(2,1)} %refs_6_.1) | copy-start | bytes 393220
  8.6 2.2 %copy-start.3 = (bf16[256,256]{1,0:T(8,128)(2,1)S(1)}, bf16[256,256]{1,0:T(8,128)(2,1)}, u32[]{:S(2)}) copy-start(bf16[256,256]{1,0:T(8,128)(2,1)} %refs_7_.1) | copy-start | bytes 393220
  8.6 2.2 %copy-start.4 = (bf16[256,256]{1,0:T(8,128)(2,1)S(1)}, bf16[256,256]{1,0:T(8,128)(2,1)}, u32[]{:S(2)}) copy-start(bf16[256,256]{1,0:T(8,128)(2,1)} %refs_8_.1) | copy-start | bytes 393220
  8.6 2.2 %copy-start.5 = (bf16[256,256]{1,0:T(8,128)(2,1)S(1)}, bf16[256,256]{1,0:T(8,128)(2,1)}, u32[]{:S(2)}) copy-start(bf16[256,256]{1,0:T(8,128)(2,1)} %refs_9_.1) | copy-start | bytes 393220
  14.7 2.0 %collective-permute-start.4 = (bf16[528,256]{1,0:T(8,128)(2,1)S(1)}, bf16[528,256]{1,0:T(8,128)(2,1)S(1)}, u32[]{:S(2)}, u32[]{:S(2)}) collective-permute-start(bf16[528,256]{1,0:T(8,128)(2,1)S(1)} %get-tuple-element.59.sents_ref), channel_id=1, source_target_pairs={{0,1},{1,0},{2,3},{3,2},{4,5},{5,4},{6,7},{7,6},{8,9},{9,8},{10,11... | collective-permute-start | bytes 811016 | tf_op jit(solution)/shard_map/ppermute | solution.py:373
  14.8 1.9 %collective-permute-start.3 = (bf16[512,256]{1,0:T(8,128)(2,1)S(1)}, bf16[512,256]{1,0:T(8,128)(2,1)S(1)}, u32[]{:S(2)}, u32[]{:S(2)}) collective-permute-start(bf16[512,256]{1,0:T(8,128)(2,1)S(1)} %get-tuple-element.57), channel_id=1, source_target_pairs={{0,1},{1,0},{2,3},{3,2},{4,5},{5,4},{6,7},{7,6},{8,9},{9,8},{10,11... | collective-permute-start | bytes 786440 | tf_op jit(solution)/shard_map/ppermute | solution.py:373
  16.8 10.2 %collective-permute-start.6 = (bf16[400,256]{1,0:T(8,128)(2,1)S(1)}, bf16[400,256]{1,0:T(8,128)(2,1)S(1)}, u32[]{:S(2)}, u32[]{:S(2)}) collective-permute-start(bf16[400,256]{1,0:T(8,128)(2,1)S(1)} %get-tuple-element.63), channel_id=1, source_target_pairs={{0,4},{1,5},{2,6},{3,7},{4,0},{5,1},{6,2},{7,3},{8,12},{9,13},{10,... | collective-permute-start | bytes 614408 | tf_op jit(solution)/shard_map/ppermute | solution.py:373
  18.4 6.6 %collective-permute-start.5 = (bf16[272,256]{1,0:T(8,128)(2,1)S(1)}, bf16[272,256]{1,0:T(8,128)(2,1)S(1)}, u32[]{:S(2)}, u32[]{:S(2)}) collective-permute-start(bf16[272,256]{1,0:T(8,128)(2,1)S(1)} %get-tuple-element.62), channel_id=1, source_target_pairs={{0,2},{1,3},{2,0},{3,1},{4,6},{5,7},{6,4},{7,5},{8,10},{9,11},{10,... | collective-permute-start | bytes 417800 | tf_op jit(solution)/shard_map/ppermute | solution.py:373
  19.9 7.0 %collective-permute-start.7 = (bf16[272,256]{1,0:T(8,128)(2,1)S(1)}, bf16[272,256]{1,0:T(8,128)(2,1)S(1)}, u32[]{:S(2)}, u32[]{:S(2)}) collective-permute-start(bf16[272,256]{1,0:T(8,128)(2,1)S(1)} %get-tuple-element.64), channel_id=1, source_target_pairs={{0,6},{1,7},{2,4},{3,5},{4,2},{5,3},{6,0},{7,1},{8,14},{9,15},{10,... | collective-permute-start | bytes 417800 | tf_op jit(solution)/shard_map/ppermute | solution.py:373
  27.1 7.1 %collective-permute-start.9 = (bf16[256,256]{1,0:T(8,128)(2,1)S(1)}, bf16[256,256]{1,0:T(8,128)(2,1)S(1)}, u32[]{:S(2)}, u32[]{:S(2)}) collective-permute-start(bf16[256,256]{1,0:T(8,128)(2,1)S(1)} %get-tuple-element.67.own_ref), channel_id=1, source_target_pairs={{0,8},{1,17},{2,10},{3,19},{4,12},{5,21},{6,14},{7,23},{8,0},{9,25... | collective-permute-start | bytes 393224 | tf_op jit(solution)/shard_map/ppermute | solution.py:373
  27.6 6.7 %collective-permute-start.8 = (bf16[144,256]{1,0:T(8,128)(2,1)S(1)}, bf16[144,256]{1,0:T(8,128)(2,1)S(1)}, u32[]{:S(2)}, u32[]{:S(2)}) collective-permute-start(bf16[144,256]{1,0:T(8,128)(2,1)S(1)} %get-tuple-element.66.refs_1_.own_ref), channel_id=1, source_target_pairs={{0,16},{1,9},{2,18},{3,11},{4,20},{5,13},{6,22},{7,15},{8,24},{9,1... | collective-permute-start | bytes 221192 | tf_op jit(solution)/shard_map/ppermute | solution.py:373
  34.2 7.1 %collective-permute-start.11 = (bf16[256,256]{1,0:T(8,128)(2,1)S(1)}, bf16[256,256]{1,0:T(8,128)(2,1)S(1)}, u32[]{:S(2)}, u32[]{:S(2)}) collective-permute-start(bf16[256,256]{1,0:T(8,128)(2,1)S(1)} %shard_map.225.refs_0_.own_ref), channel_id=1, source_target_pairs={{0,16},{1,9},{2,18},{3,11},{4,20},{5,13},{6,22},{7,15},{8,24},{9,1... | collective-permute-start | bytes 393224 | tf_op jit(solution)/shard_map/ppermute | solution.py:373
  34.3 7.0 %collective-permute-start.10 = (bf16[144,256]{1,0:T(8,128)(2,1)S(1)}, bf16[144,256]{1,0:T(8,128)(2,1)S(1)}, u32[]{:S(2)}, u32[]{:S(2)}) collective-permute-start(bf16[144,256]{1,0:T(8,128)(2,1)S(1)} %shard_map.226.refs_0_.own_ref), channel_id=1, source_target_pairs={{0,8},{1,17},{2,10},{3,19},{4,12},{5,21},{6,14},{7,23},{8,0},{9,25... | collective-permute-start | bytes 221192 | tf_op jit(solution)/shard_map/ppermute | solution.py:373
  41.4 6.0 %collective-permute-start.14 = (bf16[256,256]{1,0:T(8,128)(2,1)S(1)}, bf16[256,256]{1,0:T(8,128)(2,1)S(1)}, u32[]{:S(2)}, u32[]{:S(2)}) collective-permute-start(bf16[256,256]{1,0:T(8,128)(2,1)S(1)} %shard_map.230.refs_0_), channel_id=1, source_target_pairs={{0,6},{1,7},{2,4},{3,5},{4,2},{5,3},{6,0},{7,1},{8,14},{9,15},{10,... | collective-permute-start | bytes 393224 | tf_op jit(solution)/shard_map/ppermute | solution.py:373
  43.3 5.4 %collective-permute-start.13 = (bf16[256,256]{1,0:T(8,128)(2,1)S(1)}, bf16[256,256]{1,0:T(8,128)(2,1)S(1)}, u32[]{:S(2)}, u32[]{:S(2)}) collective-permute-start(bf16[256,256]{1,0:T(8,128)(2,1)S(1)} %shard_map.230.refs_0_), channel_id=1, source_target_pairs={{0,4},{1,5},{2,6},{3,7},{4,0},{5,1},{6,2},{7,3},{8,12},{9,13},{10,... | collective-permute-start | bytes 393224 | tf_op jit(solution)/shard_map/ppermute | solution.py:373
  43.8 5.0 %collective-permute-start.12 = (bf16[256,256]{1,0:T(8,128)(2,1)S(1)}, bf16[256,256]{1,0:T(8,128)(2,1)S(1)}, u32[]{:S(2)}, u32[]{:S(2)}) collective-permute-start(bf16[256,256]{1,0:T(8,128)(2,1)S(1)} %shard_map.230.refs_0_), channel_id=1, source_target_pairs={{0,2},{1,3},{2,0},{3,1},{4,6},{5,7},{6,4},{7,5},{8,10},{9,11},{10,... | collective-permute-start | bytes 393224 | tf_op jit(solution)/shard_map/ppermute | solution.py:373
  44.9 4.3 %collective-permute-start.15 = (bf16[256,256]{1,0:T(8,128)(2,1)S(1)}, bf16[256,256]{1,0:T(8,128)(2,1)S(1)}, u32[]{:S(2)}, u32[]{:S(2)}) collective-permute-start(bf16[256,256]{1,0:T(8,128)(2,1)S(1)} %shard_map.230.refs_0_), channel_id=1, source_target_pairs={{0,1},{1,0},{2,3},{3,2},{4,5},{5,4},{6,7},{7,6},{8,9},{9,8},{10,11... | collective-permute-start | bytes 393224 | tf_op jit(solution)/shard_map/ppermute | solution.py:373
  47.4 1.9 %collective-permute-start.18 = (bf16[256,256]{1,0:T(8,128)(2,1)S(1)}, bf16[256,256]{1,0:T(8,128)(2,1)S(1)}, u32[]{:S(2)}, u32[]{:S(2)}) collective-permute-start(bf16[256,256]{1,0:T(8,128)(2,1)S(1)} %shard_map.231.refs_3_), channel_id=1, source_target_pairs={{0,1},{1,0},{2,3},{3,2},{4,5},{5,4},{6,7},{7,6},{8,9},{9,8},{10,11... | collective-permute-start | bytes 393224 | tf_op jit(solution)/shard_map/ppermute | solution.py:373
  48.7 1.3 %collective-permute-start.17 = (bf16[256,256]{1,0:T(8,128)(2,1)S(1)}, bf16[256,256]{1,0:T(8,128)(2,1)S(1)}, u32[]{:S(2)}, u32[]{:S(2)}) collective-permute-start(bf16[256,256]{1,0:T(8,128)(2,1)S(1)} %collective-permute-done.13.refs_2_), channel_id=1, source_target_pairs={{0,1},{1,0},{2,3},{3,2},{4,5},{5,4},{6,7},{7,6},{8,9},{9,8},{10,11... | collective-permute-start | bytes 393224 | tf_op jit(solution)/shard_map/ppermute | solution.py:373
  48.8 1.4 %collective-permute-start.16 = (bf16[256,256]{1,0:T(8,128)(2,1)S(1)}, bf16[256,256]{1,0:T(8,128)(2,1)S(1)}, u32[]{:S(2)}, u32[]{:S(2)}) collective-permute-start(bf16[256,256]{1,0:T(8,128)(2,1)S(1)} %collective-permute-done.12.refs_1_), channel_id=1, source_target_pairs={{0,1},{1,0},{2,3},{3,2},{4,5},{5,4},{6,7},{7,6},{8,9},{9,8},{10,11... | collective-permute-start | bytes 393224 | tf_op jit(solution)/shard_map/ppermute | solution.py:373

commit v6 on v5

--- a/solution.py
+++ b/solution.py
@@ -241,9 +241,10 @@
     sort_units(square_s, keeps_ref, sends_ref, bits)
 
 
-def pair_kernel(slots, keepw_ref, recvw_ref, keeps_ref, sents_ref, recvs_ref, *refs):
+def pair_kernel(slots, apart, keepw_ref, recvw_ref, keeps_ref, sents_ref, recvs_ref, *refs):
     slot_refs = refs[: sum(slots)]
-    out_refs = refs[sum(slots) :]
+    out_refs = refs[sum(slots) + apart :]
+    relay(refs[sum(slots) : sum(slots) + apart], out_refs[4:])
     rows = keepw_ref.shape[0] // 4
     wide = (keepw_ref[...].astype(F32) + recvw_ref[...].astype(F32)).astype(BF16)
     square = (keeps_ref[...].astype(F32) + recvs_ref[: 4 * rows, :].astype(F32)).astype(BF16)
@@ -410,9 +411,9 @@
     flat = {1 << (b + rep_bits): k for k, b in enumerate(bits)}
     quad_slots = [flat.get(bit) for bit in (2, 4, 6)]
     orders = (list(zip(high_bits, high_bits[::-1])), list(zip(high_bits[::-1], high_bits)))
-    high_slots = [(flat.get(even), flat.get(odd)) for even, odd in orders[0]]
+    apart = [k for bit, k in flat.items() if bit > 4]
     slots = [(k, k) for k in quad_slots if k is not None]
-    slots += [pair for pair in high_slots if pair != (None, None)]
+    slots += [(k, k) for k in apart]
 
     others = [swapped(feats, b) for b in bits]
     count = len(bits)
@@ -474,7 +475,7 @@
     )
     slot_rows = iter(slot_rows)
     slot_quad = [None if k is None else next(slot_rows) for k in quad_slots]
-    slot_high = [None if pair == (None, None) else next(slot_rows) for pair in high_slots]
+    slot_apart = list(slot_rows)
 
     def present(*items):
         return [x for x in items if x is not None]
@@ -486,40 +487,39 @@
     recv_wide = flipped(send_wide, 1, 1)
     recv_square = flipped(send_square, 1, 1)
     data = 2 * half + SMALL
+    block = struct((rows, width), BF16)
     own_quad, *send_quad = call(
-        functools.partial(pair_kernel, [x is not None for x in slot_quad]),
-        (struct((data, width), BF16),) + tuple(sized(data, x) for x in slot_quad),
+        functools.partial(pair_kernel, [x is not None for x in slot_quad], len(apart)),
+        (struct((data, width), BF16),) + tuple(sized(data, x) for x in slot_quad) + (block,) * len(apart),
         keep_wide,
         recv_wide,
         keep_square,
         send_square,
         recv_square,
         *present(*slot_quad),
-    )
+        *slot_apart,
+    )
+    send_quad, send_apart = send_quad[:3], send_quad[3:]
     recv_quad = [flipped(x, bit, bit) for x, bit in zip(send_quad, (2, 4, 6))]
     returned = [x for x, slot in zip(recv_quad, slot_quad) if slot is not None]
-    starts = [data] * len(returned)
+    starts = [data] * len(returned) + [0] * len(apart)
+    recv_apart = [swapped(x, bits[k]) for x, k in zip(send_apart, apart)]
+    returned += recv_apart
     wide, square = call(
-        functools.partial(quad_kernel, slot_high[0] is not None),
-        (sized(half, slot_high[0]), struct((half + SMALL, width), BF16)),
+        functools.partial(quad_kernel, False),
+        (struct((half, width), BF16), struct((half + SMALL, width), BF16)),
         own_quad,
         *recv_quad,
-        *present(slot_high[0]),
+        *recv_apart,
     )
     for k in range(len(high_bits)):
         recv_wide = flipped(wide, *orders[0][k])
         recv_square = flipped(square, *orders[1][k])
-        if slot_high[k] is not None:
-            returned.append(recv_wide)
-            starts.append(half)
-        slot = slot_high[k + 1] if k + 1 < len(high_bits) else None
-        extra = present(slot)
         wide = call(
-            functools.partial(double_kernel, half, False, slot is not None),
-            sized(half, slot),
+            functools.partial(double_kernel, half, False, False),
+            struct((half, width), BF16),
             wide,
             recv_wide,
-            *extra,
             square,
         )
         square = call(
@@ -529,9 +529,6 @@
             recv_square,
             wide,
         )
-    base = call(join_kernel, struct((2 * half, width), BF16), wide, square)
-    near = [base] + [flipped(base, bit, bit) for bit in (2, 4, 6)]
-    over = [flipped(x, 1, 1) for x in near]
     block = struct((rows, width), BF16)
     one = struct((1, width), F32)
     full = struct((width, width), F32)

time: 51.9 us -> 49.6 us (0.956)
  waiting for transfers between devices: 23.6 us -> 19.6 us
  starting transfers between devices: 19.4 us -> 21.1 us
    ppermute x16, waiting for transfers between devices: 22.1 us -> 14.2 us  [flipped(): return lax.ppermute(x, AXES, pairs)]
    ppermute x3 -> x5, waiting for transfers between devices: 1.5 us -> 5.34 us  [swapped(): lax.ppermute(x, 'dom', [(i, i ^ 1 << bit) for i in range(lax.axis_size('d...]
    ppermute x3 -> x5, starting transfers between devices: 7.2 us -> 8.97 us  [swapped(): lax.ppermute(x, 'dom', [(i, i ^ 1 << bit) for i in range(lax.axis_size('d...]
  transfers between devices with their start and end apart: 19 -> 21, of which waited for: 12 -> 14; matrix products, arithmetic and copies ran while one was open for 0% -> 0% of each run, Pallas kernels for 3% -> 3%
where the time goes in v6:
time: 49.6 us; the launch traced here: 49.4 us
  starting transfers between devices  21.1 us (43%)
  waiting for transfers between devices  19.6 us (40%)
  Pallas kernels  7.18 us (14%)
  between operations  0.87 us (2%)
  local copies, waits for them, and re-layouts  0.72 us (1%)
    ppermute x16, waiting for transfers between devices, flipped(): return lax.ppermute(x, AXES, pairs)  14.2 us
    ppermute x16, starting transfers between devices, flipped(): return lax.ppermute(x, AXES, pairs)  12.1 us
    ppermute x5, starting transfers between devices, swapped(): lax.ppermute(x, 'dom', [(i, i ^ 1 << bit) for i in range(lax.axis_size('d...  8.97 us
    pallas_call x12, Pallas kernels, call(): pl.pallas_call(kernel, out_shape=outs, in_specs=in_specs or [VM] * len(ar...  5.72 us
    ppermute x5, waiting for transfers between devices, swapped(): lax.ppermute(x, 'dom', [(i, i ^ 1 << bit) for i in range(lax.axis_size('d...  5.34 us
    pallas_call x1, Pallas kernels, local(): pl.pallas_call(spread_kernel, out_shape=(full,) * 4 + (struct((width, 2 *...  1.46 us
  transfers between devices with their start and end apart: 21, of which 14 were waited for; matrix products, arithmetic and copies ran while one was open for 0% of the time, Pallas kernels for 3%

profile of v6, /device:TPU:0, one launch (start us, length us, event | category | flops | bytes accessed | tf_op | source)
XLA Modules:
  0.0 49.4 jit_solution(17974995508070580171)
XLA Ops:
  0.7 4.1 %collective-permute-start.2 = (bf16[128,256]{1,0:T(8,128)(2,1)}, bf16[128,256]{1,0:T(8,128)(2,1)S(1)}, u32[]{:S(2)}, u32[]{:S(2)}) collective-permute-start(bf16[128,256]{1,0:T(8,128)(2,1)} %bitcast.10), channel_id=1, source_target_pairs={{0,16},{4,20},{8,24},{12,28},{16,0},{20,4},{24,8},{28,12},{1,17},{... | collective-permute-start | bytes 196616 | tf_op jit(solution)/shard_map/ppermute | solution.py:407
  4.8 1.6 %collective-permute-start.1 = (bf16[128,256]{1,0:T(8,128)(2,1)}, bf16[128,256]{1,0:T(8,128)(2,1)S(1)}, u32[]{:S(2)}, u32[]{:S(2)}) collective-permute-start(bf16[128,256]{1,0:T(8,128)(2,1)} %bitcast.11), channel_id=1, source_target_pairs={{0,8},{4,12},{8,0},{12,4},{16,24},{20,28},{24,16},{28,20},{1,9},{5... | collective-permute-start | bytes 196616 | tf_op jit(solution)/shard_map/ppermute | solution.py:407
  6.3 1.5 %collective-permute-start = (bf16[128,256]{1,0:T(8,128)(2,1)}, bf16[128,256]{1,0:T(8,128)(2,1)S(1)}, u32[]{:S(2)}, u32[]{:S(2)}) collective-permute-start(bf16[128,256]{1,0:T(8,128)(2,1)} %bitcast.12), channel_id=1, source_target_pairs={{0,4},{4,0},{8,12},{12,8},{16,20},{20,16},{24,28},{28,24},{1,5},{5... | collective-permute-start | bytes 196616 | tf_op jit(solution)/shard_map/ppermute | solution.py:407
  7.9 0.0 copy-start.9
  7.9 0.0 copy-start.11
  7.9 0.6 %copy-done.10 = f32[256]{0:T(256)S(1)} copy-done((f32[256]{0:T(256)S(1)}, f32[256]{0:T(256)}, u32[]{:S(2)}) %copy-start.10) | copy-done | bytes 1048
  8.5 0.0 copy-done.8
  8.6 0.0 copy-done.9
  8.6 0.0 copy-start.3
  8.6 0.0 copy-start.4
  8.6 0.0 copy-start.5
  8.6 0.7 %shard_map.221 = (f32[128,512]{1,0:T(8,128)S(1)}, f32[8,512]{1,0:T(8,128)S(1)}, bf16[128,256]{1,0:T(8,128)(2,1)S(1)}, bf16[128,256]{1,0:T(8,128)(2,1)S(1)}, f32[1,256]{1,0:T(1,128)S(1)}, /*index=5*/f32[1,256]{1,0:T(1,128)S(1)}) custom-call(f32[8,128]{1,0:T(8,128)S(1)} %shard_map.220.flag_ref, s32[4,128]{1,0:T(4,128)S(1)} %bitcast.14, f32[4]{0:T(128)S(1)} %copy-done.11, ...), custom_call_target="tpu_custom_call" | custom-call | flops 10000000000 | bytes 1 | tf_op jit(solution)/shard_map/pallas_call | solution.py:361
  9.3 0.0 collective-permute-done.2.refs_3_
  9.3 1.5 %collective-permute-done.refs_1_ = bf16[128,256]{1,0:T(8,128)(2,1)S(1)} collective-permute-done((bf16[128,256]{1,0:T(8,128)(2,1)}, bf16[128,256]{1,0:T(8,128)(2,1)S(1)}, u32[]{:S(2)}, u32[]{:S(2)}) %collective-permute-start) | collective-permute-done | bytes 65568 | tf_op jit(solution)/shard_map/ppermute | solution.py:407
  10.9 3.8 %shard_map.222 = (bf16[128,256]{1,0:T(8,128)(2,1)S(1)}, bf16[512,256]{1,0:T(8,128)(2,1)S(1)}, bf16[512,256]{1,0:T(8,128)(2,1)S(1)}, bf16[512,256]{1,0:T(8,128)(2...) custom-call(bf16[128,256]{1,0:T(8,128)(2,1)S(1)} %get-tuple-element., ...), custom_call_target="tpu_custom_call" | custom-call | tf_op jit(solution)/shard_map/pallas_call | solution.py:361
  14.7 0.1 collective-permute-start.4
  14.8 0.5 %collective-permute-start.3 = (bf16[512,256]{1,0:T(8,128)(2,1)S(1)}, bf16[512,256]{1,0:T(8,128)(2,1)S(1)}, u32[]{:S(2)}, u32[]{:S(2)}) collective-permute-start(bf16[512,256]{1,0:T(8,128)(2,1)S(1)} %get-tuple-element.59), channel_id=1, source_target_pairs={{0,1},{1,0},{2,3},{3,2},{4,5},{5,4},{6,7},{7,6},{8,9},{9,8},{10,11... | collective-permute-start | bytes 786440 | tf_op jit(solution)/shard_map/ppermute | solution.py:374
  15.3 1.4 %collective-permute-done.3.recvw_ref = bf16[512,256]{1,0:T(8,128)(2,1)S(1)} collective-permute-done((bf16[512,256]{1,0:T(8,128)(2,1)S(1)}, bf16[512,256]{1,0:T(8,128)(2,1)S(1)}, u32[]{:S(2)}, u32[]{:S(2)}) %collective-permute-start.3) | collective-permute-done | bytes 262176 | tf_op jit(solution)/shard_map/ppermute | solution.py:374
  16.7 0.1 shard_map.223
  16.8 1.6 %collective-permute-start.6 = (bf16[400,256]{1,0:T(8,128)(2,1)S(1)}, bf16[400,256]{1,0:T(8,128)(2,1)S(1)}, u32[]{:S(2)}, u32[]{:S(2)}) collective-permute-start(bf16[400,256]{1,0:T(8,128)(2,1)S(1)} %get-tuple-element.67), channel_id=1, source_target_pairs={{0,4},{1,5},{2,6},{3,7},{4,0},{5,1},{6,2},{7,3},{8,12},{9,13},{10,... | collective-permute-start | bytes 614408 | tf_op jit(solution)/shard_map/ppermute | solution.py:374
  18.4 1.5 %collective-permute-start.5 = (bf16[272,256]{1,0:T(8,128)(2,1)S(1)}, bf16[272,256]{1,0:T(8,128)(2,1)S(1)}, u32[]{:S(2)}, u32[]{:S(2)}) collective-permute-start(bf16[272,256]{1,0:T(8,128)(2,1)S(1)} %get-tuple-element.66), channel_id=1, source_target_pairs={{0,2},{1,3},{2,0},{3,1},{4,6},{5,7},{6,4},{7,5},{8,10},{9,11},{10,... | collective-permute-start | bytes 417800 | tf_op jit(solution)/shard_map/ppermute | solution.py:374
  19.9 0.5 collective-permute-start.7
  20.4 0.4 collective-permute-start.8
  20.8 1.3 %collective-permute-start.9 = (bf16[128,256]{1,0:T(8,128)(2,1)S(1)}, bf16[128,256]{1,0:T(8,128)(2,1)S(1)}, u32[]{:S(2)}, u32[]{:S(2)}) collective-permute-start(bf16[128,256]{1,0:T(8,128)(2,1)S(1)} %get-tuple-element.70), channel_id=1, source_target_pairs={{0,16},{4,20},{8,24},{12,28},{16,0},{20,4},{24,8},{28,12},{1,17},{... | collective-permute-start | bytes 196616 | tf_op jit(solution)/shard_map/ppermute | solution.py:407
  22.2 2.6 %collective-permute-done.8.refs_0_.refs_7_ = bf16[128,256]{1,0:T(8,128)(2,1)S(1)} collective-permute-done((bf16[128,256]{1,0:T(8,128)(2,1)S(1)}, bf16[128,256]{1,0:T(8,128)(2,1)S(1)}, u32[]{:S(2)}, u32[]{:S(2)}) %collective-permute-start.8) | collective-permute-done | bytes 65568 | tf_op jit(solution)/shard_map/ppermute | solution.py:407
  24.8 1.3 %collective-permute-done.9.refs_1_.refs_8_ = bf16[128,256]{1,0:T(8,128)(2,1)S(1)} collective-permute-done((bf16[128,256]{1,0:T(8,128)(2,1)S(1)}, bf16[128,256]{1,0:T(8,128)(2,1)S(1)}, u32[]{:S(2)}, u32[]{:S(2)}) %collective-permute-start.9) | collective-permute-done | bytes 65568 | tf_op jit(solution)/shard_map/ppermute | solution.py:407
  26.0 0.9 %collective-permute-done.7.three_ref = bf16[272,256]{1,0:T(8,128)(2,1)S(1)} collective-permute-done((bf16[272,256]{1,0:T(8,128)(2,1)S(1)}, bf16[272,256]{1,0:T(8,128)(2,1)S(1)}, u32[]{:S(2)}, u32[]{:S(2)}) %collective-permute-start.7) | collective-permute-done | bytes 139296 | tf_op jit(solution)/shard_map/ppermute | solution.py:374
  26.9 0.1 collective-permute-done.6.two_ref.refs_6_
  27.0 0.1 shard_map.224
  27.1 0.4 collective-permute-start.10
  27.5 1.4 %collective-permute-start.11 = (bf16[128,256]{1,0:T(8,128)(2,1)S(1)}, bf16[128,256]{1,0:T(8,128)(2,1)S(1)}, u32[]{:S(2)}, u32[]{:S(2)}) collective-permute-start(bf16[128,256]{1,0:T(8,128)(2,1)S(1)} %get-tuple-element.72.own_ref), channel_id=1, source_target_pairs={{0,8},{1,17},{2,10},{3,19},{4,12},{5,21},{6,14},{7,23},{8,0},{9,25... | collective-permute-start | bytes 196616 | tf_op jit(solution)/shard_map/ppermute | solution.py:374
  28.9 2.8 %collective-permute-done.11.recv_ref = bf16[128,256]{1,0:T(8,128)(2,1)S(1)} collective-permute-done((bf16[128,256]{1,0:T(8,128)(2,1)S(1)}, bf16[128,256]{1,0:T(8,128)(2,1)S(1)}, u32[]{:S(2)}, u32[]{:S(2)}) %collective-permute-start.11) | collective-permute-done | bytes 65568 | tf_op jit(solution)/shard_map/ppermute | solution.py:374
  31.8 1.4 %collective-permute-done.10.recv_ref = bf16[144,256]{1,0:T(8,128)(2,1)S(1)} collective-permute-done((bf16[144,256]{1,0:T(8,128)(2,1)S(1)}, bf16[144,256]{1,0:T(8,128)(2,1)S(1)}, u32[]{:S(2)}, u32[]{:S(2)}) %collective-permute-start.10) | collective-permute-done | bytes 73760 | tf_op jit(solution)/shard_map/ppermute | solution.py:374
  33.3 0.1 collective-permute-start.12
  33.3 2.4 %collective-permute-start.13 = (bf16[128,256]{1,0:T(8,128)(2,1)S(1)}, bf16[128,256]{1,0:T(8,128)(2,1)S(1)}, u32[]{:S(2)}, u32[]{:S(2)}) collective-permute-start(bf16[128,256]{1,0:T(8,128)(2,1)S(1)} %shard_map.225.refs_0_.own_ref), channel_id=1, source_target_pairs={{0,16},{1,9},{2,18},{3,11},{4,20},{5,13},{6,22},{7,15},{8,24},{9,1... | collective-permute-start | bytes 196616 | tf_op jit(solution)/shard_map/ppermute | solution.py:374
  35.8 2.8 %collective-permute-done.13.recv_ref = bf16[128,256]{1,0:T(8,128)(2,1)S(1)} collective-permute-done((bf16[128,256]{1,0:T(8,128)(2,1)S(1)}, bf16[128,256]{1,0:T(8,128)(2,1)S(1)}, u32[]{:S(2)}, u32[]{:S(2)}) %collective-permute-start.13) | collective-permute-done | bytes 65568 | tf_op jit(solution)/shard_map/ppermute | solution.py:374
  38.7 2.5 %collective-permute-start.16 = (bf16[256,256]{1,0:T(8,128)(2,1)S(1)}, bf16[256,256]{1,0:T(8,128)(2,1)S(1)}, u32[]{:S(2)}, u32[]{:S(2)}) collective-permute-start(bf16[256,256]{1,0:T(8,128)(2,1)S(1)} %shard_map.230.refs_0_), channel_id=1, source_target_pairs={{0,6},{1,7},{2,4},{3,5},{4,2},{5,3},{6,0},{7,1},{8,14},{9,15},{10,... | collective-permute-start | bytes 393224 | tf_op jit(solution)/shard_map/ppermute | solution.py:374
  41.1 0.5 %collective-permute-start.15 = (bf16[256,256]{1,0:T(8,128)(2,1)S(1)}, bf16[256,256]{1,0:T(8,128)(2,1)S(1)}, u32[]{:S(2)}, u32[]{:S(2)}) collective-permute-start(bf16[256,256]{1,0:T(8,128)(2,1)S(1)} %shard_map.230.refs_0_), channel_id=1, source_target_pairs={{0,4},{1,5},{2,6},{3,7},{4,0},{5,1},{6,2},{7,3},{8,12},{9,13},{10,... | collective-permute-start | bytes 393224 | tf_op jit(solution)/shard_map/ppermute | solution.py:374
  41.6 0.6 %collective-permute-start.14 = (bf16[256,256]{1,0:T(8,128)(2,1)S(1)}, bf16[256,256]{1,0:T(8,128)(2,1)S(1)}, u32[]{:S(2)}, u32[]{:S(2)}) collective-permute-start(bf16[256,256]{1,0:T(8,128)(2,1)S(1)} %shard_map.230.refs_0_), channel_id=1, source_target_pairs={{0,2},{1,3},{2,0},{3,1},{4,6},{5,7},{6,4},{7,5},{8,10},{9,11},{10,... | collective-permute-start | bytes 393224 | tf_op jit(solution)/shard_map/ppermute | solution.py:374
  42.2 0.9 %shard_map.229 = (bf16[128,256]{1,0:T(8,128)(2,1)}, bf16[128,256]{1,0:T(8,128)(2,1)}, f32[1,256]{1,0:T(1,128)}, f32[1,256]{1,0:T(1,128)}, f32[4]{0:T(128)}, /*index=5*/f32[4]{0:T(128)}, f32[8,128]{1,0:T(8,128)S(1)}) custom-call(bf16[128,256]{1,0:T(8,128)(2,1)S(1)} %get-tuple-element.49.refs_0_, bf16[128,256]{1,0:T(8,128)(2,1)S(1)} %get-tuple-element.55.refs_1_, ...), custom_call_target="tpu_custom_call" | custom-call | tf_op jit(solution)/shard_map/pallas_call | solution.py:361
  43.1 1.5 %collective-permute-done.16.source_ref = bf16[256,256]{1,0:T(8,128)(2,1)S(1)} collective-permute-done((bf16[256,256]{1,0:T(8,128)(2,1)S(1)}, bf16[256,256]{1,0:T(8,128)(2,1)S(1)}, u32[]{:S(2)}, u32[]{:S(2)}) %collective-permute-start.16) | collective-permute-done | bytes 131104 | tf_op jit(solution)/shard_map/ppermute | solution.py:374
  44.6 0.1 collective-permute-start.20
  44.7 1.4 %collective-permute-done.15.refs_2_ = bf16[256,256]{1,0:T(8,128)(2,1)S(1)} collective-permute-done((bf16[256,256]{1,0:T(8,128)(2,1)S(1)}, bf16[256,256]{1,0:T(8,128)(2,1)S(1)}, u32[]{:S(2)}, u32[]{:S(2)}) %collective-permute-start.15) | collective-permute-done | bytes 131104 | tf_op jit(solution)/shard_map/ppermute | solution.py:374
  46.1 0.5 %collective-permute-done.14.refs_1_ = bf16[256,256]{1,0:T(8,128)(2,1)S(1)} collective-permute-done((bf16[256,256]{1,0:T(8,128)(2,1)S(1)}, bf16[256,256]{1,0:T(8,128)(2,1)S(1)}, u32[]{:S(2)}, u32[]{:S(2)}) %collective-permute-start.14) | collective-permute-done | bytes 131104 | tf_op jit(solution)/shard_map/ppermute | solution.py:374
  46.6 0.0 collective-permute-start.18
  46.6 0.8 %collective-permute-done.19.refs_6_ = bf16[256,256]{1,0:T(8,128)(2,1)S(1)} collective-permute-done((bf16[256,256]{1,0:T(8,128)(2,1)S(1)}, bf16[256,256]{1,0:T(8,128)(2,1)S(1)}, u32[]{:S(2)}, u32[]{:S(2)}) %collective-permute-start.19) | collective-permute-done | bytes 131104 | tf_op jit(solution)/shard_map/ppermute | solution.py:374
  47.4 0.5 %collective-permute-done.18.refs_5_ = bf16[256,256]{1,0:T(8,128)(2,1)S(1)} collective-permute-done((bf16[256,256]{1,0:T(8,128)(2,1)S(1)}, bf16[256,256]{1,0:T(8,128)(2,1)S(1)}, u32[]{:S(2)}, u32[]{:S(2)}) %collective-permute-start.18) | collective-permute-done | bytes 131104 | tf_op jit(solution)/shard_map/ppermute | solution.py:374
  47.9 1.5 %shard_map.232 = (f32[256,256]{1,0:T(8,128)}, f32[256,256]{1,0:T(8,128)}, f32[256,256]{1,0:T(8,128)}, f32[256,256]{1,0:T(8,128)}, f32[256,512]{1,0:T(8,128)}, /*index=5*/f32[512,256]{1,0:T(8,128)}) custom-call(bf16[256,256]{1,0:T(8,128)(2,1)S(1)} %shard_map.230.refs_0_, bf16[256,256]{1,0:T(8,128)(2,1)S(1)} %collective-permute-done.14.refs_1_, ...), custom_call_target="tpu_custom_call" | custom-call | tf_op jit(solution)/shard_map/pallas_call | solution.py:551
  (33 shorter events, 0.2 us)
Async XLA Ops:
  0.6 7.3 %copy-start.6 = (bf16[1,128,256]{2,1,0:T(8,128)(2,1)S(1)}, bf16[1,128,256]{2,1,0:T(8,128)(2,1)}, u32[]{:S(2)}) copy-start(bf16[1,128,256]{2,1,0:T(8,128)(2,1)} %param.16) | copy-start | bytes 196612
  0.7 7.3 %copy-start.7 = (bf16[1,128,256]{2,1,0:T(8,128)(2,1)S(1)}, bf16[1,128,256]{2,1,0:T(8,128)(2,1)}, u32[]{:S(2)}) copy-start(bf16[1,128,256]{2,1,0:T(8,128)(2,1)} %param.15) | copy-start | bytes 196612
  0.7 8.6 %collective-permute-start.2 = (bf16[128,256]{1,0:T(8,128)(2,1)}, bf16[128,256]{1,0:T(8,128)(2,1)S(1)}, u32[]{:S(2)}, u32[]{:S(2)}) collective-permute-start(bf16[128,256]{1,0:T(8,128)(2,1)} %bitcast.10), channel_id=1, source_target_pairs={{0,16},{4,20},{8,24},{12,28},{16,0},{20,4},{24,8},{28,12},{1,17},{... | collective-permute-start | bytes 196616 | tf_op jit(solution)/shard_map/ppermute | solution.py:407
  4.8 4.5 %collective-permute-start.1 = (bf16[128,256]{1,0:T(8,128)(2,1)}, bf16[128,256]{1,0:T(8,128)(2,1)S(1)}, u32[]{:S(2)}, u32[]{:S(2)}) collective-permute-start(bf16[128,256]{1,0:T(8,128)(2,1)} %bitcast.11), channel_id=1, source_target_pairs={{0,8},{4,12},{8,0},{12,4},{16,24},{20,28},{24,16},{28,20},{1,9},{5... | collective-permute-start | bytes 196616 | tf_op jit(solution)/shard_map/ppermute | solution.py:407
  6.3 4.5 %collective-permute-start = (bf16[128,256]{1,0:T(8,128)(2,1)}, bf16[128,256]{1,0:T(8,128)(2,1)S(1)}, u32[]{:S(2)}, u32[]{:S(2)}) collective-permute-start(bf16[128,256]{1,0:T(8,128)(2,1)} %bitcast.12), channel_id=1, source_target_pairs={{0,4},{4,0},{8,12},{12,8},{16,20},{20,16},{24,28},{28,24},{1,5},{5... | collective-permute-start | bytes 196616 | tf_op jit(solution)/shard_map/ppermute | solution.py:407
  7.9 0.7 %copy-start.10 = (f32[256]{0:T(256)S(1)}, f32[256]{0:T(256)}, u32[]{:S(2)}) copy-start(f32[256]{0:T(256)} %param.22) | copy-start | bytes 3076
  7.9 0.7 %copy-start.12 = (f32[4]{0:T(128)S(1)}, f32[4]{0:T(128)}, u32[]{:S(2)}) copy-start(f32[4]{0:T(128)} %far_ref.1) | copy-start | bytes 52
  7.9 0.7 %copy-start.8 = (s32[1,4,1,128]{3,2,1,0:T(1,128)S(1)}, s32[1,4,1,128]{3,2,1,0:T(1,128)}, u32[]{:S(2)}) copy-start(s32[1,4,1,128]{3,2,1,0:T(1,128)} %param.27) | copy-start | bytes 6148
  7.9 0.7 %copy-start.9 = (f32[256]{0:T(256)S(1)}, f32[256]{0:T(256)}, u32[]{:S(2)}) copy-start(f32[256]{0:T(256)} %param.17) | copy-start | bytes 3076
  7.9 0.7 %copy-start.11 = (f32[4]{0:T(128)S(1)}, f32[4]{0:T(128)}, u32[]{:S(2)}) copy-start(f32[4]{0:T(128)} %local_ref.1) | copy-start | bytes 52
  8.6 2.2 %copy-start = (bf16[256,512]{1,0:T(8,128)(2,1)S(1)}, bf16[256,512]{1,0:T(8,128)(2,1)}, u32[]{:S(2)}) copy-start(bf16[256,512]{1,0:T(8,128)(2,1)} %refs_11_.1) | copy-start | bytes 786436
  8.6 2.2 %copy-start.1 = (bf16[512,256]{1,0:T(8,128)(2,1)S(1)}, bf16[512,256]{1,0:T(8,128)(2,1)}, u32[]{:S(2)}) copy-start(bf16[512,256]{1,0:T(8,128)(2,1)} %refs_12_.1) | copy-start | bytes 786436
  8.6 2.2 %copy-start.2 = (bf16[256,256]{1,0:T(8,128)(2,1)S(1)}, bf16[256,256]{1,0:T(8,128)(2,1)}, u32[]{:S(2)}) copy-start(bf16[256,256]{1,0:T(8,128)(2,1)} %refs_6_.1) | copy-start | bytes 393220
  8.6 2.2 %copy-start.3 = (bf16[256,256]{1,0:T(8,128)(2,1)S(1)}, bf16[256,256]{1,0:T(8,128)(2,1)}, u32[]{:S(2)}) copy-start(bf16[256,256]{1,0:T(8,128)(2,1)} %refs_7_.1) | copy-start | bytes 393220
  8.6 2.2 %copy-start.4 = (bf16[256,256]{1,0:T(8,128)(2,1)S(1)}, bf16[256,256]{1,0:T(8,128)(2,1)}, u32[]{:S(2)}) copy-start(bf16[256,256]{1,0:T(8,128)(2,1)} %refs_8_.1) | copy-start | bytes 393220
  8.6 2.2 %copy-start.5 = (bf16[256,256]{1,0:T(8,128)(2,1)S(1)}, bf16[256,256]{1,0:T(8,128)(2,1)}, u32[]{:S(2)}) copy-start(bf16[256,256]{1,0:T(8,128)(2,1)} %refs_9_.1) | copy-start | bytes 393220
  14.7 2.0 %collective-permute-start.4 = (bf16[528,256]{1,0:T(8,128)(2,1)S(1)}, bf16[528,256]{1,0:T(8,128)(2,1)S(1)}, u32[]{:S(2)}, u32[]{:S(2)}) collective-permute-start(bf16[528,256]{1,0:T(8,128)(2,1)S(1)} %get-tuple-element.61.sents_ref), channel_id=1, source_target_pairs={{0,1},{1,0},{2,3},{3,2},{4,5},{5,4},{6,7},{7,6},{8,9},{9,8},{10,11... | collective-permute-start | bytes 811016 | tf_op jit(solution)/shard_map/ppermute | solution.py:374
  14.8 1.9 %collective-permute-start.3 = (bf16[512,256]{1,0:T(8,128)(2,1)S(1)}, bf16[512,256]{1,0:T(8,128)(2,1)S(1)}, u32[]{:S(2)}, u32[]{:S(2)}) collective-permute-start(bf16[512,256]{1,0:T(8,128)(2,1)S(1)} %get-tuple-element.59), channel_id=1, source_target_pairs={{0,1},{1,0},{2,3},{3,2},{4,5},{5,4},{6,7},{7,6},{8,9},{9,8},{10,11... | collective-permute-start | bytes 786440 | tf_op jit(solution)/shard_map/ppermute | solution.py:374
  16.8 10.2 %collective-permute-start.6 = (bf16[400,256]{1,0:T(8,128)(2,1)S(1)}, bf16[400,256]{1,0:T(8,128)(2,1)S(1)}, u32[]{:S(2)}, u32[]{:S(2)}) collective-permute-start(bf16[400,256]{1,0:T(8,128)(2,1)S(1)} %get-tuple-element.67), channel_id=1, source_target_pairs={{0,4},{1,5},{2,6},{3,7},{4,0},{5,1},{6,2},{7,3},{8,12},{9,13},{10,... | collective-permute-start | bytes 614408 | tf_op jit(solution)/shard_map/ppermute | solution.py:374
  18.4 7.6 %collective-permute-start.5 = (bf16[272,256]{1,0:T(8,128)(2,1)S(1)}, bf16[272,256]{1,0:T(8,128)(2,1)S(1)}, u32[]{:S(2)}, u32[]{:S(2)}) collective-permute-start(bf16[272,256]{1,0:T(8,128)(2,1)S(1)} %get-tuple-element.66), channel_id=1, source_target_pairs={{0,2},{1,3},{2,0},{3,1},{4,6},{5,7},{6,4},{7,5},{8,10},{9,11},{10,... | collective-permute-start | bytes 417800 | tf_op jit(solution)/shard_map/ppermute | solution.py:374
  19.9 7.0 %collective-permute-start.7 = (bf16[272,256]{1,0:T(8,128)(2,1)S(1)}, bf16[272,256]{1,0:T(8,128)(2,1)S(1)}, u32[]{:S(2)}, u32[]{:S(2)}) collective-permute-start(bf16[272,256]{1,0:T(8,128)(2,1)S(1)} %get-tuple-element.68), channel_id=1, source_target_pairs={{0,6},{1,7},{2,4},{3,5},{4,2},{5,3},{6,0},{7,1},{8,14},{9,15},{10,... | collective-permute-start | bytes 417800 | tf_op jit(solution)/shard_map/ppermute | solution.py:374
  20.4 4.4 %collective-permute-start.8 = (bf16[128,256]{1,0:T(8,128)(2,1)S(1)}, bf16[128,256]{1,0:T(8,128)(2,1)S(1)}, u32[]{:S(2)}, u32[]{:S(2)}) collective-permute-start(bf16[128,256]{1,0:T(8,128)(2,1)S(1)} %get-tuple-element.69), channel_id=1, source_target_pairs={{0,8},{4,12},{8,0},{12,4},{16,24},{20,28},{24,16},{28,20},{1,9},{5... | collective-permute-start | bytes 196616 | tf_op jit(solution)/shard_map/ppermute | solution.py:407
  20.8 5.2 %collective-permute-start.9 = (bf16[128,256]{1,0:T(8,128)(2,1)S(1)}, bf16[128,256]{1,0:T(8,128)(2,1)S(1)}, u32[]{:S(2)}, u32[]{:S(2)}) collective-permute-start(bf16[128,256]{1,0:T(8,128)(2,1)S(1)} %get-tuple-element.70), channel_id=1, source_target_pairs={{0,16},{4,20},{8,24},{12,28},{16,0},{20,4},{24,8},{28,12},{1,17},{... | collective-permute-start | bytes 196616 | tf_op jit(solution)/shard_map/ppermute | solution.py:407
  27.1 6.2 %collective-permute-start.10 = (bf16[144,256]{1,0:T(8,128)(2,1)S(1)}, bf16[144,256]{1,0:T(8,128)(2,1)S(1)}, u32[]{:S(2)}, u32[]{:S(2)}) collective-permute-start(bf16[144,256]{1,0:T(8,128)(2,1)S(1)} %get-tuple-element.71.refs_0_.own_ref), channel_id=1, source_target_pairs={{0,16},{1,9},{2,18},{3,11},{4,20},{5,13},{6,22},{7,15},{8,24},{9,1... | collective-permute-start | bytes 221192 | tf_op jit(solution)/shard_map/ppermute | solution.py:374
  27.5 4.3 %collective-permute-start.11 = (bf16[128,256]{1,0:T(8,128)(2,1)S(1)}, bf16[128,256]{1,0:T(8,128)(2,1)S(1)}, u32[]{:S(2)}, u32[]{:S(2)}) collective-permute-start(bf16[128,256]{1,0:T(8,128)(2,1)S(1)} %get-tuple-element.72.own_ref), channel_id=1, source_target_pairs={{0,8},{1,17},{2,10},{3,19},{4,12},{5,21},{6,14},{7,23},{8,0},{9,25... | collective-permute-start | bytes 196616 | tf_op jit(solution)/shard_map/ppermute | solution.py:374
  33.3 5.3 %collective-permute-start.12 = (bf16[144,256]{1,0:T(8,128)(2,1)S(1)}, bf16[144,256]{1,0:T(8,128)(2,1)S(1)}, u32[]{:S(2)}, u32[]{:S(2)}) collective-permute-start(bf16[144,256]{1,0:T(8,128)(2,1)S(1)} %shard_map.226.refs_0_.own_ref), channel_id=1, source_target_pairs={{0,8},{1,17},{2,10},{3,19},{4,12},{5,21},{6,14},{7,23},{8,0},{9,25... | collective-permute-start | bytes 221192 | tf_op jit(solution)/shard_map/ppermute | solution.py:374
  33.3 5.2 %collective-permute-start.13 = (bf16[128,256]{1,0:T(8,128)(2,1)S(1)}, bf16[128,256]{1,0:T(8,128)(2,1)S(1)}, u32[]{:S(2)}, u32[]{:S(2)}) collective-permute-start(bf16[128,256]{1,0:T(8,128)(2,1)S(1)} %shard_map.225.refs_0_.own_ref), channel_id=1, source_target_pairs={{0,16},{1,9},{2,18},{3,11},{4,20},{5,13},{6,22},{7,15},{8,24},{9,1... | collective-permute-start | bytes 196616 | tf_op jit(solution)/shard_map/ppermute | solution.py:374
  38.7 5.9 %collective-permute-start.16 = (bf16[256,256]{1,0:T(8,128)(2,1)S(1)}, bf16[256,256]{1,0:T(8,128)(2,1)S(1)}, u32[]{:S(2)}, u32[]{:S(2)}) collective-permute-start(bf16[256,256]{1,0:T(8,128)(2,1)S(1)} %shard_map.230.refs_0_), channel_id=1, source_target_pairs={{0,6},{1,7},{2,4},{3,5},{4,2},{5,3},{6,0},{7,1},{8,14},{9,15},{10,... | collective-permute-start | bytes 393224 | tf_op jit(solution)/shard_map/ppermute | solution.py:374
  41.1 5.0 %collective-permute-start.15 = (bf16[256,256]{1,0:T(8,128)(2,1)S(1)}, bf16[256,256]{1,0:T(8,128)(2,1)S(1)}, u32[]{:S(2)}, u32[]{:S(2)}) collective-permute-start(bf16[256,256]{1,0:T(8,128)(2,1)S(1)} %shard_map.230.refs_0_), channel_id=1, source_target_pairs={{0,4},{1,5},{2,6},{3,7},{4,0},{5,1},{6,2},{7,3},{8,12},{9,13},{10,... | collective-permute-start | bytes 393224 | tf_op jit(solution)/shard_map/ppermute | solution.py:374
  41.6 5.0 %collective-permute-start.14 = (bf16[256,256]{1,0:T(8,128)(2,1)S(1)}, bf16[256,256]{1,0:T(8,128)(2,1)S(1)}, u32[]{:S(2)}, u32[]{:S(2)}) collective-permute-start(bf16[256,256]{1,0:T(8,128)(2,1)S(1)} %shard_map.230.refs_0_), channel_id=1, source_target_pairs={{0,2},{1,3},{2,0},{3,1},{4,6},{5,7},{6,4},{7,5},{8,10},{9,11},{10,... | collective-permute-start | bytes 393224 | tf_op jit(solution)/shard_map/ppermute | solution.py:374
  42.2 4.4 %collective-permute-start.17 = (bf16[256,256]{1,0:T(8,128)(2,1)S(1)}, bf16[256,256]{1,0:T(8,128)(2,1)S(1)}, u32[]{:S(2)}, u32[]{:S(2)}) collective-permute-start(bf16[256,256]{1,0:T(8,128)(2,1)S(1)} %shard_map.230.refs_0_), channel_id=1, source_target_pairs={{0,1},{1,0},{2,3},{3,2},{4,5},{5,4},{6,7},{7,6},{8,9},{9,8},{10,11... | collective-permute-start | bytes 393224 | tf_op jit(solution)/shard_map/ppermute | solution.py:374
  44.6 2.0 %collective-permute-start.20 = (bf16[256,256]{1,0:T(8,128)(2,1)S(1)}, bf16[256,256]{1,0:T(8,128)(2,1)S(1)}, u32[]{:S(2)}, u32[]{:S(2)}) collective-permute-start(bf16[256,256]{1,0:T(8,128)(2,1)S(1)} %shard_map.231.refs_3_), channel_id=1, source_target_pairs={{0,1},{1,0},{2,3},{3,2},{4,5},{5,4},{6,7},{7,6},{8,9},{9,8},{10,11... | collective-permute-start | bytes 393224 | tf_op jit(solution)/shard_map/ppermute | solution.py:374
  46.1 1.3 %collective-permute-start.19 = (bf16[256,256]{1,0:T(8,128)(2,1)S(1)}, bf16[256,256]{1,0:T(8,128)(2,1)S(1)}, u32[]{:S(2)}, u32[]{:S(2)}) collective-permute-start(bf16[256,256]{1,0:T(8,128)(2,1)S(1)} %collective-permute-done.15.refs_2_), channel_id=1, source_target_pairs={{0,1},{1,0},{2,3},{3,2},{4,5},{5,4},{6,7},{7,6},{8,9},{9,8},{10,11... | collective-permute-start | bytes 393224 | tf_op jit(solution)/shard_map/ppermute | solution.py:374
  46.6 1.3 %collective-permute-start.18 = (bf16[256,256]{1,0:T(8,128)(2,1)S(1)}, bf16[256,256]{1,0:T(8,128)(2,1)S(1)}, u32[]{:S(2)}, u32[]{:S(2)}) collective-permute-start(bf16[256,256]{1,0:T(8,128)(2,1)S(1)} %collective-permute-done.14.refs_1_), channel_id=1, source_target_pairs={{0,1},{1,0},{2,3},{3,2},{4,5},{5,4},{6,7},{7,6},{8,9},{9,8},{10,11... | collective-permute-start | bytes 393224 | tf_op jit(solution)/shard_map/ppermute | solution.py:374

commit v7 on v6

--- a/solution.py
+++ b/solution.py
@@ -105,14 +105,16 @@
         scale_ref[h : h + 1, :] = jnp.where(near, local_ref[h], far_ref[h])
 
 
-def sort_units(units_ref, keep_ref, send_ref, bits):
+def unit_of(units_ref, owner, rel):
+    rows = units_ref.shape[0] // 8
+    return units_ref[pl.ds(pl.multiple_of((owner * 4 + rel) * rows, rows), rows), :]
+
+
+def sort_units(units_ref, send_ref, bits):
     core, quad = bits
     rows = units_ref.shape[0] // 8
     for r in range(4):
-        span = slice(r * rows, (r + 1) * rows)
-        for owner, out_ref in ((core, keep_ref), (1 - core, send_ref)):
-            start = pl.multiple_of((owner * 4 + (quad ^ r)) * rows, rows)
-            out_ref[span, :] = units_ref[pl.ds(start, rows), :]
+        send_ref[r * rows : (r + 1) * rows, :] = unit_of(units_ref, 1 - core, quad ^ r)
 
 
 def collapse(matrix, masks):
@@ -138,9 +140,9 @@
         scale_ref,
         count_ref,
     ) = refs[count + 1 : count + 12]
-    out_ref, keepw_ref, sendw_ref, keeps_ref, sends_ref, own_ref, mixed_ref = refs[count + 12 : count + 19]
+    out_ref, wide_s, sendw_ref, square_s, sends_ref, own_ref, mixed_ref = refs[count + 12 : count + 19]
     slot_refs = refs[count + 19 : count + 19 + len(slots)]
-    raw_s, tanh_s, weight_s, dscore_s, wide_s, square_s = refs[count + 19 + len(slots) :]
+    raw_s, tanh_s, weight_s, dscore_s = refs[count + 19 + len(slots) :]
 
     rows, width = out_ref.shape
     heads = raw_s.shape[0] // rows
@@ -236,24 +238,25 @@
         gains = jnp.where(column == heads + h, far_terms[h], gains)
     line = lax.broadcasted_iota(jnp.int32, (SMALL // 2, width), 0)
     small = jnp.where(line == 0, grad_gain1, jnp.where(line == 1, grad_gain2, jnp.where(line == 2, gains, 0.0)))
-    sends_ref[keeps_ref.shape[0] :, :] = split_parts(small)
-    sort_units(wide_s, keepw_ref, sendw_ref, bits)
-    sort_units(square_s, keeps_ref, sends_ref, bits)
+    sends_ref[sendw_ref.shape[0] :, :] = split_parts(small)
+    sort_units(wide_s, sendw_ref, bits)
+    sort_units(square_s, sends_ref, bits)
 
 
 def pair_kernel(slots, apart, keepw_ref, recvw_ref, keeps_ref, sents_ref, recvs_ref, *refs):
     slot_refs = refs[: sum(slots)]
     out_refs = refs[sum(slots) + apart :]
     relay(refs[sum(slots) : sum(slots) + apart], out_refs[4:])
-    rows = keepw_ref.shape[0] // 4
-    wide = (keepw_ref[...].astype(F32) + recvw_ref[...].astype(F32)).astype(BF16)
-    square = (keeps_ref[...].astype(F32) + recvs_ref[: 4 * rows, :].astype(F32)).astype(BF16)
+    rows = keepw_ref.shape[0] // 8
+    core, quad = device_bits()
     packed = split_parts(join_parts(sents_ref[4 * rows :, :]) + join_parts(recvs_ref[4 * rows :, :]))
     used = 0
     for r in range(4):
         span = slice(r * rows, (r + 1) * rows)
-        out_refs[r][:rows, :] = wide[span]
-        out_refs[r][rows : 2 * rows, :] = square[span]
+        wide = unit_of(keepw_ref, core, quad ^ r).astype(F32) + recvw_ref[span, :].astype(F32)
+        square = unit_of(keeps_ref, core, quad ^ r).astype(F32) + recvs_ref[span, :].astype(F32)
+        out_refs[r][:rows, :] = wide.astype(BF16)
+        out_refs[r][rows : 2 * rows, :] = square.astype(BF16)
         out_refs[r][2 * rows : 2 * rows + SMALL, :] = packed
         if r and slots[r - 1]:
             out_refs[r][2 * rows + SMALL :, :] = slot_refs[used][...]
@@ -315,36 +318,32 @@
     out_ref[...] = source_ref[...]
 
 
-def spread_kernel(*refs):
-    piece_refs = refs[:8]
-    wq_ref, wk_ref, wv_ref, wo_ref, up_ref, down_ref, pieces, chunks, sems = refs[8:]
+def spread_kernel(own, *refs):
+    piece_refs = refs[:4]
+    wq_ref, wk_ref, wv_ref, wo_ref, up_ref, down_ref, pieces, chunks, sems = refs[-9:]
     width = wq_ref.shape[0]
     half = width // 2
     core, quad = device_bits()
-    relay(piece_refs, [pieces.at[k] for k in range(8)])
-    targets = [
-        up_ref.at[:, :width],
-        up_ref.at[:, width:],
-        down_ref.at[:width, :],
-        down_ref.at[width:, :],
-        wq_ref,
-        wk_ref,
-        wv_ref,
-        wo_ref,
-    ]
-    copies = []
-    for chunk, target in enumerate(targets):
-        first = 0 if chunk < 4 else half
-        for part in range(2):
-            unit = 2 * (chunk % 4) + part
-            rel = (core ^ (unit >> 2)) * 4 + (quad ^ (unit & 3))
-            value = pieces[rel, first : first + half, :]
-            chunks[chunk, part * half : (part + 1) * half, :] = value.astype(F32)
-        copy = pltpu.make_async_copy(chunks.at[chunk], target, sems.at[chunk])
-        copy.start()
-        copies.append(copy)
-    for copy in copies:
-        copy.wait()
+    side = core if own else 1 - core
+    relay(piece_refs, [pieces.at[k] for k in range(4)])
+    low = [up_ref.at[:, :width], up_ref.at[:, width:], wq_ref, wk_ref]
+    high = [down_ref.at[:width, :], down_ref.at[width:, :], wv_ref, wo_ref]
+
+    for bit, targets in enumerate((low, high)):
+
+        @pl.when(side == bit)
+        def _():
+            copies = []
+            for slot, target in enumerate(targets):
+                first = 0 if slot < 2 else half
+                for part in range(2):
+                    value = pieces[quad ^ (2 * (slot % 2) + part), first : first + half, :]
+                    chunks[slot, part * half : (part + 1) * half, :] = value.astype(F32)
+                copy = pltpu.make_async_copy(chunks.at[slot], target, sems.at[slot])
+                copy.start()
+                copies.append(copy)
+            for copy in copies:
+                copy.wait()
 
 
 def struct(shape, dtype):
@@ -443,9 +442,9 @@
         functools.partial(layer_kernel, slots, count),
         (
             struct((rows, width), BF16),
+            struct((4 * width, width), BF16),
             struct((2 * width, width), BF16),
-            struct((2 * width, width), BF16),
-            struct((2 * width, width), BF16),
+            struct((4 * width, width), BF16),
             struct((2 * width + SMALL, width), BF16),
             struct((rows, width), F32),
             struct((rows, width), F32),
@@ -469,8 +468,6 @@
             pltpu.VMEM((stacked, tall + rows), F32),
             pltpu.VMEM((stacked, tall + rows), BF16),
             pltpu.VMEM((stacked, tall + rows), BF16),
-            pltpu.VMEM((4 * width, width), BF16),
-            pltpu.VMEM((4 * width, width), BF16),
         ],
     )
     slot_rows = iter(slot_rows)
@@ -548,18 +545,23 @@
     near = [base] + [flipped(base, bit, bit) for bit in (2, 4, 6)]
     near[3] = call(after_kernel, struct(base.shape, BF16), near[3], ended)
     over = [flipped(x, 1, 1) for x in near]
-    grad_wq, grad_wk, grad_wv, grad_wout, grad_up, grad_down = pl.pallas_call(
-        spread_kernel,
-        out_shape=(full,) * 4 + (struct((width, 2 * width), F32), struct((2 * width, width), F32)),
-        in_specs=[VM] * 8,
-        out_specs=(ANY,) * 6,
-        scratch_shapes=[
-            pltpu.VMEM((8, width, width), BF16),
-            pltpu.VMEM((8, width, width), F32),
-            pltpu.SemaphoreType.DMA((8,)),
-        ],
-        compiler_params=PARAMS,
-    )(*near, *over)
+    grads = (full,) * 4 + (struct((width, 2 * width), F32), struct((2 * width, width), F32))
+    for own in (True, False):
+        before = [] if own else grads
+        grads = pl.pallas_call(
+            functools.partial(spread_kernel, own),
+            out_shape=tuple(struct(x.shape, x.dtype) for x in grads),
+            in_specs=[VM] * 4 + [ANY] * len(before),
+            out_specs=(ANY,) * 6,
+            scratch_shapes=[
+                pltpu.VMEM((4, width, width), BF16),
+                pltpu.VMEM((4, width, width), F32),
+                pltpu.SemaphoreType.DMA((4,)),
+            ],
+            input_output_aliases={4 + k: k for k in range(len(before))},
+            compiler_params=PARAMS,
+        )(*(near if own else over), *before)
+    grad_wq, grad_wk, grad_wv, grad_wout, grad_up, grad_down = grads
     return (
         node_out[None],
         grad_feats[None],

time: 49.6 us -> 49.2 us (level)
  waiting for transfers between devices: 19.6 us -> 18.5 us
  Pallas kernels: 7.18 us -> 7.81 us
    ppermute x16, waiting for transfers between devices: 14.2 us -> 13.1 us  [flipped(): return lax.ppermute(x, AXES, pairs)]
    pallas_call x1 -> x2, Pallas kernels: 1.46 us -> 2.09 us  [local(): pl.pallas_call(functools.partial(spread_kernel, own), out_shape=tuple((st...]
  transfers between devices with their start and end apart: 21 -> 21, of which waited for: 14 -> 13; matrix products, arithmetic and copies ran while one was open for 0% -> 0% of each run, Pallas kernels for 3% -> 5%
where the time goes in v7:
time: 49.2 us; the launch traced here: 49 us
  starting transfers between devices  21.1 us (43%)
  waiting for transfers between devices  18.5 us (38%)
  Pallas kernels  7.81 us (16%)
  between operations  0.9 us (2%)
  local copies, waits for them, and re-layouts  0.72 us (1%)
    ppermute x16, waiting for transfers between devices, flipped(): return lax.ppermute(x, AXES, pairs)  13.1 us
    ppermute x16, starting transfers between devices, flipped(): return lax.ppermute(x, AXES, pairs)  12.1 us
    ppermute x5, starting transfers between devices, swapped(): lax.ppermute(x, 'dom', [(i, i ^ 1 << bit) for i in range(lax.axis_size('d...  8.97 us
    pallas_call x12, Pallas kernels, call(): pl.pallas_call(kernel, out_shape=outs, in_specs=in_specs or [VM] * len(ar...  5.72 us
    ppermute x5, waiting for transfers between devices, swapped(): lax.ppermute(x, 'dom', [(i, i ^ 1 << bit) for i in range(lax.axis_size('d...  5.34 us
    pallas_call x2, Pallas kernels, local(): pl.pallas_call(functools.partial(spread_kernel, own), out_shape=tuple((st...  2.09 us
  transfers between devices with their start and end apart: 21, of which 13 were waited for; matrix products, arithmetic and copies ran while one was open for 0% of the time, Pallas kernels for 5%

profile of v7, /device:TPU:0, one launch (start us, length us, event | category | flops | bytes accessed | tf_op | source)
XLA Modules:
  0.0 49.0 jit_solution(7252308797606527557)
XLA Ops:
  0.7 4.1 %collective-permute-start.2 = (bf16[128,256]{1,0:T(8,128)(2,1)}, bf16[128,256]{1,0:T(8,128)(2,1)S(1)}, u32[]{:S(2)}, u32[]{:S(2)}) collective-permute-start(bf16[128,256]{1,0:T(8,128)(2,1)} %bitcast.10), channel_id=1, source_target_pairs={{0,16},{4,20},{8,24},{12,28},{16,0},{20,4},{24,8},{28,12},{1,17},{... | collective-permute-start | bytes 196616 | tf_op jit(solution)/shard_map/ppermute | solution.py:406
  4.8 1.6 %collective-permute-start.1 = (bf16[128,256]{1,0:T(8,128)(2,1)}, bf16[128,256]{1,0:T(8,128)(2,1)S(1)}, u32[]{:S(2)}, u32[]{:S(2)}) collective-permute-start(bf16[128,256]{1,0:T(8,128)(2,1)} %bitcast.11), channel_id=1, source_target_pairs={{0,8},{4,12},{8,0},{12,4},{16,24},{20,28},{24,16},{28,20},{1,9},{5... | collective-permute-start | bytes 196616 | tf_op jit(solution)/shard_map/ppermute | solution.py:406
  6.3 1.5 %collective-permute-start = (bf16[128,256]{1,0:T(8,128)(2,1)}, bf16[128,256]{1,0:T(8,128)(2,1)S(1)}, u32[]{:S(2)}, u32[]{:S(2)}) collective-permute-start(bf16[128,256]{1,0:T(8,128)(2,1)} %bitcast.12), channel_id=1, source_target_pairs={{0,4},{4,0},{8,12},{12,8},{16,20},{20,16},{24,28},{28,24},{1,5},{5... | collective-permute-start | bytes 196616 | tf_op jit(solution)/shard_map/ppermute | solution.py:406
  7.9 0.0 copy-start.9
  7.9 0.0 copy-start.11
  7.9 0.6 %copy-done.10 = f32[256]{0:T(256)S(1)} copy-done((f32[256]{0:T(256)S(1)}, f32[256]{0:T(256)}, u32[]{:S(2)}) %copy-start.10) | copy-done | bytes 1048
  8.5 0.0 copy-done.8
  8.6 0.0 copy-done.9
  8.6 0.0 copy-start.3
  8.6 0.0 copy-start.4
  8.6 0.0 copy-start.5
  8.6 0.7 %shard_map.221 = (f32[128,512]{1,0:T(8,128)S(1)}, f32[8,512]{1,0:T(8,128)S(1)}, bf16[128,256]{1,0:T(8,128)(2,1)S(1)}, bf16[128,256]{1,0:T(8,128)(2,1)S(1)}, f32[1,256]{1,0:T(1,128)S(1)}, /*index=5*/f32[1,256]{1,0:T(1,128)S(1)}) custom-call(f32[8,128]{1,0:T(8,128)S(1)} %shard_map.220.flag_ref, s32[4,128]{1,0:T(4,128)S(1)} %bitcast.14, f32[4]{0:T(128)S(1)} %copy-done.11, ...), custom_call_target="tpu_custom_call" | custom-call | flops 10000000000 | bytes 1 | tf_op jit(solution)/shard_map/pallas_call | solution.py:360
  9.3 0.0 collective-permute-done.1.refs_2_
  9.3 1.5 %collective-permute-done.refs_1_ = bf16[128,256]{1,0:T(8,128)(2,1)S(1)} collective-permute-done((bf16[128,256]{1,0:T(8,128)(2,1)}, bf16[128,256]{1,0:T(8,128)(2,1)S(1)}, u32[]{:S(2)}, u32[]{:S(2)}) %collective-permute-start) | collective-permute-done | bytes 65568 | tf_op jit(solution)/shard_map/ppermute | solution.py:406
  10.9 3.8 %shard_map.222 = (bf16[128,256]{1,0:T(8,128)(2,1)S(1)}, bf16[1024,256]{1,0:T(8,128)(2,1)S(1)}, bf16[512,256]{1,0:T(8,128)(2,1)S(1)}, bf16[1024,256]{1,0:T(8,128)...) custom-call(bf16[128,256]{1,0:T(8,128)(2,1)S(1)} %get-tuple-element., ...), custom_call_target="tpu_custom_call" | custom-call | tf_op jit(solution)/shard_map/pallas_call | solution.py:360
  14.7 0.1 collective-permute-start.4
  14.8 0.5 %collective-permute-start.3 = (bf16[512,256]{1,0:T(8,128)(2,1)S(1)}, bf16[512,256]{1,0:T(8,128)(2,1)S(1)}, u32[]{:S(2)}, u32[]{:S(2)}) collective-permute-start(bf16[512,256]{1,0:T(8,128)(2,1)S(1)} %get-tuple-element.65), channel_id=1, source_target_pairs={{0,1},{1,0},{2,3},{3,2},{4,5},{5,4},{6,7},{7,6},{8,9},{9,8},{10,11... | collective-permute-start | bytes 786440 | tf_op jit(solution)/shard_map/ppermute | solution.py:373
  15.3 1.4 %collective-permute-done.3.recvw_ref = bf16[512,256]{1,0:T(8,128)(2,1)S(1)} collective-permute-done((bf16[512,256]{1,0:T(8,128)(2,1)S(1)}, bf16[512,256]{1,0:T(8,128)(2,1)S(1)}, u32[]{:S(2)}, u32[]{:S(2)}) %collective-permute-start.3) | collective-permute-done | bytes 262176 | tf_op jit(solution)/shard_map/ppermute | solution.py:373
  16.7 0.1 shard_map.223
  16.8 1.6 %collective-permute-start.6 = (bf16[400,256]{1,0:T(8,128)(2,1)S(1)}, bf16[400,256]{1,0:T(8,128)(2,1)S(1)}, u32[]{:S(2)}, u32[]{:S(2)}) collective-permute-start(bf16[400,256]{1,0:T(8,128)(2,1)S(1)} %get-tuple-element.73), channel_id=1, source_target_pairs={{0,4},{1,5},{2,6},{3,7},{4,0},{5,1},{6,2},{7,3},{8,12},{9,13},{10,... | collective-permute-start | bytes 614408 | tf_op jit(solution)/shard_map/ppermute | solution.py:373
  18.4 1.5 %collective-permute-start.5 = (bf16[272,256]{1,0:T(8,128)(2,1)S(1)}, bf16[272,256]{1,0:T(8,128)(2,1)S(1)}, u32[]{:S(2)}, u32[]{:S(2)}) collective-permute-start(bf16[272,256]{1,0:T(8,128)(2,1)S(1)} %get-tuple-element.72), channel_id=1, source_target_pairs={{0,2},{1,3},{2,0},{3,1},{4,6},{5,7},{6,4},{7,5},{8,10},{9,11},{10,... | collective-permute-start | bytes 417800 | tf_op jit(solution)/shard_map/ppermute | solution.py:373
  19.9 0.5 collective-permute-start.7
  20.4 0.4 collective-permute-start.8
  20.8 1.3 %collective-permute-start.9 = (bf16[128,256]{1,0:T(8,128)(2,1)S(1)}, bf16[128,256]{1,0:T(8,128)(2,1)S(1)}, u32[]{:S(2)}, u32[]{:S(2)}) collective-permute-start(bf16[128,256]{1,0:T(8,128)(2,1)S(1)} %get-tuple-element.76), channel_id=1, source_target_pairs={{0,16},{4,20},{8,24},{12,28},{16,0},{20,4},{24,8},{28,12},{1,17},{... | collective-permute-start | bytes 196616 | tf_op jit(solution)/shard_map/ppermute | solution.py:406
  22.2 2.6 %collective-permute-done.8.refs_0_.refs_7_ = bf16[128,256]{1,0:T(8,128)(2,1)S(1)} collective-permute-done((bf16[128,256]{1,0:T(8,128)(2,1)S(1)}, bf16[128,256]{1,0:T(8,128)(2,1)S(1)}, u32[]{:S(2)}, u32[]{:S(2)}) %collective-permute-start.8) | collective-permute-done | bytes 65568 | tf_op jit(solution)/shard_map/ppermute | solution.py:406
  24.7 1.3 %collective-permute-done.9.refs_1_.refs_8_ = bf16[128,256]{1,0:T(8,128)(2,1)S(1)} collective-permute-done((bf16[128,256]{1,0:T(8,128)(2,1)S(1)}, bf16[128,256]{1,0:T(8,128)(2,1)S(1)}, u32[]{:S(2)}, u32[]{:S(2)}) %collective-permute-start.9) | collective-permute-done | bytes 65568 | tf_op jit(solution)/shard_map/ppermute | solution.py:406
  26.0 0.9 %collective-permute-done.7.three_ref = bf16[272,256]{1,0:T(8,128)(2,1)S(1)} collective-permute-done((bf16[272,256]{1,0:T(8,128)(2,1)S(1)}, bf16[272,256]{1,0:T(8,128)(2,1)S(1)}, u32[]{:S(2)}, u32[]{:S(2)}) %collective-permute-start.7) | collective-permute-done | bytes 139296 | tf_op jit(solution)/shard_map/ppermute | solution.py:373
  26.9 0.1 collective-permute-done.6.two_ref.refs_6_
  27.0 0.1 shard_map.224
  27.1 0.4 collective-permute-start.10
  27.5 1.4 %collective-permute-start.11 = (bf16[128,256]{1,0:T(8,128)(2,1)S(1)}, bf16[128,256]{1,0:T(8,128)(2,1)S(1)}, u32[]{:S(2)}, u32[]{:S(2)}) collective-permute-start(bf16[128,256]{1,0:T(8,128)(2,1)S(1)} %get-tuple-element.78.own_ref), channel_id=1, source_target_pairs={{0,8},{1,17},{2,10},{3,19},{4,12},{5,21},{6,14},{7,23},{8,0},{9,25... | collective-permute-start | bytes 196616 | tf_op jit(solution)/shard_map/ppermute | solution.py:373
  28.9 2.8 %collective-permute-done.11.recv_ref = bf16[128,256]{1,0:T(8,128)(2,1)S(1)} collective-permute-done((bf16[128,256]{1,0:T(8,128)(2,1)S(1)}, bf16[128,256]{1,0:T(8,128)(2,1)S(1)}, u32[]{:S(2)}, u32[]{:S(2)}) %collective-permute-start.11) | collective-permute-done | bytes 65568 | tf_op jit(solution)/shard_map/ppermute | solution.py:373
  31.8 1.4 %collective-permute-done.10.recv_ref = bf16[144,256]{1,0:T(8,128)(2,1)S(1)} collective-permute-done((bf16[144,256]{1,0:T(8,128)(2,1)S(1)}, bf16[144,256]{1,0:T(8,128)(2,1)S(1)}, u32[]{:S(2)}, u32[]{:S(2)}) %collective-permute-start.10) | collective-permute-done | bytes 73760 | tf_op jit(solution)/shard_map/ppermute | solution.py:373
  33.3 0.1 collective-permute-start.12
  33.3 2.4 %collective-permute-start.13 = (bf16[128,256]{1,0:T(8,128)(2,1)S(1)}, bf16[128,256]{1,0:T(8,128)(2,1)S(1)}, u32[]{:S(2)}, u32[]{:S(2)}) collective-permute-start(bf16[128,256]{1,0:T(8,128)(2,1)S(1)} %shard_map.225.refs_0_.own_ref), channel_id=1, source_target_pairs={{0,16},{1,9},{2,18},{3,11},{4,20},{5,13},{6,22},{7,15},{8,24},{9,1... | collective-permute-start | bytes 196616 | tf_op jit(solution)/shard_map/ppermute | solution.py:373
  35.8 2.8 %collective-permute-done.13.recv_ref = bf16[128,256]{1,0:T(8,128)(2,1)S(1)} collective-permute-done((bf16[128,256]{1,0:T(8,128)(2,1)S(1)}, bf16[128,256]{1,0:T(8,128)(2,1)S(1)}, u32[]{:S(2)}, u32[]{:S(2)}) %collective-permute-start.13) | collective-permute-done | bytes 65568 | tf_op jit(solution)/shard_map/ppermute | solution.py:373
  38.6 2.5 %collective-permute-start.19 = (bf16[256,256]{1,0:T(8,128)(2,1)S(1)}, bf16[256,256]{1,0:T(8,128)(2,1)S(1)}, u32[]{:S(2)}, u32[]{:S(2)}) collective-permute-start(bf16[256,256]{1,0:T(8,128)(2,1)S(1)} %shard_map.230.refs_0_), channel_id=1, source_target_pairs={{0,6},{1,7},{2,4},{3,5},{4,2},{5,3},{6,0},{7,1},{8,14},{9,15},{10,... | collective-permute-start | bytes 393224 | tf_op jit(solution)/shard_map/ppermute | solution.py:373
  41.1 0.5 %collective-permute-start.17 = (bf16[256,256]{1,0:T(8,128)(2,1)S(1)}, bf16[256,256]{1,0:T(8,128)(2,1)S(1)}, u32[]{:S(2)}, u32[]{:S(2)}) collective-permute-start(bf16[256,256]{1,0:T(8,128)(2,1)S(1)} %shard_map.230.refs_0_), channel_id=1, source_target_pairs={{0,4},{1,5},{2,6},{3,7},{4,0},{5,1},{6,2},{7,3},{8,12},{9,13},{10,... | collective-permute-start | bytes 393224 | tf_op jit(solution)/shard_map/ppermute | solution.py:373
  41.6 0.6 %collective-permute-start.15 = (bf16[256,256]{1,0:T(8,128)(2,1)S(1)}, bf16[256,256]{1,0:T(8,128)(2,1)S(1)}, u32[]{:S(2)}, u32[]{:S(2)}) collective-permute-start(bf16[256,256]{1,0:T(8,128)(2,1)S(1)} %shard_map.230.refs_0_), channel_id=1, source_target_pairs={{0,2},{1,3},{2,0},{3,1},{4,6},{5,7},{6,4},{7,5},{8,10},{9,11},{10,... | collective-permute-start | bytes 393224 | tf_op jit(solution)/shard_map/ppermute | solution.py:373
  42.2 0.9 %shard_map.229 = (bf16[128,256]{1,0:T(8,128)(2,1)}, bf16[128,256]{1,0:T(8,128)(2,1)}, f32[1,256]{1,0:T(1,128)}, f32[1,256]{1,0:T(1,128)}, f32[4]{0:T(128)}, /*index=5*/f32[4]{0:T(128)}, f32[8,128]{1,0:T(8,128)S(1)}) custom-call(bf16[128,256]{1,0:T(8,128)(2,1)S(1)} %get-tuple-element.55.refs_0_, bf16[128,256]{1,0:T(8,128)(2,1)S(1)} %get-tuple-element.61.refs_1_, ...), custom_call_target="tpu_custom_call" | custom-call | tf_op jit(solution)/shard_map/pallas_call | solution.py:360
  43.1 1.5 %collective-permute-done.19.source_ref = bf16[256,256]{1,0:T(8,128)(2,1)S(1)} collective-permute-done((bf16[256,256]{1,0:T(8,128)(2,1)S(1)}, bf16[256,256]{1,0:T(8,128)(2,1)S(1)}, u32[]{:S(2)}, u32[]{:S(2)}) %collective-permute-start.19) | collective-permute-done | bytes 131104 | tf_op jit(solution)/shard_map/ppermute | solution.py:373
  44.6 0.1 collective-permute-start.20
  44.7 1.4 %collective-permute-done.17.refs_2_ = bf16[256,256]{1,0:T(8,128)(2,1)S(1)} collective-permute-done((bf16[256,256]{1,0:T(8,128)(2,1)S(1)}, bf16[256,256]{1,0:T(8,128)(2,1)S(1)}, u32[]{:S(2)}, u32[]{:S(2)}) %collective-permute-start.17) | collective-permute-done | bytes 131104 | tf_op jit(solution)/shard_map/ppermute | solution.py:373
  46.1 0.5 %collective-permute-done.15.refs_1_ = bf16[256,256]{1,0:T(8,128)(2,1)S(1)} collective-permute-done((bf16[256,256]{1,0:T(8,128)(2,1)S(1)}, bf16[256,256]{1,0:T(8,128)(2,1)S(1)}, u32[]{:S(2)}, u32[]{:S(2)}) %collective-permute-start.15) | collective-permute-done | bytes 131104 | tf_op jit(solution)/shard_map/ppermute | solution.py:373
  46.6 0.0 collective-permute-start.16
  46.6 1.0 %shard_map.232 = (f32[256,256]{1,0:T(8,128)}, f32[256,256]{1,0:T(8,128)}, f32[256,256]{1,0:T(8,128)}, f32[256,256]{1,0:T(8,128)}, f32[256,512]{1,0:T(8,128)}, /*index=5*/f32[512,256]{1,0:T(8,128)}) custom-call(bf16[256,256]{1,0:T(8,128)(2,1)S(1)} %shard_map.230.refs_0_, bf16[256,256]{1,0:T(8,128)(2,1)S(1)} %collective-permute-done.15.refs_1_, ...), custom_call_target="tpu_custom_call" | custom-call | tf_op jit(solution)/shard_map/pallas_call | solution.py:551
  47.7 0.3 collective-permute-done.16.refs_1_
  47.9 1.0 %shard_map.233 = (f32[256,256]{1,0:T(8,128)}, f32[256,256]{1,0:T(8,128)}, f32[256,256]{1,0:T(8,128)}, f32[256,256]{1,0:T(8,128)}, f32[256,512]{1,0:T(8,128)}, /*index=5*/f32[512,256]{1,0:T(8,128)}) custom-call(bf16[256,256]{1,0:T(8,128)(2,1)S(1)} %collective-permute-done.14.refs_0_, ...), custom_call_target="tpu_custom_call", output_to_operand_aliasing={{0}: (4, {}), {1}: (5, {}), {2}: (6, {}), {3}: (7, {}), {4}... | custom-call | tf_op jit(solution)/shard_map/pallas_call | solution.py:551
  (34 shorter events, 0.2 us)
Async XLA Ops:
  0.6 7.3 %copy-start.6 = (bf16[1,128,256]{2,1,0:T(8,128)(2,1)S(1)}, bf16[1,128,256]{2,1,0:T(8,128)(2,1)}, u32[]{:S(2)}) copy-start(bf16[1,128,256]{2,1,0:T(8,128)(2,1)} %param.16) | copy-start | bytes 196612
  0.7 7.3 %copy-start.7 = (bf16[1,128,256]{2,1,0:T(8,128)(2,1)S(1)}, bf16[1,128,256]{2,1,0:T(8,128)(2,1)}, u32[]{:S(2)}) copy-start(bf16[1,128,256]{2,1,0:T(8,128)(2,1)} %param.15) | copy-start | bytes 196612
  0.7 8.6 %collective-permute-start.2 = (bf16[128,256]{1,0:T(8,128)(2,1)}, bf16[128,256]{1,0:T(8,128)(2,1)S(1)}, u32[]{:S(2)}, u32[]{:S(2)}) collective-permute-start(bf16[128,256]{1,0:T(8,128)(2,1)} %bitcast.10), channel_id=1, source_target_pairs={{0,16},{4,20},{8,24},{12,28},{16,0},{20,4},{24,8},{28,12},{1,17},{... | collective-permute-start | bytes 196616 | tf_op jit(solution)/shard_map/ppermute | solution.py:406
  4.8 4.5 %collective-permute-start.1 = (bf16[128,256]{1,0:T(8,128)(2,1)}, bf16[128,256]{1,0:T(8,128)(2,1)S(1)}, u32[]{:S(2)}, u32[]{:S(2)}) collective-permute-start(bf16[128,256]{1,0:T(8,128)(2,1)} %bitcast.11), channel_id=1, source_target_pairs={{0,8},{4,12},{8,0},{12,4},{16,24},{20,28},{24,16},{28,20},{1,9},{5... | collective-permute-start | bytes 196616 | tf_op jit(solution)/shard_map/ppermute | solution.py:406
  6.3 4.5 %collective-permute-start = (bf16[128,256]{1,0:T(8,128)(2,1)}, bf16[128,256]{1,0:T(8,128)(2,1)S(1)}, u32[]{:S(2)}, u32[]{:S(2)}) collective-permute-start(bf16[128,256]{1,0:T(8,128)(2,1)} %bitcast.12), channel_id=1, source_target_pairs={{0,4},{4,0},{8,12},{12,8},{16,20},{20,16},{24,28},{28,24},{1,5},{5... | collective-permute-start | bytes 196616 | tf_op jit(solution)/shard_map/ppermute | solution.py:406
  7.9 0.7 %copy-start.10 = (f32[256]{0:T(256)S(1)}, f32[256]{0:T(256)}, u32[]{:S(2)}) copy-start(f32[256]{0:T(256)} %param.22) | copy-start | bytes 3076
  7.9 0.7 %copy-start.12 = (f32[4]{0:T(128)S(1)}, f32[4]{0:T(128)}, u32[]{:S(2)}) copy-start(f32[4]{0:T(128)} %far_ref.1) | copy-start | bytes 52
  7.9 0.7 %copy-start.8 = (s32[1,4,1,128]{3,2,1,0:T(1,128)S(1)}, s32[1,4,1,128]{3,2,1,0:T(1,128)}, u32[]{:S(2)}) copy-start(s32[1,4,1,128]{3,2,1,0:T(1,128)} %param.27) | copy-start | bytes 6148
  7.9 0.7 %copy-start.9 = (f32[256]{0:T(256)S(1)}, f32[256]{0:T(256)}, u32[]{:S(2)}) copy-start(f32[256]{0:T(256)} %param.17) | copy-start | bytes 3076
  7.9 0.7 %copy-start.11 = (f32[4]{0:T(128)S(1)}, f32[4]{0:T(128)}, u32[]{:S(2)}) copy-start(f32[4]{0:T(128)} %local_ref.1) | copy-start | bytes 52
  8.6 2.2 %copy-start = (bf16[256,512]{1,0:T(8,128)(2,1)S(1)}, bf16[256,512]{1,0:T(8,128)(2,1)}, u32[]{:S(2)}) copy-start(bf16[256,512]{1,0:T(8,128)(2,1)} %refs_11_.1) | copy-start | bytes 786436
  8.6 2.2 %copy-start.1 = (bf16[512,256]{1,0:T(8,128)(2,1)S(1)}, bf16[512,256]{1,0:T(8,128)(2,1)}, u32[]{:S(2)}) copy-start(bf16[512,256]{1,0:T(8,128)(2,1)} %refs_12_.1) | copy-start | bytes 786436
  8.6 2.2 %copy-start.2 = (bf16[256,256]{1,0:T(8,128)(2,1)S(1)}, bf16[256,256]{1,0:T(8,128)(2,1)}, u32[]{:S(2)}) copy-start(bf16[256,256]{1,0:T(8,128)(2,1)} %refs_6_.1) | copy-start | bytes 393220
  8.6 2.2 %copy-start.3 = (bf16[256,256]{1,0:T(8,128)(2,1)S(1)}, bf16[256,256]{1,0:T(8,128)(2,1)}, u32[]{:S(2)}) copy-start(bf16[256,256]{1,0:T(8,128)(2,1)} %refs_7_.1) | copy-start | bytes 393220
  8.6 2.2 %copy-start.4 = (bf16[256,256]{1,0:T(8,128)(2,1)S(1)}, bf16[256,256]{1,0:T(8,128)(2,1)}, u32[]{:S(2)}) copy-start(bf16[256,256]{1,0:T(8,128)(2,1)} %refs_8_.1) | copy-start | bytes 393220
  8.6 2.2 %copy-start.5 = (bf16[256,256]{1,0:T(8,128)(2,1)S(1)}, bf16[256,256]{1,0:T(8,128)(2,1)}, u32[]{:S(2)}) copy-start(bf16[256,256]{1,0:T(8,128)(2,1)} %refs_9_.1) | copy-start | bytes 393220
  14.7 2.0 %collective-permute-start.4 = (bf16[528,256]{1,0:T(8,128)(2,1)S(1)}, bf16[528,256]{1,0:T(8,128)(2,1)S(1)}, u32[]{:S(2)}, u32[]{:S(2)}) collective-permute-start(bf16[528,256]{1,0:T(8,128)(2,1)S(1)} %get-tuple-element.67.sents_ref), channel_id=1, source_target_pairs={{0,1},{1,0},{2,3},{3,2},{4,5},{5,4},{6,7},{7,6},{8,9},{9,8},{10,11... | collective-permute-start | bytes 811016 | tf_op jit(solution)/shard_map/ppermute | solution.py:373
  14.8 1.9 %collective-permute-start.3 = (bf16[512,256]{1,0:T(8,128)(2,1)S(1)}, bf16[512,256]{1,0:T(8,128)(2,1)S(1)}, u32[]{:S(2)}, u32[]{:S(2)}) collective-permute-start(bf16[512,256]{1,0:T(8,128)(2,1)S(1)} %get-tuple-element.65), channel_id=1, source_target_pairs={{0,1},{1,0},{2,3},{3,2},{4,5},{5,4},{6,7},{7,6},{8,9},{9,8},{10,11... | collective-permute-start | bytes 786440 | tf_op jit(solution)/shard_map/ppermute | solution.py:373
  16.8 10.2 %collective-permute-start.6 = (bf16[400,256]{1,0:T(8,128)(2,1)S(1)}, bf16[400,256]{1,0:T(8,128)(2,1)S(1)}, u32[]{:S(2)}, u32[]{:S(2)}) collective-permute-start(bf16[400,256]{1,0:T(8,128)(2,1)S(1)} %get-tuple-element.73), channel_id=1, source_target_pairs={{0,4},{1,5},{2,6},{3,7},{4,0},{5,1},{6,2},{7,3},{8,12},{9,13},{10,... | collective-permute-start | bytes 614408 | tf_op jit(solution)/shard_map/ppermute | solution.py:373
  18.4 7.6 %collective-permute-start.5 = (bf16[272,256]{1,0:T(8,128)(2,1)S(1)}, bf16[272,256]{1,0:T(8,128)(2,1)S(1)}, u32[]{:S(2)}, u32[]{:S(2)}) collective-permute-start(bf16[272,256]{1,0:T(8,128)(2,1)S(1)} %get-tuple-element.72), channel_id=1, source_target_pairs={{0,2},{1,3},{2,0},{3,1},{4,6},{5,7},{6,4},{7,5},{8,10},{9,11},{10,... | collective-permute-start | bytes 417800 | tf_op jit(solution)/shard_map/ppermute | solution.py:373
  19.9 7.0 %collective-permute-start.7 = (bf16[272,256]{1,0:T(8,128)(2,1)S(1)}, bf16[272,256]{1,0:T(8,128)(2,1)S(1)}, u32[]{:S(2)}, u32[]{:S(2)}) collective-permute-start(bf16[272,256]{1,0:T(8,128)(2,1)S(1)} %get-tuple-element.74), channel_id=1, source_target_pairs={{0,6},{1,7},{2,4},{3,5},{4,2},{5,3},{6,0},{7,1},{8,14},{9,15},{10,... | collective-permute-start | bytes 417800 | tf_op jit(solution)/shard_map/ppermute | solution.py:373
  20.4 4.4 %collective-permute-start.8 = (bf16[128,256]{1,0:T(8,128)(2,1)S(1)}, bf16[128,256]{1,0:T(8,128)(2,1)S(1)}, u32[]{:S(2)}, u32[]{:S(2)}) collective-permute-start(bf16[128,256]{1,0:T(8,128)(2,1)S(1)} %get-tuple-element.75), channel_id=1, source_target_pairs={{0,8},{4,12},{8,0},{12,4},{16,24},{20,28},{24,16},{28,20},{1,9},{5... | collective-permute-start | bytes 196616 | tf_op jit(solution)/shard_map/ppermute | solution.py:406
  20.8 5.2 %collective-permute-start.9 = (bf16[128,256]{1,0:T(8,128)(2,1)S(1)}, bf16[128,256]{1,0:T(8,128)(2,1)S(1)}, u32[]{:S(2)}, u32[]{:S(2)}) collective-permute-start(bf16[128,256]{1,0:T(8,128)(2,1)S(1)} %get-tuple-element.76), channel_id=1, source_target_pairs={{0,16},{4,20},{8,24},{12,28},{16,0},{20,4},{24,8},{28,12},{1,17},{... | collective-permute-start | bytes 196616 | tf_op jit(solution)/shard_map/ppermute | solution.py:406
  27.1 6.2 %collective-permute-start.10 = (bf16[144,256]{1,0:T(8,128)(2,1)S(1)}, bf16[144,256]{1,0:T(8,128)(2,1)S(1)}, u32[]{:S(2)}, u32[]{:S(2)}) collective-permute-start(bf16[144,256]{1,0:T(8,128)(2,1)S(1)} %get-tuple-element.77.refs_0_.own_ref), channel_id=1, source_target_pairs={{0,16},{1,9},{2,18},{3,11},{4,20},{5,13},{6,22},{7,15},{8,24},{9,1... | collective-permute-start | bytes 221192 | tf_op jit(solution)/shard_map/ppermute | solution.py:373
  27.5 4.3 %collective-permute-start.11 = (bf16[128,256]{1,0:T(8,128)(2,1)S(1)}, bf16[128,256]{1,0:T(8,128)(2,1)S(1)}, u32[]{:S(2)}, u32[]{:S(2)}) collective-permute-start(bf16[128,256]{1,0:T(8,128)(2,1)S(1)} %get-tuple-element.78.own_ref), channel_id=1, source_target_pairs={{0,8},{1,17},{2,10},{3,19},{4,12},{5,21},{6,14},{7,23},{8,0},{9,25... | collective-permute-start | bytes 196616 | tf_op jit(solution)/shard_map/ppermute | solution.py:373
  33.3 5.3 %collective-permute-start.12 = (bf16[144,256]{1,0:T(8,128)(2,1)S(1)}, bf16[144,256]{1,0:T(8,128)(2,1)S(1)}, u32[]{:S(2)}, u32[]{:S(2)}) collective-permute-start(bf16[144,256]{1,0:T(8,128)(2,1)S(1)} %shard_map.226.refs_0_.own_ref), channel_id=1, source_target_pairs={{0,8},{1,17},{2,10},{3,19},{4,12},{5,21},{6,14},{7,23},{8,0},{9,25... | collective-permute-start | bytes 221192 | tf_op jit(solution)/shard_map/ppermute | solution.py:373
  33.3 5.2 %collective-permute-start.13 = (bf16[128,256]{1,0:T(8,128)(2,1)S(1)}, bf16[128,256]{1,0:T(8,128)(2,1)S(1)}, u32[]{:S(2)}, u32[]{:S(2)}) collective-permute-start(bf16[128,256]{1,0:T(8,128)(2,1)S(1)} %shard_map.225.refs_0_.own_ref), channel_id=1, source_target_pairs={{0,16},{1,9},{2,18},{3,11},{4,20},{5,13},{6,22},{7,15},{8,24},{9,1... | collective-permute-start | bytes 196616 | tf_op jit(solution)/shard_map/ppermute | solution.py:373
  38.6 5.9 %collective-permute-start.19 = (bf16[256,256]{1,0:T(8,128)(2,1)S(1)}, bf16[256,256]{1,0:T(8,128)(2,1)S(1)}, u32[]{:S(2)}, u32[]{:S(2)}) collective-permute-start(bf16[256,256]{1,0:T(8,128)(2,1)S(1)} %shard_map.230.refs_0_), channel_id=1, source_target_pairs={{0,6},{1,7},{2,4},{3,5},{4,2},{5,3},{6,0},{7,1},{8,14},{9,15},{10,... | collective-permute-start | bytes 393224 | tf_op jit(solution)/shard_map/ppermute | solution.py:373
  41.1 5.0 %collective-permute-start.17 = (bf16[256,256]{1,0:T(8,128)(2,1)S(1)}, bf16[256,256]{1,0:T(8,128)(2,1)S(1)}, u32[]{:S(2)}, u32[]{:S(2)}) collective-permute-start(bf16[256,256]{1,0:T(8,128)(2,1)S(1)} %shard_map.230.refs_0_), channel_id=1, source_target_pairs={{0,4},{1,5},{2,6},{3,7},{4,0},{5,1},{6,2},{7,3},{8,12},{9,13},{10,... | collective-permute-start | bytes 393224 | tf_op jit(solution)/shard_map/ppermute | solution.py:373
  41.6 5.0 %collective-permute-start.15 = (bf16[256,256]{1,0:T(8,128)(2,1)S(1)}, bf16[256,256]{1,0:T(8,128)(2,1)S(1)}, u32[]{:S(2)}, u32[]{:S(2)}) collective-permute-start(bf16[256,256]{1,0:T(8,128)(2,1)S(1)} %shard_map.230.refs_0_), channel_id=1, source_target_pairs={{0,2},{1,3},{2,0},{3,1},{4,6},{5,7},{6,4},{7,5},{8,10},{9,11},{10,... | collective-permute-start | bytes 393224 | tf_op jit(solution)/shard_map/ppermute | solution.py:373
  42.2 5.5 %collective-permute-start.14 = (bf16[256,256]{1,0:T(8,128)(2,1)S(1)}, bf16[256,256]{1,0:T(8,128)(2,1)S(1)}, u32[]{:S(2)}, u32[]{:S(2)}) collective-permute-start(bf16[256,256]{1,0:T(8,128)(2,1)S(1)} %shard_map.230.refs_0_), channel_id=1, source_target_pairs={{0,1},{1,0},{2,3},{3,2},{4,5},{5,4},{6,7},{7,6},{8,9},{9,8},{10,11... | collective-permute-start | bytes 393224 | tf_op jit(solution)/shard_map/ppermute | solution.py:373
  44.6 3.1 %collective-permute-start.20 = (bf16[256,256]{1,0:T(8,128)(2,1)S(1)}, bf16[256,256]{1,0:T(8,128)(2,1)S(1)}, u32[]{:S(2)}, u32[]{:S(2)}) collective-permute-start(bf16[256,256]{1,0:T(8,128)(2,1)S(1)} %shard_map.231.refs_3_), channel_id=1, source_target_pairs={{0,1},{1,0},{2,3},{3,2},{4,5},{5,4},{6,7},{7,6},{8,9},{9,8},{10,11... | collective-permute-start | bytes 393224 | tf_op jit(solution)/shard_map/ppermute | solution.py:373
  46.1 1.6 %collective-permute-start.18 = (bf16[256,256]{1,0:T(8,128)(2,1)S(1)}, bf16[256,256]{1,0:T(8,128)(2,1)S(1)}, u32[]{:S(2)}, u32[]{:S(2)}) collective-permute-start(bf16[256,256]{1,0:T(8,128)(2,1)S(1)} %collective-permute-done.17.refs_2_), channel_id=1, source_target_pairs={{0,1},{1,0},{2,3},{3,2},{4,5},{5,4},{6,7},{7,6},{8,9},{9,8},{10,11... | collective-permute-start | bytes 393224 | tf_op jit(solution)/shard_map/ppermute | solution.py:373
  46.6 1.3 %collective-permute-start.16 = (bf16[256,256]{1,0:T(8,128)(2,1)S(1)}, bf16[256,256]{1,0:T(8,128)(2,1)S(1)}, u32[]{:S(2)}, u32[]{:S(2)}) collective-permute-start(bf16[256,256]{1,0:T(8,128)(2,1)S(1)} %collective-permute-done.15.refs_1_), channel_id=1, source_target_pairs={{0,1},{1,0},{2,3},{3,2},{4,5},{5,4},{6,7},{7,6},{8,9},{9,8},{10,11... | collective-permute-start | bytes 393224 | tf_op jit(solution)/shard_map/ppermute | solution.py:373

commit v8 on v7

--- a/solution.py
+++ b/solution.py
@@ -165,6 +165,7 @@
     query_stack = stack_heads(queries, head_masks)
     raw_s[...] = dot_rhs_t(query_stack, key_all) * scale
 
+    back = dot_rhs_t(upstream, wdown_ref[...])
     counts = count_ref[...]
     for h in range(heads):
         block = pl.ds(h * rows, rows)
@@ -181,25 +182,25 @@
     preact = dot(hidden2, wup_ref[...])
     act32, derivative = gelu_parts(preact)
     act = act32.astype(BF16)
-    out_ref[...] = (mixed.astype(F32) + dot(act, wdown_ref[...])).astype(BF16)
-    grad_down = dot_lhs_t(act, upstream)
-    wide_s[2 * width : 3 * width, :] = grad_down[:width].astype(BF16)
-    wide_s[3 * width : 4 * width, :] = grad_down[width:].astype(BF16)
-    grad_pre = (dot_rhs_t(upstream, wdown_ref[...]) * derivative).astype(BF16)
-    grad_up = dot_lhs_t(hidden2, grad_pre)
-    wide_s[0 * width : 1 * width, :] = grad_up[:, :width].astype(BF16)
-    wide_s[1 * width : 2 * width, :] = grad_up[:, width:].astype(BF16)
+    grad_pre = (back * derivative).astype(BF16)
     grad_hidden2 = dot_rhs_t(grad_pre, wup_ref[...])
     grad_gain2 = jnp.sum(grad_hidden2 * normed2, axis=0, keepdims=True)
     grad_mixed = upstream.astype(F32) + norm_backward(grad_hidden2, normed2, inverse2, gain2)
     mixed_ref[...] = grad_mixed
     grad_mixed16 = grad_mixed.astype(BF16)
-    square_s[3 * width : 4 * width, :] = dot_lhs_t(attended, grad_mixed16).astype(BF16)
     grad_att = dot_rhs_t(grad_mixed16, wo_ref[...]).astype(BF16).astype(F32)
     grad_stack = stack_heads(grad_att, head_masks)
     product = grad_att * attended32
     dots = dot_rhs_t(grad_stack, value_all)
 
+    out_ref[...] = (mixed.astype(F32) + dot(act, wdown_ref[...])).astype(BF16)
+    grad_down = dot_lhs_t(act, upstream)
+    wide_s[2 * width : 3 * width, :] = grad_down[:width].astype(BF16)
+    wide_s[3 * width : 4 * width, :] = grad_down[width:].astype(BF16)
+    grad_up = dot_lhs_t(hidden2, grad_pre)
+    wide_s[0 * width : 1 * width, :] = grad_up[:, :width].astype(BF16)
+    wide_s[1 * width : 2 * width, :] = grad_up[:, width:].astype(BF16)
+    square_s[3 * width : 4 * width, :] = dot_lhs_t(attended, grad_mixed16).astype(BF16)
     local_terms = []
     far_terms = []
     for h in range(heads):

time: 49.2 us -> 48.8 us (level)
  no operation moved by 1% of the time
where the time goes in v8:
time: 48.8 us; the launch traced here: 48.7 us
  starting transfers between devices  21.1 us (43%)
  waiting for transfers between devices  18.5 us (38%)
  Pallas kernels  7.49 us (15%)
  between operations  0.9 us (2%)
  local copies, waits for them, and re-layouts  0.72 us (1%)
    ppermute x16, waiting for transfers between devices, flipped(): return lax.ppermute(x, AXES, pairs)  13.2 us
    ppermute x16, starting transfers between devices, flipped(): return lax.ppermute(x, AXES, pairs)  12.1 us
    ppermute x5, starting transfers between devices, swapped(): lax.ppermute(x, 'dom', [(i, i ^ 1 << bit) for i in range(lax.axis_size('d...  8.97 us
    pallas_call x12, Pallas kernels, call(): pl.pallas_call(kernel, out_shape=outs, in_specs=in_specs or [VM] * len(ar...  5.4 us
    ppermute x5, waiting for transfers between devices, swapped(): lax.ppermute(x, 'dom', [(i, i ^ 1 << bit) for i in range(lax.axis_size('d...  5.34 us
    pallas_call x2, Pallas kernels, local(): pl.pallas_call(functools.partial(spread_kernel, own), out_shape=tuple((st...  2.09 us
  transfers between devices with their start and end apart: 21, of which 13 were waited for; matrix products, arithmetic and copies ran while one was open for 0% of the time, Pallas kernels for 5%

profile of v8, /device:TPU:0, one launch (start us, length us, event | category | flops | bytes accessed | tf_op | source)
XLA Modules:
  0.0 48.7 jit_solution(14230264974490363055)
XLA Ops:
  0.7 4.1 %collective-permute-start.2 = (bf16[128,256]{1,0:T(8,128)(2,1)}, bf16[128,256]{1,0:T(8,128)(2,1)S(1)}, u32[]{:S(2)}, u32[]{:S(2)}) collective-permute-start(bf16[128,256]{1,0:T(8,128)(2,1)} %bitcast.10), channel_id=1, source_target_pairs={{0,16},{4,20},{8,24},{12,28},{16,0},{20,4},{24,8},{28,12},{1,17},{... | collective-permute-start | bytes 196616 | tf_op jit(solution)/shard_map/ppermute | solution.py:407
  4.8 1.6 %collective-permute-start.1 = (bf16[128,256]{1,0:T(8,128)(2,1)}, bf16[128,256]{1,0:T(8,128)(2,1)S(1)}, u32[]{:S(2)}, u32[]{:S(2)}) collective-permute-start(bf16[128,256]{1,0:T(8,128)(2,1)} %bitcast.11), channel_id=1, source_target_pairs={{0,8},{4,12},{8,0},{12,4},{16,24},{20,28},{24,16},{28,20},{1,9},{5... | collective-permute-start | bytes 196616 | tf_op jit(solution)/shard_map/ppermute | solution.py:407
  6.3 1.5 %collective-permute-start = (bf16[128,256]{1,0:T(8,128)(2,1)}, bf16[128,256]{1,0:T(8,128)(2,1)S(1)}, u32[]{:S(2)}, u32[]{:S(2)}) collective-permute-start(bf16[128,256]{1,0:T(8,128)(2,1)} %bitcast.12), channel_id=1, source_target_pairs={{0,4},{4,0},{8,12},{12,8},{16,20},{20,16},{24,28},{28,24},{1,5},{5... | collective-permute-start | bytes 196616 | tf_op jit(solution)/shard_map/ppermute | solution.py:407
  7.9 0.0 copy-start.9
  7.9 0.0 copy-start.11
  7.9 0.6 %copy-done.10 = f32[256]{0:T(256)S(1)} copy-done((f32[256]{0:T(256)S(1)}, f32[256]{0:T(256)}, u32[]{:S(2)}) %copy-start.10) | copy-done | bytes 1048
  8.5 0.0 copy-done.8
  8.6 0.0 copy-done.9
  8.6 0.0 copy-start.3
  8.6 0.0 copy-start.4
  8.6 0.0 copy-start.5
  8.6 0.7 %shard_map.221 = (f32[128,512]{1,0:T(8,128)S(1)}, f32[8,512]{1,0:T(8,128)S(1)}, bf16[128,256]{1,0:T(8,128)(2,1)S(1)}, bf16[128,256]{1,0:T(8,128)(2,1)S(1)}, f32[1,256]{1,0:T(1,128)S(1)}, /*index=5*/f32[1,256]{1,0:T(1,128)S(1)}) custom-call(f32[8,128]{1,0:T(8,128)S(1)} %shard_map.220.flag_ref, s32[4,128]{1,0:T(4,128)S(1)} %bitcast.14, f32[4]{0:T(128)S(1)} %copy-done.11, ...), custom_call_target="tpu_custom_call" | custom-call | flops 10000000000 | bytes 1 | tf_op jit(solution)/shard_map/pallas_call | solution.py:361
  9.3 0.0 collective-permute-done.2.refs_3_
  9.3 1.5 %collective-permute-done.refs_1_ = bf16[128,256]{1,0:T(8,128)(2,1)S(1)} collective-permute-done((bf16[128,256]{1,0:T(8,128)(2,1)}, bf16[128,256]{1,0:T(8,128)(2,1)S(1)}, u32[]{:S(2)}, u32[]{:S(2)}) %collective-permute-start) | collective-permute-done | bytes 65568 | tf_op jit(solution)/shard_map/ppermute | solution.py:407
  10.9 3.5 %shard_map.222 = (bf16[128,256]{1,0:T(8,128)(2,1)S(1)}, bf16[1024,256]{1,0:T(8,128)(2,1)S(1)}, bf16[512,256]{1,0:T(8,128)(2,1)S(1)}, bf16[1024,256]{1,0:T(8,128)...) custom-call(bf16[128,256]{1,0:T(8,128)(2,1)S(1)} %get-tuple-element., ...), custom_call_target="tpu_custom_call" | custom-call | tf_op jit(solution)/shard_map/pallas_call | solution.py:361
  14.4 0.1 collective-permute-start.4
  14.5 0.5 %collective-permute-start.3 = (bf16[512,256]{1,0:T(8,128)(2,1)S(1)}, bf16[512,256]{1,0:T(8,128)(2,1)S(1)}, u32[]{:S(2)}, u32[]{:S(2)}) collective-permute-start(bf16[512,256]{1,0:T(8,128)(2,1)S(1)} %get-tuple-element.65), channel_id=1, source_target_pairs={{0,1},{1,0},{2,3},{3,2},{4,5},{5,4},{6,7},{7,6},{8,9},{9,8},{10,11... | collective-permute-start | bytes 786440 | tf_op jit(solution)/shard_map/ppermute | solution.py:374
  15.0 1.4 %collective-permute-done.3.recvw_ref = bf16[512,256]{1,0:T(8,128)(2,1)S(1)} collective-permute-done((bf16[512,256]{1,0:T(8,128)(2,1)S(1)}, bf16[512,256]{1,0:T(8,128)(2,1)S(1)}, u32[]{:S(2)}, u32[]{:S(2)}) %collective-permute-start.3) | collective-permute-done | bytes 262176 | tf_op jit(solution)/shard_map/ppermute | solution.py:374
  16.4 0.1 shard_map.223
  16.5 1.6 %collective-permute-start.6 = (bf16[400,256]{1,0:T(8,128)(2,1)S(1)}, bf16[400,256]{1,0:T(8,128)(2,1)S(1)}, u32[]{:S(2)}, u32[]{:S(2)}) collective-permute-start(bf16[400,256]{1,0:T(8,128)(2,1)S(1)} %get-tuple-element.73), channel_id=1, source_target_pairs={{0,4},{1,5},{2,6},{3,7},{4,0},{5,1},{6,2},{7,3},{8,12},{9,13},{10,... | collective-permute-start | bytes 614408 | tf_op jit(solution)/shard_map/ppermute | solution.py:374
  18.1 1.5 %collective-permute-start.5 = (bf16[272,256]{1,0:T(8,128)(2,1)S(1)}, bf16[272,256]{1,0:T(8,128)(2,1)S(1)}, u32[]{:S(2)}, u32[]{:S(2)}) collective-permute-start(bf16[272,256]{1,0:T(8,128)(2,1)S(1)} %get-tuple-element.72), channel_id=1, source_target_pairs={{0,2},{1,3},{2,0},{3,1},{4,6},{5,7},{6,4},{7,5},{8,10},{9,11},{10,... | collective-permute-start | bytes 417800 | tf_op jit(solution)/shard_map/ppermute | solution.py:374
  19.6 0.5 collective-permute-start.7
  20.1 0.4 collective-permute-start.8
  20.5 1.3 %collective-permute-start.9 = (bf16[128,256]{1,0:T(8,128)(2,1)S(1)}, bf16[128,256]{1,0:T(8,128)(2,1)S(1)}, u32[]{:S(2)}, u32[]{:S(2)}) collective-permute-start(bf16[128,256]{1,0:T(8,128)(2,1)S(1)} %get-tuple-element.76), channel_id=1, source_target_pairs={{0,16},{4,20},{8,24},{12,28},{16,0},{20,4},{24,8},{28,12},{1,17},{... | collective-permute-start | bytes 196616 | tf_op jit(solution)/shard_map/ppermute | solution.py:407
  21.8 2.6 %collective-permute-done.8.refs_0_.refs_7_ = bf16[128,256]{1,0:T(8,128)(2,1)S(1)} collective-permute-done((bf16[128,256]{1,0:T(8,128)(2,1)S(1)}, bf16[128,256]{1,0:T(8,128)(2,1)S(1)}, u32[]{:S(2)}, u32[]{:S(2)}) %collective-permute-start.8) | collective-permute-done | bytes 65568 | tf_op jit(solution)/shard_map/ppermute | solution.py:407
  24.4 1.3 %collective-permute-done.9.refs_1_.refs_8_ = bf16[128,256]{1,0:T(8,128)(2,1)S(1)} collective-permute-done((bf16[128,256]{1,0:T(8,128)(2,1)S(1)}, bf16[128,256]{1,0:T(8,128)(2,1)S(1)}, u32[]{:S(2)}, u32[]{:S(2)}) %collective-permute-start.9) | collective-permute-done | bytes 65568 | tf_op jit(solution)/shard_map/ppermute | solution.py:407
  25.7 0.9 %collective-permute-done.7.three_ref = bf16[272,256]{1,0:T(8,128)(2,1)S(1)} collective-permute-done((bf16[272,256]{1,0:T(8,128)(2,1)S(1)}, bf16[272,256]{1,0:T(8,128)(2,1)S(1)}, u32[]{:S(2)}, u32[]{:S(2)}) %collective-permute-start.7) | collective-permute-done | bytes 139296 | tf_op jit(solution)/shard_map/ppermute | solution.py:374
  26.6 0.1 collective-permute-done.6.two_ref.refs_6_
  26.7 0.1 shard_map.224
  26.8 0.4 collective-permute-start.10
  27.2 1.4 %collective-permute-start.11 = (bf16[128,256]{1,0:T(8,128)(2,1)S(1)}, bf16[128,256]{1,0:T(8,128)(2,1)S(1)}, u32[]{:S(2)}, u32[]{:S(2)}) collective-permute-start(bf16[128,256]{1,0:T(8,128)(2,1)S(1)} %get-tuple-element.78.own_ref), channel_id=1, source_target_pairs={{0,8},{1,17},{2,10},{3,19},{4,12},{5,21},{6,14},{7,23},{8,0},{9,25... | collective-permute-start | bytes 196616 | tf_op jit(solution)/shard_map/ppermute | solution.py:374
  28.6 2.8 %collective-permute-done.11.recv_ref = bf16[128,256]{1,0:T(8,128)(2,1)S(1)} collective-permute-done((bf16[128,256]{1,0:T(8,128)(2,1)S(1)}, bf16[128,256]{1,0:T(8,128)(2,1)S(1)}, u32[]{:S(2)}, u32[]{:S(2)}) %collective-permute-start.11) | collective-permute-done | bytes 65568 | tf_op jit(solution)/shard_map/ppermute | solution.py:374
  31.5 1.5 %collective-permute-done.10.recv_ref = bf16[144,256]{1,0:T(8,128)(2,1)S(1)} collective-permute-done((bf16[144,256]{1,0:T(8,128)(2,1)S(1)}, bf16[144,256]{1,0:T(8,128)(2,1)S(1)}, u32[]{:S(2)}, u32[]{:S(2)}) %collective-permute-start.10) | collective-permute-done | bytes 73760 | tf_op jit(solution)/shard_map/ppermute | solution.py:374
  32.9 0.1 collective-permute-start.12
  33.0 2.4 %collective-permute-start.13 = (bf16[128,256]{1,0:T(8,128)(2,1)S(1)}, bf16[128,256]{1,0:T(8,128)(2,1)S(1)}, u32[]{:S(2)}, u32[]{:S(2)}) collective-permute-start(bf16[128,256]{1,0:T(8,128)(2,1)S(1)} %shard_map.225.refs_0_.own_ref), channel_id=1, source_target_pairs={{0,16},{1,9},{2,18},{3,11},{4,20},{5,13},{6,22},{7,15},{8,24},{9,1... | collective-permute-start | bytes 196616 | tf_op jit(solution)/shard_map/ppermute | solution.py:374
  35.4 2.8 %collective-permute-done.13.recv_ref = bf16[128,256]{1,0:T(8,128)(2,1)S(1)} collective-permute-done((bf16[128,256]{1,0:T(8,128)(2,1)S(1)}, bf16[128,256]{1,0:T(8,128)(2,1)S(1)}, u32[]{:S(2)}, u32[]{:S(2)}) %collective-permute-start.13) | collective-permute-done | bytes 65568 | tf_op jit(solution)/shard_map/ppermute | solution.py:374
  38.3 2.5 %collective-permute-start.19 = (bf16[256,256]{1,0:T(8,128)(2,1)S(1)}, bf16[256,256]{1,0:T(8,128)(2,1)S(1)}, u32[]{:S(2)}, u32[]{:S(2)}) collective-permute-start(bf16[256,256]{1,0:T(8,128)(2,1)S(1)} %shard_map.230.refs_0_), channel_id=1, source_target_pairs={{0,6},{1,7},{2,4},{3,5},{4,2},{5,3},{6,0},{7,1},{8,14},{9,15},{10,... | collective-permute-start | bytes 393224 | tf_op jit(solution)/shard_map/ppermute | solution.py:374
  40.8 0.5 %collective-permute-start.17 = (bf16[256,256]{1,0:T(8,128)(2,1)S(1)}, bf16[256,256]{1,0:T(8,128)(2,1)S(1)}, u32[]{:S(2)}, u32[]{:S(2)}) collective-permute-start(bf16[256,256]{1,0:T(8,128)(2,1)S(1)} %shard_map.230.refs_0_), channel_id=1, source_target_pairs={{0,4},{1,5},{2,6},{3,7},{4,0},{5,1},{6,2},{7,3},{8,12},{9,13},{10,... | collective-permute-start | bytes 393224 | tf_op jit(solution)/shard_map/ppermute | solution.py:374
  41.3 0.6 %collective-permute-start.15 = (bf16[256,256]{1,0:T(8,128)(2,1)S(1)}, bf16[256,256]{1,0:T(8,128)(2,1)S(1)}, u32[]{:S(2)}, u32[]{:S(2)}) collective-permute-start(bf16[256,256]{1,0:T(8,128)(2,1)S(1)} %shard_map.230.refs_0_), channel_id=1, source_target_pairs={{0,2},{1,3},{2,0},{3,1},{4,6},{5,7},{6,4},{7,5},{8,10},{9,11},{10,... | collective-permute-start | bytes 393224 | tf_op jit(solution)/shard_map/ppermute | solution.py:374
  41.9 0.9 %shard_map.229 = (bf16[128,256]{1,0:T(8,128)(2,1)}, bf16[128,256]{1,0:T(8,128)(2,1)}, f32[1,256]{1,0:T(1,128)}, f32[1,256]{1,0:T(1,128)}, f32[4]{0:T(128)}, /*index=5*/f32[4]{0:T(128)}, f32[8,128]{1,0:T(8,128)S(1)}) custom-call(bf16[128,256]{1,0:T(8,128)(2,1)S(1)} %get-tuple-element.55.refs_0_, bf16[128,256]{1,0:T(8,128)(2,1)S(1)} %get-tuple-element.61.refs_1_, ...), custom_call_target="tpu_custom_call" | custom-call | tf_op jit(solution)/shard_map/pallas_call | solution.py:361
  42.8 1.5 %collective-permute-done.19.source_ref = bf16[256,256]{1,0:T(8,128)(2,1)S(1)} collective-permute-done((bf16[256,256]{1,0:T(8,128)(2,1)S(1)}, bf16[256,256]{1,0:T(8,128)(2,1)S(1)}, u32[]{:S(2)}, u32[]{:S(2)}) %collective-permute-start.19) | collective-permute-done | bytes 131104 | tf_op jit(solution)/shard_map/ppermute | solution.py:374
  44.3 0.1 collective-permute-start.20
  44.4 1.4 %collective-permute-done.17.refs_2_ = bf16[256,256]{1,0:T(8,128)(2,1)S(1)} collective-permute-done((bf16[256,256]{1,0:T(8,128)(2,1)S(1)}, bf16[256,256]{1,0:T(8,128)(2,1)S(1)}, u32[]{:S(2)}, u32[]{:S(2)}) %collective-permute-start.17) | collective-permute-done | bytes 131104 | tf_op jit(solution)/shard_map/ppermute | solution.py:374
  45.8 0.5 %collective-permute-done.15.refs_1_ = bf16[256,256]{1,0:T(8,128)(2,1)S(1)} collective-permute-done((bf16[256,256]{1,0:T(8,128)(2,1)S(1)}, bf16[256,256]{1,0:T(8,128)(2,1)S(1)}, u32[]{:S(2)}, u32[]{:S(2)}) %collective-permute-start.15) | collective-permute-done | bytes 131104 | tf_op jit(solution)/shard_map/ppermute | solution.py:374
  46.3 0.0 collective-permute-start.16
  46.3 1.0 %shard_map.232 = (f32[256,256]{1,0:T(8,128)}, f32[256,256]{1,0:T(8,128)}, f32[256,256]{1,0:T(8,128)}, f32[256,256]{1,0:T(8,128)}, f32[256,512]{1,0:T(8,128)}, /*index=5*/f32[512,256]{1,0:T(8,128)}) custom-call(bf16[256,256]{1,0:T(8,128)(2,1)S(1)} %shard_map.230.refs_0_, bf16[256,256]{1,0:T(8,128)(2,1)S(1)} %collective-permute-done.15.refs_1_, ...), custom_call_target="tpu_custom_call" | custom-call | tf_op jit(solution)/shard_map/pallas_call | solution.py:552
  47.4 0.3 collective-permute-done.16.refs_1_
  47.6 1.0 %shard_map.233 = (f32[256,256]{1,0:T(8,128)}, f32[256,256]{1,0:T(8,128)}, f32[256,256]{1,0:T(8,128)}, f32[256,256]{1,0:T(8,128)}, f32[256,512]{1,0:T(8,128)}, /*index=5*/f32[512,256]{1,0:T(8,128)}) custom-call(bf16[256,256]{1,0:T(8,128)(2,1)S(1)} %collective-permute-done.14.refs_0_, ...), custom_call_target="tpu_custom_call", output_to_operand_aliasing={{0}: (4, {}), {1}: (5, {}), {2}: (6, {}), {3}: (7, {}), {4}... | custom-call | tf_op jit(solution)/shard_map/pallas_call | solution.py:552
  (34 shorter events, 0.2 us)
Async XLA Ops:
  0.6 7.3 %copy-start.6 = (bf16[1,128,256]{2,1,0:T(8,128)(2,1)S(1)}, bf16[1,128,256]{2,1,0:T(8,128)(2,1)}, u32[]{:S(2)}) copy-start(bf16[1,128,256]{2,1,0:T(8,128)(2,1)} %param.16) | copy-start | bytes 196612
  0.7 7.3 %copy-start.7 = (bf16[1,128,256]{2,1,0:T(8,128)(2,1)S(1)}, bf16[1,128,256]{2,1,0:T(8,128)(2,1)}, u32[]{:S(2)}) copy-start(bf16[1,128,256]{2,1,0:T(8,128)(2,1)} %param.15) | copy-start | bytes 196612
  0.7 8.6 %collective-permute-start.2 = (bf16[128,256]{1,0:T(8,128)(2,1)}, bf16[128,256]{1,0:T(8,128)(2,1)S(1)}, u32[]{:S(2)}, u32[]{:S(2)}) collective-permute-start(bf16[128,256]{1,0:T(8,128)(2,1)} %bitcast.10), channel_id=1, source_target_pairs={{0,16},{4,20},{8,24},{12,28},{16,0},{20,4},{24,8},{28,12},{1,17},{... | collective-permute-start | bytes 196616 | tf_op jit(solution)/shard_map/ppermute | solution.py:407
  4.8 4.5 %collective-permute-start.1 = (bf16[128,256]{1,0:T(8,128)(2,1)}, bf16[128,256]{1,0:T(8,128)(2,1)S(1)}, u32[]{:S(2)}, u32[]{:S(2)}) collective-permute-start(bf16[128,256]{1,0:T(8,128)(2,1)} %bitcast.11), channel_id=1, source_target_pairs={{0,8},{4,12},{8,0},{12,4},{16,24},{20,28},{24,16},{28,20},{1,9},{5... | collective-permute-start | bytes 196616 | tf_op jit(solution)/shard_map/ppermute | solution.py:407
  6.3 4.5 %collective-permute-start = (bf16[128,256]{1,0:T(8,128)(2,1)}, bf16[128,256]{1,0:T(8,128)(2,1)S(1)}, u32[]{:S(2)}, u32[]{:S(2)}) collective-permute-start(bf16[128,256]{1,0:T(8,128)(2,1)} %bitcast.12), channel_id=1, source_target_pairs={{0,4},{4,0},{8,12},{12,8},{16,20},{20,16},{24,28},{28,24},{1,5},{5... | collective-permute-start | bytes 196616 | tf_op jit(solution)/shard_map/ppermute | solution.py:407
  7.9 0.7 %copy-start.10 = (f32[256]{0:T(256)S(1)}, f32[256]{0:T(256)}, u32[]{:S(2)}) copy-start(f32[256]{0:T(256)} %param.22) | copy-start | bytes 3076
  7.9 0.7 %copy-start.12 = (f32[4]{0:T(128)S(1)}, f32[4]{0:T(128)}, u32[]{:S(2)}) copy-start(f32[4]{0:T(128)} %far_ref.1) | copy-start | bytes 52
  7.9 0.7 %copy-start.8 = (s32[1,4,1,128]{3,2,1,0:T(1,128)S(1)}, s32[1,4,1,128]{3,2,1,0:T(1,128)}, u32[]{:S(2)}) copy-start(s32[1,4,1,128]{3,2,1,0:T(1,128)} %param.27) | copy-start | bytes 6148
  7.9 0.7 %copy-start.9 = (f32[256]{0:T(256)S(1)}, f32[256]{0:T(256)}, u32[]{:S(2)}) copy-start(f32[256]{0:T(256)} %param.17) | copy-start | bytes 3076
  7.9 0.7 %copy-start.11 = (f32[4]{0:T(128)S(1)}, f32[4]{0:T(128)}, u32[]{:S(2)}) copy-start(f32[4]{0:T(128)} %local_ref.1) | copy-start | bytes 52
  8.6 2.2 %copy-start = (bf16[256,512]{1,0:T(8,128)(2,1)S(1)}, bf16[256,512]{1,0:T(8,128)(2,1)}, u32[]{:S(2)}) copy-start(bf16[256,512]{1,0:T(8,128)(2,1)} %refs_11_.1) | copy-start | bytes 786436
  8.6 2.2 %copy-start.1 = (bf16[512,256]{1,0:T(8,128)(2,1)S(1)}, bf16[512,256]{1,0:T(8,128)(2,1)}, u32[]{:S(2)}) copy-start(bf16[512,256]{1,0:T(8,128)(2,1)} %refs_12_.1) | copy-start | bytes 786436
  8.6 2.2 %copy-start.2 = (bf16[256,256]{1,0:T(8,128)(2,1)S(1)}, bf16[256,256]{1,0:T(8,128)(2,1)}, u32[]{:S(2)}) copy-start(bf16[256,256]{1,0:T(8,128)(2,1)} %refs_6_.1) | copy-start | bytes 393220
  8.6 2.2 %copy-start.3 = (bf16[256,256]{1,0:T(8,128)(2,1)S(1)}, bf16[256,256]{1,0:T(8,128)(2,1)}, u32[]{:S(2)}) copy-start(bf16[256,256]{1,0:T(8,128)(2,1)} %refs_7_.1) | copy-start | bytes 393220
  8.6 2.2 %copy-start.4 = (bf16[256,256]{1,0:T(8,128)(2,1)S(1)}, bf16[256,256]{1,0:T(8,128)(2,1)}, u32[]{:S(2)}) copy-start(bf16[256,256]{1,0:T(8,128)(2,1)} %refs_8_.1) | copy-start | bytes 393220
  8.6 2.2 %copy-start.5 = (bf16[256,256]{1,0:T(8,128)(2,1)S(1)}, bf16[256,256]{1,0:T(8,128)(2,1)}, u32[]{:S(2)}) copy-start(bf16[256,256]{1,0:T(8,128)(2,1)} %refs_9_.1) | copy-start | bytes 393220
  14.4 2.0 %collective-permute-start.4 = (bf16[528,256]{1,0:T(8,128)(2,1)S(1)}, bf16[528,256]{1,0:T(8,128)(2,1)S(1)}, u32[]{:S(2)}, u32[]{:S(2)}) collective-permute-start(bf16[528,256]{1,0:T(8,128)(2,1)S(1)} %get-tuple-element.67.sents_ref), channel_id=1, source_target_pairs={{0,1},{1,0},{2,3},{3,2},{4,5},{5,4},{6,7},{7,6},{8,9},{9,8},{10,11... | collective-permute-start | bytes 811016 | tf_op jit(solution)/shard_map/ppermute | solution.py:374
  14.5 1.9 %collective-permute-start.3 = (bf16[512,256]{1,0:T(8,128)(2,1)S(1)}, bf16[512,256]{1,0:T(8,128)(2,1)S(1)}, u32[]{:S(2)}, u32[]{:S(2)}) collective-permute-start(bf16[512,256]{1,0:T(8,128)(2,1)S(1)} %get-tuple-element.65), channel_id=1, source_target_pairs={{0,1},{1,0},{2,3},{3,2},{4,5},{5,4},{6,7},{7,6},{8,9},{9,8},{10,11... | collective-permute-start | bytes 786440 | tf_op jit(solution)/shard_map/ppermute | solution.py:374
  16.5 10.2 %collective-permute-start.6 = (bf16[400,256]{1,0:T(8,128)(2,1)S(1)}, bf16[400,256]{1,0:T(8,128)(2,1)S(1)}, u32[]{:S(2)}, u32[]{:S(2)}) collective-permute-start(bf16[400,256]{1,0:T(8,128)(2,1)S(1)} %get-tuple-element.73), channel_id=1, source_target_pairs={{0,4},{1,5},{2,6},{3,7},{4,0},{5,1},{6,2},{7,3},{8,12},{9,13},{10,... | collective-permute-start | bytes 614408 | tf_op jit(solution)/shard_map/ppermute | solution.py:374
  18.1 7.6 %collective-permute-start.5 = (bf16[272,256]{1,0:T(8,128)(2,1)S(1)}, bf16[272,256]{1,0:T(8,128)(2,1)S(1)}, u32[]{:S(2)}, u32[]{:S(2)}) collective-permute-start(bf16[272,256]{1,0:T(8,128)(2,1)S(1)} %get-tuple-element.72), channel_id=1, source_target_pairs={{0,2},{1,3},{2,0},{3,1},{4,6},{5,7},{6,4},{7,5},{8,10},{9,11},{10,... | collective-permute-start | bytes 417800 | tf_op jit(solution)/shard_map/ppermute | solution.py:374
  19.6 7.0 %collective-permute-start.7 = (bf16[272,256]{1,0:T(8,128)(2,1)S(1)}, bf16[272,256]{1,0:T(8,128)(2,1)S(1)}, u32[]{:S(2)}, u32[]{:S(2)}) collective-permute-start(bf16[272,256]{1,0:T(8,128)(2,1)S(1)} %get-tuple-element.74), channel_id=1, source_target_pairs={{0,6},{1,7},{2,4},{3,5},{4,2},{5,3},{6,0},{7,1},{8,14},{9,15},{10,... | collective-permute-start | bytes 417800 | tf_op jit(solution)/shard_map/ppermute | solution.py:374
  20.1 4.4 %collective-permute-start.8 = (bf16[128,256]{1,0:T(8,128)(2,1)S(1)}, bf16[128,256]{1,0:T(8,128)(2,1)S(1)}, u32[]{:S(2)}, u32[]{:S(2)}) collective-permute-start(bf16[128,256]{1,0:T(8,128)(2,1)S(1)} %get-tuple-element.75), channel_id=1, source_target_pairs={{0,8},{4,12},{8,0},{12,4},{16,24},{20,28},{24,16},{28,20},{1,9},{5... | collective-permute-start | bytes 196616 | tf_op jit(solution)/shard_map/ppermute | solution.py:407
  20.5 5.2 %collective-permute-start.9 = (bf16[128,256]{1,0:T(8,128)(2,1)S(1)}, bf16[128,256]{1,0:T(8,128)(2,1)S(1)}, u32[]{:S(2)}, u32[]{:S(2)}) collective-permute-start(bf16[128,256]{1,0:T(8,128)(2,1)S(1)} %get-tuple-element.76), channel_id=1, source_target_pairs={{0,16},{4,20},{8,24},{12,28},{16,0},{20,4},{24,8},{28,12},{1,17},{... | collective-permute-start | bytes 196616 | tf_op jit(solution)/shard_map/ppermute | solution.py:407
  26.8 6.2 %collective-permute-start.10 = (bf16[144,256]{1,0:T(8,128)(2,1)S(1)}, bf16[144,256]{1,0:T(8,128)(2,1)S(1)}, u32[]{:S(2)}, u32[]{:S(2)}) collective-permute-start(bf16[144,256]{1,0:T(8,128)(2,1)S(1)} %get-tuple-element.77.refs_0_.own_ref), channel_id=1, source_target_pairs={{0,16},{1,9},{2,18},{3,11},{4,20},{5,13},{6,22},{7,15},{8,24},{9,1... | collective-permute-start | bytes 221192 | tf_op jit(solution)/shard_map/ppermute | solution.py:374
  27.2 4.3 %collective-permute-start.11 = (bf16[128,256]{1,0:T(8,128)(2,1)S(1)}, bf16[128,256]{1,0:T(8,128)(2,1)S(1)}, u32[]{:S(2)}, u32[]{:S(2)}) collective-permute-start(bf16[128,256]{1,0:T(8,128)(2,1)S(1)} %get-tuple-element.78.own_ref), channel_id=1, source_target_pairs={{0,8},{1,17},{2,10},{3,19},{4,12},{5,21},{6,14},{7,23},{8,0},{9,25... | collective-permute-start | bytes 196616 | tf_op jit(solution)/shard_map/ppermute | solution.py:374
  32.9 5.3 %collective-permute-start.12 = (bf16[144,256]{1,0:T(8,128)(2,1)S(1)}, bf16[144,256]{1,0:T(8,128)(2,1)S(1)}, u32[]{:S(2)}, u32[]{:S(2)}) collective-permute-start(bf16[144,256]{1,0:T(8,128)(2,1)S(1)} %shard_map.226.refs_0_.own_ref), channel_id=1, source_target_pairs={{0,8},{1,17},{2,10},{3,19},{4,12},{5,21},{6,14},{7,23},{8,0},{9,25... | collective-permute-start | bytes 221192 | tf_op jit(solution)/shard_map/ppermute | solution.py:374
  33.0 5.2 %collective-permute-start.13 = (bf16[128,256]{1,0:T(8,128)(2,1)S(1)}, bf16[128,256]{1,0:T(8,128)(2,1)S(1)}, u32[]{:S(2)}, u32[]{:S(2)}) collective-permute-start(bf16[128,256]{1,0:T(8,128)(2,1)S(1)} %shard_map.225.refs_0_.own_ref), channel_id=1, source_target_pairs={{0,16},{1,9},{2,18},{3,11},{4,20},{5,13},{6,22},{7,15},{8,24},{9,1... | collective-permute-start | bytes 196616 | tf_op jit(solution)/shard_map/ppermute | solution.py:374
  38.3 5.9 %collective-permute-start.19 = (bf16[256,256]{1,0:T(8,128)(2,1)S(1)}, bf16[256,256]{1,0:T(8,128)(2,1)S(1)}, u32[]{:S(2)}, u32[]{:S(2)}) collective-permute-start(bf16[256,256]{1,0:T(8,128)(2,1)S(1)} %shard_map.230.refs_0_), channel_id=1, source_target_pairs={{0,6},{1,7},{2,4},{3,5},{4,2},{5,3},{6,0},{7,1},{8,14},{9,15},{10,... | collective-permute-start | bytes 393224 | tf_op jit(solution)/shard_map/ppermute | solution.py:374
  40.8 5.0 %collective-permute-start.17 = (bf16[256,256]{1,0:T(8,128)(2,1)S(1)}, bf16[256,256]{1,0:T(8,128)(2,1)S(1)}, u32[]{:S(2)}, u32[]{:S(2)}) collective-permute-start(bf16[256,256]{1,0:T(8,128)(2,1)S(1)} %shard_map.230.refs_0_), channel_id=1, source_target_pairs={{0,4},{1,5},{2,6},{3,7},{4,0},{5,1},{6,2},{7,3},{8,12},{9,13},{10,... | collective-permute-start | bytes 393224 | tf_op jit(solution)/shard_map/ppermute | solution.py:374
  41.3 5.0 %collective-permute-start.15 = (bf16[256,256]{1,0:T(8,128)(2,1)S(1)}, bf16[256,256]{1,0:T(8,128)(2,1)S(1)}, u32[]{:S(2)}, u32[]{:S(2)}) collective-permute-start(bf16[256,256]{1,0:T(8,128)(2,1)S(1)} %shard_map.230.refs_0_), channel_id=1, source_target_pairs={{0,2},{1,3},{2,0},{3,1},{4,6},{5,7},{6,4},{7,5},{8,10},{9,11},{10,... | collective-permute-start | bytes 393224 | tf_op jit(solution)/shard_map/ppermute | solution.py:374
  41.9 5.5 %collective-permute-start.14 = (bf16[256,256]{1,0:T(8,128)(2,1)S(1)}, bf16[256,256]{1,0:T(8,128)(2,1)S(1)}, u32[]{:S(2)}, u32[]{:S(2)}) collective-permute-start(bf16[256,256]{1,0:T(8,128)(2,1)S(1)} %shard_map.230.refs_0_), channel_id=1, source_target_pairs={{0,1},{1,0},{2,3},{3,2},{4,5},{5,4},{6,7},{7,6},{8,9},{9,8},{10,11... | collective-permute-start | bytes 393224 | tf_op jit(solution)/shard_map/ppermute | solution.py:374
  44.3 3.1 %collective-permute-start.20 = (bf16[256,256]{1,0:T(8,128)(2,1)S(1)}, bf16[256,256]{1,0:T(8,128)(2,1)S(1)}, u32[]{:S(2)}, u32[]{:S(2)}) collective-permute-start(bf16[256,256]{1,0:T(8,128)(2,1)S(1)} %shard_map.231.refs_3_), channel_id=1, source_target_pairs={{0,1},{1,0},{2,3},{3,2},{4,5},{5,4},{6,7},{7,6},{8,9},{9,8},{10,11... | collective-permute-start | bytes 393224 | tf_op jit(solution)/shard_map/ppermute | solution.py:374
  45.8 1.6 %collective-permute-start.18 = (bf16[256,256]{1,0:T(8,128)(2,1)S(1)}, bf16[256,256]{1,0:T(8,128)(2,1)S(1)}, u32[]{:S(2)}, u32[]{:S(2)}) collective-permute-start(bf16[256,256]{1,0:T(8,128)(2,1)S(1)} %collective-permute-done.17.refs_2_), channel_id=1, source_target_pairs={{0,1},{1,0},{2,3},{3,2},{4,5},{5,4},{6,7},{7,6},{8,9},{9,8},{10,11... | collective-permute-start | bytes 393224 | tf_op jit(solution)/shard_map/ppermute | solution.py:374
  46.3 1.3 %collective-permute-start.16 = (bf16[256,256]{1,0:T(8,128)(2,1)S(1)}, bf16[256,256]{1,0:T(8,128)(2,1)S(1)}, u32[]{:S(2)}, u32[]{:S(2)}) collective-permute-start(bf16[256,256]{1,0:T(8,128)(2,1)S(1)} %collective-permute-done.15.refs_1_), channel_id=1, source_target_pairs={{0,1},{1,0},{2,3},{3,2},{4,5},{5,4},{6,7},{7,6},{8,9},{9,8},{10,11... | collective-permute-start | bytes 393224 | tf_op jit(solution)/shard_map/ppermute | solution.py:374

commit v9 on v8

--- a/solution.py
+++ b/solution.py
@@ -200,7 +200,7 @@
     grad_up = dot_lhs_t(hidden2, grad_pre)
     wide_s[0 * width : 1 * width, :] = grad_up[:, :width].astype(BF16)
     wide_s[1 * width : 2 * width, :] = grad_up[:, width:].astype(BF16)
-    square_s[3 * width : 4 * width, :] = dot_lhs_t(attended, grad_mixed16).astype(BF16)
+    sort_units(wide_s, sendw_ref, bits)
     local_terms = []
     far_terms = []
     for h in range(heads):
@@ -215,6 +215,7 @@
         far_terms.append(jnp.sum(terms[:, rows:], axis=1, keepdims=True))
         dscore_s[block, :] = (sloped * (scale_ref[h : h + 1, :] * scale)).astype(BF16)
 
+    square_s[3 * width : 4 * width, :] = dot_lhs_t(attended, grad_mixed16).astype(BF16)
     grad_query = collapse(dot(dscore_s[...], key_all), head_masks).astype(BF16)
     grad_key = dot_lhs_t(dscore_s[...], query_stack).astype(BF16)
     grad_value = dot_lhs_t(weight_s[...], grad_stack).astype(BF16)
@@ -240,7 +241,6 @@
     line = lax.broadcasted_iota(jnp.int32, (SMALL // 2, width), 0)
     small = jnp.where(line == 0, grad_gain1, jnp.where(line == 1, grad_gain2, jnp.where(line == 2, gains, 0.0)))
     sends_ref[sendw_ref.shape[0] :, :] = split_parts(small)
-    sort_units(wide_s, sendw_ref, bits)
     sort_units(square_s, sends_ref, bits)
 
 
@@ -410,7 +410,7 @@
     high_bits = [1 << k for k in range(3, size.bit_length() - 1)]
     flat = {1 << (b + rep_bits): k for k, b in enumerate(bits)}
     quad_slots = [flat.get(bit) for bit in (2, 4, 6)]
-    orders = (list(zip(high_bits, high_bits[::-1])), list(zip(high_bits[::-1], high_bits)))
+    orders = (list(zip(high_bits, high_bits)), list(zip(high_bits[::-1], high_bits[::-1])))
     apart = [k for bit, k in flat.items() if bit > 4]
     slots = [(k, k) for k in quad_slots if k is not None]
     slots += [(k, k) for k in apart]

time: 48.8 us -> 48.8 us (level)
  no operation moved by 1% of the time
where the time goes in v9:
time: 48.8 us; the launch traced here: 48.7 us
  starting transfers between devices  21.1 us (43%)
  waiting for transfers between devices  18.5 us (38%)
  Pallas kernels  7.5 us (15%)
  between operations  0.89 us (2%)
  local copies, waits for them, and re-layouts  0.72 us (1%)
    ppermute x16, waiting for transfers between devices, flipped(): return lax.ppermute(x, AXES, pairs)  13.1 us
    ppermute x16, starting transfers between devices, flipped(): return lax.ppermute(x, AXES, pairs)  12.1 us
    ppermute x5, starting transfers between devices, swapped(): lax.ppermute(x, 'dom', [(i, i ^ 1 << bit) for i in range(lax.axis_size('d...  8.97 us
    pallas_call x12, Pallas kernels, call(): pl.pallas_call(kernel, out_shape=outs, in_specs=in_specs or [VM] * len(ar...  5.41 us
    ppermute x5, waiting for transfers between devices, swapped(): lax.ppermute(x, 'dom', [(i, i ^ 1 << bit) for i in range(lax.axis_size('d...  5.34 us
    pallas_call x2, Pallas kernels, local(): pl.pallas_call(functools.partial(spread_kernel, own), out_shape=tuple((st...  2.09 us
  transfers between devices with their start and end apart: 21, of which 13 were waited for; matrix products, arithmetic and copies ran while one was open for 0% of the time, Pallas kernels for 5%

profile of v9, /device:TPU:0, one launch (start us, length us, event | category | flops | bytes accessed | tf_op | source)
XLA Modules:
  0.0 48.7 jit_solution(13020435841316059807)
XLA Ops:
  0.7 4.1 %collective-permute-start.2 = (bf16[128,256]{1,0:T(8,128)(2,1)}, bf16[128,256]{1,0:T(8,128)(2,1)S(1)}, u32[]{:S(2)}, u32[]{:S(2)}) collective-permute-start(bf16[128,256]{1,0:T(8,128)(2,1)} %bitcast.10), channel_id=1, source_target_pairs={{0,16},{4,20},{8,24},{12,28},{16,0},{20,4},{24,8},{28,12},{1,17},{... | collective-permute-start | bytes 196616 | tf_op jit(solution)/shard_map/ppermute | solution.py:407
  4.8 1.6 %collective-permute-start.1 = (bf16[128,256]{1,0:T(8,128)(2,1)}, bf16[128,256]{1,0:T(8,128)(2,1)S(1)}, u32[]{:S(2)}, u32[]{:S(2)}) collective-permute-start(bf16[128,256]{1,0:T(8,128)(2,1)} %bitcast.11), channel_id=1, source_target_pairs={{0,8},{4,12},{8,0},{12,4},{16,24},{20,28},{24,16},{28,20},{1,9},{5... | collective-permute-start | bytes 196616 | tf_op jit(solution)/shard_map/ppermute | solution.py:407
  6.3 1.5 %collective-permute-start = (bf16[128,256]{1,0:T(8,128)(2,1)}, bf16[128,256]{1,0:T(8,128)(2,1)S(1)}, u32[]{:S(2)}, u32[]{:S(2)}) collective-permute-start(bf16[128,256]{1,0:T(8,128)(2,1)} %bitcast.12), channel_id=1, source_target_pairs={{0,4},{4,0},{8,12},{12,8},{16,20},{20,16},{24,28},{28,24},{1,5},{5... | collective-permute-start | bytes 196616 | tf_op jit(solution)/shard_map/ppermute | solution.py:407
  7.9 0.0 copy-start.9
  7.9 0.0 copy-start.11
  7.9 0.6 %copy-done.10 = f32[256]{0:T(256)S(1)} copy-done((f32[256]{0:T(256)S(1)}, f32[256]{0:T(256)}, u32[]{:S(2)}) %copy-start.10) | copy-done | bytes 1048
  8.5 0.0 copy-done.8
  8.6 0.0 copy-done.9
  8.6 0.0 copy-start.3
  8.6 0.0 copy-start.4
  8.6 0.0 copy-start.5
  8.6 0.7 %shard_map.221 = (f32[128,512]{1,0:T(8,128)S(1)}, f32[8,512]{1,0:T(8,128)S(1)}, bf16[128,256]{1,0:T(8,128)(2,1)S(1)}, bf16[128,256]{1,0:T(8,128)(2,1)S(1)}, f32[1,256]{1,0:T(1,128)S(1)}, /*index=5*/f32[1,256]{1,0:T(1,128)S(1)}) custom-call(f32[8,128]{1,0:T(8,128)S(1)} %shard_map.220.flag_ref, s32[4,128]{1,0:T(4,128)S(1)} %bitcast.14, f32[4]{0:T(128)S(1)} %copy-done.11, ...), custom_call_target="tpu_custom_call" | custom-call | flops 10000000000 | bytes 1 | tf_op jit(solution)/shard_map/pallas_call | solution.py:361
  9.3 0.0 collective-permute-done.2.refs_3_
  9.3 1.5 %collective-permute-done.refs_1_ = bf16[128,256]{1,0:T(8,128)(2,1)S(1)} collective-permute-done((bf16[128,256]{1,0:T(8,128)(2,1)}, bf16[128,256]{1,0:T(8,128)(2,1)S(1)}, u32[]{:S(2)}, u32[]{:S(2)}) %collective-permute-start) | collective-permute-done | bytes 65568 | tf_op jit(solution)/shard_map/ppermute | solution.py:407
  10.9 3.5 %shard_map.222 = (bf16[128,256]{1,0:T(8,128)(2,1)S(1)}, bf16[1024,256]{1,0:T(8,128)(2,1)S(1)}, bf16[512,256]{1,0:T(8,128)(2,1)S(1)}, bf16[1024,256]{1,0:T(8,128)...) custom-call(bf16[128,256]{1,0:T(8,128)(2,1)S(1)} %get-tuple-element., ...), custom_call_target="tpu_custom_call" | custom-call | tf_op jit(solution)/shard_map/pallas_call | solution.py:361
  14.4 0.1 collective-permute-start.4
  14.5 0.5 %collective-permute-start.3 = (bf16[512,256]{1,0:T(8,128)(2,1)S(1)}, bf16[512,256]{1,0:T(8,128)(2,1)S(1)}, u32[]{:S(2)}, u32[]{:S(2)}) collective-permute-start(bf16[512,256]{1,0:T(8,128)(2,1)S(1)} %get-tuple-element.65), channel_id=1, source_target_pairs={{0,1},{1,0},{2,3},{3,2},{4,5},{5,4},{6,7},{7,6},{8,9},{9,8},{10,11... | collective-permute-start | bytes 786440 | tf_op jit(solution)/shard_map/ppermute | solution.py:374
  15.0 1.4 %collective-permute-done.3.recvw_ref = bf16[512,256]{1,0:T(8,128)(2,1)S(1)} collective-permute-done((bf16[512,256]{1,0:T(8,128)(2,1)S(1)}, bf16[512,256]{1,0:T(8,128)(2,1)S(1)}, u32[]{:S(2)}, u32[]{:S(2)}) %collective-permute-start.3) | collective-permute-done | bytes 262176 | tf_op jit(solution)/shard_map/ppermute | solution.py:374
  16.4 0.1 shard_map.223
  16.5 1.6 %collective-permute-start.6 = (bf16[400,256]{1,0:T(8,128)(2,1)S(1)}, bf16[400,256]{1,0:T(8,128)(2,1)S(1)}, u32[]{:S(2)}, u32[]{:S(2)}) collective-permute-start(bf16[400,256]{1,0:T(8,128)(2,1)S(1)} %get-tuple-element.73), channel_id=1, source_target_pairs={{0,4},{1,5},{2,6},{3,7},{4,0},{5,1},{6,2},{7,3},{8,12},{9,13},{10,... | collective-permute-start | bytes 614408 | tf_op jit(solution)/shard_map/ppermute | solution.py:374
  18.1 1.5 %collective-permute-start.5 = (bf16[272,256]{1,0:T(8,128)(2,1)S(1)}, bf16[272,256]{1,0:T(8,128)(2,1)S(1)}, u32[]{:S(2)}, u32[]{:S(2)}) collective-permute-start(bf16[272,256]{1,0:T(8,128)(2,1)S(1)} %get-tuple-element.72), channel_id=1, source_target_pairs={{0,2},{1,3},{2,0},{3,1},{4,6},{5,7},{6,4},{7,5},{8,10},{9,11},{10,... | collective-permute-start | bytes 417800 | tf_op jit(solution)/shard_map/ppermute | solution.py:374
  19.6 0.5 collective-permute-start.7
  20.1 0.4 collective-permute-start.8
  20.5 1.3 %collective-permute-start.9 = (bf16[128,256]{1,0:T(8,128)(2,1)S(1)}, bf16[128,256]{1,0:T(8,128)(2,1)S(1)}, u32[]{:S(2)}, u32[]{:S(2)}) collective-permute-start(bf16[128,256]{1,0:T(8,128)(2,1)S(1)} %get-tuple-element.76), channel_id=1, source_target_pairs={{0,16},{4,20},{8,24},{12,28},{16,0},{20,4},{24,8},{28,12},{1,17},{... | collective-permute-start | bytes 196616 | tf_op jit(solution)/shard_map/ppermute | solution.py:407
  21.9 2.6 %collective-permute-done.8.refs_0_.refs_7_ = bf16[128,256]{1,0:T(8,128)(2,1)S(1)} collective-permute-done((bf16[128,256]{1,0:T(8,128)(2,1)S(1)}, bf16[128,256]{1,0:T(8,128)(2,1)S(1)}, u32[]{:S(2)}, u32[]{:S(2)}) %collective-permute-start.8) | collective-permute-done | bytes 65568 | tf_op jit(solution)/shard_map/ppermute | solution.py:407
  24.4 1.3 %collective-permute-done.9.refs_1_.refs_8_ = bf16[128,256]{1,0:T(8,128)(2,1)S(1)} collective-permute-done((bf16[128,256]{1,0:T(8,128)(2,1)S(1)}, bf16[128,256]{1,0:T(8,128)(2,1)S(1)}, u32[]{:S(2)}, u32[]{:S(2)}) %collective-permute-start.9) | collective-permute-done | bytes 65568 | tf_op jit(solution)/shard_map/ppermute | solution.py:407
  25.7 0.9 %collective-permute-done.7.three_ref = bf16[272,256]{1,0:T(8,128)(2,1)S(1)} collective-permute-done((bf16[272,256]{1,0:T(8,128)(2,1)S(1)}, bf16[272,256]{1,0:T(8,128)(2,1)S(1)}, u32[]{:S(2)}, u32[]{:S(2)}) %collective-permute-start.7) | collective-permute-done | bytes 139296 | tf_op jit(solution)/shard_map/ppermute | solution.py:374
  26.6 0.1 collective-permute-done.6.two_ref.refs_6_
  26.7 0.1 shard_map.224
  26.8 0.4 collective-permute-start.10
  27.2 1.4 %collective-permute-start.11 = (bf16[128,256]{1,0:T(8,128)(2,1)S(1)}, bf16[128,256]{1,0:T(8,128)(2,1)S(1)}, u32[]{:S(2)}, u32[]{:S(2)}) collective-permute-start(bf16[128,256]{1,0:T(8,128)(2,1)S(1)} %get-tuple-element.78.own_ref), channel_id=1, source_target_pairs={{0,8},{1,9},{2,10},{3,11},{4,12},{5,13},{6,14},{7,15},{8,0},{9,1},... | collective-permute-start | bytes 196616 | tf_op jit(solution)/shard_map/ppermute | solution.py:374
  28.6 3.2 %collective-permute-done.11.recv_ref = bf16[128,256]{1,0:T(8,128)(2,1)S(1)} collective-permute-done((bf16[128,256]{1,0:T(8,128)(2,1)S(1)}, bf16[128,256]{1,0:T(8,128)(2,1)S(1)}, u32[]{:S(2)}, u32[]{:S(2)}) %collective-permute-start.11) | collective-permute-done | bytes 65568 | tf_op jit(solution)/shard_map/ppermute | solution.py:374
  31.8 1.1 %collective-permute-done.10.recv_ref = bf16[144,256]{1,0:T(8,128)(2,1)S(1)} collective-permute-done((bf16[144,256]{1,0:T(8,128)(2,1)S(1)}, bf16[144,256]{1,0:T(8,128)(2,1)S(1)}, u32[]{:S(2)}, u32[]{:S(2)}) %collective-permute-start.10) | collective-permute-done | bytes 73760 | tf_op jit(solution)/shard_map/ppermute | solution.py:374
  32.9 0.1 collective-permute-start.12
  33.0 2.4 %collective-permute-start.13 = (bf16[128,256]{1,0:T(8,128)(2,1)S(1)}, bf16[128,256]{1,0:T(8,128)(2,1)S(1)}, u32[]{:S(2)}, u32[]{:S(2)}) collective-permute-start(bf16[128,256]{1,0:T(8,128)(2,1)S(1)} %shard_map.225.refs_0_.own_ref), channel_id=1, source_target_pairs={{0,16},{1,17},{2,18},{3,19},{4,20},{5,21},{6,22},{7,23},{8,24},{9,... | collective-permute-start | bytes 196616 | tf_op jit(solution)/shard_map/ppermute | solution.py:374
  35.4 2.8 %collective-permute-done.13.recv_ref = bf16[128,256]{1,0:T(8,128)(2,1)S(1)} collective-permute-done((bf16[128,256]{1,0:T(8,128)(2,1)S(1)}, bf16[128,256]{1,0:T(8,128)(2,1)S(1)}, u32[]{:S(2)}, u32[]{:S(2)}) %collective-permute-start.13) | collective-permute-done | bytes 65568 | tf_op jit(solution)/shard_map/ppermute | solution.py:374
  38.3 2.5 %collective-permute-start.19 = (bf16[256,256]{1,0:T(8,128)(2,1)S(1)}, bf16[256,256]{1,0:T(8,128)(2,1)S(1)}, u32[]{:S(2)}, u32[]{:S(2)}) collective-permute-start(bf16[256,256]{1,0:T(8,128)(2,1)S(1)} %shard_map.230.refs_0_), channel_id=1, source_target_pairs={{0,6},{1,7},{2,4},{3,5},{4,2},{5,3},{6,0},{7,1},{8,14},{9,15},{10,... | collective-permute-start | bytes 393224 | tf_op jit(solution)/shard_map/ppermute | solution.py:374
  40.8 0.5 %collective-permute-start.17 = (bf16[256,256]{1,0:T(8,128)(2,1)S(1)}, bf16[256,256]{1,0:T(8,128)(2,1)S(1)}, u32[]{:S(2)}, u32[]{:S(2)}) collective-permute-start(bf16[256,256]{1,0:T(8,128)(2,1)S(1)} %shard_map.230.refs_0_), channel_id=1, source_target_pairs={{0,4},{1,5},{2,6},{3,7},{4,0},{5,1},{6,2},{7,3},{8,12},{9,13},{10,... | collective-permute-start | bytes 393224 | tf_op jit(solution)/shard_map/ppermute | solution.py:374
  41.3 0.5 %collective-permute-start.15 = (bf16[256,256]{1,0:T(8,128)(2,1)S(1)}, bf16[256,256]{1,0:T(8,128)(2,1)S(1)}, u32[]{:S(2)}, u32[]{:S(2)}) collective-permute-start(bf16[256,256]{1,0:T(8,128)(2,1)S(1)} %shard_map.230.refs_0_), channel_id=1, source_target_pairs={{0,2},{1,3},{2,0},{3,1},{4,6},{5,7},{6,4},{7,5},{8,10},{9,11},{10,... | collective-permute-start | bytes 393224 | tf_op jit(solution)/shard_map/ppermute | solution.py:374
  41.8 0.9 %shard_map.229 = (bf16[128,256]{1,0:T(8,128)(2,1)}, bf16[128,256]{1,0:T(8,128)(2,1)}, f32[1,256]{1,0:T(1,128)}, f32[1,256]{1,0:T(1,128)}, f32[4]{0:T(128)}, /*index=5*/f32[4]{0:T(128)}, f32[8,128]{1,0:T(8,128)S(1)}) custom-call(bf16[128,256]{1,0:T(8,128)(2,1)S(1)} %get-tuple-element.55.refs_0_, bf16[128,256]{1,0:T(8,128)(2,1)S(1)} %get-tuple-element.61.refs_1_, ...), custom_call_target="tpu_custom_call" | custom-call | tf_op jit(solution)/shard_map/pallas_call | solution.py:361
  42.8 1.5 %collective-permute-done.19.source_ref = bf16[256,256]{1,0:T(8,128)(2,1)S(1)} collective-permute-done((bf16[256,256]{1,0:T(8,128)(2,1)S(1)}, bf16[256,256]{1,0:T(8,128)(2,1)S(1)}, u32[]{:S(2)}, u32[]{:S(2)}) %collective-permute-start.19) | collective-permute-done | bytes 131104 | tf_op jit(solution)/shard_map/ppermute | solution.py:374
  44.2 0.1 collective-permute-start.20
  44.3 1.5 %collective-permute-done.17.refs_2_ = bf16[256,256]{1,0:T(8,128)(2,1)S(1)} collective-permute-done((bf16[256,256]{1,0:T(8,128)(2,1)S(1)}, bf16[256,256]{1,0:T(8,128)(2,1)S(1)}, u32[]{:S(2)}, u32[]{:S(2)}) %collective-permute-start.17) | collective-permute-done | bytes 131104 | tf_op jit(solution)/shard_map/ppermute | solution.py:374
  45.8 0.5 %collective-permute-done.15.refs_1_ = bf16[256,256]{1,0:T(8,128)(2,1)S(1)} collective-permute-done((bf16[256,256]{1,0:T(8,128)(2,1)S(1)}, bf16[256,256]{1,0:T(8,128)(2,1)S(1)}, u32[]{:S(2)}, u32[]{:S(2)}) %collective-permute-start.15) | collective-permute-done | bytes 131104 | tf_op jit(solution)/shard_map/ppermute | solution.py:374
  46.3 0.0 collective-permute-start.16
  46.3 1.0 %shard_map.232 = (f32[256,256]{1,0:T(8,128)}, f32[256,256]{1,0:T(8,128)}, f32[256,256]{1,0:T(8,128)}, f32[256,256]{1,0:T(8,128)}, f32[256,512]{1,0:T(8,128)}, /*index=5*/f32[512,256]{1,0:T(8,128)}) custom-call(bf16[256,256]{1,0:T(8,128)(2,1)S(1)} %shard_map.230.refs_0_, bf16[256,256]{1,0:T(8,128)(2,1)S(1)} %collective-permute-done.15.refs_1_, ...), custom_call_target="tpu_custom_call" | custom-call | tf_op jit(solution)/shard_map/pallas_call | solution.py:552
  47.4 0.2 collective-permute-done.16.refs_1_
  47.6 1.0 %shard_map.233 = (f32[256,256]{1,0:T(8,128)}, f32[256,256]{1,0:T(8,128)}, f32[256,256]{1,0:T(8,128)}, f32[256,256]{1,0:T(8,128)}, f32[256,512]{1,0:T(8,128)}, /*index=5*/f32[512,256]{1,0:T(8,128)}) custom-call(bf16[256,256]{1,0:T(8,128)(2,1)S(1)} %collective-permute-done.14.refs_0_, ...), custom_call_target="tpu_custom_call", output_to_operand_aliasing={{0}: (4, {}), {1}: (5, {}), {2}: (6, {}), {3}: (7, {}), {4}... | custom-call | tf_op jit(solution)/shard_map/pallas_call | solution.py:552
  (34 shorter events, 0.2 us)
Async XLA Ops:
  0.6 7.3 %copy-start.6 = (bf16[1,128,256]{2,1,0:T(8,128)(2,1)S(1)}, bf16[1,128,256]{2,1,0:T(8,128)(2,1)}, u32[]{:S(2)}) copy-start(bf16[1,128,256]{2,1,0:T(8,128)(2,1)} %param.16) | copy-start | bytes 196612
  0.7 7.3 %copy-start.7 = (bf16[1,128,256]{2,1,0:T(8,128)(2,1)S(1)}, bf16[1,128,256]{2,1,0:T(8,128)(2,1)}, u32[]{:S(2)}) copy-start(bf16[1,128,256]{2,1,0:T(8,128)(2,1)} %param.15) | copy-start | bytes 196612
  0.7 8.6 %collective-permute-start.2 = (bf16[128,256]{1,0:T(8,128)(2,1)}, bf16[128,256]{1,0:T(8,128)(2,1)S(1)}, u32[]{:S(2)}, u32[]{:S(2)}) collective-permute-start(bf16[128,256]{1,0:T(8,128)(2,1)} %bitcast.10), channel_id=1, source_target_pairs={{0,16},{4,20},{8,24},{12,28},{16,0},{20,4},{24,8},{28,12},{1,17},{... | collective-permute-start | bytes 196616 | tf_op jit(solution)/shard_map/ppermute | solution.py:407
  4.8 4.5 %collective-permute-start.1 = (bf16[128,256]{1,0:T(8,128)(2,1)}, bf16[128,256]{1,0:T(8,128)(2,1)S(1)}, u32[]{:S(2)}, u32[]{:S(2)}) collective-permute-start(bf16[128,256]{1,0:T(8,128)(2,1)} %bitcast.11), channel_id=1, source_target_pairs={{0,8},{4,12},{8,0},{12,4},{16,24},{20,28},{24,16},{28,20},{1,9},{5... | collective-permute-start | bytes 196616 | tf_op jit(solution)/shard_map/ppermute | solution.py:407
  6.3 4.5 %collective-permute-start = (bf16[128,256]{1,0:T(8,128)(2,1)}, bf16[128,256]{1,0:T(8,128)(2,1)S(1)}, u32[]{:S(2)}, u32[]{:S(2)}) collective-permute-start(bf16[128,256]{1,0:T(8,128)(2,1)} %bitcast.12), channel_id=1, source_target_pairs={{0,4},{4,0},{8,12},{12,8},{16,20},{20,16},{24,28},{28,24},{1,5},{5... | collective-permute-start | bytes 196616 | tf_op jit(solution)/shard_map/ppermute | solution.py:407
  7.9 0.7 %copy-start.10 = (f32[256]{0:T(256)S(1)}, f32[256]{0:T(256)}, u32[]{:S(2)}) copy-start(f32[256]{0:T(256)} %param.22) | copy-start | bytes 3076
  7.9 0.7 %copy-start.12 = (f32[4]{0:T(128)S(1)}, f32[4]{0:T(128)}, u32[]{:S(2)}) copy-start(f32[4]{0:T(128)} %far_ref.1) | copy-start | bytes 52
  7.9 0.7 %copy-start.8 = (s32[1,4,1,128]{3,2,1,0:T(1,128)S(1)}, s32[1,4,1,128]{3,2,1,0:T(1,128)}, u32[]{:S(2)}) copy-start(s32[1,4,1,128]{3,2,1,0:T(1,128)} %param.27) | copy-start | bytes 6148
  7.9 0.7 %copy-start.9 = (f32[256]{0:T(256)S(1)}, f32[256]{0:T(256)}, u32[]{:S(2)}) copy-start(f32[256]{0:T(256)} %param.17) | copy-start | bytes 3076
  7.9 0.7 %copy-start.11 = (f32[4]{0:T(128)S(1)}, f32[4]{0:T(128)}, u32[]{:S(2)}) copy-start(f32[4]{0:T(128)} %local_ref.1) | copy-start | bytes 52
  8.6 2.2 %copy-start = (bf16[256,512]{1,0:T(8,128)(2,1)S(1)}, bf16[256,512]{1,0:T(8,128)(2,1)}, u32[]{:S(2)}) copy-start(bf16[256,512]{1,0:T(8,128)(2,1)} %refs_11_.1) | copy-start | bytes 786436
  8.6 2.2 %copy-start.1 = (bf16[512,256]{1,0:T(8,128)(2,1)S(1)}, bf16[512,256]{1,0:T(8,128)(2,1)}, u32[]{:S(2)}) copy-start(bf16[512,256]{1,0:T(8,128)(2,1)} %refs_12_.1) | copy-start | bytes 786436
  8.6 2.2 %copy-start.2 = (bf16[256,256]{1,0:T(8,128)(2,1)S(1)}, bf16[256,256]{1,0:T(8,128)(2,1)}, u32[]{:S(2)}) copy-start(bf16[256,256]{1,0:T(8,128)(2,1)} %refs_6_.1) | copy-start | bytes 393220
  8.6 2.2 %copy-start.3 = (bf16[256,256]{1,0:T(8,128)(2,1)S(1)}, bf16[256,256]{1,0:T(8,128)(2,1)}, u32[]{:S(2)}) copy-start(bf16[256,256]{1,0:T(8,128)(2,1)} %refs_7_.1) | copy-start | bytes 393220
  8.6 2.2 %copy-start.4 = (bf16[256,256]{1,0:T(8,128)(2,1)S(1)}, bf16[256,256]{1,0:T(8,128)(2,1)}, u32[]{:S(2)}) copy-start(bf16[256,256]{1,0:T(8,128)(2,1)} %refs_8_.1) | copy-start | bytes 393220
  8.6 2.2 %copy-start.5 = (bf16[256,256]{1,0:T(8,128)(2,1)S(1)}, bf16[256,256]{1,0:T(8,128)(2,1)}, u32[]{:S(2)}) copy-start(bf16[256,256]{1,0:T(8,128)(2,1)} %refs_9_.1) | copy-start | bytes 393220
  14.4 2.0 %collective-permute-start.4 = (bf16[528,256]{1,0:T(8,128)(2,1)S(1)}, bf16[528,256]{1,0:T(8,128)(2,1)S(1)}, u32[]{:S(2)}, u32[]{:S(2)}) collective-permute-start(bf16[528,256]{1,0:T(8,128)(2,1)S(1)} %get-tuple-element.67.sents_ref), channel_id=1, source_target_pairs={{0,1},{1,0},{2,3},{3,2},{4,5},{5,4},{6,7},{7,6},{8,9},{9,8},{10,11... | collective-permute-start | bytes 811016 | tf_op jit(solution)/shard_map/ppermute | solution.py:374
  14.5 1.9 %collective-permute-start.3 = (bf16[512,256]{1,0:T(8,128)(2,1)S(1)}, bf16[512,256]{1,0:T(8,128)(2,1)S(1)}, u32[]{:S(2)}, u32[]{:S(2)}) collective-permute-start(bf16[512,256]{1,0:T(8,128)(2,1)S(1)} %get-tuple-element.65), channel_id=1, source_target_pairs={{0,1},{1,0},{2,3},{3,2},{4,5},{5,4},{6,7},{7,6},{8,9},{9,8},{10,11... | collective-permute-start | bytes 786440 | tf_op jit(solution)/shard_map/ppermute | solution.py:374
  16.5 10.2 %collective-permute-start.6 = (bf16[400,256]{1,0:T(8,128)(2,1)S(1)}, bf16[400,256]{1,0:T(8,128)(2,1)S(1)}, u32[]{:S(2)}, u32[]{:S(2)}) collective-permute-start(bf16[400,256]{1,0:T(8,128)(2,1)S(1)} %get-tuple-element.73), channel_id=1, source_target_pairs={{0,4},{1,5},{2,6},{3,7},{4,0},{5,1},{6,2},{7,3},{8,12},{9,13},{10,... | collective-permute-start | bytes 614408 | tf_op jit(solution)/shard_map/ppermute | solution.py:374
  18.1 7.6 %collective-permute-start.5 = (bf16[272,256]{1,0:T(8,128)(2,1)S(1)}, bf16[272,256]{1,0:T(8,128)(2,1)S(1)}, u32[]{:S(2)}, u32[]{:S(2)}) collective-permute-start(bf16[272,256]{1,0:T(8,128)(2,1)S(1)} %get-tuple-element.72), channel_id=1, source_target_pairs={{0,2},{1,3},{2,0},{3,1},{4,6},{5,7},{6,4},{7,5},{8,10},{9,11},{10,... | collective-permute-start | bytes 417800 | tf_op jit(solution)/shard_map/ppermute | solution.py:374
  19.6 7.0 %collective-permute-start.7 = (bf16[272,256]{1,0:T(8,128)(2,1)S(1)}, bf16[272,256]{1,0:T(8,128)(2,1)S(1)}, u32[]{:S(2)}, u32[]{:S(2)}) collective-permute-start(bf16[272,256]{1,0:T(8,128)(2,1)S(1)} %get-tuple-element.74), channel_id=1, source_target_pairs={{0,6},{1,7},{2,4},{3,5},{4,2},{5,3},{6,0},{7,1},{8,14},{9,15},{10,... | collective-permute-start | bytes 417800 | tf_op jit(solution)/shard_map/ppermute | solution.py:374
  20.1 4.4 %collective-permute-start.8 = (bf16[128,256]{1,0:T(8,128)(2,1)S(1)}, bf16[128,256]{1,0:T(8,128)(2,1)S(1)}, u32[]{:S(2)}, u32[]{:S(2)}) collective-permute-start(bf16[128,256]{1,0:T(8,128)(2,1)S(1)} %get-tuple-element.75), channel_id=1, source_target_pairs={{0,8},{4,12},{8,0},{12,4},{16,24},{20,28},{24,16},{28,20},{1,9},{5... | collective-permute-start | bytes 196616 | tf_op jit(solution)/shard_map/ppermute | solution.py:407
  20.5 5.2 %collective-permute-start.9 = (bf16[128,256]{1,0:T(8,128)(2,1)S(1)}, bf16[128,256]{1,0:T(8,128)(2,1)S(1)}, u32[]{:S(2)}, u32[]{:S(2)}) collective-permute-start(bf16[128,256]{1,0:T(8,128)(2,1)S(1)} %get-tuple-element.76), channel_id=1, source_target_pairs={{0,16},{4,20},{8,24},{12,28},{16,0},{20,4},{24,8},{28,12},{1,17},{... | collective-permute-start | bytes 196616 | tf_op jit(solution)/shard_map/ppermute | solution.py:407
  26.8 6.1 %collective-permute-start.10 = (bf16[144,256]{1,0:T(8,128)(2,1)S(1)}, bf16[144,256]{1,0:T(8,128)(2,1)S(1)}, u32[]{:S(2)}, u32[]{:S(2)}) collective-permute-start(bf16[144,256]{1,0:T(8,128)(2,1)S(1)} %get-tuple-element.77.refs_0_.own_ref), channel_id=1, source_target_pairs={{0,16},{1,17},{2,18},{3,19},{4,20},{5,21},{6,22},{7,23},{8,24},{9,... | collective-permute-start | bytes 221192 | tf_op jit(solution)/shard_map/ppermute | solution.py:374
  27.2 4.6 %collective-permute-start.11 = (bf16[128,256]{1,0:T(8,128)(2,1)S(1)}, bf16[128,256]{1,0:T(8,128)(2,1)S(1)}, u32[]{:S(2)}, u32[]{:S(2)}) collective-permute-start(bf16[128,256]{1,0:T(8,128)(2,1)S(1)} %get-tuple-element.78.own_ref), channel_id=1, source_target_pairs={{0,8},{1,9},{2,10},{3,11},{4,12},{5,13},{6,14},{7,15},{8,0},{9,1},... | collective-permute-start | bytes 196616 | tf_op jit(solution)/shard_map/ppermute | solution.py:374
  32.9 5.3 %collective-permute-start.12 = (bf16[144,256]{1,0:T(8,128)(2,1)S(1)}, bf16[144,256]{1,0:T(8,128)(2,1)S(1)}, u32[]{:S(2)}, u32[]{:S(2)}) collective-permute-start(bf16[144,256]{1,0:T(8,128)(2,1)S(1)} %shard_map.226.refs_0_.own_ref), channel_id=1, source_target_pairs={{0,8},{1,9},{2,10},{3,11},{4,12},{5,13},{6,14},{7,15},{8,0},{9,1},... | collective-permute-start | bytes 221192 | tf_op jit(solution)/shard_map/ppermute | solution.py:374
  33.0 5.2 %collective-permute-start.13 = (bf16[128,256]{1,0:T(8,128)(2,1)S(1)}, bf16[128,256]{1,0:T(8,128)(2,1)S(1)}, u32[]{:S(2)}, u32[]{:S(2)}) collective-permute-start(bf16[128,256]{1,0:T(8,128)(2,1)S(1)} %shard_map.225.refs_0_.own_ref), channel_id=1, source_target_pairs={{0,16},{1,17},{2,18},{3,19},{4,20},{5,21},{6,22},{7,23},{8,24},{9,... | collective-permute-start | bytes 196616 | tf_op jit(solution)/shard_map/ppermute | solution.py:374
  38.3 5.9 %collective-permute-start.19 = (bf16[256,256]{1,0:T(8,128)(2,1)S(1)}, bf16[256,256]{1,0:T(8,128)(2,1)S(1)}, u32[]{:S(2)}, u32[]{:S(2)}) collective-permute-start(bf16[256,256]{1,0:T(8,128)(2,1)S(1)} %shard_map.230.refs_0_), channel_id=1, source_target_pairs={{0,6},{1,7},{2,4},{3,5},{4,2},{5,3},{6,0},{7,1},{8,14},{9,15},{10,... | collective-permute-start | bytes 393224 | tf_op jit(solution)/shard_map/ppermute | solution.py:374
  40.8 5.0 %collective-permute-start.17 = (bf16[256,256]{1,0:T(8,128)(2,1)S(1)}, bf16[256,256]{1,0:T(8,128)(2,1)S(1)}, u32[]{:S(2)}, u32[]{:S(2)}) collective-permute-start(bf16[256,256]{1,0:T(8,128)(2,1)S(1)} %shard_map.230.refs_0_), channel_id=1, source_target_pairs={{0,4},{1,5},{2,6},{3,7},{4,0},{5,1},{6,2},{7,3},{8,12},{9,13},{10,... | collective-permute-start | bytes 393224 | tf_op jit(solution)/shard_map/ppermute | solution.py:374
  41.3 5.0 %collective-permute-start.15 = (bf16[256,256]{1,0:T(8,128)(2,1)S(1)}, bf16[256,256]{1,0:T(8,128)(2,1)S(1)}, u32[]{:S(2)}, u32[]{:S(2)}) collective-permute-start(bf16[256,256]{1,0:T(8,128)(2,1)S(1)} %shard_map.230.refs_0_), channel_id=1, source_target_pairs={{0,2},{1,3},{2,0},{3,1},{4,6},{5,7},{6,4},{7,5},{8,10},{9,11},{10,... | collective-permute-start | bytes 393224 | tf_op jit(solution)/shard_map/ppermute | solution.py:374
  41.8 5.5 %collective-permute-start.14 = (bf16[256,256]{1,0:T(8,128)(2,1)S(1)}, bf16[256,256]{1,0:T(8,128)(2,1)S(1)}, u32[]{:S(2)}, u32[]{:S(2)}) collective-permute-start(bf16[256,256]{1,0:T(8,128)(2,1)S(1)} %shard_map.230.refs_0_), channel_id=1, source_target_pairs={{0,1},{1,0},{2,3},{3,2},{4,5},{5,4},{6,7},{7,6},{8,9},{9,8},{10,11... | collective-permute-start | bytes 393224 | tf_op jit(solution)/shard_map/ppermute | solution.py:374
  44.2 3.1 %collective-permute-start.20 = (bf16[256,256]{1,0:T(8,128)(2,1)S(1)}, bf16[256,256]{1,0:T(8,128)(2,1)S(1)}, u32[]{:S(2)}, u32[]{:S(2)}) collective-permute-start(bf16[256,256]{1,0:T(8,128)(2,1)S(1)} %shard_map.231.refs_3_), channel_id=1, source_target_pairs={{0,1},{1,0},{2,3},{3,2},{4,5},{5,4},{6,7},{7,6},{8,9},{9,8},{10,11... | collective-permute-start | bytes 393224 | tf_op jit(solution)/shard_map/ppermute | solution.py:374
  45.8 1.6 %collective-permute-start.18 = (bf16[256,256]{1,0:T(8,128)(2,1)S(1)}, bf16[256,256]{1,0:T(8,128)(2,1)S(1)}, u32[]{:S(2)}, u32[]{:S(2)}) collective-permute-start(bf16[256,256]{1,0:T(8,128)(2,1)S(1)} %collective-permute-done.17.refs_2_), channel_id=1, source_target_pairs={{0,1},{1,0},{2,3},{3,2},{4,5},{5,4},{6,7},{7,6},{8,9},{9,8},{10,11... | collective-permute-start | bytes 393224 | tf_op jit(solution)/shard_map/ppermute | solution.py:374
  46.3 1.3 %collective-permute-start.16 = (bf16[256,256]{1,0:T(8,128)(2,1)S(1)}, bf16[256,256]{1,0:T(8,128)(2,1)S(1)}, u32[]{:S(2)}, u32[]{:S(2)}) collective-permute-start(bf16[256,256]{1,0:T(8,128)(2,1)S(1)} %collective-permute-done.15.refs_1_), channel_id=1, source_target_pairs={{0,1},{1,0},{2,3},{3,2},{4,5},{5,4},{6,7},{7,6},{8,9},{9,8},{10,11... | collective-permute-start | bytes 393224 | tf_op jit(solution)/shard_map/ppermute | solution.py:374
